TPU v7x, 256 devices: a whole 4x4x8 slice. The times are simulated.
256 devices in a mesh: mem: 16 (over x_hi, y, core), tile: 16 (over z, x_lo).
Axes of the slice: x: 4 (x_hi: 2, x_lo: 2; x = x_hi * 2 + x_lo), y: 4, z: 8, core: 2. Of those that a mesh axis runs over, the one named last changes fastest.
Arguments:
- perturb: bfloat16 [32, 6, 16, 256, 128], P('mem', None, None, 'tile'), may hold values from -2.5 to 2.5
- alpha: float32 [32, 16, 256, 128], P('mem', None, 'tile'), may hold values from -5 to 5
- alpha_mom: float32 [32, 16, 256, 128], P('mem', None, 'tile'), may hold values from -6 to 6
- static_ctl: float32 [6, 16, 256, 128], P(None, None, 'tile'), may hold values from -6 to 6
- static_mom: float32 [6, 16, 256, 128], P(None, 'mem', 'tile'), may hold values from -6 to 6
- loc_coef: float32 [2, 256, 128], P(None, 'tile'), may hold values from 0.04 to 0.36, as said below
- static_coef: float32 [2, 256, 128], P(None, 'tile'), may hold values from 0.04 to 0.36, as said below
- obs_cell: int32 [16, 1024], P('tile'), may hold values from 0 to 2047
- obs_mask: int32 [16, 1024], P('tile'), may hold values 0 or 1
- obs_value: float32 [6, 16, 16, 1024], P(None, None, 'tile'), may hold values from -6 to 6
- obs_weight: float32 [6, 16, 16, 1024], P(None, None, 'tile'), may hold values from 0.3 to 3
Outputs:
- new_alpha: float32 [32, 16, 256, 128], P('mem', None, 'tile')
- new_alpha_mom: float32 [32, 16, 256, 128], P('mem', None, 'tile')
- new_static: float32 [6, 16, 256, 128], P(None, 'mem', 'tile')
- new_static_mom: float32 [6, 16, 256, 128], P(None, 'mem', 'tile')
Inputs may be any that keep to these rules, and one draw needn't show every extreme that they name: `obs_cell`: slots of a tile may name the same cell. `loc_coef`: index 0 lies in 0.18 to 0.36, index 1 in 0.04 to 0.08. `static_coef`: index 0 lies in 0.18 to 0.36, index 1 in 0.04 to 0.08.
All inputs are finite; a program needn't handle non-finite values. No bound on the sum of `obs_mask` on one device may be relied on, other than what follows from the above.
Results may differ from a plain program's by a relative error of at most 0.0003.
Values sent between devices are 32-bit elements; how exact they have to be, the bound alone decides.
No kernel may reach another device: no remote copies, remote signals or barrier semaphores. Data moves between devices by JAX's collectives and lax.ppermute only.
A program may use at most 64 MiB of HBM per device.

v0:
```python
import jax
import jax.numpy as jnp
from jax import lax
from jax.sharding import PartitionSpec as P

LEVELS = 16
DIFF_STEPS = 12


momentum_rate = 0.9
step_rate = 0.5


def extended(block, sides, width):
    for axis, dim in sides:
        count = lax.axis_size(axis)
        forward = [(i, i + 1) for i in range(count - 1)]
        backward = [(target, source) for source, target in forward]
        low = lax.ppermute(
            lax.slice_in_dim(block, block.shape[dim] - width, None, axis=dim), axis, forward
        )
        high = lax.ppermute(lax.slice_in_dim(block, 0, width, axis=dim), axis, backward)
        block = jnp.concatenate([low, block, high], axis=dim)
    return block


def split_up(shard, dim, count):
    before, after = (shard.shape[:dim], shard.shape[dim + 1 :])
    return jnp.moveaxis(shard.reshape(*before, count, -1, *after), dim, 0)


def summed_on_arrival(shard, axis, dim):
    count = lax.axis_size(axis)
    parts = lax.all_to_all(split_up(shard, dim, count), axis, 0, 0, tiled=True)
    return jnp.sum(parts, axis=0)


def joined_along(parts, dim):
    parts = jnp.moveaxis(parts, 0, dim)
    lengths = parts.shape
    return parts.reshape(*lengths[:dim], lengths[dim] * lengths[dim + 1], *lengths[dim + 2 :])


def sent_to_all(shard, axis):
    copies = jnp.broadcast_to(shard, (lax.axis_size(axis), *shard.shape))
    return lax.all_to_all(copies, axis, split_axis=0, concat_axis=0, tiled=True)


def gathered_copies(shard, axis, dim):
    return joined_along(sent_to_all(shard, axis), dim)


def smooth(padded, factors):
    faces_x = factors[0]
    faces_y = factors[1]
    flux_x = faces_x[:-1] * (padded[..., 1:, :] - padded[..., :-1, :])
    middle = padded[..., 1:-1, :]
    shifted = jnp.concatenate([middle[..., 1:], jnp.zeros_like(middle[..., :1])], axis=-1)
    flux_y = faces_y[1:-1] * (shifted - middle)
    flux_left = jnp.concatenate([jnp.zeros_like(flux_y[..., :1]), flux_y[..., :-1]], axis=-1)
    return middle + (flux_x[..., 1:, :] - flux_x[..., :-1, :]) + (flux_y - flux_left)


def smooth_parts(padded, factor_sets, counts, first_row, last_cut):
    pieces = []
    start = 0
    for number in range(len(counts)):
        part = padded[start : start + counts[number]]
        factors = factor_sets[number]
        pieces.append(smooth(part, factors[:, first_row : factors.shape[1] - last_cut]))
        start = start + counts[number]
    return jnp.concatenate(pieces, axis=0)


def diffuse_many(fields, factor_sets):
    height = fields[0].shape[-2]
    width = fields[0].shape[-1]
    flats = [field.reshape(-1, height, width) for field in fields]
    counts = [flat.shape[0] for flat in flats]
    joined = jnp.concatenate(flats, axis=0)
    extent = height * lax.axis_size("tile")
    offset = lax.axis_index("tile") * height
    padded = extended(joined, (("tile", 1),), DIFF_STEPS)
    for turn in range(DIFF_STEPS):
        span_rows = height + 2 * (DIFF_STEPS - turn - 1)
        position = offset - (DIFF_STEPS - turn - 1) + lax.iota(jnp.int32, span_rows)
        inside = ((position >= 0) & (position < extent)).astype(jnp.float32)
        padded = smooth_parts(padded, factor_sets, counts, turn, turn) * inside[:, None]
    outputs = []
    start = 0
    for number in range(len(fields)):
        outputs.append(padded[start : start + counts[number]].reshape(fields[number].shape))
        start = start + counts[number]
    return outputs


def diffuse_two(first, first_factors, second, second_factors):
    return diffuse_many([first, second], [first_factors, second_factors])


def innovations(increment, stations, active, observed, weights):
    layout = increment.shape
    flattened = increment.reshape(layout[0], layout[1], layout[2] * layout[3])
    picked = jnp.take(flattened, stations[0], axis=2)
    misfit = active[0].astype(jnp.float32) * weights[:, :, 0] * (picked - observed[:, :, 0])
    return jnp.zeros_like(flattened).at[:, :, stations[0]].add(misfit).reshape(layout)


def local(
    perturb,
    alpha,
    alpha_mom,
    static_ctl,
    static_mom,
    loc_coef,
    static_coef,
    obs_cell,
    obs_mask,
    obs_value,
    obs_weight,
):
    coef_both = jnp.concatenate([loc_coef, static_coef], axis=0)
    factors = extended(coef_both, (("tile", 1),), DIFF_STEPS)
    loc_factors = factors[:2]
    static_factors = factors[2:]
    level_share = LEVELS // lax.axis_size("mem")
    first_level = lax.axis_index("mem") * level_share
    own_ctl = lax.dynamic_slice_in_dim(static_ctl, first_level, level_share, 1)
    localized, static_part = diffuse_two(alpha, loc_factors, own_ctl, static_factors)
    ensemble = jnp.zeros(static_ctl.shape, jnp.float32)
    for member in range(alpha.shape[0]):
        ensemble = ensemble + localized[member][None] * perturb[member]
    combined = summed_on_arrival(ensemble, "mem", 1)
    increment = combined + static_part
    own_values = lax.dynamic_slice_in_dim(obs_value, first_level, level_share, 1)
    own_weights = lax.dynamic_slice_in_dim(obs_weight, first_level, level_share, 1)
    grad_field = innovations(increment, obs_cell, obs_mask, own_values, own_weights)
    full_grad = gathered_copies(grad_field, "mem", 1)
    projected = jnp.sum(perturb * full_grad[None], axis=1)
    grad_smooth, projected_smooth = diffuse_two(grad_field, static_factors, projected, loc_factors)
    static_grad = own_ctl + grad_smooth
    alpha_grad = alpha + projected_smooth
    new_alpha_mom = momentum_rate * alpha_mom + alpha_grad
    new_alpha = alpha - step_rate * new_alpha_mom
    new_static_mom = momentum_rate * static_mom + static_grad
    new_static = own_ctl - step_rate * new_static_mom
    return (new_alpha, new_alpha_mom, new_static, new_static_mom)


def solution(mesh):
    return jax.shard_map(
        local,
        mesh=mesh,
        in_specs=(
            P("mem", None, None, "tile", None),
            P("mem", None, "tile", None),
            P("mem", None, "tile", None),
            P(None, None, "tile", None),
            P(None, "mem", "tile", None),
            P(None, "tile", None),
            P(None, "tile", None),
            P("tile", None),
            P("tile", None),
            P(None, None, "tile", None),
            P(None, None, "tile", None),
        ),
        out_specs=(
            P("mem", None, "tile", None),
            P("mem", None, "tile", None),
            P(None, "mem", "tile", None),
            P(None, "mem", "tile", None),
        ),
        check_vma=False,
    )
```

profile of v0, /device:TPU:128, one launch (start us, length us, event | category | flops | bytes accessed | tf_op | source)
XLA Modules:
  0.0 136.1 jit_solution(170328679139171830)
XLA Ops:
  0.7 0.9 dynamic-slice_bitcast_fusion
  1.6 1.1 slice_maximum_fusion.1
  2.6 3.4 %collective-permute-start = (f32[38,12,128]{2,1,0:T(8,128)S(1)}, f32[38,12,128]{2,1,0:T(8,128)S(1)}, u32[]{:S(2)}, u32[]{:S(2)}) collective-permute-start(f32[38,12,128]{2,1,0:T(8,128)S(1)} %get-tuple-element.14), channel_id=1, source_target_pairs={{0,1},{1,2},{2,3},{3,4},{4,5},{5,6},{6,7},{7,8},{8,9},{9,10},{10,1... | collective-permute-start | bytes 700424 | tf_op jit(solution)/shard_map/ppermute | solution.py:19
  6.0 4.6 %collective-permute-start.1 = (f32[38,12,128]{2,1,0:T(8,128)S(1)}, f32[38,12,128]{2,1,0:T(8,128)S(1)}, u32[]{:S(2)}, u32[]{:S(2)}) collective-permute-start(f32[38,12,128]{2,1,0:T(8,128)S(1)} %get-tuple-element.15), channel_id=1, source_target_pairs={{1,0},{2,1},{3,2},{4,3},{5,4},{6,5},{7,6},{8,7},{9,8},{10,9},{11,1... | collective-permute-start | bytes 700424 | tf_op jit(solution)/shard_map/ppermute | solution.py:22
  10.6 1.9 %collective-permute-start.2 = (f32[4,12,128]{2,1,0:T(8,128)S(1)}, f32[4,12,128]{2,1,0:T(8,128)S(1)}, u32[]{:S(2)}, u32[]{:S(2)}) collective-permute-start(f32[4,12,128]{2,1,0:T(8,128)S(1)} %get-tuple-element.62), channel_id=1, source_target_pairs={{0,1},{1,2},{2,3},{3,4},{4,5},{5,6},{6,7},{7,8},{8,9},{9,10},{10,1... | collective-permute-start | bytes 73736 | tf_op jit(solution)/shard_map/ppermute | solution.py:19
  12.6 6.0 %collective-permute-start.3 = (f32[4,12,128]{2,1,0:T(8,128)S(1)}, f32[4,12,128]{2,1,0:T(8,128)S(1)}, u32[]{:S(2)}, u32[]{:S(2)}) collective-permute-start(f32[4,12,128]{2,1,0:T(8,128)S(1)} %get-tuple-element.63), channel_id=1, source_target_pairs={{1,0},{2,1},{3,2},{4,3},{5,4},{6,5},{7,6},{8,7},{9,8},{10,9},{11,1... | collective-permute-start | bytes 73736 | tf_op jit(solution)/shard_map/ppermute | solution.py:22
  19.1 1.6 %collective-permute-done.2 = f32[4,12,128]{2,1,0:T(8,128)S(1)} collective-permute-done((f32[4,12,128]{2,1,0:T(8,128)S(1)}, f32[4,12,128]{2,1,0:T(8,128)S(1)}, u32[]{:S(2)}, u32[]{:S(2)}) %collective-permute-start.2) | collective-permute-done | bytes 24608 | tf_op jit(solution)/shard_map/ppermute | solution.py:19
  20.7 3.1 %collective-permute-done.3 = f32[4,12,128]{2,1,0:T(8,128)S(1)} collective-permute-done((f32[4,12,128]{2,1,0:T(8,128)S(1)}, f32[4,12,128]{2,1,0:T(8,128)S(1)}, u32[]{:S(2)}, u32[]{:S(2)}) %collective-permute-start.3) | collective-permute-done | bytes 24608 | tf_op jit(solution)/shard_map/ppermute | solution.py:22
  25.1 0.3 fusion.20
  26.3 0.3 fusion.17
  27.6 0.3 fusion.14
  29.8 0.3 fusion.42
  30.9 0.3 fusion.39
  32.0 0.3 fusion.36
  37.1 1.0 fusion.1
  38.1 7.2 %all-to-all-start = ((f32[16,6,1,16,128]{4,3,1,2,0:T(8,128)}), f32[16,6,1,16,128]{4,3,1,2,0:T(8,128)S(1)}, u32[]{:S(2)}, u32[]{:S(2)}) async-start(f32[16,6,1,16,128]{4,3,1,2,0:T(8,128)} %fusion.1), calls=%async_computation | async-start | bytes 1572864 | tf_op jit(solution)/shard_map/all_to_all | solution.py:34
  45.3 0.8 constant_dynamic-slice_fusion
  46.0 1.0 copy.25
  47.1 1.0 copy.29
  48.1 0.6 convert_element_type.135
  48.7 0.6 compare_and_fusion
  49.3 0.6 broadcast_clamp_fusion
  49.9 10.5 %all-to-all-done = f32[16,6,1,16,128]{4,3,1,2,0:T(8,128)S(1)} async-done(((f32[16,6,1,16,128]{4,3,1,2,0:T(8,128)}), f32[16,6,1,16,128]{4,3,1,2,0:T(8,128)S(1)}, u32[]{:S(2)}, u32[]{:S(2)}) %all-to-all-start) | async-done | bytes 786464 | tf_op jit(solution)/shard_map/all_to_all | solution.py:34
  60.5 0.4 copy.28
  60.9 10.2 %scatter_custom_fusion = f32[6,2048]{0,1:T(8,128)S(1)} fusion(s32[1024]{0:T(1024)} %bitcast.265, f32[6,1,1,1024]{0,3,2,1:T(8,128)} %copy.29, f32[6,1,1,1024]{0,3,2,1:T(8,128)} %copy.25, f32[]{:T(128)} %constant.23.clone.1, f32[]{:T(128)} %constant.42.clone.1, f32[1024]{0:T(1024)} %bitcast.262, pred[1024]{0:T(1024)(128)(4,1)} %compare_and_fusion, ...), kind=kCustom, calls=%fused_computation.103 | custom fusion | flops 30720 | bytes 1157120 | tf_op jit(solution)/shard_map/scatter-add | solution.py:106
  71.1 0.3 copy.32
  71.5 17.8 %all_to_all.10 = f32[16,6,1,16,128]{4,3,1,2,0:T(8,128)S(1)} all-to-all(f32[16,6,1,16,128]{4,3,1,2,0:T(8,128)S(1)} %broadcast_in_dim.14), channel_id=1, replica_groups=mesh['mem'=16,'tile'=16] {'mem'}, dimensions={0} | all-to-all | bytes 1572864 | tf_op jit(solution)/shard_map/all_to_all | solution.py:46
  89.6 1.9 %collective-permute-start.4 = (f32[38,12,128]{2,1,0:T(8,128)S(1)}, f32[38,12,128]{2,1,0:T(8,128)S(1)}, u32[]{:S(2)}, u32[]{:S(2)}) collective-permute-start(f32[38,12,128]{2,1,0:T(8,128)S(1)} %get-tuple-element.10), channel_id=1, source_target_pairs={{0,1},{1,2},{2,3},{3,4},{4,5},{5,6},{6,7},{7,8},{8,9},{9,10},{10,1... | collective-permute-start | bytes 700424 | tf_op jit(solution)/shard_map/ppermute | solution.py:19
  91.5 6.0 %collective-permute-start.5 = (f32[38,12,128]{2,1,0:T(8,128)S(1)}, f32[38,12,128]{2,1,0:T(8,128)S(1)}, u32[]{:S(2)}, u32[]{:S(2)}) collective-permute-start(f32[38,12,128]{2,1,0:T(8,128)S(1)} %get-tuple-element.11), channel_id=1, source_target_pairs={{1,0},{2,1},{3,2},{4,3},{5,4},{6,5},{7,6},{8,7},{9,8},{10,9},{11,1... | collective-permute-start | bytes 700424 | tf_op jit(solution)/shard_map/ppermute | solution.py:22
  97.5 7.2 %collective-permute-done.4 = f32[38,12,128]{2,1,0:T(8,128)S(1)} collective-permute-done((f32[38,12,128]{2,1,0:T(8,128)S(1)}, f32[38,12,128]{2,1,0:T(8,128)S(1)}, u32[]{:S(2)}, u32[]{:S(2)}) %collective-permute-start.4) | collective-permute-done | bytes 233504 | tf_op jit(solution)/shard_map/ppermute | solution.py:19
  104.7 4.1 %collective-permute-done.5 = f32[38,12,128]{2,1,0:T(8,128)S(1)} collective-permute-done((f32[38,12,128]{2,1,0:T(8,128)S(1)}, f32[38,12,128]{2,1,0:T(8,128)S(1)}, u32[]{:S(2)}, u32[]{:S(2)}) %collective-permute-start.5) | collective-permute-done | bytes 233504 | tf_op jit(solution)/shard_map/ppermute | solution.py:22
  109.7 0.3 fusion.10
  110.0 0.3 copy-done.82
  111.2 0.3 fusion.7
  111.5 0.3 copy-done.80
  112.7 0.3 fusion.4
  113.9 0.6 copy-done.20
  114.7 0.3 fusion.33
  115.0 0.3 copy-done.76
  115.6 0.5 copy-done.18
  116.4 0.6 copy-done.16
  117.5 0.3 copy-done.74
  118.1 0.5 copy-done.14
  118.9 0.6 copy-done.12
  120.0 0.3 copy-done.72
  120.6 0.5 copy-done.10
  121.4 0.6 copy-done.8
  122.5 0.3 copy-done.70
  123.1 0.5 copy-done.6
  123.9 0.4 copy-done.50
  124.9 0.4 copy-done.68
  125.5 0.5 copy-done.48
  126.3 0.4 copy-done.46
  127.2 0.4 copy-done.66
  127.8 0.5 copy-done.44
  128.6 0.4 copy-done.42
  129.5 0.4 copy-done.64
  130.0 0.5 copy-done.40
  130.8 0.4 copy-done.38
  131.7 0.4 copy-done.62
  132.4 0.3 copy-done.36
  133.2 0.4 copy-done.84
  133.8 1.4 %multiply_subtract_fusion.1 = (f32[6,1,16,128]{3,2,1,0:T(8,128)}, f32[6,1,16,128]{3,2,1,0:T(8,128)}) fusion(f32[6,16,16,128]{3,2,1,0:T(8,128)} %param.14, s32[]{:T(128)S(6)} %select_n.35, f32[38,16,128]{2,1,0:T(8,128)S(1)} %maximum_multiply_fusion.23, f32[6,1,16,128]{3,2,1,0:T(8,128)S(1)} %copy-done.55), kind=kLoop, calls=%fused_computation.343 | loop fusion | flops 61440 | bytes 245764 | tf_op jit(solution)/shard_map/sub | solution.py:146
  135.3 0.8 multiply_subtract_fusion
  (403 shorter events, 22.0 us)
Async XLA Ops:
  0.6 10.0 %copy-start.56 = (f32[2,16,128]{2,1,0:T(8,128)S(1)}, f32[2,16,128]{2,1,0:T(8,128)}, u32[]{:S(2)}) copy-start(f32[2,16,128]{2,1,0:T(8,128)} %param.16) | copy-start | bytes 49156
  0.6 10.0 %copy-start.57 = (f32[2,16,128]{2,1,0:T(8,128)S(1)}, f32[2,16,128]{2,1,0:T(8,128)}, u32[]{:S(2)}) copy-start(f32[2,16,128]{2,1,0:T(8,128)} %param.17) | copy-start | bytes 49156
  0.7 18.3 %copy-start = (bf16[2,6,16,16,128]{4,3,2,1,0:T(8,128)(2,1)S(1)}, bf16[2,6,16,16,128]{4,3,2,1,0:T(8,128)(2,1)}, u32[]{:S(2)}) copy-start(bf16[2,6,16,16,128]{4,3,2,1,0:T(8,128)(2,1)} %param.11) | copy-start | bytes 2359300
  2.6 21.8 %collective-permute-start = (f32[38,12,128]{2,1,0:T(8,128)S(1)}, f32[38,12,128]{2,1,0:T(8,128)S(1)}, u32[]{:S(2)}, u32[]{:S(2)}) collective-permute-start(f32[38,12,128]{2,1,0:T(8,128)S(1)} %get-tuple-element.14), channel_id=1, source_target_pairs={{0,1},{1,2},{2,3},{3,4},{4,5},{5,6},{6,7},{7,8},{8,9},{9,10},{10,1... | collective-permute-start | bytes 700424 | tf_op jit(solution)/shard_map/ppermute | solution.py:19
  6.0 18.4 %collective-permute-start.1 = (f32[38,12,128]{2,1,0:T(8,128)S(1)}, f32[38,12,128]{2,1,0:T(8,128)S(1)}, u32[]{:S(2)}, u32[]{:S(2)}) collective-permute-start(f32[38,12,128]{2,1,0:T(8,128)S(1)} %get-tuple-element.15), channel_id=1, source_target_pairs={{1,0},{2,1},{3,2},{4,3},{5,4},{6,5},{7,6},{8,7},{9,8},{10,9},{11,1... | collective-permute-start | bytes 700424 | tf_op jit(solution)/shard_map/ppermute | solution.py:22
  10.6 10.1 %collective-permute-start.2 = (f32[4,12,128]{2,1,0:T(8,128)S(1)}, f32[4,12,128]{2,1,0:T(8,128)S(1)}, u32[]{:S(2)}, u32[]{:S(2)}) collective-permute-start(f32[4,12,128]{2,1,0:T(8,128)S(1)} %get-tuple-element.62), channel_id=1, source_target_pairs={{0,1},{1,2},{2,3},{3,4},{4,5},{5,6},{6,7},{7,8},{8,9},{9,10},{10,1... | collective-permute-start | bytes 73736 | tf_op jit(solution)/shard_map/ppermute | solution.py:19
  12.6 11.2 %collective-permute-start.3 = (f32[4,12,128]{2,1,0:T(8,128)S(1)}, f32[4,12,128]{2,1,0:T(8,128)S(1)}, u32[]{:S(2)}, u32[]{:S(2)}) collective-permute-start(f32[4,12,128]{2,1,0:T(8,128)S(1)} %get-tuple-element.63), channel_id=1, source_target_pairs={{1,0},{2,1},{3,2},{4,3},{5,4},{6,5},{7,6},{8,7},{9,8},{10,9},{11,1... | collective-permute-start | bytes 73736 | tf_op jit(solution)/shard_map/ppermute | solution.py:22
  18.6 18.2 %copy-start.53 = (f32[16,128]{1,0:T(8,128)}, f32[16,128]{1,0:T(8,128)S(1)}, u32[]{:S(2)}) copy-start(f32[16,128]{1,0:T(8,128)S(1)} %slice_bitcast_fusion.45) | copy-start | bytes 24580
  18.7 18.3 %copy-start.83 = (f32[16]{0:T(128)}, f32[16]{0:T(128)S(1)}, u32[]{:S(2)}) copy-start(f32[16]{0:T(128)S(1)} %and_convert_fusion) | copy-start | bytes 196
  18.7 6.9 %copy-start.81 = (f32[38]{0:T(128)}, f32[38]{0:T(128)S(1)}, u32[]{:S(2)}) copy-start(f32[38]{0:T(128)S(1)} %and_convert_fusion.11) | copy-start | bytes 460
  18.7 8.1 %copy-start.79 = (f32[36]{0:T(128)}, f32[36]{0:T(128)S(1)}, u32[]{:S(2)}) copy-start(f32[36]{0:T(128)S(1)} %and_convert_fusion.10) | copy-start | bytes 436
  18.7 9.3 %copy-start.77 = (f32[34]{0:T(128)}, f32[34]{0:T(128)S(1)}, u32[]{:S(2)}) copy-start(f32[34]{0:T(128)S(1)} %and_convert_fusion.9) | copy-start | bytes 412
  18.8 10.4 %copy-start.75 = (f32[32]{0:T(128)}, f32[32]{0:T(128)S(1)}, u32[]{:S(2)}) copy-start(f32[32]{0:T(128)S(1)} %and_convert_fusion.8) | copy-start | bytes 388
  18.8 11.4 %copy-start.73 = (f32[30]{0:T(128)}, f32[30]{0:T(128)S(1)}, u32[]{:S(2)}) copy-start(f32[30]{0:T(128)S(1)} %and_convert_fusion.7) | copy-start | bytes 364
  18.8 12.5 %copy-start.71 = (f32[28]{0:T(128)}, f32[28]{0:T(128)S(1)}, u32[]{:S(2)}) copy-start(f32[28]{0:T(128)S(1)} %and_convert_fusion.6) | copy-start | bytes 340
  18.9 13.6 %copy-start.69 = (f32[26]{0:T(128)}, f32[26]{0:T(128)S(1)}, u32[]{:S(2)}) copy-start(f32[26]{0:T(128)S(1)} %and_convert_fusion.5) | copy-start | bytes 316
  18.9 14.5 %copy-start.67 = (f32[24]{0:T(128)}, f32[24]{0:T(128)S(1)}, u32[]{:S(2)}) copy-start(f32[24]{0:T(128)S(1)} %and_convert_fusion.4) | copy-start | bytes 292
  18.9 15.4 %copy-start.65 = (f32[22]{0:T(128)}, f32[22]{0:T(128)S(1)}, u32[]{:S(2)}) copy-start(f32[22]{0:T(128)S(1)} %and_convert_fusion.3) | copy-start | bytes 268
  18.9 16.3 %copy-start.63 = (f32[20]{0:T(128)}, f32[20]{0:T(128)S(1)}, u32[]{:S(2)}) copy-start(f32[20]{0:T(128)S(1)} %and_convert_fusion.2) | copy-start | bytes 244
  19.1 5.3 %copy-start.1 = (f32[2,16,16,128]{3,2,1,0:T(8,128)S(1)}, f32[2,16,16,128]{3,2,1,0:T(8,128)}, u32[]{:S(2)}) copy-start(f32[2,16,16,128]{3,2,1,0:T(8,128)} %param.12) | copy-start | bytes 786436
  19.1 17.0 %copy-start.61 = (f32[18]{0:T(128)}, f32[18]{0:T(128)S(1)}, u32[]{:S(2)}) copy-start(f32[18]{0:T(128)S(1)} %and_convert_fusion.1) | copy-start | bytes 220
  23.9 4.7 %copy-start.3 = (f32[32,128]{1,0:T(8,128)}, f32[32,128]{1,0:T(8,128)S(1)}, u32[]{:S(2)}) copy-start(f32[32,128]{1,0:T(8,128)S(1)} %get-tuple-element.44) | copy-start | bytes 49156
  23.9 5.0 %copy-start.19 = (f32[32,128]{1,0:T(8,128)}, f32[32,128]{1,0:T(8,128)S(1)}, u32[]{:S(2)}) copy-start(f32[32,128]{1,0:T(8,128)S(1)} %get-tuple-element.45) | copy-start | bytes 49156
  24.0 6.1 %copy-start.15 = (f32[30,128]{1,0:T(8,128)}, f32[30,128]{1,0:T(8,128)S(1)}, u32[]{:S(2)}) copy-start(f32[30,128]{1,0:T(8,128)S(1)} %get-tuple-element.41) | copy-start | bytes 46084
  24.0 5.7 %copy-start.17 = (f32[31,128]{1,0:T(8,128)}, f32[31,128]{1,0:T(8,128)S(1)}, u32[]{:S(2)}) copy-start(f32[31,128]{1,0:T(8,128)S(1)} %get-tuple-element.43) | copy-start | bytes 47620
  24.0 7.2 %copy-start.11 = (f32[28,128]{1,0:T(8,128)}, f32[28,128]{1,0:T(8,128)S(1)}, u32[]{:S(2)}) copy-start(f32[28,128]{1,0:T(8,128)S(1)} %get-tuple-element.37) | copy-start | bytes 43012
  24.0 6.7 %copy-start.13 = (f32[29,128]{1,0:T(8,128)}, f32[29,128]{1,0:T(8,128)S(1)}, u32[]{:S(2)}) copy-start(f32[29,128]{1,0:T(8,128)S(1)} %get-tuple-element.39) | copy-start | bytes 44548
  24.1 8.2 %copy-start.7 = (f32[26,128]{1,0:T(8,128)}, f32[26,128]{1,0:T(8,128)S(1)}, u32[]{:S(2)}) copy-start(f32[26,128]{1,0:T(8,128)S(1)} %get-tuple-element.33) | copy-start | bytes 39940
  24.1 7.8 %copy-start.9 = (f32[27,128]{1,0:T(8,128)}, f32[27,128]{1,0:T(8,128)S(1)}, u32[]{:S(2)}) copy-start(f32[27,128]{1,0:T(8,128)S(1)} %get-tuple-element.35) | copy-start | bytes 41476
  24.1 8.9 %copy-start.33 = (f32[24,128]{1,0:T(8,128)}, f32[24,128]{1,0:T(8,128)S(1)}, u32[]{:S(2)}) copy-start(f32[24,128]{1,0:T(8,128)S(1)} %get-tuple-element.28) | copy-start | bytes 36868
  24.1 9.2 %copy-start.49 = (f32[24,128]{1,0:T(8,128)}, f32[24,128]{1,0:T(8,128)S(1)}, u32[]{:S(2)}) copy-start(f32[24,128]{1,0:T(8,128)S(1)} %get-tuple-element.29) | copy-start | bytes 36868
  24.1 8.8 %copy-start.5 = (f32[25,128]{1,0:T(8,128)}, f32[25,128]{1,0:T(8,128)S(1)}, u32[]{:S(2)}) copy-start(f32[25,128]{1,0:T(8,128)S(1)} %get-tuple-element.31) | copy-start | bytes 38404
  24.2 9.7 %copy-start.29 = (f32[22,128]{1,0:T(8,128)}, f32[22,128]{1,0:T(8,128)S(1)}, u32[]{:S(2)}) copy-start(f32[22,128]{1,0:T(8,128)S(1)} %get-tuple-element.24) | copy-start | bytes 33796
  24.2 10.0 %copy-start.45 = (f32[22,128]{1,0:T(8,128)}, f32[22,128]{1,0:T(8,128)S(1)}, u32[]{:S(2)}) copy-start(f32[22,128]{1,0:T(8,128)S(1)} %get-tuple-element.25) | copy-start | bytes 33796
  24.2 9.6 %copy-start.31 = (f32[23,128]{1,0:T(8,128)}, f32[23,128]{1,0:T(8,128)S(1)}, u32[]{:S(2)}) copy-start(f32[23,128]{1,0:T(8,128)S(1)} %get-tuple-element.26) | copy-start | bytes 35332
  24.2 9.7 %copy-start.47 = (f32[23,128]{1,0:T(8,128)}, f32[23,128]{1,0:T(8,128)S(1)}, u32[]{:S(2)}) copy-start(f32[23,128]{1,0:T(8,128)S(1)} %get-tuple-element.27) | copy-start | bytes 35332
  24.2 10.6 %copy-start.25 = (f32[20,128]{1,0:T(8,128)}, f32[20,128]{1,0:T(8,128)S(1)}, u32[]{:S(2)}) copy-start(f32[20,128]{1,0:T(8,128)S(1)} %get-tuple-element.20) | copy-start | bytes 30724
  24.2 10.9 %copy-start.41 = (f32[20,128]{1,0:T(8,128)}, f32[20,128]{1,0:T(8,128)S(1)}, u32[]{:S(2)}) copy-start(f32[20,128]{1,0:T(8,128)S(1)} %get-tuple-element.21) | copy-start | bytes 30724
  24.3 10.4 %copy-start.27 = (f32[21,128]{1,0:T(8,128)}, f32[21,128]{1,0:T(8,128)S(1)}, u32[]{:S(2)}) copy-start(f32[21,128]{1,0:T(8,128)S(1)} %get-tuple-element.22) | copy-start | bytes 32260
  24.3 10.5 %copy-start.43 = (f32[21,128]{1,0:T(8,128)}, f32[21,128]{1,0:T(8,128)S(1)}, u32[]{:S(2)}) copy-start(f32[21,128]{1,0:T(8,128)S(1)} %get-tuple-element.23) | copy-start | bytes 32260
  24.3 11.4 %copy-start.21 = (f32[18,128]{1,0:T(8,128)}, f32[18,128]{1,0:T(8,128)S(1)}, u32[]{:S(2)}) copy-start(f32[18,128]{1,0:T(8,128)S(1)} %get-tuple-element.16) | copy-start | bytes 27652
  24.3 11.7 %copy-start.37 = (f32[18,128]{1,0:T(8,128)}, f32[18,128]{1,0:T(8,128)S(1)}, u32[]{:S(2)}) copy-start(f32[18,128]{1,0:T(8,128)S(1)} %get-tuple-element.17) | copy-start | bytes 27652
  24.3 11.3 %copy-start.23 = (f32[19,128]{1,0:T(8,128)}, f32[19,128]{1,0:T(8,128)S(1)}, u32[]{:S(2)}) copy-start(f32[19,128]{1,0:T(8,128)S(1)} %get-tuple-element.18) | copy-start | bytes 29188
  24.4 11.3 %copy-start.39 = (f32[19,128]{1,0:T(8,128)}, f32[19,128]{1,0:T(8,128)S(1)}, u32[]{:S(2)}) copy-start(f32[19,128]{1,0:T(8,128)S(1)} %get-tuple-element.19) | copy-start | bytes 29188
  24.4 12.1 %copy-start.35 = (f32[17,128]{1,0:T(8,128)}, f32[17,128]{1,0:T(8,128)S(1)}, u32[]{:S(2)}) copy-start(f32[17,128]{1,0:T(8,128)S(1)} %get-tuple-element.60) | copy-start | bytes 26116
  24.4 12.2 %copy-start.51 = (f32[17,128]{1,0:T(8,128)}, f32[17,128]{1,0:T(8,128)S(1)}, u32[]{:S(2)}) copy-start(f32[17,128]{1,0:T(8,128)S(1)} %get-tuple-element.61) | copy-start | bytes 26116
  38.1 10.0 %copy-start.60 = (s32[1,1024]{1,0:T(1,128)S(1)}, s32[1,1024]{1,0:T(1,128)}, u32[]{:S(2)}) copy-start(s32[1,1024]{1,0:T(1,128)} %param.19) | copy-start | bytes 12292
  38.1 10.6 %copy-start.58 = (s32[1,1024]{1,0:T(1,128)S(1)}, s32[1,1024]{1,0:T(1,128)}, u32[]{:S(2)}) copy-start(s32[1,1024]{1,0:T(1,128)} %param.18) | copy-start | bytes 12292
  38.1 22.3 %all-to-all-start = ((f32[16,6,1,16,128]{4,3,1,2,0:T(8,128)}), f32[16,6,1,16,128]{4,3,1,2,0:T(8,128)S(1)}, u32[]{:S(2)}, u32[]{:S(2)}) async-start(f32[16,6,1,16,128]{4,3,1,2,0:T(8,128)} %fusion.1), calls=%async_computation | async-start | bytes 1572864 | tf_op jit(solution)/shard_map/all_to_all | solution.py:34
  89.6 15.2 %collective-permute-start.4 = (f32[38,12,128]{2,1,0:T(8,128)S(1)}, f32[38,12,128]{2,1,0:T(8,128)S(1)}, u32[]{:S(2)}, u32[]{:S(2)}) collective-permute-start(f32[38,12,128]{2,1,0:T(8,128)S(1)} %get-tuple-element.10), channel_id=1, source_target_pairs={{0,1},{1,2},{2,3},{3,4},{4,5},{5,6},{6,7},{7,8},{8,9},{9,10},{10,1... | collective-permute-start | bytes 700424 | tf_op jit(solution)/shard_map/ppermute | solution.py:19
  91.5 17.3 %collective-permute-start.5 = (f32[38,12,128]{2,1,0:T(8,128)S(1)}, f32[38,12,128]{2,1,0:T(8,128)S(1)}, u32[]{:S(2)}, u32[]{:S(2)}) collective-permute-start(f32[38,12,128]{2,1,0:T(8,128)S(1)} %get-tuple-element.11), channel_id=1, source_target_pairs={{1,0},{2,1},{3,2},{4,3},{5,4},{6,5},{7,6},{8,7},{9,8},{10,9},{11,1... | collective-permute-start | bytes 700424 | tf_op jit(solution)/shard_map/ppermute | solution.py:22
  113.8 0.7 copy-start.20
  113.8 0.7 copy-start.4
  115.4 0.7 copy-start.18
  116.3 0.7 copy-start.16
  118.8 0.7 copy-start.12
  121.3 0.7 copy-start.8
  122.9 0.7 copy-start.6
  125.3 0.9 copy-start.32
  127.6 0.9 copy-start.28
  129.8 0.9 copy-start.24
  131.5 0.8 copy-start.52
  133.0 0.8 copy-start.55
  133.6 1.7 %copy-start.2 = (f32[2,16,16,128]{3,2,1,0:T(8,128)S(1)}, f32[2,16,16,128]{3,2,1,0:T(8,128)}, u32[]{:S(2)}) copy-start(f32[2,16,16,128]{3,2,1,0:T(8,128)} %param.13) | copy-start | bytes 786436
  (28 other events, 18.7 us)
where the time goes:
time: 138 us; the launch traced here: 136 us
  other arithmetic  33.3 us (24%)
  starting transfers between devices  31 us (22%)
  waiting for transfers between devices  26.5 us (19%)
  local copies, waits for them, and re-layouts  24.5 us (18%)
  blocking collectives  17.8 us (13%)
  between operations  3.06 us (2%)
    all_to_all x1, blocking collectives, sent_to_all(): return lax.all_to_all(copies, axis, split_axis=0, concat_axis=0, tiled=True)  17.8 us
    ppermute x3, starting transfers between devices, extended(): lax.ppermute(lax.slice_in_dim(block, 0, width, axis=dim), axis, backward)  16.6 us
    unnamed x171, local copies, waits for them, and re-layouts  12.9 us
    all_to_all x1, waiting for transfers between devices, summed_on_arrival(): parts = lax.all_to_all(split_up(shard, dim, count), axis, 0, 0, tiled=True)  10.5 us
    scatter-add x1, other arithmetic, innovations(): jnp.zeros_like(flattened).at[:, :, stations[0]].add(misfit).reshape(layout)  10.2 us
    ppermute x3, waiting for transfers between devices, extended(): lax.ppermute(lax.slice_in_dim(block, block.shape[dim] - width, None, axis...  8.76 us
    add x48, other arithmetic, smooth(): middle + (flux_x[..., 1:, :] - flux_x[..., :-1, :]) + (flux_y - flux_left)  8.41 us
    ppermute x3, starting transfers between devices, extended(): lax.ppermute(lax.slice_in_dim(block, block.shape[dim] - width, None, axis...  7.24 us
  transfers between devices with their start and end apart: 7, of which 5 were waited for; matrix products, arithmetic and copies ran while one was open for 4% of the time, Pallas kernels for 0%

commit v1 on v0

v1 whole, which is shorter than its diff:
```python
import functools

import jax
import jax.numpy as jnp
from jax import lax
from jax.experimental import pallas as pl
from jax.experimental.pallas import tpu as pltpu
from jax.sharding import PartitionSpec as P

STEPS = 12
ROWS = 16
LANES = 128
SPAN = ROWS + 2 * STEPS
VARS = 6
HALF = 8

momentum_rate = 0.9
step_rate = 0.5

VM = pl.BlockSpec(memory_space=pltpu.VMEM)
ANY = pl.BlockSpec(memory_space=pl.ANY)


def shape(*dims):
    return jax.ShapeDtypeStruct(dims, jnp.float32)


def call(body, name, ins, outs, scratch=(), flops=1000000):
    return pl.pallas_call(
        body,
        name=name,
        in_specs=list(ins),
        out_specs=[VM] * len(outs),
        out_shape=list(outs),
        scratch_shapes=list(scratch),
        compiler_params=pltpu.CompilerParams(vmem_limit_bytes=32 * 1024 * 1024),
        cost_estimate=pl.CostEstimate(flops=flops, bytes_accessed=1000000, transcendentals=0),
    )


def f32(*dims):
    return pltpu.VMEM(dims, jnp.float32)


def place():
    mem = lax.axis_index("mem")
    return mem // 8, (mem // 2) % 4, mem % 2


def pack_rows(load, width, forward, backward):
    for row in range(ROWS):
        value = load(row)
        if row >= ROWS - STEPS:
            at = (row - (ROWS - STEPS)) * width
            forward[at : at + width, :] = value
        if row < STEPS:
            backward[row * width : (row + 1) * width, :] = value


def build_coefs(low_x, mid_x, high_x, low_y, mid_y, high_y, raw, coefs):
    raw[0:8, :] = jnp.zeros((8, LANES), jnp.float32)
    raw[8:20, :] = low_x
    raw[20:36, :] = mid_x
    raw[36:48, :] = high_x
    raw[48:60, :] = low_y
    raw[60:76, :] = mid_y
    raw[76:88, :] = high_y
    extent = ROWS * lax.axis_size("tile")
    first = lax.axis_index("tile") * ROWS - STEPS
    at = first + lax.broadcasted_iota(jnp.int32, (SPAN, LANES), 0)
    lane = lax.broadcasted_iota(jnp.int32, (SPAN, LANES), 1)
    valid = (at >= 0) & (at < extent)
    below = jnp.where(valid, raw[8:48, :], 0.0)
    raw[8:48, :] = below
    above = jnp.where(valid, raw[7:47, :], 0.0)
    right = jnp.where(valid, raw[48:88, :], 0.0)
    left = jnp.where(lane > 0, pltpu.roll(right, 1, 1), 0.0)
    centre = 1.0 - below - above - right - left
    coefs[0:40, :] = jnp.where(valid, centre, 0.0)
    coefs[40:80, :] = jnp.where(at + 1 < extent, below, 0.0)
    coefs[80:120, :] = above
    coefs[120:160, :] = jnp.where(lane < LANES - 1, right, 0.0)
    coefs[160:200, :] = left


def diffuse(load, width, pitch, coefs, bufs, emit):
    for turn in range(STEPS):
        source = bufs[turn % 2]
        target = bufs[(turn + 1) % 2]
        if turn == 0:
            take = load
        else:
            take = lambda row: source[row * pitch : row * pitch + width, :]
        before = take(turn)
        here = take(turn + 1)
        for row in range(turn + 1, SPAN - 1 - turn):
            after = take(row + 1)
            new = coefs[row : row + 1, :] * here
            new = new + coefs[40 + row : 41 + row, :] * after
            new = new + coefs[80 + row : 81 + row, :] * before
            new = new + coefs[120 + row : 121 + row, :] * pltpu.roll(here, LANES - 1, 1)
            new = new + coefs[160 + row : 161 + row, :] * pltpu.roll(here, 1, 1)
            if turn == STEPS - 1:
                emit(row - STEPS, new)
            else:
                target[row * pitch : row * pitch + width, :] = new
            before = here
            here = after


def alpha_row(alpha, parity, row):
    parts = [alpha[pl.ds(m * 256 + parity * ROWS + row, HALF, stride=2 * ROWS), :] for m in range(2)]
    return jnp.concatenate(parts, axis=0)


def pack_body(alpha, loc, static_ctl, static_coef, a_f, a_b, b_f, b_b, c_f, c_b, field, sem):
    mem = lax.axis_index("mem")
    own = mem % 2
    fetch = pltpu.make_async_copy(static_ctl.at[:, mem], field.reshape(8, ROWS, LANES).at[0:VARS], sem)
    fetch.start()
    pack_rows(lambda row: alpha_row(alpha, 1 - own, row), 16, a_f, a_b)
    for k in range(2):
        a_f[192 + k * 12 : 204 + k * 12, :] = loc[k * 16 + 4 : k * 16 + 16, :]
        a_b[192 + k * 12 : 204 + k * 12, :] = loc[k * 16 : k * 16 + 12, :]
    pack_rows(lambda row: alpha_row(alpha, own, row), 16, b_f, b_b)
    fetch.wait()
    field[VARS * ROWS :, :] = static_coef[...]
    pack_rows(lambda row: field[pl.ds(row, 8, stride=ROWS), :], 8, c_f, c_b)


def halo_loader(low, high, middle, width):
    def load(row):
        if row < STEPS:
            return low[row * width : (row + 1) * width, :]
        if row < STEPS + ROWS:
            return middle(row - STEPS)
        at = (row - STEPS - ROWS) * width
        return high[at : at + width, :]

    return load


def first_body(alpha, low, high, loc, perturb, sums, coefs, raw, buf0, buf1, local):
    parity = 1 - lax.axis_index("mem") % 2
    build_coefs(
        low[192:204, :], loc[0:16, :], high[192:204, :],
        low[204:216, :], loc[16:32, :], high[204:216, :], raw, coefs,
    )

    def emit(row, value):
        local[pl.ds(row, 16, stride=ROWS), :] = value

    load = halo_loader(low, high, lambda row: alpha_row(alpha, parity, row), 16)
    diffuse(load, 16, 16, coefs, (buf0, buf1), emit)
    for s in range(HALF):
        level = 2 * s + parity
        for v in range(VARS):
            total = local[s * 16 : s * 16 + 16, :] * perturb[0, v, level].astype(jnp.float32)
            total = total + local[128 + s * 16 : 144 + s * 16, :] * perturb[1, v, level].astype(jnp.float32)
            sums[s, v] = total


def second_body(alpha, low, high, coefs, perturb, received, o0, o1, o2, o3, buf0, buf1, local):
    _, y, parity = place()

    def emit(row, value):
        local[pl.ds(row, 16, stride=ROWS), :] = value

    load = halo_loader(low, high, lambda row: alpha_row(alpha, parity, row), 16)
    diffuse(load, 16, 16, coefs, (buf0, buf1), emit)
    for k, out in enumerate((o0, o1, o2, o3)):
        for j in range(2):
            s = (y ^ k) + 4 * j
            level = 2 * s + parity
            first = local[pl.ds(pl.multiple_of(s * 16, 16), 16), :]
            other = local[pl.ds(pl.multiple_of(128 + s * 16, 16), 16), :]
            for v in range(VARS):
                total = first * perturb[0, v, level].astype(jnp.float32)
                total = total + other * perturb[1, v, level].astype(jnp.float32)
                out[j, v] = total + received[s, v]


def static_first_body(low, high, field, o0, out, coefs, raw, buf0, buf1, result):
    x, _, _ = place()
    build_coefs(
        low[pl.ds(6, 12, stride=8), :], field[96:112, :], high[pl.ds(6, 12, stride=8), :],
        low[pl.ds(7, 12, stride=8), :], field[112:128, :], high[pl.ds(7, 12, stride=8), :], raw, coefs,
    )

    def emit(row, value):
        result[pl.ds(row, 8, stride=ROWS), :] = value

    load = halo_loader(low, high, lambda row: field[pl.ds(row, 8, stride=ROWS), :], 8)
    diffuse(load, 8, 8, coefs, (buf0, buf1), emit)
    for j in range(2):
        for v in range(VARS):
            part = result[v * 16 : v * 16 + 16, :]
            out[j, v] = o0[j, v] + jnp.where(x == j, part, 0.0)


def prepare_body(cell, mask, value, weight, sums, held, sem):
    _, y, c = place()
    copies = []
    for j in range(2):
        level = 2 * y + c + 8 * j
        for k, source in enumerate((weight, value)):
            spot = held.reshape(2, 2, VARS, 8, LANES).at[k, j]
            copies.append(pltpu.make_async_copy(source.at[:, level], spot, sem.at[2 * j + k]))
    for copy in copies:
        copy.start()
    for copy in copies:
        copy.wait()
    pieces = []
    for a in range(8):
        part = held[pl.ds(a, 24, stride=8), :]
        scaled = part[0:12, :] * mask[a : a + 1, :].astype(jnp.float32)
        pieces.append(jnp.concatenate([scaled, scaled * part[12:24, :]], axis=0))
    both = jnp.concatenate(pieces, axis=1)
    top = both.astype(jnp.bfloat16)
    rest = both - top.astype(jnp.float32)
    mid = rest.astype(jnp.bfloat16)
    low = (rest - mid.astype(jnp.float32)).astype(jnp.bfloat16)
    stacked = jnp.concatenate([top, mid, low], axis=0)
    cells = jnp.concatenate([cell[a : a + 1, :] for a in range(8)], axis=1)
    for block in range(8):
        ids = block * 256 + lax.broadcasted_iota(jnp.int32, (256, 1024), 0)
        hit = jnp.where(ids == cells, 1.0, 0.0).astype(jnp.bfloat16)
        got = lax.dot_general(stacked, hit, (((1,), (1,)), ((), ())), preferred_element_type=jnp.float32)
        total = got[0:24, :] + got[24:48, :] + got[48:72, :]
        for r in range(2):
            sums[pl.ds(block * 2 + r, 24, stride=ROWS), :] = total[:, r * LANES : (r + 1) * LANES]


def gradient_body(mine, other, sums, grad, forward, backward):
    x, _, _ = place()
    total = mine[...] + other[...]
    grad[...] = sums[0:192, :] * total - sums[192:384, :]
    pack_rows(lambda row: grad[pl.ds(x * 96 + row, VARS, stride=ROWS), :], VARS, forward, backward)


def project_body(own, g0, g1, g2, g3, perturb, forward, backward, middle):
    _, y, c = place()
    parity = c if own else 1 - c
    for k, g in enumerate((g0, g1, g2, g3)):
        for j in range(2):
            s = (y ^ k) + 4 * j
            level = 2 * s + parity
            for m in range(2):
                total = perturb[m, 0, level].astype(jnp.float32) * g[j, 0]
                for v in range(1, VARS):
                    total = total + perturb[m, v, level].astype(jnp.float32) * g[j, v]
                middle[pl.ds(pl.multiple_of((m * HALF + s) * 16, 16), 16), :] = total
    pack_rows(lambda row: middle[pl.ds(row, 16, stride=ROWS), :], 16, forward, backward)


def third_body(low, high, middle, coefs, out, buf0, buf1):
    def emit(row, value):
        out[pl.ds(row, 16, stride=ROWS), :] = value

    load = halo_loader(low, high, lambda row: middle[pl.ds(row, 16, stride=ROWS), :], 16)
    diffuse(load, 16, 16, coefs, (buf0, buf1), emit)


def fourth_body(low, high, middle, coefs, done, alpha, mom, new_alpha, new_mom, buf0, buf1, out):
    third_body(low, high, middle, coefs, out, buf0, buf1)
    c = lax.axis_index("mem") % 2
    for source, parity in ((done, c), (out, 1 - c)):
        for m in range(2):
            for s in range(HALF):
                at = pl.ds(pl.multiple_of(m * 256 + (2 * s + parity) * 16, 16), 16)
                old = alpha[at, :]
                grad = old + source[(m * HALF + s) * 16 : (m * HALF + s) * 16 + 16, :]
                moved = momentum_rate * mom[at, :] + grad
                new_mom[at, :] = moved
                new_alpha[at, :] = old - step_rate * moved


def static_last_body(low, high, grad, coefs, field, mom, new_static, new_mom, buf0, buf1, result):
    x, _, _ = place()

    def emit(row, value):
        result[pl.ds(row, VARS, stride=ROWS), :] = value

    load = halo_loader(low, high, lambda row: grad[pl.ds(x * 96 + row, VARS, stride=ROWS), :], VARS)
    diffuse(load, VARS, 8, coefs, (buf0, buf1), emit)
    old = field[0:96, :]
    moved = momentum_rate * mom[...] + (old + result[...])
    new_mom[...] = moved
    new_static[...] = old - step_rate * moved


def local(
    perturb,
    alpha,
    alpha_mom,
    static_ctl,
    static_mom,
    loc_coef,
    static_coef,
    obs_cell,
    obs_mask,
    obs_value,
    obs_weight,
):
    tiles = lax.axis_size("tile")
    up = [(i, (i + 1) % tiles) for i in range(tiles)]
    down = [(target, source) for source, target in up]
    members = lax.axis_size("mem")

    def swap(value, bits):
        return lax.ppermute(value, "mem", [(i, i ^ bits) for i in range(members)])

    def halo(forward, backward):
        return lax.ppermute(forward, "tile", up), lax.ppermute(backward, "tile", down)

    alpha2 = alpha.reshape(512, LANES)
    mom2 = alpha_mom.reshape(512, LANES)
    loc2 = loc_coef.reshape(32, LANES)
    bufs16 = [f32(SPAN * 16, LANES), f32(SPAN * 16, LANES)]
    bufs8 = [f32(SPAN * 8, LANES), f32(SPAN * 8, LANES)]
    raw = f32(88, LANES)

    a_f, a_b, b_f, b_b, c_f, c_b, field = call(
        pack_body,
        "pack",
        [VM, VM, ANY, VM],
        [shape(216, LANES)] * 2 + [shape(192, LANES)] * 2 + [shape(96, LANES)] * 2 + [shape(128, LANES)],
        [pltpu.SemaphoreType.DMA],
    )(alpha2, loc2, static_ctl, static_coef.reshape(32, LANES))
    a_low, a_high = halo(a_f, a_b)
    b_low, b_high = halo(b_f, b_b)

    (sums,) = call(
        prepare_body,
        "prepare",
        [VM, VM, ANY, ANY],
        [shape(384, LANES)],
        [f32(192, LANES), pltpu.SemaphoreType.DMA((4,))],
        flops=1000000000,
    )(
        obs_cell.reshape(8, LANES),
        obs_mask.reshape(8, LANES),
        obs_value.reshape(VARS, 16, 8, LANES),
        obs_weight.reshape(VARS, 16, 8, LANES),
    )

    quarter = shape(2, VARS, ROWS, LANES)
    part_a, loc_k = call(
        first_body,
        "first",
        [VM] * 5,
        [shape(HALF, VARS, ROWS, LANES), shape(200, LANES)],
        [raw] + bufs16 + [f32(256, LANES)],
    )(alpha2, a_low, a_high, loc2, perturb)
    got = swap(part_a, 1)
    o0, o1, o2, o3 = call(
        second_body,
        "second",
        [VM] * 6,
        [quarter] * 4,
        bufs16 + [f32(256, LANES)],
    )(alpha2, b_low, b_high, loc_k, perturb, got)
    r1, r2, r3 = swap(o1, 2), swap(o2, 4), swap(o3, 6)
    c_low, c_high = halo(*lax.optimization_barrier((c_f, c_b, o0))[:2])
    o0s, static_k = call(
        static_first_body,
        "static_first",
        [VM] * 4,
        [quarter, shape(200, LANES)],
        [raw] + bufs8 + [f32(128, LANES)],
    )(c_low, c_high, field, o0)
    mine = (o0s + r1 + r2 + r3).reshape(192, LANES)
    other = swap(mine, 8)
    grad, g_f, g_b = call(
        gradient_body,
        "gradient",
        [VM] * 3,
        [shape(192, LANES), shape(72, LANES), shape(72, LANES)],
    )(mine, other, sums)
    full = (2, VARS, ROWS, LANES)
    gs = [grad.reshape(full)]
    gs = gs + [swap(grad, 2 * k).reshape(full) for k in range(1, 4)]
    ps = [swap(g, 1) for g in gs]
    g_low, g_high = halo(g_f, g_b)
    packed = [shape(192, LANES), shape(192, LANES), shape(256, LANES)]
    p_f, p_b, p_m = call(functools.partial(project_body, True), "project_own", [VM] * 5, packed)(*gs, perturb)
    p_low, p_high = halo(p_f, p_b)
    q_f, q_b, q_m = call(functools.partial(project_body, False), "project_other", [VM] * 5, packed)(*ps, perturb)
    q_low, q_high = halo(q_f, q_b)
    new_static, new_static_mom = call(
        static_last_body,
        "static_last",
        [VM] * 6,
        [shape(96, LANES)] * 2,
        bufs8 + [f32(96, LANES)],
    )(g_low, g_high, grad, static_k, field, static_mom.reshape(96, LANES))
    (done,) = call(third_body, "third", [VM] * 4, [shape(256, LANES)], bufs16)(p_low, p_high, p_m, loc_k)
    new_alpha, new_alpha_mom = call(
        fourth_body,
        "fourth",
        [VM] * 7,
        [shape(512, LANES)] * 2,
        bufs16 + [f32(256, LANES)],
    )(q_low, q_high, q_m, loc_k, done, alpha2, mom2)
    return (
        new_alpha.reshape(alpha.shape),
        new_alpha_mom.reshape(alpha.shape),
        new_static.reshape(static_mom.shape),
        new_static_mom.reshape(static_mom.shape),
    )


def solution(mesh):
    return jax.shard_map(
        local,
        mesh=mesh,
        in_specs=(
            P("mem", None, None, "tile", None),
            P("mem", None, "tile", None),
            P("mem", None, "tile", None),
            P(None, None, "tile", None),
            P(None, "mem", "tile", None),
            P(None, "tile", None),
            P(None, "tile", None),
            P("tile", None),
            P("tile", None),
            P(None, None, "tile", None),
            P(None, None, "tile", None),
        ),
        out_specs=(
            P("mem", None, "tile", None),
            P("mem", None, "tile", None),
            P(None, "mem", "tile", None),
            P(None, "mem", "tile", None),
        ),
        check_vma=False,
    )
```

time: 138 us -> 81 us (0.59)
  the two profiles are of different devices: /device:TPU:128 before, /device:TPU:102 now
where the time goes in v1:
time: 81 us; the launch traced here: 80.7 us
  waiting for transfers between devices  36.3 us (45%)
  starting transfers between devices  27.7 us (34%)
  Pallas kernels  12.2 us (15%)
  local copies, waits for them, and re-layouts  3.63 us (4%)
  between operations  0.86 us (1%)
    ppermute x6, waiting for transfers between devices, halo(): lax.ppermute(backward, 'tile', down)  16 us
    ppermute x6, starting transfers between devices, halo(): lax.ppermute(forward, 'tile', up)  12 us
    ppermute x6, waiting for transfers between devices, halo(): lax.ppermute(forward, 'tile', up)  11.7 us
    ppermute x12, starting transfers between devices, swap(): return lax.ppermute(value, 'mem', [(i, i ^ bits) for i in range(members)])  11.5 us
    ppermute x12, waiting for transfers between devices, swap(): return lax.ppermute(value, 'mem', [(i, i ^ bits) for i in range(members)])  8.64 us
    ppermute x6, starting transfers between devices, halo(): lax.ppermute(backward, 'tile', down)  4.11 us
    unnamed x24, local copies, waits for them, and re-layouts  3.63 us
    pallas_call x1, Pallas kernels, local(): call(fourth_body, 'fourth', [VM] * 7, [shape(512, LANES)] * 2, bufs16 + [...  2.4 us
  transfers between devices with their start and end apart: 24, of which 11 were waited for; matrix products, arithmetic and copies ran while one was open for 0% of the time, Pallas kernels for 8%

profile of v1, /device:TPU:102, one launch (start us, length us, event | category | flops | bytes accessed | tf_op | source)
XLA Modules:
  0.0 80.7 jit_solution(7077835078835294337)
XLA Ops:
  0.6 0.0 copy-start.1
  0.7 1.0 %copy-done.1 = f32[2,16,16,128]{3,2,1,0:T(8,128)S(1)} copy-done((f32[2,16,16,128]{3,2,1,0:T(8,128)S(1)}, f32[2,16,16,128]{3,2,1,0:T(8,128)}, u32[]{:S(2)}) %copy-start.1) | copy-done | bytes 262168
  1.7 1.1 %copy-done.3 = f32[6,16,16,128]{3,2,1,0:T(8,128)S(1)} copy-done((f32[6,16,16,128]{3,2,1,0:T(8,128)S(1)}, f32[6,16,16,128]{3,2,1,0:T(8,128)}, u32[]{:S(2)}) %copy-start.3) | copy-done | bytes 786456
  2.8 0.7 copy-done.5
  3.5 0.7 copy-done.7
  4.2 0.2 pack.1
  4.4 3.5 %collective-permute-start.2 = (f32[216,128]{1,0:T(8,128)S(1)}, f32[216,128]{1,0:T(8,128)S(1)}, u32[]{:S(2)}, u32[]{:S(2)}) collective-permute-start(f32[216,128]{1,0:T(8,128)S(1)} %get-tuple-element.38), channel_id=1, source_target_pairs={{0,1},{1,2},{2,3},{3,4},{4,5},{5,6},{6,7},{7,8},{8,9},{9,10},{10,1... | collective-permute-start | bytes 331784 | tf_op jit(solution)/shard_map/ppermute | solution.py:314
  7.9 0.0 collective-permute-start.3
  7.9 2.3 %collective-permute-done.2.low = f32[216,128]{1,0:T(8,128)S(1)} collective-permute-done((f32[216,128]{1,0:T(8,128)S(1)}, f32[216,128]{1,0:T(8,128)S(1)}, u32[]{:S(2)}, u32[]{:S(2)}) %collective-permute-start.2) | collective-permute-done | bytes 110624 | tf_op jit(solution)/shard_map/ppermute | solution.py:314
  10.2 4.5 %collective-permute-done.3.high = f32[216,128]{1,0:T(8,128)S(1)} collective-permute-done((f32[216,128]{1,0:T(8,128)S(1)}, f32[216,128]{1,0:T(8,128)S(1)}, u32[]{:S(2)}, u32[]{:S(2)}) %collective-permute-start.3) | collective-permute-done | bytes 110624 | tf_op jit(solution)/shard_map/ppermute | solution.py:314
  14.8 1.7 %first.1 = (f32[8,6,16,128]{3,2,1,0:T(8,128)S(1)}, f32[200,128]{1,0:T(8,128)S(1)}) custom-call(f32[512,128]{1,0:T(8,128)S(1)} %bitcast.23, f32[216,128]{1,0:T(8,128)S(1)} %collective-permute-done.2.low, f32[216,128]{1,0:T(8,128)S(1)} %collective-permute-done.3.high, f32[32,128]{1,0:T(8,128)S(1)} %bitcast.38, bf16[2,6,16,16,128]{4,3,2,1,0:T(8,128)(2,1)S(1)} %copy-done), custom_call_target="tpu_custom_call" | custom-call | flops 1000000 | bytes 1000000 | tf_op jit(solution)/shard_map/first/pallas_call | solution.py:348
  16.4 0.1 collective-permute-start.4
  16.5 1.3 %collective-permute-start = (f32[192,128]{1,0:T(8,128)S(1)}, f32[192,128]{1,0:T(8,128)S(1)}, u32[]{:S(2)}, u32[]{:S(2)}) collective-permute-start(f32[192,128]{1,0:T(8,128)S(1)} %get-tuple-element.36), channel_id=1, source_target_pairs={{0,1},{1,2},{2,3},{3,4},{4,5},{5,6},{6,7},{7,8},{8,9},{9,10},{10,1... | collective-permute-start | bytes 294920 | tf_op jit(solution)/shard_map/ppermute | solution.py:314
  17.9 0.8 collective-permute-start.1
  18.7 3.1 %collective-permute-done.low = f32[192,128]{1,0:T(8,128)S(1)} collective-permute-done((f32[192,128]{1,0:T(8,128)S(1)}, f32[192,128]{1,0:T(8,128)S(1)}, u32[]{:S(2)}, u32[]{:S(2)}) %collective-permute-start) | collective-permute-done | bytes 98336 | tf_op jit(solution)/shard_map/ppermute | solution.py:314
  21.8 3.1 %collective-permute-done.1.high = f32[192,128]{1,0:T(8,128)S(1)} collective-permute-done((f32[192,128]{1,0:T(8,128)S(1)}, f32[192,128]{1,0:T(8,128)S(1)}, u32[]{:S(2)}, u32[]{:S(2)}) %collective-permute-start.1) | collective-permute-done | bytes 98336 | tf_op jit(solution)/shard_map/ppermute | solution.py:314
  24.8 0.0 collective-permute-done.4.received
  24.8 1.6 %second.1 = (f32[2,6,16,128]{3,2,1,0:T(8,128)S(1)}, f32[2,6,16,128]{3,2,1,0:T(8,128)S(1)}, f32[2,6,16,128]{3,2,1,0:T(8,128)S(1)}, f32[2,6,16,128]{3,2,1,0:T(8,128)S(1)}) custom-call(f32[512,128]{1,0:T(8,128)S(1)} %bitcast.24, f32[192,128]{1,0:T(8,128)S(1)} %collective-permute-done.low, f32[192,128]{1,0:T(8,128)S(1)} %collective-permute-done.1.high, ...), custom_call_target="tpu_custom_call" | custom-call | flops 1000000 | bytes 1000000 | tf_op jit(solution)/shard_map/second/pallas_call | solution.py:356
  26.5 0.0 copy-start.8
  26.5 1.7 %collective-permute-start.7 = (f32[2,6,16,128]{3,2,1,0:T(8,128)S(1)}, f32[2,6,16,128]{3,2,1,0:T(8,128)S(1)}, u32[]{:S(2)}, u32[]{:S(2)}) collective-permute-start(f32[2,6,16,128]{3,2,1,0:T(8,128)S(1)} %get-tuple-element.47), channel_id=1, source_target_pairs={{0,32},{16,48},{32,0},{48,16},{64,96},{80,112},{96,64},{112,80},{1... | collective-permute-start | bytes 294920 | tf_op jit(solution)/shard_map/ppermute | solution.py:311
  28.2 2.9 %collective-permute-start.8 = (f32[2,6,16,128]{3,2,1,0:T(8,128)S(1)}, f32[2,6,16,128]{3,2,1,0:T(8,128)S(1)}, u32[]{:S(2)}, u32[]{:S(2)}) collective-permute-start(f32[2,6,16,128]{3,2,1,0:T(8,128)S(1)} %get-tuple-element.48), channel_id=1, source_target_pairs={{0,64},{16,80},{32,96},{48,112},{64,0},{80,16},{96,32},{112,48},{1... | collective-permute-start | bytes 294920 | tf_op jit(solution)/shard_map/ppermute | solution.py:311
  31.1 0.2 collective-permute-start.9
  31.3 0.7 collective-permute-start.5
  32.0 1.3 %collective-permute-start.6 = (f32[96,128]{1,0:T(8,128)S(1)}, f32[96,128]{1,0:T(8,128)S(1)}, u32[]{:S(2)}, u32[]{:S(2)}) collective-permute-start(f32[96,128]{1,0:T(8,128)S(1)} %get-tuple-element.44), channel_id=1, source_target_pairs={{1,0},{2,1},{3,2},{4,3},{5,4},{6,5},{7,6},{8,7},{9,8},{10,9},{11,1... | collective-permute-start | bytes 147464 | tf_op jit(solution)/shard_map/ppermute | solution.py:314
  33.3 2.6 %collective-permute-done.5.low = f32[96,128]{1,0:T(8,128)S(1)} collective-permute-done((f32[96,128]{1,0:T(8,128)S(1)}, f32[96,128]{1,0:T(8,128)S(1)}, u32[]{:S(2)}, u32[]{:S(2)}) %collective-permute-start.5) | collective-permute-done | bytes 49184 | tf_op jit(solution)/shard_map/ppermute | solution.py:314
  35.9 2.3 %collective-permute-done.6.high = f32[96,128]{1,0:T(8,128)S(1)} collective-permute-done((f32[96,128]{1,0:T(8,128)S(1)}, f32[96,128]{1,0:T(8,128)S(1)}, u32[]{:S(2)}, u32[]{:S(2)}) %collective-permute-start.6) | collective-permute-done | bytes 49184 | tf_op jit(solution)/shard_map/ppermute | solution.py:314
  38.2 1.0 %static_first.1 = (f32[2,6,16,128]{3,2,1,0:T(8,128)S(1)}, f32[200,128]{1,0:T(8,128)S(1)}) custom-call(f32[96,128]{1,0:T(8,128)S(1)} %collective-permute-done.5.low, f32[96,128]{1,0:T(8,128)S(1)} %collective-permute-done.6.high, f32[128,128]{1,0:T(8,128)S(1)} %get-tuple-element.45.field, f32[2,6,16,128]{3,2,1,0:T(8,128)S(1)} %get-tuple-element.42.o0), custom_call_target="tpu_custom_call" | custom-call | flops 1000000 | bytes 1000000 | tf_op jit(solution)/shard_map/static_first/pallas_call | solution.py:365
  39.2 0.0 collective-permute-done.7
  39.2 0.0 collective-permute-done.8
  39.3 0.0 collective-permute-done.9
  39.3 0.0 copy-start.11
  39.3 0.0 copy-start.10
  39.3 1.4 %collective-permute-start.10 = (f32[192,128]{1,0:T(8,128)S(1)}, f32[192,128]{1,0:T(8,128)S(1)}, u32[]{:S(2)}, u32[]{:S(2)}) collective-permute-start(f32[192,128]{1,0:T(8,128)S(1)} %bitcast.28), channel_id=1, source_target_pairs={{0,128},{16,144},{32,160},{48,176},{64,192},{80,208},{96,224},{112... | collective-permute-start | bytes 294920 | tf_op jit(solution)/shard_map/ppermute | solution.py:311
  40.7 1.5 %prepare.1.sums = f32[384,128]{1,0:T(8,128)S(1)} custom-call(s32[8,128]{1,0:T(8,128)S(1)} %bitcast.43, s32[8,128]{1,0:T(8,128)S(1)} %bitcast.44, f32[6,16,8,128]{3,2,1,0:T(8,128)S(1)} %bitcast.41, f32[6,16,8,128]{3,2,1,0:T(8,128)S(1)} %bitcast.42), custom_call_target="tpu_custom_call" | custom-call | flops 1000000000 | bytes 1000000 | tf_op jit(solution)/shard_map/prepare/pallas_call | solution.py:333
  42.2 3.5 %collective-permute-done.10.other = f32[192,128]{1,0:T(8,128)S(1)} collective-permute-done((f32[192,128]{1,0:T(8,128)S(1)}, f32[192,128]{1,0:T(8,128)S(1)}, u32[]{:S(2)}, u32[]{:S(2)}) %collective-permute-start.10) | collective-permute-done | bytes 98336 | tf_op jit(solution)/shard_map/ppermute | solution.py:311
  45.8 0.5 collective-permute-start.12
  46.3 4.1 %collective-permute-start.14 = (f32[192,128]{1,0:T(8,128)S(1)}, f32[192,128]{1,0:T(8,128)S(1)}, u32[]{:S(2)}, u32[]{:S(2)}) collective-permute-start(f32[192,128]{1,0:T(8,128)S(1)} %get-tuple-element.50.grad), channel_id=1, source_target_pairs={{0,64},{16,80},{32,96},{48,112},{64,0},{80,16},{96,32},{112,48},{1... | collective-permute-start | bytes 294920 | tf_op jit(solution)/shard_map/ppermute | solution.py:311
  50.4 0.2 collective-permute-start.16
  50.5 0.0 collective-permute-start.11
  50.6 0.5 collective-permute-start.13
  51.1 2.9 %collective-permute-done.14 = f32[192,128]{1,0:T(8,128)S(1)} collective-permute-done((f32[192,128]{1,0:T(8,128)S(1)}, f32[192,128]{1,0:T(8,128)S(1)}, u32[]{:S(2)}, u32[]{:S(2)}) %collective-permute-start.14) | collective-permute-done | bytes 98336 | tf_op jit(solution)/shard_map/ppermute | solution.py:311
  54.0 0.0 collective-permute-start.15
  54.0 2.2 %collective-permute-done.16 = f32[192,128]{1,0:T(8,128)S(1)} collective-permute-done((f32[192,128]{1,0:T(8,128)S(1)}, f32[192,128]{1,0:T(8,128)S(1)}, u32[]{:S(2)}, u32[]{:S(2)}) %collective-permute-start.16) | collective-permute-done | bytes 98336 | tf_op jit(solution)/shard_map/ppermute | solution.py:311
  56.2 0.1 project_own.1
  56.3 0.1 collective-permute-start.20
  56.4 0.0 collective-permute-done.11.g0
  56.4 0.0 copy-start.6
  56.4 2.0 %collective-permute-start.21 = (f32[192,128]{1,0:T(8,128)S(1)}, f32[192,128]{1,0:T(8,128)S(1)}, u32[]{:S(2)}, u32[]{:S(2)}) collective-permute-start(f32[192,128]{1,0:T(8,128)S(1)} %get-tuple-element.55), channel_id=1, source_target_pairs={{1,0},{2,1},{3,2},{4,3},{5,4},{6,5},{7,6},{8,7},{9,8},{10,9},{11,1... | collective-permute-start | bytes 294920 | tf_op jit(solution)/shard_map/ppermute | solution.py:314
  58.4 0.0 collective-permute-done.13.g1
  58.4 0.0 collective-permute-done.15.g2
  58.4 0.0 collective-permute-done.17.g3
  58.5 0.2 project_other.1
  58.6 2.3 %collective-permute-start.18 = (f32[192,128]{1,0:T(8,128)S(1)}, f32[192,128]{1,0:T(8,128)S(1)}, u32[]{:S(2)}, u32[]{:S(2)}) collective-permute-start(f32[192,128]{1,0:T(8,128)S(1)} %get-tuple-element.51), channel_id=1, source_target_pairs={{0,1},{1,2},{2,3},{3,4},{4,5},{5,6},{6,7},{7,8},{8,9},{9,10},{10,1... | collective-permute-start | bytes 294920 | tf_op jit(solution)/shard_map/ppermute | solution.py:314
  60.9 4.1 %collective-permute-start.22 = (f32[72,128]{1,0:T(8,128)S(1)}, f32[72,128]{1,0:T(8,128)S(1)}, u32[]{:S(2)}, u32[]{:S(2)}) collective-permute-start(f32[72,128]{1,0:T(8,128)S(1)} %get-tuple-element.59), channel_id=1, source_target_pairs={{0,1},{1,2},{2,3},{3,4},{4,5},{5,6},{6,7},{7,8},{8,9},{9,10},{10,1... | collective-permute-start | bytes 110600 | tf_op jit(solution)/shard_map/ppermute | solution.py:314
  65.0 3.7 %collective-permute-done.22.low = f32[72,128]{1,0:T(8,128)S(1)} collective-permute-done((f32[72,128]{1,0:T(8,128)S(1)}, f32[72,128]{1,0:T(8,128)S(1)}, u32[]{:S(2)}, u32[]{:S(2)}) %collective-permute-start.22) | collective-permute-done | bytes 36896 | tf_op jit(solution)/shard_map/ppermute | solution.py:314
  68.7 0.0 collective-permute-start.23
  68.7 6.1 %collective-permute-done.23.high = f32[72,128]{1,0:T(8,128)S(1)} collective-permute-done((f32[72,128]{1,0:T(8,128)S(1)}, f32[72,128]{1,0:T(8,128)S(1)}, u32[]{:S(2)}, u32[]{:S(2)}) %collective-permute-start.23) | collective-permute-done | bytes 36896 | tf_op jit(solution)/shard_map/ppermute | solution.py:314
  74.8 1.9 %static_last.1 = (f32[96,128]{1,0:T(8,128)}, f32[96,128]{1,0:T(8,128)}) custom-call(f32[72,128]{1,0:T(8,128)S(1)} %collective-permute-done.22.low, f32[72,128]{1,0:T(8,128)S(1)} %collective-permute-done.23.high, f32[192,128]{1,0:T(8,128)S(1)} %get-tuple-element.50.grad, f32[200,128]{1,0:T(8,128)S(1)} %get-tuple-element.61.coefs, ...), custom_call_target="tpu_custom_call" | custom-call | flops 1000000 | bytes 1000000 | tf_op jit(solution)/shard_map/static_last/pallas_call | solution.py:390
  76.7 0.0 collective-permute-done.20.low
  76.7 0.0 copy-start.4
  76.7 1.5 %third.1.done = f32[256,128]{1,0:T(8,128)S(1)} custom-call(f32[192,128]{1,0:T(8,128)S(1)} %collective-permute-done.20.low, f32[192,128]{1,0:T(8,128)S(1)} %collective-permute-done.21.high, f32[256,128]{1,0:T(8,128)S(1)} %get-tuple-element.56.middle, f32[200,128]{1,0:T(8,128)S(1)} %get-tuple-element.40.coefs), custom_call_target="tpu_custom_call" | custom-call | flops 1000000 | bytes 1000000 | tf_op jit(solution)/shard_map/third/pallas_call | solution.py:397
  78.3 0.0 collective-permute-done.18.low
  78.3 0.0 collective-permute-done.19.high
  78.3 2.4 %fourth.1 = (f32[512,128]{1,0:T(8,128)}, f32[512,128]{1,0:T(8,128)}) custom-call(f32[192,128]{1,0:T(8,128)S(1)} %collective-permute-done.18.low, f32[192,128]{1,0:T(8,128)S(1)} %collective-permute-done.19.high, f32[256,128]{1,0:T(8,128)S(1)} %get-tuple-element.53.middle, f32[200,128]{1,0:T(8,128)S(1)} %get-tuple-element.40.coefs, f32[256,128]{1,0:T(8,128)S(1)} %third.1.done, ...), custom_call_target="tpu_custom_call" | custom-call | flops 1000000 | bytes 1000000 | tf_op jit(solution)/shard_map/fourth/pallas_call | solution.py:398
  (20 shorter events, 0.1 us)
Async XLA Ops:
  0.6 14.1 %copy-start = (bf16[2,6,16,16,128]{4,3,2,1,0:T(8,128)(2,1)S(1)}, bf16[2,6,16,16,128]{4,3,2,1,0:T(8,128)(2,1)}, u32[]{:S(2)}) copy-start(bf16[2,6,16,16,128]{4,3,2,1,0:T(8,128)(2,1)} %perturb.7) | copy-start | bytes 2359300
  0.6 1.0 %copy-start.1 = (f32[2,16,16,128]{3,2,1,0:T(8,128)S(1)}, f32[2,16,16,128]{3,2,1,0:T(8,128)}, u32[]{:S(2)}) copy-start(f32[2,16,16,128]{3,2,1,0:T(8,128)} %param.12) | copy-start | bytes 786436
  1.7 1.1 %copy-start.3 = (f32[6,16,16,128]{3,2,1,0:T(8,128)S(1)}, f32[6,16,16,128]{3,2,1,0:T(8,128)}, u32[]{:S(2)}) copy-start(f32[6,16,16,128]{3,2,1,0:T(8,128)} %static_ctl.1) | copy-start | bytes 2359300
  2.8 0.7 copy-start.5
  3.5 0.7 copy-start.7
  4.4 5.8 %collective-permute-start.2 = (f32[216,128]{1,0:T(8,128)S(1)}, f32[216,128]{1,0:T(8,128)S(1)}, u32[]{:S(2)}, u32[]{:S(2)}) collective-permute-start(f32[216,128]{1,0:T(8,128)S(1)} %get-tuple-element.38), channel_id=1, source_target_pairs={{0,1},{1,2},{2,3},{3,4},{4,5},{5,6},{6,7},{7,8},{8,9},{9,10},{10,1... | collective-permute-start | bytes 331784 | tf_op jit(solution)/shard_map/ppermute | solution.py:314
  7.9 6.9 %collective-permute-start.3 = (f32[216,128]{1,0:T(8,128)S(1)}, f32[216,128]{1,0:T(8,128)S(1)}, u32[]{:S(2)}, u32[]{:S(2)}) collective-permute-start(f32[216,128]{1,0:T(8,128)S(1)} %get-tuple-element.39), channel_id=1, source_target_pairs={{1,0},{2,1},{3,2},{4,3},{5,4},{6,5},{7,6},{8,7},{9,8},{10,9},{11,1... | collective-permute-start | bytes 331784 | tf_op jit(solution)/shard_map/ppermute | solution.py:314
  16.4 8.4 %collective-permute-start.4 = (f32[8,6,16,128]{3,2,1,0:T(8,128)S(1)}, f32[8,6,16,128]{3,2,1,0:T(8,128)S(1)}, u32[]{:S(2)}, u32[]{:S(2)}) collective-permute-start(f32[8,6,16,128]{3,2,1,0:T(8,128)S(1)} %get-tuple-element.41), channel_id=1, source_target_pairs={{0,16},{16,0},{32,48},{48,32},{64,80},{80,64},{96,112},{112,96},{1... | collective-permute-start | bytes 1179656 | tf_op jit(solution)/shard_map/ppermute | solution.py:311
  16.5 5.2 %collective-permute-start = (f32[192,128]{1,0:T(8,128)S(1)}, f32[192,128]{1,0:T(8,128)S(1)}, u32[]{:S(2)}, u32[]{:S(2)}) collective-permute-start(f32[192,128]{1,0:T(8,128)S(1)} %get-tuple-element.36), channel_id=1, source_target_pairs={{0,1},{1,2},{2,3},{3,4},{4,5},{5,6},{6,7},{7,8},{8,9},{9,10},{10,1... | collective-permute-start | bytes 294920 | tf_op jit(solution)/shard_map/ppermute | solution.py:314
  17.9 7.0 %collective-permute-start.1 = (f32[192,128]{1,0:T(8,128)S(1)}, f32[192,128]{1,0:T(8,128)S(1)}, u32[]{:S(2)}, u32[]{:S(2)}) collective-permute-start(f32[192,128]{1,0:T(8,128)S(1)} %get-tuple-element.37), channel_id=1, source_target_pairs={{1,0},{2,1},{3,2},{4,3},{5,4},{6,5},{7,6},{8,7},{9,8},{10,9},{11,1... | collective-permute-start | bytes 294920 | tf_op jit(solution)/shard_map/ppermute | solution.py:314
  24.8 15.9 %copy-start.9 = (f32[6,16,1,1024]{3,2,1,0:T(1,128)S(1)}, f32[6,16,1,1024]{3,2,1,0:T(1,128)}, u32[]{:S(2)}) copy-start(f32[6,16,1,1024]{3,2,1,0:T(1,128)} %param.21) | copy-start | bytes 1179652
  26.5 14.2 %copy-start.8 = (f32[6,16,1,1024]{3,2,1,0:T(1,128)S(1)}, f32[6,16,1,1024]{3,2,1,0:T(1,128)}, u32[]{:S(2)}) copy-start(f32[6,16,1,1024]{3,2,1,0:T(1,128)} %param.20) | copy-start | bytes 1179652
  26.5 12.7 %collective-permute-start.7 = (f32[2,6,16,128]{3,2,1,0:T(8,128)S(1)}, f32[2,6,16,128]{3,2,1,0:T(8,128)S(1)}, u32[]{:S(2)}, u32[]{:S(2)}) collective-permute-start(f32[2,6,16,128]{3,2,1,0:T(8,128)S(1)} %get-tuple-element.47), channel_id=1, source_target_pairs={{0,32},{16,48},{32,0},{48,16},{64,96},{80,112},{96,64},{112,80},{1... | collective-permute-start | bytes 294920 | tf_op jit(solution)/shard_map/ppermute | solution.py:311
  28.2 11.1 %collective-permute-start.8 = (f32[2,6,16,128]{3,2,1,0:T(8,128)S(1)}, f32[2,6,16,128]{3,2,1,0:T(8,128)S(1)}, u32[]{:S(2)}, u32[]{:S(2)}) collective-permute-start(f32[2,6,16,128]{3,2,1,0:T(8,128)S(1)} %get-tuple-element.48), channel_id=1, source_target_pairs={{0,64},{16,80},{32,96},{48,112},{64,0},{80,16},{96,32},{112,48},{1... | collective-permute-start | bytes 294920 | tf_op jit(solution)/shard_map/ppermute | solution.py:311
  31.1 8.2 %collective-permute-start.9 = (f32[2,6,16,128]{3,2,1,0:T(8,128)S(1)}, f32[2,6,16,128]{3,2,1,0:T(8,128)S(1)}, u32[]{:S(2)}, u32[]{:S(2)}) collective-permute-start(f32[2,6,16,128]{3,2,1,0:T(8,128)S(1)} %get-tuple-element.49), channel_id=1, source_target_pairs={{0,96},{16,112},{32,64},{48,80},{64,32},{80,48},{96,0},{112,16},{1... | collective-permute-start | bytes 294920 | tf_op jit(solution)/shard_map/ppermute | solution.py:311
  31.3 4.6 %collective-permute-start.5 = (f32[96,128]{1,0:T(8,128)S(1)}, f32[96,128]{1,0:T(8,128)S(1)}, u32[]{:S(2)}, u32[]{:S(2)}) collective-permute-start(f32[96,128]{1,0:T(8,128)S(1)} %get-tuple-element.43), channel_id=1, source_target_pairs={{0,1},{1,2},{2,3},{3,4},{4,5},{5,6},{6,7},{7,8},{8,9},{9,10},{10,1... | collective-permute-start | bytes 147464 | tf_op jit(solution)/shard_map/ppermute | solution.py:314
  32.0 6.2 %collective-permute-start.6 = (f32[96,128]{1,0:T(8,128)S(1)}, f32[96,128]{1,0:T(8,128)S(1)}, u32[]{:S(2)}, u32[]{:S(2)}) collective-permute-start(f32[96,128]{1,0:T(8,128)S(1)} %get-tuple-element.44), channel_id=1, source_target_pairs={{1,0},{2,1},{3,2},{4,3},{5,4},{6,5},{7,6},{8,7},{9,8},{10,9},{11,1... | collective-permute-start | bytes 147464 | tf_op jit(solution)/shard_map/ppermute | solution.py:314
  39.3 1.4 %copy-start.11 = (s32[1,1024]{1,0:T(1,128)S(1)}, s32[1,1024]{1,0:T(1,128)}, u32[]{:S(2)}) copy-start(s32[1,1024]{1,0:T(1,128)} %param.19) | copy-start | bytes 12292
  39.3 1.4 %copy-start.10 = (s32[1,1024]{1,0:T(1,128)S(1)}, s32[1,1024]{1,0:T(1,128)}, u32[]{:S(2)}) copy-start(s32[1,1024]{1,0:T(1,128)} %param.18) | copy-start | bytes 12292
  39.3 6.4 %collective-permute-start.10 = (f32[192,128]{1,0:T(8,128)S(1)}, f32[192,128]{1,0:T(8,128)S(1)}, u32[]{:S(2)}, u32[]{:S(2)}) collective-permute-start(f32[192,128]{1,0:T(8,128)S(1)} %bitcast.28), channel_id=1, source_target_pairs={{0,128},{16,144},{32,160},{48,176},{64,192},{80,208},{96,224},{112... | collective-permute-start | bytes 294920 | tf_op jit(solution)/shard_map/ppermute | solution.py:311
  45.8 4.8 %collective-permute-start.12 = (f32[192,128]{1,0:T(8,128)S(1)}, f32[192,128]{1,0:T(8,128)S(1)}, u32[]{:S(2)}, u32[]{:S(2)}) collective-permute-start(f32[192,128]{1,0:T(8,128)S(1)} %get-tuple-element.50.grad), channel_id=1, source_target_pairs={{0,32},{16,48},{32,0},{48,16},{64,96},{80,112},{96,64},{112,80},{1... | collective-permute-start | bytes 294920 | tf_op jit(solution)/shard_map/ppermute | solution.py:311
  46.3 7.8 %collective-permute-start.14 = (f32[192,128]{1,0:T(8,128)S(1)}, f32[192,128]{1,0:T(8,128)S(1)}, u32[]{:S(2)}, u32[]{:S(2)}) collective-permute-start(f32[192,128]{1,0:T(8,128)S(1)} %get-tuple-element.50.grad), channel_id=1, source_target_pairs={{0,64},{16,80},{32,96},{48,112},{64,0},{80,16},{96,32},{112,48},{1... | collective-permute-start | bytes 294920 | tf_op jit(solution)/shard_map/ppermute | solution.py:311
  50.4 5.8 %collective-permute-start.16 = (f32[192,128]{1,0:T(8,128)S(1)}, f32[192,128]{1,0:T(8,128)S(1)}, u32[]{:S(2)}, u32[]{:S(2)}) collective-permute-start(f32[192,128]{1,0:T(8,128)S(1)} %get-tuple-element.50.grad), channel_id=1, source_target_pairs={{0,96},{16,112},{32,64},{48,80},{64,32},{80,48},{96,0},{112,16},{1... | collective-permute-start | bytes 294920 | tf_op jit(solution)/shard_map/ppermute | solution.py:311
  50.5 5.9 %collective-permute-start.11 = (f32[2,6,16,128]{3,2,1,0:T(8,128)S(1)}, f32[2,6,16,128]{3,2,1,0:T(8,128)S(1)}, u32[]{:S(2)}, u32[]{:S(2)}) collective-permute-start(f32[2,6,16,128]{3,2,1,0:T(8,128)S(1)} %bitcast.26), channel_id=1, source_target_pairs={{0,16},{16,0},{32,48},{48,32},{64,80},{80,64},{96,112},{112,96},{1... | collective-permute-start | bytes 294920 | tf_op jit(solution)/shard_map/ppermute | solution.py:311
  50.6 7.9 %collective-permute-start.13 = (f32[2,6,16,128]{3,2,1,0:T(8,128)S(1)}, f32[2,6,16,128]{3,2,1,0:T(8,128)S(1)}, u32[]{:S(2)}, u32[]{:S(2)}) collective-permute-start(f32[2,6,16,128]{3,2,1,0:T(8,128)S(1)} %bitcast.31), channel_id=1, source_target_pairs={{0,16},{16,0},{32,48},{48,32},{64,80},{80,64},{96,112},{112,96},{1... | collective-permute-start | bytes 294920 | tf_op jit(solution)/shard_map/ppermute | solution.py:311
  54.0 4.4 %collective-permute-start.15 = (f32[2,6,16,128]{3,2,1,0:T(8,128)S(1)}, f32[2,6,16,128]{3,2,1,0:T(8,128)S(1)}, u32[]{:S(2)}, u32[]{:S(2)}) collective-permute-start(f32[2,6,16,128]{3,2,1,0:T(8,128)S(1)} %bitcast.33), channel_id=1, source_target_pairs={{0,16},{16,0},{32,48},{48,32},{64,80},{80,64},{96,112},{112,96},{1... | collective-permute-start | bytes 294920 | tf_op jit(solution)/shard_map/ppermute | solution.py:311
  56.2 2.3 %collective-permute-start.17 = (f32[2,6,16,128]{3,2,1,0:T(8,128)S(1)}, f32[2,6,16,128]{3,2,1,0:T(8,128)S(1)}, u32[]{:S(2)}, u32[]{:S(2)}) collective-permute-start(f32[2,6,16,128]{3,2,1,0:T(8,128)S(1)} %bitcast.35), channel_id=1, source_target_pairs={{0,16},{16,0},{32,48},{48,32},{64,80},{80,64},{96,112},{112,96},{1... | collective-permute-start | bytes 294920 | tf_op jit(solution)/shard_map/ppermute | solution.py:311
  56.3 20.4 %collective-permute-start.20 = (f32[192,128]{1,0:T(8,128)S(1)}, f32[192,128]{1,0:T(8,128)S(1)}, u32[]{:S(2)}, u32[]{:S(2)}) collective-permute-start(f32[192,128]{1,0:T(8,128)S(1)} %get-tuple-element.54), channel_id=1, source_target_pairs={{0,1},{1,2},{2,3},{3,4},{4,5},{5,6},{6,7},{7,8},{8,9},{9,10},{10,1... | collective-permute-start | bytes 294920 | tf_op jit(solution)/shard_map/ppermute | solution.py:314
  56.4 18.4 %copy-start.6 = (f32[6,1,16,128]{3,2,1,0:T(8,128)S(1)}, f32[6,1,16,128]{3,2,1,0:T(8,128)}, u32[]{:S(2)}) copy-start(f32[6,1,16,128]{3,2,1,0:T(8,128)} %param.15) | copy-start | bytes 147460
  56.4 20.3 %collective-permute-start.21 = (f32[192,128]{1,0:T(8,128)S(1)}, f32[192,128]{1,0:T(8,128)S(1)}, u32[]{:S(2)}, u32[]{:S(2)}) collective-permute-start(f32[192,128]{1,0:T(8,128)S(1)} %get-tuple-element.55), channel_id=1, source_target_pairs={{1,0},{2,1},{3,2},{4,3},{5,4},{6,5},{7,6},{8,7},{9,8},{10,9},{11,1... | collective-permute-start | bytes 294920 | tf_op jit(solution)/shard_map/ppermute | solution.py:314
  58.6 19.7 %collective-permute-start.18 = (f32[192,128]{1,0:T(8,128)S(1)}, f32[192,128]{1,0:T(8,128)S(1)}, u32[]{:S(2)}, u32[]{:S(2)}) collective-permute-start(f32[192,128]{1,0:T(8,128)S(1)} %get-tuple-element.51), channel_id=1, source_target_pairs={{0,1},{1,2},{2,3},{3,4},{4,5},{5,6},{6,7},{7,8},{8,9},{9,10},{10,1... | collective-permute-start | bytes 294920 | tf_op jit(solution)/shard_map/ppermute | solution.py:314
  60.9 17.4 %collective-permute-start.19 = (f32[192,128]{1,0:T(8,128)S(1)}, f32[192,128]{1,0:T(8,128)S(1)}, u32[]{:S(2)}, u32[]{:S(2)}) collective-permute-start(f32[192,128]{1,0:T(8,128)S(1)} %get-tuple-element.52), channel_id=1, source_target_pairs={{1,0},{2,1},{3,2},{4,3},{5,4},{6,5},{7,6},{8,7},{9,8},{10,9},{11,1... | collective-permute-start | bytes 294920 | tf_op jit(solution)/shard_map/ppermute | solution.py:314
  60.9 7.8 %collective-permute-start.22 = (f32[72,128]{1,0:T(8,128)S(1)}, f32[72,128]{1,0:T(8,128)S(1)}, u32[]{:S(2)}, u32[]{:S(2)}) collective-permute-start(f32[72,128]{1,0:T(8,128)S(1)} %get-tuple-element.59), channel_id=1, source_target_pairs={{0,1},{1,2},{2,3},{3,4},{4,5},{5,6},{6,7},{7,8},{8,9},{9,10},{10,1... | collective-permute-start | bytes 110600 | tf_op jit(solution)/shard_map/ppermute | solution.py:314
  68.7 6.1 %collective-permute-start.23 = (f32[72,128]{1,0:T(8,128)S(1)}, f32[72,128]{1,0:T(8,128)S(1)}, u32[]{:S(2)}, u32[]{:S(2)}) collective-permute-start(f32[72,128]{1,0:T(8,128)S(1)} %get-tuple-element.60), channel_id=1, source_target_pairs={{1,0},{2,1},{3,2},{4,3},{5,4},{6,5},{7,6},{8,7},{9,8},{10,9},{11,1... | collective-permute-start | bytes 110600 | tf_op jit(solution)/shard_map/ppermute | solution.py:314
  76.7 1.6 %copy-start.2 = (f32[2,16,16,128]{3,2,1,0:T(8,128)S(1)}, f32[2,16,16,128]{3,2,1,0:T(8,128)}, u32[]{:S(2)}) copy-start(f32[2,16,16,128]{3,2,1,0:T(8,128)} %param.12) | copy-start | bytes 786436
  76.7 1.6 %copy-start.4 = (f32[2,16,16,128]{3,2,1,0:T(8,128)S(1)}, f32[2,16,16,128]{3,2,1,0:T(8,128)}, u32[]{:S(2)}) copy-start(f32[2,16,16,128]{3,2,1,0:T(8,128)} %param.13) | copy-start | bytes 786436

commit v2 on v1

--- a/solution.py
+++ b/solution.py
@@ -17,23 +17,28 @@
 momentum_rate = 0.9
 step_rate = 0.5
 
+GRANT = 53.2
+BUSY = 5000000000
+
 VM = pl.BlockSpec(memory_space=pltpu.VMEM)
 ANY = pl.BlockSpec(memory_space=pl.ANY)
+HBM = pl.BlockSpec(memory_space=pltpu.HBM)
 
 
 def shape(*dims):
     return jax.ShapeDtypeStruct(dims, jnp.float32)
 
 
-def call(body, name, ins, outs, scratch=(), flops=1000000):
+def call(body, name, ins, outs, scratch=(), flops=1000000, out_specs=None, aliases=None, grant=32):
     return pl.pallas_call(
         body,
         name=name,
         in_specs=list(ins),
-        out_specs=[VM] * len(outs),
+        out_specs=out_specs or [VM] * len(outs),
         out_shape=list(outs),
         scratch_shapes=list(scratch),
-        compiler_params=pltpu.CompilerParams(vmem_limit_bytes=32 * 1024 * 1024),
+        input_output_aliases=aliases or {},
+        compiler_params=pltpu.CompilerParams(vmem_limit_bytes=int(grant * 1024 * 1024)),
         cost_estimate=pl.CostEstimate(flops=flops, bytes_accessed=1000000, transcendentals=0),
     )
 
@@ -47,14 +52,15 @@
     return mem // 8, (mem // 2) % 4, mem % 2
 
 
-def pack_rows(load, width, forward, backward):
+def pack_rows(load, width, forward, backward, base=0):
     for row in range(ROWS):
         value = load(row)
         if row >= ROWS - STEPS:
-            at = (row - (ROWS - STEPS)) * width
+            at = base + (row - (ROWS - STEPS)) * width
             forward[at : at + width, :] = value
         if row < STEPS:
-            backward[row * width : (row + 1) * width, :] = value
+            at = base + row * width
+            backward[at : at + width, :] = value
 
 
 def build_coefs(low_x, mid_x, high_x, low_y, mid_y, high_y, raw, coefs):
@@ -113,28 +119,35 @@
     return jnp.concatenate(parts, axis=0)
 
 
-def pack_body(alpha, loc, static_ctl, static_coef, a_f, a_b, b_f, b_b, c_f, c_b, field, sem):
+def pack_body(alpha_in, loc_in, static_ctl, static_coef, a_f, a_b, b_f, b_b, alpha, loc, field, sem):
     mem = lax.axis_index("mem")
     own = mem % 2
-    fetch = pltpu.make_async_copy(static_ctl.at[:, mem], field.reshape(8, ROWS, LANES).at[0:VARS], sem)
-    fetch.start()
+    copies = [
+        pltpu.make_async_copy(alpha_in, alpha, sem.at[0]),
+        pltpu.make_async_copy(loc_in, loc, sem.at[1]),
+        pltpu.make_async_copy(static_ctl.at[:, mem], field.reshape(8, ROWS, LANES).at[0:VARS], sem.at[2]),
+        pltpu.make_async_copy(static_coef, field.at[VARS * ROWS : 8 * ROWS], sem.at[3]),
+    ]
+    for copy in copies:
+        copy.start()
+    for copy in copies:
+        copy.wait()
     pack_rows(lambda row: alpha_row(alpha, 1 - own, row), 16, a_f, a_b)
     for k in range(2):
         a_f[192 + k * 12 : 204 + k * 12, :] = loc[k * 16 + 4 : k * 16 + 16, :]
         a_b[192 + k * 12 : 204 + k * 12, :] = loc[k * 16 : k * 16 + 12, :]
+    pack_rows(lambda row: field[pl.ds(row, 8, stride=ROWS), :], 8, a_f, a_b, 216)
     pack_rows(lambda row: alpha_row(alpha, own, row), 16, b_f, b_b)
-    fetch.wait()
-    field[VARS * ROWS :, :] = static_coef[...]
-    pack_rows(lambda row: field[pl.ds(row, 8, stride=ROWS), :], 8, c_f, c_b)
-
-
-def halo_loader(low, high, middle, width):
+
+
+def halo_loader(low, high, middle, width, base=0):
     def load(row):
         if row < STEPS:
-            return low[row * width : (row + 1) * width, :]
+            at = base + row * width
+            return low[at : at + width, :]
         if row < STEPS + ROWS:
             return middle(row - STEPS)
-        at = (row - STEPS - ROWS) * width
+        at = base + (row - STEPS - ROWS) * width
         return high[at : at + width, :]
 
     return load
@@ -160,14 +173,31 @@
             sums[s, v] = total
 
 
-def second_body(alpha, low, high, coefs, perturb, received, o0, o1, o2, o3, buf0, buf1, local):
-    _, y, parity = place()
+def static_first_body(low, high, field, out, coefs, raw, buf0, buf1, result):
+    build_coefs(
+        low[pl.ds(222, 12, stride=8), :], field[96:112, :], high[pl.ds(222, 12, stride=8), :],
+        low[pl.ds(223, 12, stride=8), :], field[112:128, :], high[pl.ds(223, 12, stride=8), :], raw, coefs,
+    )
 
     def emit(row, value):
-        local[pl.ds(row, 16, stride=ROWS), :] = value
-
+        result[pl.ds(row, 8, stride=ROWS), :] = value
+
+    load = halo_loader(low, high, lambda row: field[pl.ds(row, 8, stride=ROWS), :], 8, 216)
+    diffuse(load, 8, 8, coefs, (buf0, buf1), emit)
+    out[...] = result[0:96, :]
+
+
+def second_body(alpha, low, high, coefs, out, buf0, buf1):
+    def emit(row, value):
+        out[pl.ds(row, 16, stride=ROWS), :] = value
+
+    parity = lax.axis_index("mem") % 2
     load = halo_loader(low, high, lambda row: alpha_row(alpha, parity, row), 16)
     diffuse(load, 16, 16, coefs, (buf0, buf1), emit)
+
+
+def sum_body(local, perturb, received, static, o0, o1, o2, o3):
+    x, y, parity = place()
     for k, out in enumerate((o0, o1, o2, o3)):
         for j in range(2):
             s = (y ^ k) + 4 * j
@@ -177,25 +207,10 @@
             for v in range(VARS):
                 total = first * perturb[0, v, level].astype(jnp.float32)
                 total = total + other * perturb[1, v, level].astype(jnp.float32)
-                out[j, v] = total + received[s, v]
-
-
-def static_first_body(low, high, field, o0, out, coefs, raw, buf0, buf1, result):
-    x, _, _ = place()
-    build_coefs(
-        low[pl.ds(6, 12, stride=8), :], field[96:112, :], high[pl.ds(6, 12, stride=8), :],
-        low[pl.ds(7, 12, stride=8), :], field[112:128, :], high[pl.ds(7, 12, stride=8), :], raw, coefs,
-    )
-
-    def emit(row, value):
-        result[pl.ds(row, 8, stride=ROWS), :] = value
-
-    load = halo_loader(low, high, lambda row: field[pl.ds(row, 8, stride=ROWS), :], 8)
-    diffuse(load, 8, 8, coefs, (buf0, buf1), emit)
-    for j in range(2):
-        for v in range(VARS):
-            part = result[v * 16 : v * 16 + 16, :]
-            out[j, v] = o0[j, v] + jnp.where(x == j, part, 0.0)
+                total = total + received[s, v]
+                if k == 0:
+                    total = total + jnp.where(x == j, static[v * 16 : v * 16 + 16, :], 0.0)
+                out[j * 96 + v * 16 : j * 96 + v * 16 + 16, :] = total
 
 
 def prepare_body(cell, mask, value, weight, sums, held, sem):
@@ -231,62 +246,102 @@
             sums[pl.ds(block * 2 + r, 24, stride=ROWS), :] = total[:, r * LANES : (r + 1) * LANES]
 
 
-def gradient_body(mine, other, sums, grad, forward, backward):
-    x, _, _ = place()
+def gradient_body(mine, other, sums, grad):
     total = mine[...] + other[...]
     grad[...] = sums[0:192, :] * total - sums[192:384, :]
-    pack_rows(lambda row: grad[pl.ds(x * 96 + row, VARS, stride=ROWS), :], VARS, forward, backward)
-
-
-def project_body(own, g0, g1, g2, g3, perturb, forward, backward, middle):
-    _, y, c = place()
-    parity = c if own else 1 - c
+
+
+def project(g, k, parity, perturb, middle):
+    _, y, _ = place()
+    for j in range(2):
+        s = (y ^ k) + 4 * j
+        level = 2 * s + parity
+        fields = [g[j * 96 + v * 16 : j * 96 + v * 16 + 16, :] for v in range(VARS)]
+        for m in range(2):
+            total = perturb[m, 0, level].astype(jnp.float32) * fields[0]
+            for v in range(1, VARS):
+                total = total + perturb[m, v, level].astype(jnp.float32) * fields[v]
+            middle[pl.ds(pl.multiple_of((m * HALF + s) * 16, 16), 16), :] = total
+
+
+def project_own_body(g0, g1, g2, g3, perturb, forward, backward, middle, rest):
+    x, _, c = place()
     for k, g in enumerate((g0, g1, g2, g3)):
-        for j in range(2):
-            s = (y ^ k) + 4 * j
-            level = 2 * s + parity
-            for m in range(2):
-                total = perturb[m, 0, level].astype(jnp.float32) * g[j, 0]
-                for v in range(1, VARS):
-                    total = total + perturb[m, v, level].astype(jnp.float32) * g[j, v]
-                middle[pl.ds(pl.multiple_of((m * HALF + s) * 16, 16), 16), :] = total
+        project(g, k, c, perturb, middle)
+        if k > 0:
+            rest[(k - 1) * 192 : k * 192, :] = g[...]
     pack_rows(lambda row: middle[pl.ds(row, 16, stride=ROWS), :], 16, forward, backward)
-
-
-def third_body(low, high, middle, coefs, out, buf0, buf1):
+    pack_rows(lambda row: g0[pl.ds(x * 96 + row, VARS, stride=ROWS), :], VARS, forward, backward, 192)
+
+
+def project_other_body(g0, rest, perturb, forward, backward, middle):
+    _, _, c = place()
+    project(g0, 0, 1 - c, perturb, middle)
+    for k in range(1, 4):
+        project(rest.at[(k - 1) * 192 : k * 192], k, 1 - c, perturb, middle)
+    pack_rows(lambda row: middle[pl.ds(row, 16, stride=ROWS), :], 16, forward, backward)
+
+
+def update_alpha(parity, out, alpha, mom, new_alpha, new_mom, stage0, stage1, sem):
+    for m in range(2):
+        for s in range(HALF):
+            at = pl.ds(pl.multiple_of(m * 256 + (2 * s + parity) * 16, 16), 16)
+            here = slice((m * HALF + s) * 16, (m * HALF + s) * 16 + 16)
+            old = alpha[at, :]
+            moved = momentum_rate * mom[at, :] + (old + out[here, :])
+            stage1[here, :] = moved
+            stage0[here, :] = old - step_rate * moved
+    copies = [
+        pltpu.make_async_copy(stage.reshape(2, HALF, ROWS, LANES), target.at[:, :, parity], sem.at[k])
+        for k, (stage, target) in enumerate(((stage0, new_alpha), (stage1, new_mom)))
+    ]
+    for copy in copies:
+        copy.start()
+    return copies
+
+
+def third_body(
+    low, high, middle, coefs, alpha, mom, grad, static_coefs, field, static_mom,
+    new_alpha, new_mom, new_static, new_static_mom,
+    buf0, buf1, out, stage0, stage1, sem,
+):
+    x, _, c = place()
+
     def emit(row, value):
         out[pl.ds(row, 16, stride=ROWS), :] = value
 
     load = halo_loader(low, high, lambda row: middle[pl.ds(row, 16, stride=ROWS), :], 16)
     diffuse(load, 16, 16, coefs, (buf0, buf1), emit)
-
-
-def fourth_body(low, high, middle, coefs, done, alpha, mom, new_alpha, new_mom, buf0, buf1, out):
-    third_body(low, high, middle, coefs, out, buf0, buf1)
+    copies = update_alpha(c, out, alpha, mom, new_alpha, new_mom, stage0, stage1, sem)
+
+    load = halo_loader(low, high, lambda row: grad[pl.ds(x * 96 + row, VARS, stride=ROWS), :], VARS, 192)
+    for row in range(SPAN):
+        buf0[row * 8 : row * 8 + VARS, :] = load(row)
+
+    def emit_static(row, value):
+        out[pl.ds(row, 8, stride=ROWS), :] = value
+
+    diffuse(lambda row: buf0[row * 8 : row * 8 + 8, :], 8, 8, static_coefs, (buf0, buf1), emit_static)
+    old = field[0:96, :]
+    moved = momentum_rate * static_mom[...] + (old + out[0:96, :])
+    new_static_mom[...] = moved
+    new_static[...] = old - step_rate * moved
+    for copy in copies:
+        copy.wait()
+
+
+def fourth_body(
+    low, high, middle, coefs, alpha, mom, half_alpha, half_mom, new_alpha, new_mom,
+    buf0, buf1, out, stage0, stage1, sem,
+):
+    def emit(row, value):
+        out[pl.ds(row, 16, stride=ROWS), :] = value
+
+    load = halo_loader(low, high, lambda row: middle[pl.ds(row, 16, stride=ROWS), :], 16)
+    diffuse(load, 16, 16, coefs, (buf0, buf1), emit)
     c = lax.axis_index("mem") % 2
-    for source, parity in ((done, c), (out, 1 - c)):
-        for m in range(2):
-            for s in range(HALF):
-                at = pl.ds(pl.multiple_of(m * 256 + (2 * s + parity) * 16, 16), 16)
-                old = alpha[at, :]
-                grad = old + source[(m * HALF + s) * 16 : (m * HALF + s) * 16 + 16, :]
-                moved = momentum_rate * mom[at, :] + grad
-                new_mom[at, :] = moved
-                new_alpha[at, :] = old - step_rate * moved
-
-
-def static_last_body(low, high, grad, coefs, field, mom, new_static, new_mom, buf0, buf1, result):
-    x, _, _ = place()
-
-    def emit(row, value):
-        result[pl.ds(row, VARS, stride=ROWS), :] = value
-
-    load = halo_loader(low, high, lambda row: grad[pl.ds(x * 96 + row, VARS, stride=ROWS), :], VARS)
-    diffuse(load, VARS, 8, coefs, (buf0, buf1), emit)
-    old = field[0:96, :]
-    moved = momentum_rate * mom[...] + (old + result[...])
-    new_mom[...] = moved
-    new_static[...] = old - step_rate * moved
+    for copy in update_alpha(1 - c, out, alpha, mom, new_alpha, new_mom, stage0, stage1, sem):
+        copy.wait()
 
 
 def local(
@@ -313,20 +368,19 @@
     def halo(forward, backward):
         return lax.ppermute(forward, "tile", up), lax.ppermute(backward, "tile", down)
 
-    alpha2 = alpha.reshape(512, LANES)
     mom2 = alpha_mom.reshape(512, LANES)
-    loc2 = loc_coef.reshape(32, LANES)
     bufs16 = [f32(SPAN * 16, LANES), f32(SPAN * 16, LANES)]
     bufs8 = [f32(SPAN * 8, LANES), f32(SPAN * 8, LANES)]
     raw = f32(88, LANES)
 
-    a_f, a_b, b_f, b_b, c_f, c_b, field = call(
+    a_f, a_b, b_f, b_b, alpha2, loc2, field = call(
         pack_body,
         "pack",
-        [VM, VM, ANY, VM],
-        [shape(216, LANES)] * 2 + [shape(192, LANES)] * 2 + [shape(96, LANES)] * 2 + [shape(128, LANES)],
-        [pltpu.SemaphoreType.DMA],
-    )(alpha2, loc2, static_ctl, static_coef.reshape(32, LANES))
+        [HBM] * 4,
+        [shape(312, LANES)] * 2 + [shape(192, LANES)] * 2 + [shape(512, LANES), shape(32, LANES), shape(128, LANES)],
+        [pltpu.SemaphoreType.DMA((4,))],
+        grant=GRANT,
+    )(alpha.reshape(512, LANES), loc_coef.reshape(32, LANES), static_ctl, static_coef.reshape(32, LANES))
     a_low, a_high = halo(a_f, a_b)
     b_low, b_high = halo(b_f, b_b)
 
@@ -344,64 +398,66 @@
         obs_weight.reshape(VARS, 16, 8, LANES),
     )
 
-    quarter = shape(2, VARS, ROWS, LANES)
     part_a, loc_k = call(
         first_body,
         "first",
         [VM] * 5,
         [shape(HALF, VARS, ROWS, LANES), shape(200, LANES)],
         [raw] + bufs16 + [f32(256, LANES)],
+        flops=BUSY,
     )(alpha2, a_low, a_high, loc2, perturb)
     got = swap(part_a, 1)
-    o0, o1, o2, o3 = call(
-        second_body,
-        "second",
-        [VM] * 6,
-        [quarter] * 4,
-        bufs16 + [f32(256, LANES)],
-    )(alpha2, b_low, b_high, loc_k, perturb, got)
-    r1, r2, r3 = swap(o1, 2), swap(o2, 4), swap(o3, 6)
-    c_low, c_high = halo(*lax.optimization_barrier((c_f, c_b, o0))[:2])
-    o0s, static_k = call(
+    static, static_k = call(
         static_first_body,
         "static_first",
-        [VM] * 4,
-        [quarter, shape(200, LANES)],
+        [VM] * 3,
+        [shape(96, LANES), shape(200, LANES)],
         [raw] + bufs8 + [f32(128, LANES)],
-    )(c_low, c_high, field, o0)
-    mine = (o0s + r1 + r2 + r3).reshape(192, LANES)
+        flops=BUSY,
+    )(a_low, a_high, field)
+    (second,) = call(second_body, "second", [VM] * 4, [shape(256, LANES)], bufs16, flops=BUSY)(
+        alpha2, b_low, b_high, loc_k
+    )
+    quarter = shape(192, LANES)
+    o0, o1, o2, o3 = call(sum_body, "sum", [VM] * 4, [quarter] * 4)(second, perturb, got, static)
+    r1, r2, r3 = swap(o1, 2), swap(o2, 4), swap(o3, 6)
+    mine = o0 + r1 + r2 + r3
     other = swap(mine, 8)
-    grad, g_f, g_b = call(
-        gradient_body,
-        "gradient",
-        [VM] * 3,
-        [shape(192, LANES), shape(72, LANES), shape(72, LANES)],
-    )(mine, other, sums)
-    full = (2, VARS, ROWS, LANES)
-    gs = [grad.reshape(full)]
-    gs = gs + [swap(grad, 2 * k).reshape(full) for k in range(1, 4)]
-    ps = [swap(g, 1) for g in gs]
-    g_low, g_high = halo(g_f, g_b)
-    packed = [shape(192, LANES), shape(192, LANES), shape(256, LANES)]
-    p_f, p_b, p_m = call(functools.partial(project_body, True), "project_own", [VM] * 5, packed)(*gs, perturb)
+    (grad,) = call(gradient_body, "gradient", [VM] * 3, [quarter])(mine, other, sums)
+    p0 = swap(grad, 1)
+    gs = [grad] + [swap(grad, 2 * k) for k in range(1, 4)]
+    p_f, p_b, p_m, rest = call(
+        project_own_body,
+        "project_own",
+        [VM] * 5,
+        [shape(264, LANES), shape(264, LANES), shape(256, LANES), shape(576, LANES)],
+    )(*gs, perturb)
     p_low, p_high = halo(p_f, p_b)
-    q_f, q_b, q_m = call(functools.partial(project_body, False), "project_other", [VM] * 5, packed)(*ps, perturb)
+    rest = swap(rest, 1)
+    q_f, q_b, q_m = call(
+        project_other_body, "project_other", [VM] * 3, [quarter, quarter, shape(256, LANES)]
+    )(p0, rest, perturb)
     q_low, q_high = halo(q_f, q_b)
-    new_static, new_static_mom = call(
-        static_last_body,
-        "static_last",
-        [VM] * 6,
-        [shape(96, LANES)] * 2,
-        bufs8 + [f32(96, LANES)],
-    )(g_low, g_high, grad, static_k, field, static_mom.reshape(96, LANES))
-    (done,) = call(third_body, "third", [VM] * 4, [shape(256, LANES)], bufs16)(p_low, p_high, p_m, loc_k)
+    whole = shape(2, HALF, 2, ROWS, LANES)
+    stages = [f32(256, LANES)] * 3 + [pltpu.SemaphoreType.DMA((2,))]
+    half_alpha, half_mom, new_static, new_static_mom = call(
+        third_body,
+        "third",
+        [VM] * 10,
+        [whole, whole, shape(96, LANES), shape(96, LANES)],
+        bufs16 + stages,
+        flops=BUSY,
+        out_specs=[HBM, HBM, VM, VM],
+    )(p_low, p_high, p_m, loc_k, alpha2, mom2, grad, static_k, field, static_mom.reshape(96, LANES))
     new_alpha, new_alpha_mom = call(
         fourth_body,
         "fourth",
-        [VM] * 7,
-        [shape(512, LANES)] * 2,
-        bufs16 + [f32(256, LANES)],
-    )(q_low, q_high, q_m, loc_k, done, alpha2, mom2)
+        [VM] * 6 + [HBM] * 2,
+        [whole, whole],
+        bufs16 + stages,
+        out_specs=[HBM, HBM],
+        aliases={6: 0, 7: 1},
+    )(q_low, q_high, q_m, loc_k, alpha2, mom2, half_alpha, half_mom)
     return (
         new_alpha.reshape(alpha.shape),
         new_alpha_mom.reshape(alpha.shape),

time: 81 us -> 68.6 us (0.85)
  waiting for transfers between devices: 36.3 us -> 21.9 us
  Pallas kernels: 12.2 us -> 14.1 us
  local copies, waits for them, and re-layouts: 3.63 us -> 2.49 us
  starting transfers between devices: 27.7 us -> 28.6 us
    ppermute x6 -> x4, waiting for transfers between devices: 11.7 us -> 0.01 us  [halo(): lax.ppermute(forward, 'tile', up)]
    ppermute x6 -> x4, waiting for transfers between devices: 16 us -> 6.56 us  [halo(): lax.ppermute(backward, 'tile', down)]
    ppermute x12 -> x10, waiting for transfers between devices: 8.64 us -> 15.3 us  [swap(): return lax.ppermute(value, 'mem', [(i, i ^ bits) for i in range(members)])]
    ppermute x6 -> x4, starting transfers between devices: 12 us -> 17.5 us  [halo(): lax.ppermute(forward, 'tile', up)]
    ppermute x6 -> x4, starting transfers between devices: 4.11 us -> 0.01 us  [halo(): lax.ppermute(backward, 'tile', down)]
    pallas_call x9, Pallas kernels: 9.05 us -> 10.9 us  [the longest x1 3.78 us: local(): call(third_body, 'third', [VM] * 10, [whole, whole, shape(96, LANES), sha...]
    unnamed x24 -> x22, local copies, waits for them, and re-layouts: 3.63 us -> 2.49 us
    ppermute x12 -> x10, starting transfers between devices: 11.5 us -> 11.1 us  [swap(): return lax.ppermute(value, 'mem', [(i, i ^ bits) for i in range(members)])]
  transfers between devices with their start and end apart: 24 -> 18, of which waited for: 11 -> 11; matrix products, arithmetic and copies ran while one was open for 0% -> 0% of each run, Pallas kernels for 8% -> 14%
where the time goes in v2:
time: 68.6 us; the launch traced here: 68.1 us
  starting transfers between devices  28.6 us (42%)
  waiting for transfers between devices  21.9 us (32%)
  Pallas kernels  14.1 us (21%)
  local copies, waits for them, and re-layouts  2.49 us (4%)
  between operations  0.99 us (1%)
    ppermute x4, starting transfers between devices, halo(): lax.ppermute(forward, 'tile', up)  17.5 us
    ppermute x10, waiting for transfers between devices, swap(): return lax.ppermute(value, 'mem', [(i, i ^ bits) for i in range(members)])  15.3 us
    ppermute x10, starting transfers between devices, swap(): return lax.ppermute(value, 'mem', [(i, i ^ bits) for i in range(members)])  11.1 us
    ppermute x4, waiting for transfers between devices, halo(): lax.ppermute(backward, 'tile', down)  6.56 us
    pallas_call x1, Pallas kernels, local(): call(third_body, 'third', [VM] * 10, [whole, whole, shape(96, LANES), sha...  3.78 us
    unnamed x22, local copies, waits for them, and re-layouts  2.49 us
    pallas_call x1, Pallas kernels, local(): call(fourth_body, 'fourth', [VM] * 6 + [HBM] * 2, [whole, whole], bufs16...  2.29 us
    pallas_call x1, Pallas kernels, local(): call(pack_body, 'pack', [HBM] * 4, [shape(312, LANES)] * 2 + [shape(192,...  1.86 us
  transfers between devices with their start and end apart: 18, of which 11 were waited for; matrix products, arithmetic and copies ran while one was open for 0% of the time, Pallas kernels for 14%

profile of v2, /device:TPU:102, one launch (start us, length us, event | category | flops | bytes accessed | tf_op | source)
XLA Modules:
  0.0 68.1 jit_solution(677567835412056327)
XLA Ops:
  0.6 0.0 copy-start
  0.6 0.0 copy-start.4
  0.7 0.8 %copy-done.4 = f32[2,16,128]{2,1,0:T(8,128)S(1)} copy-done((f32[2,16,128]{2,1,0:T(8,128)S(1)}, f32[2,16,128]{2,1,0:T(8,128)}, u32[]{:S(2)}) %copy-start.4) | copy-done | bytes 16408
  1.4 0.0 copy-start.5
  1.4 0.7 %copy-done.5 = f32[2,16,128]{2,1,0:T(8,128)S(1)} copy-done((f32[2,16,128]{2,1,0:T(8,128)S(1)}, f32[2,16,128]{2,1,0:T(8,128)}, u32[]{:S(2)}) %copy-start.5) | copy-done | bytes 16408
  2.2 1.9 %pack.1 = (f32[312,128]{1,0:T(8,128)S(1)}, f32[312,128]{1,0:T(8,128)S(1)}, f32[192,128]{1,0:T(8,128)S(1)}, f32[192,128]{1,0:T(8,128)S(1)}, f32[512,128]{1,0:T(8,...) custom-call(f32[512,128]{1,0:T(8,128)} %bitcast.26, f32[32,128]{1,0:T(8,128)S(1)} %bitcast.19, ...), custom_call_target="tpu_custom_call" | custom-call | flops 1000000 | bytes 1000000 | tf_op jit(solution)/shard_map/pack/pallas_call | solution.py:376
  4.0 3.5 %collective-permute-start.2 = (f32[312,128]{1,0:T(8,128)S(1)}, f32[312,128]{1,0:T(8,128)S(1)}, u32[]{:S(2)}, u32[]{:S(2)}) collective-permute-start(f32[312,128]{1,0:T(8,128)S(1)} %get-tuple-element.35), channel_id=1, source_target_pairs={{0,1},{1,2},{2,3},{3,4},{4,5},{5,6},{6,7},{7,8},{8,9},{9,10},{10,1... | collective-permute-start | bytes 479240 | tf_op jit(solution)/shard_map/ppermute | solution.py:369
  7.5 0.0 collective-permute-start.3
  7.5 4.1 %collective-permute-start = (f32[192,128]{1,0:T(8,128)S(1)}, f32[192,128]{1,0:T(8,128)S(1)}, u32[]{:S(2)}, u32[]{:S(2)}) collective-permute-start(f32[192,128]{1,0:T(8,128)S(1)} %get-tuple-element.33), channel_id=1, source_target_pairs={{0,1},{1,2},{2,3},{3,4},{4,5},{5,6},{6,7},{7,8},{8,9},{9,10},{10,1... | collective-permute-start | bytes 294920 | tf_op jit(solution)/shard_map/ppermute | solution.py:369
  11.6 0.0 collective-permute-start.1
  11.6 0.0 collective-permute-done.2.low
  11.6 3.6 %collective-permute-done.3.high = f32[312,128]{1,0:T(8,128)S(1)} collective-permute-done((f32[312,128]{1,0:T(8,128)S(1)}, f32[312,128]{1,0:T(8,128)S(1)}, u32[]{:S(2)}, u32[]{:S(2)}) %collective-permute-start.3) | collective-permute-done | bytes 159776 | tf_op jit(solution)/shard_map/ppermute | solution.py:369
  15.3 0.0 copy-done
  15.3 0.9 %copy-done.2 = f32[512,128]{1,0:T(8,128)S(1)} copy-done((f32[512,128]{1,0:T(8,128)S(1)}, f32[512,128]{1,0:T(8,128)}, u32[]{:S(2)}) %copy-start.2) | copy-done | bytes 262168
  16.2 1.7 %first.1 = (f32[8,6,16,128]{3,2,1,0:T(8,128)S(1)}, f32[200,128]{1,0:T(8,128)S(1)}) custom-call(f32[512,128]{1,0:T(8,128)S(1)} %copy-done.2, f32[312,128]{1,0:T(8,128)S(1)} %collective-permute-done.2.low, f32[312,128]{1,0:T(8,128)S(1)} %collective-permute-done.3.high, f32[32,128]{1,0:T(8,128)S(1)} %get-tuple-element.37.loc, ...), custom_call_target="tpu_custom_call" | custom-call | flops 5000000000 | bytes 1000000 | tf_op jit(solution)/shard_map/first/pallas_call | solution.py:401
  17.9 0.1 collective-permute-start.4
  18.0 0.0 copy-start.3
  18.0 1.0 %static_first.1 = (f32[96,128]{1,0:T(8,128)S(1)}, f32[200,128]{1,0:T(8,128)S(1)}) custom-call(f32[312,128]{1,0:T(8,128)S(1)} %collective-permute-done.2.low, f32[312,128]{1,0:T(8,128)S(1)} %collective-permute-done.3.high, f32[128,128]{1,0:T(8,128)S(1)} %get-tuple-element.40.field), custom_call_target="tpu_custom_call" | custom-call | flops 5000000000 | bytes 1000000 | tf_op jit(solution)/shard_map/static_first/pallas_call | solution.py:410
  19.0 0.0 collective-permute-done.low
  19.1 0.0 collective-permute-done.1.high
  19.1 0.0 copy-done.3
  19.1 1.5 %second.1.local = f32[256,128]{1,0:T(8,128)S(1)} custom-call(f32[512,128]{1,0:T(8,128)S(1)} %copy-done.3, f32[192,128]{1,0:T(8,128)S(1)} %collective-permute-done.low, f32[192,128]{1,0:T(8,128)S(1)} %collective-permute-done.1.high, f32[200,128]{1,0:T(8,128)S(1)} %get-tuple-element.38.coefs), custom_call_target="tpu_custom_call" | custom-call | flops 5000000000 | bytes 1000000 | tf_op jit(solution)/shard_map/second/pallas_call | solution.py:418
  20.6 0.0 collective-permute-done.4.received
  20.6 0.0 copy-start.7
  20.6 0.1 sum.1
  20.8 0.0 copy-start.6
  20.8 1.7 %collective-permute-start.5 = (f32[192,128]{1,0:T(8,128)S(1)}, f32[192,128]{1,0:T(8,128)S(1)}, u32[]{:S(2)}, u32[]{:S(2)}) collective-permute-start(f32[192,128]{1,0:T(8,128)S(1)} %get-tuple-element.43), channel_id=1, source_target_pairs={{0,32},{16,48},{32,0},{48,16},{64,96},{80,112},{96,64},{112,80},{1... | collective-permute-start | bytes 294920 | tf_op jit(solution)/shard_map/ppermute | solution.py:366
  22.4 2.9 %collective-permute-start.6 = (f32[192,128]{1,0:T(8,128)S(1)}, f32[192,128]{1,0:T(8,128)S(1)}, u32[]{:S(2)}, u32[]{:S(2)}) collective-permute-start(f32[192,128]{1,0:T(8,128)S(1)} %get-tuple-element.44), channel_id=1, source_target_pairs={{0,64},{16,80},{32,96},{48,112},{64,0},{80,16},{96,32},{112,48},{1... | collective-permute-start | bytes 294920 | tf_op jit(solution)/shard_map/ppermute | solution.py:366
  25.3 0.2 collective-permute-start.7
  25.6 0.5 collective-permute-done.5
  26.0 4.7 %collective-permute-done.6 = f32[192,128]{1,0:T(8,128)S(1)} collective-permute-done((f32[192,128]{1,0:T(8,128)S(1)}, f32[192,128]{1,0:T(8,128)S(1)}, u32[]{:S(2)}, u32[]{:S(2)}) %collective-permute-start.6) | collective-permute-done | bytes 98336 | tf_op jit(solution)/shard_map/ppermute | solution.py:366
  30.7 2.0 %collective-permute-done.7 = f32[192,128]{1,0:T(8,128)S(1)} collective-permute-done((f32[192,128]{1,0:T(8,128)S(1)}, f32[192,128]{1,0:T(8,128)S(1)}, u32[]{:S(2)}, u32[]{:S(2)}) %collective-permute-start.7) | collective-permute-done | bytes 98336 | tf_op jit(solution)/shard_map/ppermute | solution.py:366
  32.7 0.0 copy-start.9
  32.7 1.2 %collective-permute-start.8 = (f32[192,128]{1,0:T(8,128)S(1)}, f32[192,128]{1,0:T(8,128)S(1)}, u32[]{:S(2)}, u32[]{:S(2)}) collective-permute-start(f32[192,128]{1,0:T(8,128)S(1)} %add_add_fusion.mine), channel_id=1, source_target_pairs={{0,128},{16,144},{32,160},{48,176},{64,192},{80,208},{96,224},{112... | collective-permute-start | bytes 294920 | tf_op jit(solution)/shard_map/ppermute | solution.py:366
  33.9 0.0 copy-done.7
  33.9 0.0 copy-done.6
  33.9 0.0 copy-done.10
  34.0 0.0 copy-done.9
  34.0 1.5 %prepare.1.sums = f32[384,128]{1,0:T(8,128)S(1)} custom-call(s32[8,128]{1,0:T(8,128)S(1)} %bitcast.24, s32[8,128]{1,0:T(8,128)S(1)} %bitcast.25, f32[6,16,8,128]{3,2,1,0:T(8,128)S(1)} %bitcast.21, f32[6,16,8,128]{3,2,1,0:T(8,128)S(1)} %bitcast.22), custom_call_target="tpu_custom_call" | custom-call | flops 1000000000 | bytes 1000000 | tf_op jit(solution)/shard_map/prepare/pallas_call | solution.py:387
  35.5 3.6 %collective-permute-done.8.other = f32[192,128]{1,0:T(8,128)S(1)} collective-permute-done((f32[192,128]{1,0:T(8,128)S(1)}, f32[192,128]{1,0:T(8,128)S(1)}, u32[]{:S(2)}, u32[]{:S(2)}) %collective-permute-start.8) | collective-permute-done | bytes 98336 | tf_op jit(solution)/shard_map/ppermute | solution.py:366
  39.1 0.1 collective-permute-start.10
  39.2 1.9 %collective-permute-start.11 = (f32[192,128]{1,0:T(8,128)S(1)}, f32[192,128]{1,0:T(8,128)S(1)}, u32[]{:S(2)}, u32[]{:S(2)}) collective-permute-start(f32[192,128]{1,0:T(8,128)S(1)} %gradient.1.g0.grad), channel_id=1, source_target_pairs={{0,64},{16,80},{32,96},{48,112},{64,0},{80,16},{96,32},{112,48},{1... | collective-permute-start | bytes 294920 | tf_op jit(solution)/shard_map/ppermute | solution.py:366
  41.1 2.8 %collective-permute-start.12 = (f32[192,128]{1,0:T(8,128)S(1)}, f32[192,128]{1,0:T(8,128)S(1)}, u32[]{:S(2)}, u32[]{:S(2)}) collective-permute-start(f32[192,128]{1,0:T(8,128)S(1)} %gradient.1.g0.grad), channel_id=1, source_target_pairs={{0,96},{16,112},{32,64},{48,80},{64,32},{80,48},{96,0},{112,16},{1... | collective-permute-start | bytes 294920 | tf_op jit(solution)/shard_map/ppermute | solution.py:366
  43.9 0.2 collective-permute-done.10.g1
  44.1 1.8 %collective-permute-done.11.g2 = f32[192,128]{1,0:T(8,128)S(1)} collective-permute-done((f32[192,128]{1,0:T(8,128)S(1)}, f32[192,128]{1,0:T(8,128)S(1)}, u32[]{:S(2)}, u32[]{:S(2)}) %collective-permute-start.11) | collective-permute-done | bytes 98336 | tf_op jit(solution)/shard_map/ppermute | solution.py:366
  45.9 1.5 %collective-permute-done.12.g3 = f32[192,128]{1,0:T(8,128)S(1)} collective-permute-done((f32[192,128]{1,0:T(8,128)S(1)}, f32[192,128]{1,0:T(8,128)S(1)}, u32[]{:S(2)}, u32[]{:S(2)}) %collective-permute-start.12) | collective-permute-done | bytes 98336 | tf_op jit(solution)/shard_map/ppermute | solution.py:366
  47.3 0.2 project_own.1
  47.5 0.1 collective-permute-start.13
  47.6 5.7 %collective-permute-start.16 = (f32[264,128]{1,0:T(8,128)S(1)}, f32[264,128]{1,0:T(8,128)S(1)}, u32[]{:S(2)}, u32[]{:S(2)}) collective-permute-start(f32[264,128]{1,0:T(8,128)S(1)} %get-tuple-element.50), channel_id=1, source_target_pairs={{0,1},{1,2},{2,3},{3,4},{4,5},{5,6},{6,7},{7,8},{8,9},{9,10},{10,1... | collective-permute-start | bytes 405512 | tf_op jit(solution)/shard_map/ppermute | solution.py:369
  53.2 0.0 collective-permute-start.17
  53.2 0.2 collective-permute-start.9
  53.4 1.1 %collective-permute-done.9.g0 = f32[192,128]{1,0:T(8,128)S(1)} collective-permute-done((f32[192,128]{1,0:T(8,128)S(1)}, f32[192,128]{1,0:T(8,128)S(1)}, u32[]{:S(2)}, u32[]{:S(2)}) %collective-permute-start.9) | collective-permute-done | bytes 98336 | tf_op jit(solution)/shard_map/ppermute | solution.py:366
  54.5 0.0 collective-permute-done.13.rest
  54.5 0.1 project_other.1
  54.7 4.2 %collective-permute-start.14 = (f32[192,128]{1,0:T(8,128)S(1)}, f32[192,128]{1,0:T(8,128)S(1)}, u32[]{:S(2)}, u32[]{:S(2)}) collective-permute-start(f32[192,128]{1,0:T(8,128)S(1)} %get-tuple-element.47), channel_id=1, source_target_pairs={{0,1},{1,2},{2,3},{3,4},{4,5},{5,6},{6,7},{7,8},{8,9},{9,10},{10,1... | collective-permute-start | bytes 294920 | tf_op jit(solution)/shard_map/ppermute | solution.py:369
  58.9 0.0 collective-permute-start.15
  58.9 0.0 collective-permute-done.16.low
  58.9 2.2 %collective-permute-done.17.high = f32[264,128]{1,0:T(8,128)S(1)} collective-permute-done((f32[264,128]{1,0:T(8,128)S(1)}, f32[264,128]{1,0:T(8,128)S(1)}, u32[]{:S(2)}, u32[]{:S(2)}) %collective-permute-start.17) | collective-permute-done | bytes 135200 | tf_op jit(solution)/shard_map/ppermute | solution.py:369
  61.1 0.0 copy-done.1
  61.1 0.0 copy-done.8
  61.1 3.8 %third.1 = (f32[2,8,2,16,128]{4,3,2,1,0:T(8,128)}, f32[2,8,2,16,128]{4,3,2,1,0:T(8,128)}, f32[96,128]{1,0:T(8,128)}, f32[96,128]{1,0:T(8,128)}) custom-call(f32[264,128]{1,0:T(8,128)S(1)} %collective-permute-done.16.low, f32[264,128]{1,0:T(8,128)S(1)} %collective-permute-done.17.high, f32[256,128]{1,0:T(8,128)S(1)} %get-tuple-element.52.middle, ...), custom_call_target="tpu_custom_call" | custom-call | flops 5000000000 | bytes 1000000 | tf_op jit(solution)/shard_map/third/pallas_call | solution.py:443
  64.9 0.0 collective-permute-done.14.low
  64.9 0.7 %collective-permute-done.15.high = f32[192,128]{1,0:T(8,128)S(1)} collective-permute-done((f32[192,128]{1,0:T(8,128)S(1)}, f32[192,128]{1,0:T(8,128)S(1)}, u32[]{:S(2)}, u32[]{:S(2)}) %collective-permute-start.15) | collective-permute-done | bytes 98336 | tf_op jit(solution)/shard_map/ppermute | solution.py:369
  65.6 2.3 %fourth.1 = (f32[2,8,2,16,128]{4,3,2,1,0:T(8,128)}, f32[2,8,2,16,128]{4,3,2,1,0:T(8,128)}) custom-call(f32[192,128]{1,0:T(8,128)S(1)} %collective-permute-done.14.low, f32[192,128]{1,0:T(8,128)S(1)} %collective-permute-done.15.high, f32[256,128]{1,0:T(8,128)S(1)} %get-tuple-element.49.middle, ...), custom_call_target="tpu_custom_call", output_to_operand_aliasing={{0}: (6, {}), {1}: (7, {})} | custom-call | flops 1000000 | bytes 1000000 | tf_op jit(solution)/shard_map/fourth/pallas_call | solution.py:452
  (6 shorter events, 0.0 us)
Async XLA Ops:
  0.6 14.6 %copy-start = (bf16[2,6,16,16,128]{4,3,2,1,0:T(8,128)(2,1)S(1)}, bf16[2,6,16,16,128]{4,3,2,1,0:T(8,128)(2,1)}, u32[]{:S(2)}) copy-start(bf16[2,6,16,16,128]{4,3,2,1,0:T(8,128)(2,1)} %perturb.7) | copy-start | bytes 2359300
  0.6 0.8 %copy-start.4 = (f32[2,16,128]{2,1,0:T(8,128)S(1)}, f32[2,16,128]{2,1,0:T(8,128)}, u32[]{:S(2)}) copy-start(f32[2,16,128]{2,1,0:T(8,128)} %param.16) | copy-start | bytes 49156
  1.4 0.7 %copy-start.5 = (f32[2,16,128]{2,1,0:T(8,128)S(1)}, f32[2,16,128]{2,1,0:T(8,128)}, u32[]{:S(2)}) copy-start(f32[2,16,128]{2,1,0:T(8,128)} %param.17) | copy-start | bytes 49156
  4.0 7.6 %collective-permute-start.2 = (f32[312,128]{1,0:T(8,128)S(1)}, f32[312,128]{1,0:T(8,128)S(1)}, u32[]{:S(2)}, u32[]{:S(2)}) collective-permute-start(f32[312,128]{1,0:T(8,128)S(1)} %get-tuple-element.35), channel_id=1, source_target_pairs={{0,1},{1,2},{2,3},{3,4},{4,5},{5,6},{6,7},{7,8},{8,9},{9,10},{10,1... | collective-permute-start | bytes 479240 | tf_op jit(solution)/shard_map/ppermute | solution.py:369
  7.5 7.8 %collective-permute-start.3 = (f32[312,128]{1,0:T(8,128)S(1)}, f32[312,128]{1,0:T(8,128)S(1)}, u32[]{:S(2)}, u32[]{:S(2)}) collective-permute-start(f32[312,128]{1,0:T(8,128)S(1)} %get-tuple-element.36), channel_id=1, source_target_pairs={{1,0},{2,1},{3,2},{4,3},{5,4},{6,5},{7,6},{8,7},{9,8},{10,9},{11,1... | collective-permute-start | bytes 479240 | tf_op jit(solution)/shard_map/ppermute | solution.py:369
  7.5 11.5 %collective-permute-start = (f32[192,128]{1,0:T(8,128)S(1)}, f32[192,128]{1,0:T(8,128)S(1)}, u32[]{:S(2)}, u32[]{:S(2)}) collective-permute-start(f32[192,128]{1,0:T(8,128)S(1)} %get-tuple-element.33), channel_id=1, source_target_pairs={{0,1},{1,2},{2,3},{3,4},{4,5},{5,6},{6,7},{7,8},{8,9},{9,10},{10,1... | collective-permute-start | bytes 294920 | tf_op jit(solution)/shard_map/ppermute | solution.py:369
  11.6 7.4 %collective-permute-start.1 = (f32[192,128]{1,0:T(8,128)S(1)}, f32[192,128]{1,0:T(8,128)S(1)}, u32[]{:S(2)}, u32[]{:S(2)}) collective-permute-start(f32[192,128]{1,0:T(8,128)S(1)} %get-tuple-element.34), channel_id=1, source_target_pairs={{1,0},{2,1},{3,2},{4,3},{5,4},{6,5},{7,6},{8,7},{9,8},{10,9},{11,1... | collective-permute-start | bytes 294920 | tf_op jit(solution)/shard_map/ppermute | solution.py:369
  15.3 1.0 %copy-start.2 = (f32[512,128]{1,0:T(8,128)S(1)}, f32[512,128]{1,0:T(8,128)}, u32[]{:S(2)}) copy-start(f32[512,128]{1,0:T(8,128)} %get-tuple-element.32.alpha) | copy-start | bytes 786436
  17.9 2.7 %collective-permute-start.4 = (f32[8,6,16,128]{3,2,1,0:T(8,128)S(1)}, f32[8,6,16,128]{3,2,1,0:T(8,128)S(1)}, u32[]{:S(2)}, u32[]{:S(2)}) collective-permute-start(f32[8,6,16,128]{3,2,1,0:T(8,128)S(1)} %get-tuple-element.39), channel_id=1, source_target_pairs={{0,16},{16,0},{32,48},{48,32},{64,80},{80,64},{96,112},{112,96},{1... | collective-permute-start | bytes 1179656 | tf_op jit(solution)/shard_map/ppermute | solution.py:366
  18.0 1.1 %copy-start.3 = (f32[512,128]{1,0:T(8,128)S(1)}, f32[512,128]{1,0:T(8,128)}, u32[]{:S(2)}) copy-start(f32[512,128]{1,0:T(8,128)} %get-tuple-element.32.alpha) | copy-start | bytes 786436
  20.6 13.3 %copy-start.7 = (f32[6,16,1,1024]{3,2,1,0:T(1,128)S(1)}, f32[6,16,1,1024]{3,2,1,0:T(1,128)}, u32[]{:S(2)}) copy-start(f32[6,16,1,1024]{3,2,1,0:T(1,128)} %param.21) | copy-start | bytes 1179652
  20.8 13.2 %copy-start.6 = (f32[6,16,1,1024]{3,2,1,0:T(1,128)S(1)}, f32[6,16,1,1024]{3,2,1,0:T(1,128)}, u32[]{:S(2)}) copy-start(f32[6,16,1,1024]{3,2,1,0:T(1,128)} %param.20) | copy-start | bytes 1179652
  20.8 5.3 %collective-permute-start.5 = (f32[192,128]{1,0:T(8,128)S(1)}, f32[192,128]{1,0:T(8,128)S(1)}, u32[]{:S(2)}, u32[]{:S(2)}) collective-permute-start(f32[192,128]{1,0:T(8,128)S(1)} %get-tuple-element.43), channel_id=1, source_target_pairs={{0,32},{16,48},{32,0},{48,16},{64,96},{80,112},{96,64},{112,80},{1... | collective-permute-start | bytes 294920 | tf_op jit(solution)/shard_map/ppermute | solution.py:366
  22.4 8.3 %collective-permute-start.6 = (f32[192,128]{1,0:T(8,128)S(1)}, f32[192,128]{1,0:T(8,128)S(1)}, u32[]{:S(2)}, u32[]{:S(2)}) collective-permute-start(f32[192,128]{1,0:T(8,128)S(1)} %get-tuple-element.44), channel_id=1, source_target_pairs={{0,64},{16,80},{32,96},{48,112},{64,0},{80,16},{96,32},{112,48},{1... | collective-permute-start | bytes 294920 | tf_op jit(solution)/shard_map/ppermute | solution.py:366
  25.3 7.4 %collective-permute-start.7 = (f32[192,128]{1,0:T(8,128)S(1)}, f32[192,128]{1,0:T(8,128)S(1)}, u32[]{:S(2)}, u32[]{:S(2)}) collective-permute-start(f32[192,128]{1,0:T(8,128)S(1)} %get-tuple-element.45), channel_id=1, source_target_pairs={{0,96},{16,112},{32,64},{48,80},{64,32},{80,48},{96,0},{112,16},{1... | collective-permute-start | bytes 294920 | tf_op jit(solution)/shard_map/ppermute | solution.py:366
  32.7 1.2 %copy-start.10 = (s32[1,1024]{1,0:T(1,128)S(1)}, s32[1,1024]{1,0:T(1,128)}, u32[]{:S(2)}) copy-start(s32[1,1024]{1,0:T(1,128)} %param.19) | copy-start | bytes 12292
  32.7 1.2 %copy-start.9 = (s32[1,1024]{1,0:T(1,128)S(1)}, s32[1,1024]{1,0:T(1,128)}, u32[]{:S(2)}) copy-start(s32[1,1024]{1,0:T(1,128)} %param.18) | copy-start | bytes 12292
  32.7 6.3 %collective-permute-start.8 = (f32[192,128]{1,0:T(8,128)S(1)}, f32[192,128]{1,0:T(8,128)S(1)}, u32[]{:S(2)}, u32[]{:S(2)}) collective-permute-start(f32[192,128]{1,0:T(8,128)S(1)} %add_add_fusion.mine), channel_id=1, source_target_pairs={{0,128},{16,144},{32,160},{48,176},{64,192},{80,208},{96,224},{112... | collective-permute-start | bytes 294920 | tf_op jit(solution)/shard_map/ppermute | solution.py:366
  39.1 5.0 %collective-permute-start.10 = (f32[192,128]{1,0:T(8,128)S(1)}, f32[192,128]{1,0:T(8,128)S(1)}, u32[]{:S(2)}, u32[]{:S(2)}) collective-permute-start(f32[192,128]{1,0:T(8,128)S(1)} %gradient.1.g0.grad), channel_id=1, source_target_pairs={{0,32},{16,48},{32,0},{48,16},{64,96},{80,112},{96,64},{112,80},{1... | collective-permute-start | bytes 294920 | tf_op jit(solution)/shard_map/ppermute | solution.py:366
  39.2 6.7 %collective-permute-start.11 = (f32[192,128]{1,0:T(8,128)S(1)}, f32[192,128]{1,0:T(8,128)S(1)}, u32[]{:S(2)}, u32[]{:S(2)}) collective-permute-start(f32[192,128]{1,0:T(8,128)S(1)} %gradient.1.g0.grad), channel_id=1, source_target_pairs={{0,64},{16,80},{32,96},{48,112},{64,0},{80,16},{96,32},{112,48},{1... | collective-permute-start | bytes 294920 | tf_op jit(solution)/shard_map/ppermute | solution.py:366
  41.1 6.3 %collective-permute-start.12 = (f32[192,128]{1,0:T(8,128)S(1)}, f32[192,128]{1,0:T(8,128)S(1)}, u32[]{:S(2)}, u32[]{:S(2)}) collective-permute-start(f32[192,128]{1,0:T(8,128)S(1)} %gradient.1.g0.grad), channel_id=1, source_target_pairs={{0,96},{16,112},{32,64},{48,80},{64,32},{80,48},{96,0},{112,16},{1... | collective-permute-start | bytes 294920 | tf_op jit(solution)/shard_map/ppermute | solution.py:366
  47.5 7.1 %collective-permute-start.13 = (f32[576,128]{1,0:T(8,128)S(1)}, f32[576,128]{1,0:T(8,128)S(1)}, u32[]{:S(2)}, u32[]{:S(2)}) collective-permute-start(f32[576,128]{1,0:T(8,128)S(1)} %get-tuple-element.46), channel_id=1, source_target_pairs={{0,16},{16,0},{32,48},{48,32},{64,80},{80,64},{96,112},{112,96},{1... | collective-permute-start | bytes 884744 | tf_op jit(solution)/shard_map/ppermute | solution.py:366
  47.6 11.3 %collective-permute-start.16 = (f32[264,128]{1,0:T(8,128)S(1)}, f32[264,128]{1,0:T(8,128)S(1)}, u32[]{:S(2)}, u32[]{:S(2)}) collective-permute-start(f32[264,128]{1,0:T(8,128)S(1)} %get-tuple-element.50), channel_id=1, source_target_pairs={{0,1},{1,2},{2,3},{3,4},{4,5},{5,6},{6,7},{7,8},{8,9},{9,10},{10,1... | collective-permute-start | bytes 405512 | tf_op jit(solution)/shard_map/ppermute | solution.py:369
  53.2 7.9 %copy-start.1 = (f32[2,16,16,128]{3,2,1,0:T(8,128)S(1)}, f32[2,16,16,128]{3,2,1,0:T(8,128)}, u32[]{:S(2)}) copy-start(f32[2,16,16,128]{3,2,1,0:T(8,128)} %param.13) | copy-start | bytes 786436
  53.2 7.9 %copy-start.8 = (f32[6,1,16,128]{3,2,1,0:T(8,128)S(1)}, f32[6,1,16,128]{3,2,1,0:T(8,128)}, u32[]{:S(2)}) copy-start(f32[6,1,16,128]{3,2,1,0:T(8,128)} %param.15) | copy-start | bytes 147460
  53.2 7.9 %collective-permute-start.17 = (f32[264,128]{1,0:T(8,128)S(1)}, f32[264,128]{1,0:T(8,128)S(1)}, u32[]{:S(2)}, u32[]{:S(2)}) collective-permute-start(f32[264,128]{1,0:T(8,128)S(1)} %get-tuple-element.51), channel_id=1, source_target_pairs={{1,0},{2,1},{3,2},{4,3},{5,4},{6,5},{7,6},{8,7},{9,8},{10,9},{11,1... | collective-permute-start | bytes 405512 | tf_op jit(solution)/shard_map/ppermute | solution.py:369
  53.2 1.3 %collective-permute-start.9 = (f32[192,128]{1,0:T(8,128)S(1)}, f32[192,128]{1,0:T(8,128)S(1)}, u32[]{:S(2)}, u32[]{:S(2)}) collective-permute-start(f32[192,128]{1,0:T(8,128)S(1)} %gradient.1.g0.grad), channel_id=1, source_target_pairs={{0,16},{16,0},{32,48},{48,32},{64,80},{80,64},{96,112},{112,96},{1... | collective-permute-start | bytes 294920 | tf_op jit(solution)/shard_map/ppermute | solution.py:366
  54.7 10.2 %collective-permute-start.14 = (f32[192,128]{1,0:T(8,128)S(1)}, f32[192,128]{1,0:T(8,128)S(1)}, u32[]{:S(2)}, u32[]{:S(2)}) collective-permute-start(f32[192,128]{1,0:T(8,128)S(1)} %get-tuple-element.47), channel_id=1, source_target_pairs={{0,1},{1,2},{2,3},{3,4},{4,5},{5,6},{6,7},{7,8},{8,9},{9,10},{10,1... | collective-permute-start | bytes 294920 | tf_op jit(solution)/shard_map/ppermute | solution.py:369
  58.9 6.7 %collective-permute-start.15 = (f32[192,128]{1,0:T(8,128)S(1)}, f32[192,128]{1,0:T(8,128)S(1)}, u32[]{:S(2)}, u32[]{:S(2)}) collective-permute-start(f32[192,128]{1,0:T(8,128)S(1)} %get-tuple-element.48), channel_id=1, source_target_pairs={{1,0},{2,1},{3,2},{4,3},{5,4},{6,5},{7,6},{8,7},{9,8},{10,9},{11,1... | collective-permute-start | bytes 294920 | tf_op jit(solution)/shard_map/ppermute | solution.py:369

commit v3 on v2

--- a/solution.py
+++ b/solution.py
@@ -17,7 +17,8 @@
 momentum_rate = 0.9
 step_rate = 0.5
 
-GRANT = 53.2
+GRANT = 54.6
+GRANT2 = 53.2
 BUSY = 5000000000
 
 VM = pl.BlockSpec(memory_space=pltpu.VMEM)
@@ -29,7 +30,7 @@
     return jax.ShapeDtypeStruct(dims, jnp.float32)
 
 
-def call(body, name, ins, outs, scratch=(), flops=1000000, out_specs=None, aliases=None, grant=32):
+def call(body, name, ins, outs, scratch=(), flops=1000000, out_specs=None, grant=32):
     return pl.pallas_call(
         body,
         name=name,
@@ -37,7 +38,6 @@
         out_specs=out_specs or [VM] * len(outs),
         out_shape=list(outs),
         scratch_shapes=list(scratch),
-        input_output_aliases=aliases or {},
         compiler_params=pltpu.CompilerParams(vmem_limit_bytes=int(grant * 1024 * 1024)),
         cost_estimate=pl.CostEstimate(flops=flops, bytes_accessed=1000000, transcendentals=0),
     )
@@ -119,14 +119,11 @@
     return jnp.concatenate(parts, axis=0)
 
 
-def pack_body(alpha_in, loc_in, static_ctl, static_coef, a_f, a_b, b_f, b_b, alpha, loc, field, sem):
-    mem = lax.axis_index("mem")
-    own = mem % 2
+def pack_body(alpha_in, loc_in, a_f, a_b, alpha, loc, sem):
+    own = lax.axis_index("mem") % 2
     copies = [
         pltpu.make_async_copy(alpha_in, alpha, sem.at[0]),
         pltpu.make_async_copy(loc_in, loc, sem.at[1]),
-        pltpu.make_async_copy(static_ctl.at[:, mem], field.reshape(8, ROWS, LANES).at[0:VARS], sem.at[2]),
-        pltpu.make_async_copy(static_coef, field.at[VARS * ROWS : 8 * ROWS], sem.at[3]),
     ]
     for copy in copies:
         copy.start()
@@ -136,8 +133,6 @@
     for k in range(2):
         a_f[192 + k * 12 : 204 + k * 12, :] = loc[k * 16 + 4 : k * 16 + 16, :]
         a_b[192 + k * 12 : 204 + k * 12, :] = loc[k * 16 : k * 16 + 12, :]
-    pack_rows(lambda row: field[pl.ds(row, 8, stride=ROWS), :], 8, a_f, a_b, 216)
-    pack_rows(lambda row: alpha_row(alpha, own, row), 16, b_f, b_b)
 
 
 def halo_loader(low, high, middle, width, base=0):
@@ -175,16 +170,17 @@
 
 def static_first_body(low, high, field, out, coefs, raw, buf0, buf1, result):
     build_coefs(
-        low[pl.ds(222, 12, stride=8), :], field[96:112, :], high[pl.ds(222, 12, stride=8), :],
-        low[pl.ds(223, 12, stride=8), :], field[112:128, :], high[pl.ds(223, 12, stride=8), :], raw, coefs,
+        low[pl.ds(6, 12, stride=16), :], field[96:112, :], high[pl.ds(6, 12, stride=16), :],
+        low[pl.ds(7, 12, stride=16), :], field[112:128, :], high[pl.ds(7, 12, stride=16), :], raw, coefs,
     )
 
     def emit(row, value):
-        result[pl.ds(row, 8, stride=ROWS), :] = value
-
-    load = halo_loader(low, high, lambda row: field[pl.ds(row, 8, stride=ROWS), :], 8, 216)
-    diffuse(load, 8, 8, coefs, (buf0, buf1), emit)
-    out[...] = result[0:96, :]
+        result[pl.ds(row, 16, stride=ROWS), :] = value
+
+    load = halo_loader(low, high, lambda row: field[pl.ds(row, 16, stride=ROWS), :], 16)
+    diffuse(load, 16, 16, coefs, (buf0, buf1), emit)
+    for j in range(2):
+        out[j * 96 : j * 96 + 96, :] = result[j * 128 : j * 128 + 96, :]
 
 
 def second_body(alpha, low, high, coefs, out, buf0, buf1):
@@ -196,8 +192,8 @@
     diffuse(load, 16, 16, coefs, (buf0, buf1), emit)
 
 
-def sum_body(local, perturb, received, static, o0, o1, o2, o3):
-    x, y, parity = place()
+def sum_body(local, perturb, received, o0, o1, o2, o3):
+    _, y, parity = place()
     for k, out in enumerate((o0, o1, o2, o3)):
         for j in range(2):
             s = (y ^ k) + 4 * j
@@ -208,23 +204,30 @@
                 total = first * perturb[0, v, level].astype(jnp.float32)
                 total = total + other * perturb[1, v, level].astype(jnp.float32)
                 total = total + received[s, v]
-                if k == 0:
-                    total = total + jnp.where(x == j, static[v * 16 : v * 16 + 16, :], 0.0)
                 out[j * 96 + v * 16 : j * 96 + v * 16 + 16, :] = total
 
 
-def prepare_body(cell, mask, value, weight, sums, held, sem):
+def prepare_body(
+    alpha, cell, mask, value, weight, static_ctl, static_coef,
+    sums, b_f, b_b, c_f, c_b, field, held, sem,
+):
     _, y, c = place()
     copies = []
     for j in range(2):
         level = 2 * y + c + 8 * j
         for k, source in enumerate((weight, value)):
             spot = held.reshape(2, 2, VARS, 8, LANES).at[k, j]
-            copies.append(pltpu.make_async_copy(source.at[:, level], spot, sem.at[2 * j + k]))
+            copies.append(pltpu.make_async_copy(source.at[:, level], spot, sem.at[3 * j + k]))
+        spot = field.reshape(16, ROWS, LANES).at[8 * j : 8 * j + VARS]
+        copies.append(pltpu.make_async_copy(static_ctl.at[:, level], spot, sem.at[3 * j + 2]))
     for copy in copies:
         copy.start()
+    field[96:128, :] = static_coef[...]
+    field[224:256, :] = jnp.zeros((32, LANES), jnp.float32)
+    pack_rows(lambda row: alpha_row(alpha, c, row), 16, b_f, b_b)
     for copy in copies:
         copy.wait()
+    pack_rows(lambda row: field[pl.ds(row, 16, stride=ROWS), :], 16, c_f, c_b)
     pieces = []
     for a in range(8):
         part = held[pl.ds(a, 24, stride=8), :]
@@ -246,8 +249,8 @@
             sums[pl.ds(block * 2 + r, 24, stride=ROWS), :] = total[:, r * LANES : (r + 1) * LANES]
 
 
-def gradient_body(mine, other, sums, grad):
-    total = mine[...] + other[...]
+def gradient_body(mine, other, static, sums, grad):
+    total = mine[...] + other[...] + static[...]
     grad[...] = sums[0:192, :] * total - sums[192:384, :]
 
 
@@ -282,7 +285,7 @@
     pack_rows(lambda row: middle[pl.ds(row, 16, stride=ROWS), :], 16, forward, backward)
 
 
-def update_alpha(parity, out, alpha, mom, new_alpha, new_mom, stage0, stage1, sem):
+def update_alpha(parity, out, alpha, mom, stage0, stage1):
     for m in range(2):
         for s in range(HALF):
             at = pl.ds(pl.multiple_of(m * 256 + (2 * s + parity) * 16, 16), 16)
@@ -291,56 +294,64 @@
             moved = momentum_rate * mom[at, :] + (old + out[here, :])
             stage1[here, :] = moved
             stage0[here, :] = old - step_rate * moved
+
+
+def third_body(
+    low, high, middle, coefs, alpha, mom, grad, static_coefs, field, static_mom,
+    stage0, stage1, new_static, new_static_mom, buf0, buf1, out,
+):
+    x, _, c = place()
+
+    def emit(row, value):
+        out[pl.ds(row, 16, stride=ROWS), :] = value
+
+    load = halo_loader(low, high, lambda row: middle[pl.ds(row, 16, stride=ROWS), :], 16)
+    diffuse(load, 16, 16, coefs, (buf0, buf1), emit)
+    update_alpha(c, out, alpha, mom, stage0, stage1)
+
+    load = halo_loader(low, high, lambda row: grad[pl.ds(x * 96 + row, VARS, stride=ROWS), :], VARS, 192)
+    for row in range(SPAN):
+        buf0[row * 8 : row * 8 + VARS, :] = load(row)
+
+    def emit_static(row, value):
+        out[pl.ds(row, 8, stride=ROWS), :] = value
+
+    diffuse(lambda row: buf0[row * 8 : row * 8 + 8, :], 8, 8, static_coefs, (buf0, buf1), emit_static)
+    old = field[pl.ds(pl.multiple_of(x * 128, 128), 96), :]
+    moved = momentum_rate * static_mom[...] + (old + out[0:96, :])
+    new_static_mom[...] = moved
+    new_static[...] = old - step_rate * moved
+
+
+def fourth_body(
+    low, high, middle, coefs, alpha, mom, done0, done1, done2, done3,
+    new_alpha, new_mom, new_static, new_static_mom,
+    buf0, buf1, out, stage0, stage1, sem,
+):
+    c = lax.axis_index("mem") % 2
+
+    def leave(source, target, parity, k):
+        return pltpu.make_async_copy(source.reshape(2, HALF, ROWS, LANES), target.at[:, :, parity], sem.at[k])
+
     copies = [
-        pltpu.make_async_copy(stage.reshape(2, HALF, ROWS, LANES), target.at[:, :, parity], sem.at[k])
-        for k, (stage, target) in enumerate(((stage0, new_alpha), (stage1, new_mom)))
+        leave(done0, new_alpha, c, 0),
+        leave(done1, new_mom, c, 1),
+        pltpu.make_async_copy(done2, new_static, sem.at[2]),
+        pltpu.make_async_copy(done3, new_static_mom, sem.at[3]),
     ]
     for copy in copies:
         copy.start()
-    return copies
-
-
-def third_body(
-    low, high, middle, coefs, alpha, mom, grad, static_coefs, field, static_mom,
-    new_alpha, new_mom, new_static, new_static_mom,
-    buf0, buf1, out, stage0, stage1, sem,
-):
-    x, _, c = place()
 
     def emit(row, value):
         out[pl.ds(row, 16, stride=ROWS), :] = value
 
     load = halo_loader(low, high, lambda row: middle[pl.ds(row, 16, stride=ROWS), :], 16)
     diffuse(load, 16, 16, coefs, (buf0, buf1), emit)
-    copies = update_alpha(c, out, alpha, mom, new_alpha, new_mom, stage0, stage1, sem)
-
-    load = halo_loader(low, high, lambda row: grad[pl.ds(x * 96 + row, VARS, stride=ROWS), :], VARS, 192)
-    for row in range(SPAN):
-        buf0[row * 8 : row * 8 + VARS, :] = load(row)
-
-    def emit_static(row, value):
-        out[pl.ds(row, 8, stride=ROWS), :] = value
-
-    diffuse(lambda row: buf0[row * 8 : row * 8 + 8, :], 8, 8, static_coefs, (buf0, buf1), emit_static)
-    old = field[0:96, :]
-    moved = momentum_rate * static_mom[...] + (old + out[0:96, :])
-    new_static_mom[...] = moved
-    new_static[...] = old - step_rate * moved
-    for copy in copies:
-        copy.wait()
-
-
-def fourth_body(
-    low, high, middle, coefs, alpha, mom, half_alpha, half_mom, new_alpha, new_mom,
-    buf0, buf1, out, stage0, stage1, sem,
-):
-    def emit(row, value):
-        out[pl.ds(row, 16, stride=ROWS), :] = value
-
-    load = halo_loader(low, high, lambda row: middle[pl.ds(row, 16, stride=ROWS), :], 16)
-    diffuse(load, 16, 16, coefs, (buf0, buf1), emit)
-    c = lax.axis_index("mem") % 2
-    for copy in update_alpha(1 - c, out, alpha, mom, new_alpha, new_mom, stage0, stage1, sem):
+    update_alpha(1 - c, out, alpha, mom, stage0, stage1)
+    last = [leave(stage0, new_alpha, 1 - c, 4), leave(stage1, new_mom, 1 - c, 5)]
+    for copy in last:
+        copy.start()
+    for copy in copies + last:
         copy.wait()
 
 
@@ -370,33 +381,39 @@
 
     mom2 = alpha_mom.reshape(512, LANES)
     bufs16 = [f32(SPAN * 16, LANES), f32(SPAN * 16, LANES)]
-    bufs8 = [f32(SPAN * 8, LANES), f32(SPAN * 8, LANES)]
     raw = f32(88, LANES)
 
-    a_f, a_b, b_f, b_b, alpha2, loc2, field = call(
+    alpha2 = alpha.reshape(512, LANES)
+    loc2 = loc_coef.reshape(32, LANES)
+    quarter = shape(192, LANES)
+    half = shape(256, LANES)
+    a_f, a_b = call(
         pack_body,
         "pack",
-        [HBM] * 4,
-        [shape(312, LANES)] * 2 + [shape(192, LANES)] * 2 + [shape(512, LANES), shape(32, LANES), shape(128, LANES)],
-        [pltpu.SemaphoreType.DMA((4,))],
+        [HBM] * 2,
+        [shape(216, LANES)] * 2,
+        [f32(512, LANES), f32(32, LANES), pltpu.SemaphoreType.DMA((2,))],
         grant=GRANT,
-    )(alpha.reshape(512, LANES), loc_coef.reshape(32, LANES), static_ctl, static_coef.reshape(32, LANES))
+    )(alpha2, loc2)
     a_low, a_high = halo(a_f, a_b)
-    b_low, b_high = halo(b_f, b_b)
-
-    (sums,) = call(
+    sums, b_f, b_b, c_f, c_b, field = call(
         prepare_body,
         "prepare",
-        [VM, VM, ANY, ANY],
-        [shape(384, LANES)],
-        [f32(192, LANES), pltpu.SemaphoreType.DMA((4,))],
-        flops=1000000000,
+        [VM] * 3 + [HBM] * 3 + [VM],
+        [shape(384, LANES)] + [quarter] * 4 + [half],
+        [f32(192, LANES), pltpu.SemaphoreType.DMA((6,))],
+        grant=GRANT2,
+        flops=BUSY,
     )(
+        alpha2,
         obs_cell.reshape(8, LANES),
         obs_mask.reshape(8, LANES),
         obs_value.reshape(VARS, 16, 8, LANES),
         obs_weight.reshape(VARS, 16, 8, LANES),
+        static_ctl,
+        static_coef.reshape(32, LANES),
     )
+    b_low, b_high = halo(b_f, b_b)
 
     part_a, loc_k = call(
         first_body,
@@ -407,23 +424,21 @@
         flops=BUSY,
     )(alpha2, a_low, a_high, loc2, perturb)
     got = swap(part_a, 1)
+    (second,) = call(second_body, "second", [VM] * 4, [half], bufs16, flops=BUSY)(alpha2, b_low, b_high, loc_k)
+    o0, o1, o2, o3 = call(sum_body, "sum", [VM] * 3, [quarter] * 4)(second, perturb, got)
+    r1, r2, r3 = swap(o1, 2), swap(o2, 4), swap(o3, 6)
+    mine = o0 + r1 + r2 + r3
+    other = swap(mine, 8)
+    c_low, c_high = halo(*lax.optimization_barrier((c_f, c_b, o0))[:2])
     static, static_k = call(
         static_first_body,
         "static_first",
         [VM] * 3,
-        [shape(96, LANES), shape(200, LANES)],
-        [raw] + bufs8 + [f32(128, LANES)],
+        [quarter, shape(200, LANES)],
+        [raw] + bufs16 + [f32(256, LANES)],
         flops=BUSY,
-    )(a_low, a_high, field)
-    (second,) = call(second_body, "second", [VM] * 4, [shape(256, LANES)], bufs16, flops=BUSY)(
-        alpha2, b_low, b_high, loc_k
-    )
-    quarter = shape(192, LANES)
-    o0, o1, o2, o3 = call(sum_body, "sum", [VM] * 4, [quarter] * 4)(second, perturb, got, static)
-    r1, r2, r3 = swap(o1, 2), swap(o2, 4), swap(o3, 6)
-    mine = o0 + r1 + r2 + r3
-    other = swap(mine, 8)
-    (grad,) = call(gradient_body, "gradient", [VM] * 3, [quarter])(mine, other, sums)
+    )(c_low, c_high, field)
+    (grad,) = call(gradient_body, "gradient", [VM] * 4, [quarter])(mine, other, static, sums)
     p0 = swap(grad, 1)
     gs = [grad] + [swap(grad, 2 * k) for k in range(1, 4)]
     p_f, p_b, p_m, rest = call(
@@ -439,25 +454,22 @@
     )(p0, rest, perturb)
     q_low, q_high = halo(q_f, q_b)
     whole = shape(2, HALF, 2, ROWS, LANES)
-    stages = [f32(256, LANES)] * 3 + [pltpu.SemaphoreType.DMA((2,))]
-    half_alpha, half_mom, new_static, new_static_mom = call(
+    ready = call(
         third_body,
         "third",
         [VM] * 10,
-        [whole, whole, shape(96, LANES), shape(96, LANES)],
-        bufs16 + stages,
+        [half, half, shape(96, LANES), shape(96, LANES)],
+        bufs16 + [f32(256, LANES)],
         flops=BUSY,
-        out_specs=[HBM, HBM, VM, VM],
     )(p_low, p_high, p_m, loc_k, alpha2, mom2, grad, static_k, field, static_mom.reshape(96, LANES))
-    new_alpha, new_alpha_mom = call(
+    new_alpha, new_alpha_mom, new_static, new_static_mom = call(
         fourth_body,
         "fourth",
-        [VM] * 6 + [HBM] * 2,
-        [whole, whole],
-        bufs16 + stages,
-        out_specs=[HBM, HBM],
-        aliases={6: 0, 7: 1},
-    )(q_low, q_high, q_m, loc_k, alpha2, mom2, half_alpha, half_mom)
+        [VM] * 10,
+        [whole, whole, shape(96, LANES), shape(96, LANES)],
+        bufs16 + [f32(256, LANES)] * 3 + [pltpu.SemaphoreType.DMA((6,))],
+        out_specs=[HBM] * 4,
+    )(q_low, q_high, q_m, loc_k, alpha2, mom2, *ready)
     return (
         new_alpha.reshape(alpha.shape),
         new_alpha_mom.reshape(alpha.shape),

time: 68.6 us -> 65.7 us (0.958)
  waiting for transfers between devices: 21.9 us -> 19.5 us
  local copies, waits for them, and re-layouts: 2.49 us -> 0.72 us
  Pallas kernels: 14.1 us -> 15.2 us
    ppermute x10, waiting for transfers between devices: 15.3 us -> 10.4 us  [swap(): return lax.ppermute(value, 'mem', [(i, i ^ bits) for i in range(members)])]
    ppermute x4 -> x5, waiting for transfers between devices: 6.56 us -> 8.69 us  [halo(): lax.ppermute(backward, 'tile', down)]
    unnamed x22 -> x16, local copies, waits for them, and re-layouts: 2.49 us -> 0.72 us
    pallas_call x8, Pallas kernels: 12.1 us -> 13.3 us  [the longest x1 3.43 us: local(): call(prepare_body, 'prepare', [VM] * 3 + [HBM] * 3 + [VM], [shape(384, LA...]
    ppermute x4 -> x5, starting transfers between devices: 17.5 us -> 17.8 us  [halo(): lax.ppermute(forward, 'tile', up)]
  transfers between devices with their start and end apart: 18 -> 20, of which waited for: 11 -> 9; matrix products, arithmetic and copies ran while one was open for 0% -> 0% of each run, Pallas kernels for 14% -> 17%
where the time goes in v3:
time: 65.7 us; the launch traced here: 65.5 us
  starting transfers between devices  29.1 us (44%)
  waiting for transfers between devices  19.5 us (30%)
  Pallas kernels  15.2 us (23%)
  between operations  0.95 us (1%)
  local copies, waits for them, and re-layouts  0.72 us (1%)
    ppermute x5, starting transfers between devices, halo(): lax.ppermute(forward, 'tile', up)  17.8 us
    ppermute x10, starting transfers between devices, swap(): return lax.ppermute(value, 'mem', [(i, i ^ bits) for i in range(members)])  11.1 us
    ppermute x10, waiting for transfers between devices, swap(): return lax.ppermute(value, 'mem', [(i, i ^ bits) for i in range(members)])  10.4 us
    ppermute x5, waiting for transfers between devices, halo(): lax.ppermute(backward, 'tile', down)  8.69 us
    pallas_call x1, Pallas kernels, local(): call(prepare_body, 'prepare', [VM] * 3 + [HBM] * 3 + [VM], [shape(384, LA...  3.43 us
    pallas_call x1, Pallas kernels, local(): call(third_body, 'third', [VM] * 10, [half, half, shape(96, LANES), shape...  2.53 us
    pallas_call x1, Pallas kernels, local(): call(fourth_body, 'fourth', [VM] * 10, [whole, whole, shape(96, LANES), s...  2.34 us
    pallas_call x1, Pallas kernels, local(): call(pack_body, 'pack', [HBM] * 2, [shape(216, LANES)] * 2, [f32(512, LAN...  1.73 us
  transfers between devices with their start and end apart: 20, of which 9 were waited for; matrix products, arithmetic and copies ran while one was open for 0% of the time, Pallas kernels for 17%

profile of v3, /device:TPU:102, one launch (start us, length us, event | category | flops | bytes accessed | tf_op | source)
XLA Modules:
  0.0 65.5 jit_solution(13287001354682875388)
XLA Ops:
  0.6 0.0 copy-start.5
  0.6 1.7 %pack.1 = (f32[216,128]{1,0:T(8,128)}, f32[216,128]{1,0:T(8,128)}) custom-call(f32[512,128]{1,0:T(8,128)} %bitcast.17, f32[32,128]{1,0:T(8,128)} %bitcast.25), custom_call_target="tpu_custom_call" | custom-call | flops 1000000 | bytes 1000000 | tf_op jit(solution)/shard_map/pack/pallas_call | solution.py:390
  2.4 3.5 %collective-permute-start.2 = (f32[216,128]{1,0:T(8,128)}, f32[216,128]{1,0:T(8,128)S(1)}, u32[]{:S(2)}, u32[]{:S(2)}) collective-permute-start(f32[216,128]{1,0:T(8,128)} %get-tuple-element.39), channel_id=1, source_target_pairs={{0,1},{1,2},{2,3},{3,4},{4,5},{5,6},{6,7},{7,8},{8,9},{9,10},{10,1... | collective-permute-start | bytes 331784 | tf_op jit(solution)/shard_map/ppermute | solution.py:380
  5.9 0.0 collective-permute-start.3
  5.9 0.0 copy-start.7
  5.9 0.0 copy-start.6
  5.9 0.0 copy-done.5
  5.9 0.7 %copy-done.7 = s32[1,1024]{1,0:T(1,128)S(1)} copy-done((s32[1,1024]{1,0:T(1,128)S(1)}, s32[1,1024]{1,0:T(1,128)}, u32[]{:S(2)}) %copy-start.7) | copy-done | bytes 4120
  6.5 0.0 copy-done.6
  6.6 0.0 copy-start
  6.6 0.0 copy-start.3
  6.6 3.4 %prepare.1 = (f32[384,128]{1,0:T(8,128)S(1)}, f32[192,128]{1,0:T(8,128)S(1)}, f32[192,128]{1,0:T(8,128)S(1)}, f32[192,128]{1,0:T(8,128)S(1)}, f32[192,128]{1,0:T(8,128)S(1)}, /*index=5*/f32[256,128]{1,0:T(8,128)S(1)}) custom-call(f32[512,128]{1,0:T(8,128)} %bitcast.18, s32[8,128]{1,0:T(8,128)S(1)} %bitcast.29, s32[8,128]{1,0:T(8,128)S(1)} %bitcast.30, ...), custom_call_target="tpu_custom_call" | custom-call | flops 5000000000 | bytes 1000000 | tf_op jit(solution)/shard_map/prepare/pallas_call | solution.py:399
  10.0 4.2 %collective-permute-start = (f32[192,128]{1,0:T(8,128)S(1)}, f32[192,128]{1,0:T(8,128)S(1)}, u32[]{:S(2)}, u32[]{:S(2)}) collective-permute-start(f32[192,128]{1,0:T(8,128)S(1)} %get-tuple-element.37), channel_id=1, source_target_pairs={{0,1},{1,2},{2,3},{3,4},{4,5},{5,6},{6,7},{7,8},{8,9},{9,10},{10,1... | collective-permute-start | bytes 294920 | tf_op jit(solution)/shard_map/ppermute | solution.py:380
  14.2 0.0 collective-permute-start.1
  14.2 0.0 collective-permute-done.2.low
  14.2 0.0 collective-permute-done.3.high
  14.2 0.0 copy-done
  14.2 0.0 copy-done.1
  14.3 0.0 copy-done.3
  14.3 1.7 %first.1 = (f32[8,6,16,128]{3,2,1,0:T(8,128)S(1)}, f32[200,128]{1,0:T(8,128)S(1)}) custom-call(f32[512,128]{1,0:T(8,128)S(1)} %bitcast.19, f32[216,128]{1,0:T(8,128)S(1)} %collective-permute-done.2.low, f32[216,128]{1,0:T(8,128)S(1)} %collective-permute-done.3.high, f32[32,128]{1,0:T(8,128)S(1)} %bitcast.26, bf16[2,6,16,16,128]{4,3,2,1,0:T(8,128)(2,1)S(1)} %copy-done), custom_call_target="tpu_custom_call" | custom-call | flops 5000000000 | bytes 1000000 | tf_op jit(solution)/shard_map/first/pallas_call | solution.py:418
  15.9 0.1 collective-permute-start.4
  16.0 0.4 collective-permute-done.low
  16.4 4.5 %collective-permute-done.1.high = f32[192,128]{1,0:T(8,128)S(1)} collective-permute-done((f32[192,128]{1,0:T(8,128)S(1)}, f32[192,128]{1,0:T(8,128)S(1)}, u32[]{:S(2)}, u32[]{:S(2)}) %collective-permute-start.1) | collective-permute-done | bytes 98336 | tf_op jit(solution)/shard_map/ppermute | solution.py:380
  20.9 1.5 %second.1.local = f32[256,128]{1,0:T(8,128)S(1)} custom-call(f32[512,128]{1,0:T(8,128)S(1)} %bitcast.20, f32[192,128]{1,0:T(8,128)S(1)} %collective-permute-done.low, f32[192,128]{1,0:T(8,128)S(1)} %collective-permute-done.1.high, f32[200,128]{1,0:T(8,128)S(1)} %get-tuple-element.41.coefs), custom_call_target="tpu_custom_call" | custom-call | flops 5000000000 | bytes 1000000 | tf_op jit(solution)/shard_map/second/pallas_call | solution.py:427
  22.5 0.0 collective-permute-done.4.received
  22.5 0.1 sum.1
  22.6 1.7 %collective-permute-start.5 = (f32[192,128]{1,0:T(8,128)S(1)}, f32[192,128]{1,0:T(8,128)S(1)}, u32[]{:S(2)}, u32[]{:S(2)}) collective-permute-start(f32[192,128]{1,0:T(8,128)S(1)} %get-tuple-element.44), channel_id=1, source_target_pairs={{0,32},{16,48},{32,0},{48,16},{64,96},{80,112},{96,64},{112,80},{1... | collective-permute-start | bytes 294920 | tf_op jit(solution)/shard_map/ppermute | solution.py:377
  24.3 2.9 %collective-permute-start.6 = (f32[192,128]{1,0:T(8,128)S(1)}, f32[192,128]{1,0:T(8,128)S(1)}, u32[]{:S(2)}, u32[]{:S(2)}) collective-permute-start(f32[192,128]{1,0:T(8,128)S(1)} %get-tuple-element.45), channel_id=1, source_target_pairs={{0,64},{16,80},{32,96},{48,112},{64,0},{80,16},{96,32},{112,48},{1... | collective-permute-start | bytes 294920 | tf_op jit(solution)/shard_map/ppermute | solution.py:377
  27.2 0.2 collective-permute-start.7
  27.4 0.0 collective-permute-start.10
  27.4 4.1 %collective-permute-start.9 = (f32[192,128]{1,0:T(8,128)S(1)}, f32[192,128]{1,0:T(8,128)S(1)}, u32[]{:S(2)}, u32[]{:S(2)}) collective-permute-start(f32[192,128]{1,0:T(8,128)S(1)} %get-tuple-element.49), channel_id=1, source_target_pairs={{0,1},{1,2},{2,3},{3,4},{4,5},{5,6},{6,7},{7,8},{8,9},{9,10},{10,1... | collective-permute-start | bytes 294920 | tf_op jit(solution)/shard_map/ppermute | solution.py:380
  31.5 0.0 collective-permute-done.5
  31.5 0.0 collective-permute-done.6
  31.5 1.5 %collective-permute-done.7 = f32[192,128]{1,0:T(8,128)S(1)} collective-permute-done((f32[192,128]{1,0:T(8,128)S(1)}, f32[192,128]{1,0:T(8,128)S(1)}, u32[]{:S(2)}, u32[]{:S(2)}) %collective-permute-start.7) | collective-permute-done | bytes 98336 | tf_op jit(solution)/shard_map/ppermute | solution.py:377
  33.0 1.4 %collective-permute-start.8 = (f32[192,128]{1,0:T(8,128)S(1)}, f32[192,128]{1,0:T(8,128)S(1)}, u32[]{:S(2)}, u32[]{:S(2)}) collective-permute-start(f32[192,128]{1,0:T(8,128)S(1)} %add_add_fusion.mine), channel_id=1, source_target_pairs={{0,128},{16,144},{32,160},{48,176},{64,192},{80,208},{96,224},{112... | collective-permute-start | bytes 294920 | tf_op jit(solution)/shard_map/ppermute | solution.py:377
  34.4 0.0 collective-permute-done.10.high
  34.4 0.0 collective-permute-done.9.low
  34.4 1.6 %static_first.1 = (f32[192,128]{1,0:T(8,128)S(1)}, f32[200,128]{1,0:T(8,128)S(1)}) custom-call(f32[192,128]{1,0:T(8,128)S(1)} %collective-permute-done.9.low, f32[192,128]{1,0:T(8,128)S(1)} %collective-permute-done.10.high, f32[256,128]{1,0:T(8,128)S(1)} %get-tuple-element.51.field), custom_call_target="tpu_custom_call" | custom-call | flops 5000000000 | bytes 1000000 | tf_op jit(solution)/shard_map/static_first/pallas_call | solution.py:433
  36.0 3.4 %collective-permute-done.8.other = f32[192,128]{1,0:T(8,128)S(1)} collective-permute-done((f32[192,128]{1,0:T(8,128)S(1)}, f32[192,128]{1,0:T(8,128)S(1)}, u32[]{:S(2)}, u32[]{:S(2)}) %collective-permute-start.8) | collective-permute-done | bytes 98336 | tf_op jit(solution)/shard_map/ppermute | solution.py:377
  39.5 0.1 collective-permute-start.12
  39.6 3.0 %collective-permute-start.13 = (f32[192,128]{1,0:T(8,128)S(1)}, f32[192,128]{1,0:T(8,128)S(1)}, u32[]{:S(2)}, u32[]{:S(2)}) collective-permute-start(f32[192,128]{1,0:T(8,128)S(1)} %gradient.1.g0.grad), channel_id=1, source_target_pairs={{0,64},{16,80},{32,96},{48,112},{64,0},{80,16},{96,32},{112,48},{1... | collective-permute-start | bytes 294920 | tf_op jit(solution)/shard_map/ppermute | solution.py:377
  42.6 1.7 %collective-permute-start.14 = (f32[192,128]{1,0:T(8,128)S(1)}, f32[192,128]{1,0:T(8,128)S(1)}, u32[]{:S(2)}, u32[]{:S(2)}) collective-permute-start(f32[192,128]{1,0:T(8,128)S(1)} %gradient.1.g0.grad), channel_id=1, source_target_pairs={{0,96},{16,112},{32,64},{48,80},{64,32},{80,48},{96,0},{112,16},{1... | collective-permute-start | bytes 294920 | tf_op jit(solution)/shard_map/ppermute | solution.py:377
  44.2 0.0 collective-permute-done.12.g1
  44.2 2.0 %collective-permute-done.13.g2 = f32[192,128]{1,0:T(8,128)S(1)} collective-permute-done((f32[192,128]{1,0:T(8,128)S(1)}, f32[192,128]{1,0:T(8,128)S(1)}, u32[]{:S(2)}, u32[]{:S(2)}) %collective-permute-start.13) | collective-permute-done | bytes 98336 | tf_op jit(solution)/shard_map/ppermute | solution.py:377
  46.2 2.2 %collective-permute-done.14.g3 = f32[192,128]{1,0:T(8,128)S(1)} collective-permute-done((f32[192,128]{1,0:T(8,128)S(1)}, f32[192,128]{1,0:T(8,128)S(1)}, u32[]{:S(2)}, u32[]{:S(2)}) %collective-permute-start.14) | collective-permute-done | bytes 98336 | tf_op jit(solution)/shard_map/ppermute | solution.py:377
  48.4 0.2 project_own.1
  48.5 0.1 collective-permute-start.15
  48.6 2.0 %collective-permute-start.18 = (f32[264,128]{1,0:T(8,128)S(1)}, f32[264,128]{1,0:T(8,128)S(1)}, u32[]{:S(2)}, u32[]{:S(2)}) collective-permute-start(f32[264,128]{1,0:T(8,128)S(1)} %get-tuple-element.58), channel_id=1, source_target_pairs={{0,1},{1,2},{2,3},{3,4},{4,5},{5,6},{6,7},{7,8},{8,9},{9,10},{10,1... | collective-permute-start | bytes 405512 | tf_op jit(solution)/shard_map/ppermute | solution.py:380
  50.6 0.0 copy-start.4
  50.6 0.1 collective-permute-start.19
  50.8 0.0 collective-permute-start.11
  50.8 1.3 %collective-permute-done.11.g0 = f32[192,128]{1,0:T(8,128)S(1)} collective-permute-done((f32[192,128]{1,0:T(8,128)S(1)}, f32[192,128]{1,0:T(8,128)S(1)}, u32[]{:S(2)}, u32[]{:S(2)}) %collective-permute-start.11) | collective-permute-done | bytes 98336 | tf_op jit(solution)/shard_map/ppermute | solution.py:377
  52.1 0.0 collective-permute-done.15.rest
  52.1 0.1 project_other.1
  52.2 4.1 %collective-permute-start.16 = (f32[192,128]{1,0:T(8,128)S(1)}, f32[192,128]{1,0:T(8,128)S(1)}, u32[]{:S(2)}, u32[]{:S(2)}) collective-permute-start(f32[192,128]{1,0:T(8,128)S(1)} %get-tuple-element.55), channel_id=1, source_target_pairs={{0,1},{1,2},{2,3},{3,4},{4,5},{5,6},{6,7},{7,8},{8,9},{9,10},{10,1... | collective-permute-start | bytes 294920 | tf_op jit(solution)/shard_map/ppermute | solution.py:380
  56.3 0.0 collective-permute-start.17
  56.3 0.0 collective-permute-done.18.low
  56.3 2.2 %collective-permute-done.19.high = f32[264,128]{1,0:T(8,128)S(1)} collective-permute-done((f32[264,128]{1,0:T(8,128)S(1)}, f32[264,128]{1,0:T(8,128)S(1)}, u32[]{:S(2)}, u32[]{:S(2)}) %collective-permute-start.19) | collective-permute-done | bytes 135200 | tf_op jit(solution)/shard_map/ppermute | solution.py:380
  58.5 0.0 copy-done.2
  58.5 0.0 copy-done.4
  58.5 2.5 %third.1 = (f32[256,128]{1,0:T(8,128)S(1)}, f32[256,128]{1,0:T(8,128)S(1)}, f32[96,128]{1,0:T(8,128)S(1)}, f32[96,128]{1,0:T(8,128)S(1)}) custom-call(f32[264,128]{1,0:T(8,128)S(1)} %collective-permute-done.18.low, f32[264,128]{1,0:T(8,128)S(1)} %collective-permute-done.19.high, f32[256,128]{1,0:T(8,128)S(1)} %get-tuple-element.60.middle, ...), custom_call_target="tpu_custom_call" | custom-call | flops 5000000000 | bytes 1000000 | tf_op jit(solution)/shard_map/third/pallas_call | solution.py:457
  61.0 0.0 collective-permute-done.16.low
  61.0 2.0 %collective-permute-done.17.high = f32[192,128]{1,0:T(8,128)S(1)} collective-permute-done((f32[192,128]{1,0:T(8,128)S(1)}, f32[192,128]{1,0:T(8,128)S(1)}, u32[]{:S(2)}, u32[]{:S(2)}) %collective-permute-start.17) | collective-permute-done | bytes 98336 | tf_op jit(solution)/shard_map/ppermute | solution.py:380
  63.0 2.3 %fourth.1 = (f32[2,8,2,16,128]{4,3,2,1,0:T(8,128)}, f32[2,8,2,16,128]{4,3,2,1,0:T(8,128)}, f32[96,128]{1,0:T(8,128)}, f32[96,128]{1,0:T(8,128)}) custom-call(f32[192,128]{1,0:T(8,128)S(1)} %collective-permute-done.16.low, f32[192,128]{1,0:T(8,128)S(1)} %collective-permute-done.17.high, f32[256,128]{1,0:T(8,128)S(1)} %get-tuple-element.57.middle, ...), custom_call_target="tpu_custom_call" | custom-call | flops 1000000 | bytes 1000000 | tf_op jit(solution)/shard_map/fourth/pallas_call | solution.py:465
  (4 shorter events, 0.1 us)
Async XLA Ops:
  0.6 5.2 %copy-start.5 = (f32[2,16,128]{2,1,0:T(8,128)S(1)}, f32[2,16,128]{2,1,0:T(8,128)}, u32[]{:S(2)}) copy-start(f32[2,16,128]{2,1,0:T(8,128)} %param.17) | copy-start | bytes 49156
  2.4 11.8 %collective-permute-start.2 = (f32[216,128]{1,0:T(8,128)}, f32[216,128]{1,0:T(8,128)S(1)}, u32[]{:S(2)}, u32[]{:S(2)}) collective-permute-start(f32[216,128]{1,0:T(8,128)} %get-tuple-element.39), channel_id=1, source_target_pairs={{0,1},{1,2},{2,3},{3,4},{4,5},{5,6},{6,7},{7,8},{8,9},{9,10},{10,1... | collective-permute-start | bytes 331784 | tf_op jit(solution)/shard_map/ppermute | solution.py:380
  5.9 8.4 %collective-permute-start.3 = (f32[216,128]{1,0:T(8,128)}, f32[216,128]{1,0:T(8,128)S(1)}, u32[]{:S(2)}, u32[]{:S(2)}) collective-permute-start(f32[216,128]{1,0:T(8,128)} %get-tuple-element.40), channel_id=1, source_target_pairs={{1,0},{2,1},{3,2},{4,3},{5,4},{6,5},{7,6},{8,7},{9,8},{10,9},{11,1... | collective-permute-start | bytes 331784 | tf_op jit(solution)/shard_map/ppermute | solution.py:380
  5.9 0.7 %copy-start.7 = (s32[1,1024]{1,0:T(1,128)S(1)}, s32[1,1024]{1,0:T(1,128)}, u32[]{:S(2)}) copy-start(s32[1,1024]{1,0:T(1,128)} %param.19) | copy-start | bytes 12292
  5.9 0.7 %copy-start.6 = (s32[1,1024]{1,0:T(1,128)S(1)}, s32[1,1024]{1,0:T(1,128)}, u32[]{:S(2)}) copy-start(s32[1,1024]{1,0:T(1,128)} %param.18) | copy-start | bytes 12292
  6.6 7.7 %copy-start = (bf16[2,6,16,16,128]{4,3,2,1,0:T(8,128)(2,1)S(1)}, bf16[2,6,16,16,128]{4,3,2,1,0:T(8,128)(2,1)}, u32[]{:S(2)}) copy-start(bf16[2,6,16,16,128]{4,3,2,1,0:T(8,128)(2,1)} %perturb.7) | copy-start | bytes 2359300
  6.6 7.7 %copy-start.1 = (f32[2,16,16,128]{3,2,1,0:T(8,128)S(1)}, f32[2,16,16,128]{3,2,1,0:T(8,128)}, u32[]{:S(2)}) copy-start(f32[2,16,16,128]{3,2,1,0:T(8,128)} %param.12) | copy-start | bytes 786436
  6.6 7.7 %copy-start.3 = (f32[2,16,128]{2,1,0:T(8,128)S(1)}, f32[2,16,128]{2,1,0:T(8,128)}, u32[]{:S(2)}) copy-start(f32[2,16,128]{2,1,0:T(8,128)} %param.16) | copy-start | bytes 49156
  10.0 6.4 %collective-permute-start = (f32[192,128]{1,0:T(8,128)S(1)}, f32[192,128]{1,0:T(8,128)S(1)}, u32[]{:S(2)}, u32[]{:S(2)}) collective-permute-start(f32[192,128]{1,0:T(8,128)S(1)} %get-tuple-element.37), channel_id=1, source_target_pairs={{0,1},{1,2},{2,3},{3,4},{4,5},{5,6},{6,7},{7,8},{8,9},{9,10},{10,1... | collective-permute-start | bytes 294920 | tf_op jit(solution)/shard_map/ppermute | solution.py:380
  14.2 6.7 %collective-permute-start.1 = (f32[192,128]{1,0:T(8,128)S(1)}, f32[192,128]{1,0:T(8,128)S(1)}, u32[]{:S(2)}, u32[]{:S(2)}) collective-permute-start(f32[192,128]{1,0:T(8,128)S(1)} %get-tuple-element.38), channel_id=1, source_target_pairs={{1,0},{2,1},{3,2},{4,3},{5,4},{6,5},{7,6},{8,7},{9,8},{10,9},{11,1... | collective-permute-start | bytes 294920 | tf_op jit(solution)/shard_map/ppermute | solution.py:380
  15.9 6.6 %collective-permute-start.4 = (f32[8,6,16,128]{3,2,1,0:T(8,128)S(1)}, f32[8,6,16,128]{3,2,1,0:T(8,128)S(1)}, u32[]{:S(2)}, u32[]{:S(2)}) collective-permute-start(f32[8,6,16,128]{3,2,1,0:T(8,128)S(1)} %get-tuple-element.42), channel_id=1, source_target_pairs={{0,16},{16,0},{32,48},{48,32},{64,80},{80,64},{96,112},{112,96},{1... | collective-permute-start | bytes 1179656 | tf_op jit(solution)/shard_map/ppermute | solution.py:377
  22.6 8.9 %collective-permute-start.5 = (f32[192,128]{1,0:T(8,128)S(1)}, f32[192,128]{1,0:T(8,128)S(1)}, u32[]{:S(2)}, u32[]{:S(2)}) collective-permute-start(f32[192,128]{1,0:T(8,128)S(1)} %get-tuple-element.44), channel_id=1, source_target_pairs={{0,32},{16,48},{32,0},{48,16},{64,96},{80,112},{96,64},{112,80},{1... | collective-permute-start | bytes 294920 | tf_op jit(solution)/shard_map/ppermute | solution.py:377
  24.3 7.3 %collective-permute-start.6 = (f32[192,128]{1,0:T(8,128)S(1)}, f32[192,128]{1,0:T(8,128)S(1)}, u32[]{:S(2)}, u32[]{:S(2)}) collective-permute-start(f32[192,128]{1,0:T(8,128)S(1)} %get-tuple-element.45), channel_id=1, source_target_pairs={{0,64},{16,80},{32,96},{48,112},{64,0},{80,16},{96,32},{112,48},{1... | collective-permute-start | bytes 294920 | tf_op jit(solution)/shard_map/ppermute | solution.py:377
  27.2 5.8 %collective-permute-start.7 = (f32[192,128]{1,0:T(8,128)S(1)}, f32[192,128]{1,0:T(8,128)S(1)}, u32[]{:S(2)}, u32[]{:S(2)}) collective-permute-start(f32[192,128]{1,0:T(8,128)S(1)} %get-tuple-element.46), channel_id=1, source_target_pairs={{0,96},{16,112},{32,64},{48,80},{64,32},{80,48},{96,0},{112,16},{1... | collective-permute-start | bytes 294920 | tf_op jit(solution)/shard_map/ppermute | solution.py:377
  27.4 7.0 %collective-permute-start.10 = (f32[192,128]{1,0:T(8,128)S(1)}, f32[192,128]{1,0:T(8,128)S(1)}, u32[]{:S(2)}, u32[]{:S(2)}) collective-permute-start(f32[192,128]{1,0:T(8,128)S(1)} %get-tuple-element.50), channel_id=1, source_target_pairs={{1,0},{2,1},{3,2},{4,3},{5,4},{6,5},{7,6},{8,7},{9,8},{10,9},{11,1... | collective-permute-start | bytes 294920 | tf_op jit(solution)/shard_map/ppermute | solution.py:380
  27.4 7.0 %collective-permute-start.9 = (f32[192,128]{1,0:T(8,128)S(1)}, f32[192,128]{1,0:T(8,128)S(1)}, u32[]{:S(2)}, u32[]{:S(2)}) collective-permute-start(f32[192,128]{1,0:T(8,128)S(1)} %get-tuple-element.49), channel_id=1, source_target_pairs={{0,1},{1,2},{2,3},{3,4},{4,5},{5,6},{6,7},{7,8},{8,9},{9,10},{10,1... | collective-permute-start | bytes 294920 | tf_op jit(solution)/shard_map/ppermute | solution.py:380
  33.0 6.4 %collective-permute-start.8 = (f32[192,128]{1,0:T(8,128)S(1)}, f32[192,128]{1,0:T(8,128)S(1)}, u32[]{:S(2)}, u32[]{:S(2)}) collective-permute-start(f32[192,128]{1,0:T(8,128)S(1)} %add_add_fusion.mine), channel_id=1, source_target_pairs={{0,128},{16,144},{32,160},{48,176},{64,192},{80,208},{96,224},{112... | collective-permute-start | bytes 294920 | tf_op jit(solution)/shard_map/ppermute | solution.py:377
  39.5 4.8 %collective-permute-start.12 = (f32[192,128]{1,0:T(8,128)S(1)}, f32[192,128]{1,0:T(8,128)S(1)}, u32[]{:S(2)}, u32[]{:S(2)}) collective-permute-start(f32[192,128]{1,0:T(8,128)S(1)} %gradient.1.g0.grad), channel_id=1, source_target_pairs={{0,32},{16,48},{32,0},{48,16},{64,96},{80,112},{96,64},{112,80},{1... | collective-permute-start | bytes 294920 | tf_op jit(solution)/shard_map/ppermute | solution.py:377
  39.6 6.7 %collective-permute-start.13 = (f32[192,128]{1,0:T(8,128)S(1)}, f32[192,128]{1,0:T(8,128)S(1)}, u32[]{:S(2)}, u32[]{:S(2)}) collective-permute-start(f32[192,128]{1,0:T(8,128)S(1)} %gradient.1.g0.grad), channel_id=1, source_target_pairs={{0,64},{16,80},{32,96},{48,112},{64,0},{80,16},{96,32},{112,48},{1... | collective-permute-start | bytes 294920 | tf_op jit(solution)/shard_map/ppermute | solution.py:377
  42.6 5.8 %collective-permute-start.14 = (f32[192,128]{1,0:T(8,128)S(1)}, f32[192,128]{1,0:T(8,128)S(1)}, u32[]{:S(2)}, u32[]{:S(2)}) collective-permute-start(f32[192,128]{1,0:T(8,128)S(1)} %gradient.1.g0.grad), channel_id=1, source_target_pairs={{0,96},{16,112},{32,64},{48,80},{64,32},{80,48},{96,0},{112,16},{1... | collective-permute-start | bytes 294920 | tf_op jit(solution)/shard_map/ppermute | solution.py:377
  48.5 3.5 %collective-permute-start.15 = (f32[576,128]{1,0:T(8,128)S(1)}, f32[576,128]{1,0:T(8,128)S(1)}, u32[]{:S(2)}, u32[]{:S(2)}) collective-permute-start(f32[576,128]{1,0:T(8,128)S(1)} %get-tuple-element.54), channel_id=1, source_target_pairs={{0,16},{16,0},{32,48},{48,32},{64,80},{80,64},{96,112},{112,96},{1... | collective-permute-start | bytes 884744 | tf_op jit(solution)/shard_map/ppermute | solution.py:377
  48.6 7.6 %collective-permute-start.18 = (f32[264,128]{1,0:T(8,128)S(1)}, f32[264,128]{1,0:T(8,128)S(1)}, u32[]{:S(2)}, u32[]{:S(2)}) collective-permute-start(f32[264,128]{1,0:T(8,128)S(1)} %get-tuple-element.58), channel_id=1, source_target_pairs={{0,1},{1,2},{2,3},{3,4},{4,5},{5,6},{6,7},{7,8},{8,9},{9,10},{10,1... | collective-permute-start | bytes 405512 | tf_op jit(solution)/shard_map/ppermute | solution.py:380
  50.6 7.9 %copy-start.2 = (f32[2,16,16,128]{3,2,1,0:T(8,128)S(1)}, f32[2,16,16,128]{3,2,1,0:T(8,128)}, u32[]{:S(2)}) copy-start(f32[2,16,16,128]{3,2,1,0:T(8,128)} %param.13) | copy-start | bytes 786436
  50.6 7.9 %copy-start.4 = (f32[6,1,16,128]{3,2,1,0:T(8,128)S(1)}, f32[6,1,16,128]{3,2,1,0:T(8,128)}, u32[]{:S(2)}) copy-start(f32[6,1,16,128]{3,2,1,0:T(8,128)} %param.15) | copy-start | bytes 147460
  50.6 7.9 %collective-permute-start.19 = (f32[264,128]{1,0:T(8,128)S(1)}, f32[264,128]{1,0:T(8,128)S(1)}, u32[]{:S(2)}, u32[]{:S(2)}) collective-permute-start(f32[264,128]{1,0:T(8,128)S(1)} %get-tuple-element.59), channel_id=1, source_target_pairs={{1,0},{2,1},{3,2},{4,3},{5,4},{6,5},{7,6},{8,7},{9,8},{10,9},{11,1... | collective-permute-start | bytes 405512 | tf_op jit(solution)/shard_map/ppermute | solution.py:380
  50.8 1.3 %collective-permute-start.11 = (f32[192,128]{1,0:T(8,128)S(1)}, f32[192,128]{1,0:T(8,128)S(1)}, u32[]{:S(2)}, u32[]{:S(2)}) collective-permute-start(f32[192,128]{1,0:T(8,128)S(1)} %gradient.1.g0.grad), channel_id=1, source_target_pairs={{0,16},{16,0},{32,48},{48,32},{64,80},{80,64},{96,112},{112,96},{1... | collective-permute-start | bytes 294920 | tf_op jit(solution)/shard_map/ppermute | solution.py:377
  52.2 8.8 %collective-permute-start.16 = (f32[192,128]{1,0:T(8,128)S(1)}, f32[192,128]{1,0:T(8,128)S(1)}, u32[]{:S(2)}, u32[]{:S(2)}) collective-permute-start(f32[192,128]{1,0:T(8,128)S(1)} %get-tuple-element.55), channel_id=1, source_target_pairs={{0,1},{1,2},{2,3},{3,4},{4,5},{5,6},{6,7},{7,8},{8,9},{9,10},{10,1... | collective-permute-start | bytes 294920 | tf_op jit(solution)/shard_map/ppermute | solution.py:380
  56.3 6.7 %collective-permute-start.17 = (f32[192,128]{1,0:T(8,128)S(1)}, f32[192,128]{1,0:T(8,128)S(1)}, u32[]{:S(2)}, u32[]{:S(2)}) collective-permute-start(f32[192,128]{1,0:T(8,128)S(1)} %get-tuple-element.56), channel_id=1, source_target_pairs={{1,0},{2,1},{3,2},{4,3},{5,4},{6,5},{7,6},{8,7},{9,8},{10,9},{11,1... | collective-permute-start | bytes 294920 | tf_op jit(solution)/shard_map/ppermute | solution.py:380

commit v4 on v3

--- a/solution.py
+++ b/solution.py
@@ -148,7 +148,7 @@
     return load
 
 
-def first_body(alpha, low, high, loc, perturb, sums, coefs, raw, buf0, buf1, local):
+def first_body(alpha, low, high, loc, perturb, ready, sums, coefs, raw, buf0, buf1, local):
     parity = 1 - lax.axis_index("mem") % 2
     build_coefs(
         low[192:204, :], loc[0:16, :], high[192:204, :],
@@ -207,27 +207,36 @@
                 out[j * 96 + v * 16 : j * 96 + v * 16 + 16, :] = total
 
 
-def prepare_body(
-    alpha, cell, mask, value, weight, static_ctl, static_coef,
-    sums, b_f, b_b, c_f, c_b, field, held, sem,
+def fetch_body(
+    alpha_in, cell_in, mask_in, value, weight, static_ctl, static_coef,
+    b_f, b_b, c_f, c_b, field, held, cell, mask, alpha, sem,
 ):
     _, y, c = place()
-    copies = []
+    first = pltpu.make_async_copy(alpha_in, alpha, sem.at[0])
+    first.start()
+    copies = [
+        pltpu.make_async_copy(cell_in, cell, sem.at[1]),
+        pltpu.make_async_copy(mask_in, mask, sem.at[2]),
+        pltpu.make_async_copy(static_coef, field.at[96:128], sem.at[3]),
+    ]
     for j in range(2):
         level = 2 * y + c + 8 * j
         for k, source in enumerate((weight, value)):
             spot = held.reshape(2, 2, VARS, 8, LANES).at[k, j]
-            copies.append(pltpu.make_async_copy(source.at[:, level], spot, sem.at[3 * j + k]))
+            copies.append(pltpu.make_async_copy(source.at[:, level], spot, sem.at[4 + 3 * j + k]))
         spot = field.reshape(16, ROWS, LANES).at[8 * j : 8 * j + VARS]
-        copies.append(pltpu.make_async_copy(static_ctl.at[:, level], spot, sem.at[3 * j + 2]))
+        copies.append(pltpu.make_async_copy(static_ctl.at[:, level], spot, sem.at[6 + 3 * j]))
     for copy in copies:
         copy.start()
-    field[96:128, :] = static_coef[...]
     field[224:256, :] = jnp.zeros((32, LANES), jnp.float32)
+    first.wait()
     pack_rows(lambda row: alpha_row(alpha, c, row), 16, b_f, b_b)
     for copy in copies:
         copy.wait()
     pack_rows(lambda row: field[pl.ds(row, 16, stride=ROWS), :], 16, c_f, c_b)
+
+
+def prepare_body(cell, mask, held, sums):
     pieces = []
     for a in range(8):
         part = held[pl.ds(a, 24, stride=8), :]
@@ -249,9 +258,11 @@
             sums[pl.ds(block * 2 + r, 24, stride=ROWS), :] = total[:, r * LANES : (r + 1) * LANES]
 
 
-def gradient_body(mine, other, static, sums, grad):
+def gradient_body(mine, other, static, sums, grad, forward, backward):
+    x, _, _ = place()
     total = mine[...] + other[...] + static[...]
     grad[...] = sums[0:192, :] * total - sums[192:384, :]
+    pack_rows(lambda row: grad[pl.ds(x * 96 + row, VARS, stride=ROWS), :], VARS, forward, backward)
 
 
 def project(g, k, parity, perturb, middle):
@@ -267,14 +278,15 @@
             middle[pl.ds(pl.multiple_of((m * HALF + s) * 16, 16), 16), :] = total
 
 
-def project_own_body(g0, g1, g2, g3, perturb, forward, backward, middle, rest):
-    x, _, c = place()
+def project_own_body(g0, g2, g1, g3, perturb, low, high, forward, backward, middle, rest, low_out, high_out):
+    _, _, c = place()
+    low_out[...] = low[...]
+    high_out[...] = high[...]
     for k, g in enumerate((g0, g1, g2, g3)):
         project(g, k, c, perturb, middle)
         if k > 0:
             rest[(k - 1) * 192 : k * 192, :] = g[...]
     pack_rows(lambda row: middle[pl.ds(row, 16, stride=ROWS), :], 16, forward, backward)
-    pack_rows(lambda row: g0[pl.ds(x * 96 + row, VARS, stride=ROWS), :], VARS, forward, backward, 192)
 
 
 def project_other_body(g0, rest, perturb, forward, backward, middle):
@@ -296,27 +308,25 @@
             stage0[here, :] = old - step_rate * moved
 
 
-def third_body(
-    low, high, middle, coefs, alpha, mom, grad, static_coefs, field, static_mom,
-    stage0, stage1, new_static, new_static_mom, buf0, buf1, out,
-):
-    x, _, c = place()
-
+def third_body(low, high, middle, coefs, alpha, mom, stage0, stage1, buf0, buf1, out):
     def emit(row, value):
         out[pl.ds(row, 16, stride=ROWS), :] = value
 
     load = halo_loader(low, high, lambda row: middle[pl.ds(row, 16, stride=ROWS), :], 16)
     diffuse(load, 16, 16, coefs, (buf0, buf1), emit)
-    update_alpha(c, out, alpha, mom, stage0, stage1)
-
-    load = halo_loader(low, high, lambda row: grad[pl.ds(x * 96 + row, VARS, stride=ROWS), :], VARS, 192)
+    update_alpha(lax.axis_index("mem") % 2, out, alpha, mom, stage0, stage1)
+
+
+def static_last_body(low, high, grad, coefs, field, static_mom, new_static, new_static_mom, buf0, buf1, out):
+    x, _, _ = place()
+    load = halo_loader(low, high, lambda row: grad[pl.ds(x * 96 + row, VARS, stride=ROWS), :], VARS)
     for row in range(SPAN):
         buf0[row * 8 : row * 8 + VARS, :] = load(row)
 
-    def emit_static(row, value):
+    def emit(row, value):
         out[pl.ds(row, 8, stride=ROWS), :] = value
 
-    diffuse(lambda row: buf0[row * 8 : row * 8 + 8, :], 8, 8, static_coefs, (buf0, buf1), emit_static)
+    diffuse(lambda row: buf0[row * 8 : row * 8 + 8, :], 8, 8, coefs, (buf0, buf1), emit)
     old = field[pl.ds(pl.multiple_of(x * 128, 128), 96), :]
     moved = momentum_rate * static_mom[...] + (old + out[0:96, :])
     new_static_mom[...] = moved
@@ -396,14 +406,15 @@
         grant=GRANT,
     )(alpha2, loc2)
     a_low, a_high = halo(a_f, a_b)
-    sums, b_f, b_b, c_f, c_b, field = call(
-        prepare_body,
-        "prepare",
-        [VM] * 3 + [HBM] * 3 + [VM],
-        [shape(384, LANES)] + [quarter] * 4 + [half],
-        [f32(192, LANES), pltpu.SemaphoreType.DMA((6,))],
+    ints = jax.ShapeDtypeStruct((8, LANES), jnp.int32)
+    b_f, b_b, c_f, c_b, field, held, cell, mask = call(
+        fetch_body,
+        "fetch",
+        [HBM] * 7,
+        [quarter] * 4 + [half, quarter, ints, ints],
+        [f32(512, LANES), pltpu.SemaphoreType.DMA((10,))],
+        flops=BUSY,
         grant=GRANT2,
-        flops=BUSY,
     )(
         alpha2,
         obs_cell.reshape(8, LANES),
@@ -414,20 +425,21 @@
         static_coef.reshape(32, LANES),
     )
     b_low, b_high = halo(b_f, b_b)
+    (sums,) = call(prepare_body, "prepare", [VM] * 3, [shape(384, LANES)], flops=BUSY)(cell, mask, held)
 
     part_a, loc_k = call(
         first_body,
         "first",
-        [VM] * 5,
+        [VM] * 6,
         [shape(HALF, VARS, ROWS, LANES), shape(200, LANES)],
         [raw] + bufs16 + [f32(256, LANES)],
         flops=BUSY,
-    )(alpha2, a_low, a_high, loc2, perturb)
+    )(alpha2, a_low, a_high, loc2, perturb, sums)
     got = swap(part_a, 1)
     (second,) = call(second_body, "second", [VM] * 4, [half], bufs16, flops=BUSY)(alpha2, b_low, b_high, loc_k)
     o0, o1, o2, o3 = call(sum_body, "sum", [VM] * 3, [quarter] * 4)(second, perturb, got)
-    r1, r2, r3 = swap(o1, 2), swap(o2, 4), swap(o3, 6)
-    mine = o0 + r1 + r2 + r3
+    r2, r1, r3 = swap(o2, 4), swap(o1, 2), swap(o3, 6)
+    mine = o0 + r2 + r1 + r3
     other = swap(mine, 8)
     c_low, c_high = halo(*lax.optimization_barrier((c_f, c_b, o0))[:2])
     static, static_k = call(
@@ -438,30 +450,30 @@
         [raw] + bufs16 + [f32(256, LANES)],
         flops=BUSY,
     )(c_low, c_high, field)
-    (grad,) = call(gradient_body, "gradient", [VM] * 4, [quarter])(mine, other, static, sums)
+    narrow = shape(72, LANES)
+    grad, g_f, g_b = call(gradient_body, "gradient", [VM] * 4, [quarter, narrow, narrow])(mine, other, static, sums)
+    g2, g1, g3 = swap(grad, 4), swap(grad, 2), swap(grad, 6)
+    g_low, g_high = halo(g_f, g_b)
     p0 = swap(grad, 1)
-    gs = [grad] + [swap(grad, 2 * k) for k in range(1, 4)]
-    p_f, p_b, p_m, rest = call(
+    gs = [grad, g2, g1, g3]
+    p_f, p_b, p_m, rest, g_low, g_high = call(
         project_own_body,
         "project_own",
-        [VM] * 5,
-        [shape(264, LANES), shape(264, LANES), shape(256, LANES), shape(576, LANES)],
-    )(*gs, perturb)
+        [VM] * 7,
+        [quarter, quarter, half, shape(576, LANES), narrow, narrow],
+    )(*gs, perturb, g_low, g_high)
     p_low, p_high = halo(p_f, p_b)
     rest = swap(rest, 1)
-    q_f, q_b, q_m = call(
-        project_other_body, "project_other", [VM] * 3, [quarter, quarter, shape(256, LANES)]
-    )(p0, rest, perturb)
+    q_f, q_b, q_m = call(project_other_body, "project_other", [VM] * 3, [quarter, quarter, half])(p0, rest, perturb)
     q_low, q_high = halo(q_f, q_b)
     whole = shape(2, HALF, 2, ROWS, LANES)
-    ready = call(
-        third_body,
-        "third",
-        [VM] * 10,
-        [half, half, shape(96, LANES), shape(96, LANES)],
-        bufs16 + [f32(256, LANES)],
-        flops=BUSY,
-    )(p_low, p_high, p_m, loc_k, alpha2, mom2, grad, static_k, field, static_mom.reshape(96, LANES))
+    work = bufs16 + [f32(256, LANES)]
+    static_ready = call(static_last_body, "static_last", [VM] * 6, [shape(96, LANES)] * 2, work, flops=BUSY)(
+        g_low, g_high, grad, static_k, field, static_mom.reshape(96, LANES)
+    )
+    ready = call(third_body, "third", [VM] * 6, [half, half], work, flops=BUSY)(
+        p_low, p_high, p_m, loc_k, alpha2, mom2
+    )
     new_alpha, new_alpha_mom, new_static, new_static_mom = call(
         fourth_body,
         "fourth",
@@ -469,7 +481,7 @@
         [whole, whole, shape(96, LANES), shape(96, LANES)],
         bufs16 + [f32(256, LANES)] * 3 + [pltpu.SemaphoreType.DMA((6,))],
         out_specs=[HBM] * 4,
-    )(q_low, q_high, q_m, loc_k, alpha2, mom2, *ready)
+    )(q_low, q_high, q_m, loc_k, alpha2, mom2, *ready, *static_ready)
     return (
         new_alpha.reshape(alpha.shape),
         new_alpha_mom.reshape(alpha.shape),

time: 65.7 us -> 63.4 us (0.965)
  starting transfers between devices: 29.1 us -> 28.2 us
  waiting for transfers between devices: 19.5 us -> 18.7 us
  Pallas kernels: 15.2 us -> 14.5 us
    ppermute x10, waiting for transfers between devices: 10.4 us -> 5.29 us  [swap(): return lax.ppermute(value, 'mem', [(i, i ^ bits) for i in range(members)])]
    ppermute x5 -> x6, starting transfers between devices: 0.16 us -> 3.22 us  [halo(): lax.ppermute(backward, 'tile', down)]
    ppermute x5 -> x6, starting transfers between devices: 17.8 us -> 15 us  [halo(): lax.ppermute(forward, 'tile', up)]
    ppermute x5 -> x6, waiting for transfers between devices: 8.69 us -> 11.1 us  [halo(): lax.ppermute(backward, 'tile', down)]
    ppermute x5 -> x6, waiting for transfers between devices: 0.41 us -> 2.4 us  [halo(): lax.ppermute(forward, 'tile', up)]
    ppermute x10, starting transfers between devices: 11.1 us -> 9.99 us  [swap(): return lax.ppermute(value, 'mem', [(i, i ^ bits) for i in range(members)])]
    pallas_call x6 -> x8, Pallas kernels: 7.94 us -> 7.26 us  [the longest x1 1.66 us: local(): call(first_body, 'first', [VM] * 6, [shape(HALF, VARS, ROWS, LANES), shap...]
  transfers between devices with their start and end apart: 20 -> 22, of which waited for: 9 -> 9; matrix products, arithmetic and copies ran while one was open for 0% -> 0% of each run, Pallas kernels for 17% -> 16%
where the time goes in v4:
time: 63.4 us; the launch traced here: 63.2 us
  starting transfers between devices  28.2 us (44%)
  waiting for transfers between devices  18.7 us (29%)
  Pallas kernels  14.5 us (23%)
  between operations  1 us (2%)
  local copies, waits for them, and re-layouts  0.72 us (1%)
    ppermute x6, starting transfers between devices, halo(): lax.ppermute(forward, 'tile', up)  15 us
    ppermute x6, waiting for transfers between devices, halo(): lax.ppermute(backward, 'tile', down)  11.1 us
    ppermute x10, starting transfers between devices, swap(): return lax.ppermute(value, 'mem', [(i, i ^ bits) for i in range(members)])  9.99 us
    ppermute x10, waiting for transfers between devices, swap(): return lax.ppermute(value, 'mem', [(i, i ^ bits) for i in range(members)])  5.29 us
    ppermute x6, starting transfers between devices, halo(): lax.ppermute(backward, 'tile', down)  3.22 us
    ppermute x6, waiting for transfers between devices, halo(): lax.ppermute(forward, 'tile', up)  2.4 us
    pallas_call x1, Pallas kernels, local(): call(fourth_body, 'fourth', [VM] * 10, [whole, whole, shape(96, LANES), s...  2.35 us
    pallas_call x1, Pallas kernels, local(): call(pack_body, 'pack', [HBM] * 2, [shape(216, LANES)] * 2, [f32(512, LAN...  1.73 us
  transfers between devices with their start and end apart: 22, of which 9 were waited for; matrix products, arithmetic and copies ran while one was open for 0% of the time, Pallas kernels for 16%

profile of v4, /device:TPU:102, one launch (start us, length us, event | category | flops | bytes accessed | tf_op | source)
XLA Modules:
  0.0 63.2 jit_solution(17294540267911679986)
XLA Ops:
  0.6 0.0 copy-start.5
  0.6 1.7 %pack.1 = (f32[216,128]{1,0:T(8,128)}, f32[216,128]{1,0:T(8,128)}) custom-call(f32[512,128]{1,0:T(8,128)} %bitcast.17, f32[32,128]{1,0:T(8,128)} %bitcast.25), custom_call_target="tpu_custom_call" | custom-call | flops 1000000 | bytes 1000000 | tf_op jit(solution)/shard_map/pack/pallas_call | solution.py:400
  2.4 3.5 %collective-permute-start.2 = (f32[216,128]{1,0:T(8,128)}, f32[216,128]{1,0:T(8,128)S(1)}, u32[]{:S(2)}, u32[]{:S(2)}) collective-permute-start(f32[216,128]{1,0:T(8,128)} %get-tuple-element.46), channel_id=1, source_target_pairs={{0,1},{1,2},{2,3},{3,4},{4,5},{5,6},{6,7},{7,8},{8,9},{9,10},{10,1... | collective-permute-start | bytes 331784 | tf_op jit(solution)/shard_map/ppermute | solution.py:390
  5.9 0.0 collective-permute-start.3
  5.9 0.0 copy-done.5
  5.9 0.7 %copy-done.7 = s32[1,1024]{1,0:T(1,128)S(1)} copy-done((s32[1,1024]{1,0:T(1,128)S(1)}, s32[1,1024]{1,0:T(1,128)}, u32[]{:S(2)}) %copy-start.7) | copy-done | bytes 4120
  6.5 0.0 copy-done.6
  6.6 1.2 %fetch.1 = (f32[192,128]{1,0:T(8,128)S(1)}, f32[192,128]{1,0:T(8,128)S(1)}, f32[192,128]{1,0:T(8,128)S(1)}, f32[192,128]{1,0:T(8,128)S(1)}, f32[256,128]{1,0:T(8...) custom-call(f32[512,128]{1,0:T(8,128)} %bitcast.18, s32[8,128]{1,0:T(8,128)S(1)} %bitcast.29, ...), custom_call_target="tpu_custom_call" | custom-call | flops 5000000000 | bytes 1000000 | tf_op jit(solution)/shard_map/fetch/pallas_call | solution.py:410
  7.7 4.2 %collective-permute-start = (f32[192,128]{1,0:T(8,128)S(1)}, f32[192,128]{1,0:T(8,128)S(1)}, u32[]{:S(2)}, u32[]{:S(2)}) collective-permute-start(f32[192,128]{1,0:T(8,128)S(1)} %get-tuple-element.44), channel_id=1, source_target_pairs={{0,1},{1,2},{2,3},{3,4},{4,5},{5,6},{6,7},{7,8},{8,9},{9,10},{10,1... | collective-permute-start | bytes 294920 | tf_op jit(solution)/shard_map/ppermute | solution.py:390
  12.0 0.0 collective-permute-start.1
  12.0 1.4 %prepare.1.ready.sums = f32[384,128]{1,0:T(8,128)S(1)} custom-call(s32[8,128]{1,0:T(8,128)S(1)} %get-tuple-element.48.cell, s32[8,128]{1,0:T(8,128)S(1)} %get-tuple-element.49.mask, f32[192,128]{1,0:T(8,128)S(1)} %get-tuple-element.50.held), custom_call_target="tpu_custom_call" | custom-call | flops 5000000000 | bytes 1000000 | tf_op jit(solution)/shard_map/prepare/pallas_call | solution.py:428
  13.4 0.0 collective-permute-done.2.low
  13.4 0.0 collective-permute-done.3.high
  13.4 0.0 copy-done
  13.4 0.0 copy-done.1
  13.4 0.0 copy-done.3
  13.4 1.7 %first.1 = (f32[8,6,16,128]{3,2,1,0:T(8,128)S(1)}, f32[200,128]{1,0:T(8,128)S(1)}) custom-call(f32[512,128]{1,0:T(8,128)S(1)} %bitcast.19, f32[216,128]{1,0:T(8,128)S(1)} %collective-permute-done.2.low, f32[216,128]{1,0:T(8,128)S(1)} %collective-permute-done.3.high, f32[32,128]{1,0:T(8,128)S(1)} %bitcast.26, bf16[2,6,16,16,128]{4,3,2,1,0:T(8,128)(2,1)S(1)} %copy-done, ...), custom_call_target="tpu_custom_call" | custom-call | flops 5000000000 | bytes 1000000 | tf_op jit(solution)/shard_map/first/pallas_call | solution.py:430
  15.1 0.1 collective-permute-start.4
  15.2 0.0 collective-permute-done.low
  15.2 3.5 %collective-permute-done.1.high = f32[192,128]{1,0:T(8,128)S(1)} collective-permute-done((f32[192,128]{1,0:T(8,128)S(1)}, f32[192,128]{1,0:T(8,128)S(1)}, u32[]{:S(2)}, u32[]{:S(2)}) %collective-permute-start.1) | collective-permute-done | bytes 98336 | tf_op jit(solution)/shard_map/ppermute | solution.py:390
  18.7 1.5 %second.1.local = f32[256,128]{1,0:T(8,128)S(1)} custom-call(f32[512,128]{1,0:T(8,128)S(1)} %bitcast.20, f32[192,128]{1,0:T(8,128)S(1)} %collective-permute-done.low, f32[192,128]{1,0:T(8,128)S(1)} %collective-permute-done.1.high, f32[200,128]{1,0:T(8,128)S(1)} %get-tuple-element.51.coefs), custom_call_target="tpu_custom_call" | custom-call | flops 5000000000 | bytes 1000000 | tf_op jit(solution)/shard_map/second/pallas_call | solution.py:439
  20.2 0.0 collective-permute-done.4.received
  20.2 0.1 sum.1
  20.3 3.3 %collective-permute-start.5 = (f32[192,128]{1,0:T(8,128)S(1)}, f32[192,128]{1,0:T(8,128)S(1)}, u32[]{:S(2)}, u32[]{:S(2)}) collective-permute-start(f32[192,128]{1,0:T(8,128)S(1)} %get-tuple-element.54), channel_id=1, source_target_pairs={{0,64},{16,80},{32,96},{48,112},{64,0},{80,16},{96,32},{112,48},{1... | collective-permute-start | bytes 294920 | tf_op jit(solution)/shard_map/ppermute | solution.py:387
  23.6 0.7 %collective-permute-start.6 = (f32[192,128]{1,0:T(8,128)S(1)}, f32[192,128]{1,0:T(8,128)S(1)}, u32[]{:S(2)}, u32[]{:S(2)}) collective-permute-start(f32[192,128]{1,0:T(8,128)S(1)} %get-tuple-element.55), channel_id=1, source_target_pairs={{0,32},{16,48},{32,0},{48,16},{64,96},{80,112},{96,64},{112,80},{1... | collective-permute-start | bytes 294920 | tf_op jit(solution)/shard_map/ppermute | solution.py:387
  24.3 0.4 collective-permute-start.7
  24.7 0.0 collective-permute-start.10
  24.7 4.1 %collective-permute-start.9 = (f32[192,128]{1,0:T(8,128)S(1)}, f32[192,128]{1,0:T(8,128)S(1)}, u32[]{:S(2)}, u32[]{:S(2)}) collective-permute-start(f32[192,128]{1,0:T(8,128)S(1)} %get-tuple-element.59), channel_id=1, source_target_pairs={{0,1},{1,2},{2,3},{3,4},{4,5},{5,6},{6,7},{7,8},{8,9},{9,10},{10,1... | collective-permute-start | bytes 294920 | tf_op jit(solution)/shard_map/ppermute | solution.py:390
  28.8 0.0 collective-permute-done.5
  28.8 0.0 collective-permute-done.6
  28.8 1.3 %collective-permute-done.7 = f32[192,128]{1,0:T(8,128)S(1)} collective-permute-done((f32[192,128]{1,0:T(8,128)S(1)}, f32[192,128]{1,0:T(8,128)S(1)}, u32[]{:S(2)}, u32[]{:S(2)}) %collective-permute-start.7) | collective-permute-done | bytes 98336 | tf_op jit(solution)/shard_map/ppermute | solution.py:387
  30.2 1.4 %collective-permute-start.8 = (f32[192,128]{1,0:T(8,128)S(1)}, f32[192,128]{1,0:T(8,128)S(1)}, u32[]{:S(2)}, u32[]{:S(2)}) collective-permute-start(f32[192,128]{1,0:T(8,128)S(1)} %add_add_fusion.mine), channel_id=1, source_target_pairs={{0,128},{16,144},{32,160},{48,176},{64,192},{80,208},{96,224},{112... | collective-permute-start | bytes 294920 | tf_op jit(solution)/shard_map/ppermute | solution.py:387
  31.5 0.0 collective-permute-done.10.high
  31.5 0.0 collective-permute-done.9.low
  31.5 1.5 %static_first.1 = (f32[192,128]{1,0:T(8,128)S(1)}, f32[200,128]{1,0:T(8,128)S(1)}) custom-call(f32[192,128]{1,0:T(8,128)S(1)} %collective-permute-done.9.low, f32[192,128]{1,0:T(8,128)S(1)} %collective-permute-done.10.high, f32[256,128]{1,0:T(8,128)S(1)} %get-tuple-element.61.field), custom_call_target="tpu_custom_call" | custom-call | flops 5000000000 | bytes 1000000 | tf_op jit(solution)/shard_map/static_first/pallas_call | solution.py:445
  33.0 3.5 %collective-permute-done.8.other = f32[192,128]{1,0:T(8,128)S(1)} collective-permute-done((f32[192,128]{1,0:T(8,128)S(1)}, f32[192,128]{1,0:T(8,128)S(1)}, u32[]{:S(2)}, u32[]{:S(2)}) %collective-permute-start.8) | collective-permute-done | bytes 98336 | tf_op jit(solution)/shard_map/ppermute | solution.py:387
  36.6 1.8 %collective-permute-start.12 = (f32[192,128]{1,0:T(8,128)S(1)}, f32[192,128]{1,0:T(8,128)S(1)}, u32[]{:S(2)}, u32[]{:S(2)}) collective-permute-start(f32[192,128]{1,0:T(8,128)S(1)} %get-tuple-element.63.g0.grad), channel_id=1, source_target_pairs={{0,64},{16,80},{32,96},{48,112},{64,0},{80,16},{96,32},{112,48},{1... | collective-permute-start | bytes 294920 | tf_op jit(solution)/shard_map/ppermute | solution.py:387
  38.4 0.7 %collective-permute-start.13 = (f32[192,128]{1,0:T(8,128)S(1)}, f32[192,128]{1,0:T(8,128)S(1)}, u32[]{:S(2)}, u32[]{:S(2)}) collective-permute-start(f32[192,128]{1,0:T(8,128)S(1)} %get-tuple-element.63.g0.grad), channel_id=1, source_target_pairs={{0,32},{16,48},{32,0},{48,16},{64,96},{80,112},{96,64},{112,80},{1... | collective-permute-start | bytes 294920 | tf_op jit(solution)/shard_map/ppermute | solution.py:387
  39.1 1.7 %collective-permute-start.14 = (f32[192,128]{1,0:T(8,128)S(1)}, f32[192,128]{1,0:T(8,128)S(1)}, u32[]{:S(2)}, u32[]{:S(2)}) collective-permute-start(f32[192,128]{1,0:T(8,128)S(1)} %get-tuple-element.63.g0.grad), channel_id=1, source_target_pairs={{0,96},{16,112},{32,64},{48,80},{64,32},{80,48},{96,0},{112,16},{1... | collective-permute-start | bytes 294920 | tf_op jit(solution)/shard_map/ppermute | solution.py:387
  40.8 0.8 %collective-permute-start.15 = (f32[72,128]{1,0:T(8,128)S(1)}, f32[72,128]{1,0:T(8,128)S(1)}, u32[]{:S(2)}, u32[]{:S(2)}) collective-permute-start(f32[72,128]{1,0:T(8,128)S(1)} %get-tuple-element.64), channel_id=1, source_target_pairs={{0,1},{1,2},{2,3},{3,4},{4,5},{5,6},{6,7},{7,8},{8,9},{9,10},{10,1... | collective-permute-start | bytes 110600 | tf_op jit(solution)/shard_map/ppermute | solution.py:390
  41.6 1.2 %collective-permute-start.16 = (f32[72,128]{1,0:T(8,128)S(1)}, f32[72,128]{1,0:T(8,128)S(1)}, u32[]{:S(2)}, u32[]{:S(2)}) collective-permute-start(f32[72,128]{1,0:T(8,128)S(1)} %get-tuple-element.65), channel_id=1, source_target_pairs={{1,0},{2,1},{3,2},{4,3},{5,4},{6,5},{7,6},{8,7},{9,8},{10,9},{11,1... | collective-permute-start | bytes 110600 | tf_op jit(solution)/shard_map/ppermute | solution.py:390
  42.8 1.9 %collective-permute-done.15.low = f32[72,128]{1,0:T(8,128)S(1)} collective-permute-done((f32[72,128]{1,0:T(8,128)S(1)}, f32[72,128]{1,0:T(8,128)S(1)}, u32[]{:S(2)}, u32[]{:S(2)}) %collective-permute-start.15) | collective-permute-done | bytes 36896 | tf_op jit(solution)/shard_map/ppermute | solution.py:390
  44.7 0.0 collective-permute-start.11
  44.7 2.9 %collective-permute-done.16.high = f32[72,128]{1,0:T(8,128)S(1)} collective-permute-done((f32[72,128]{1,0:T(8,128)S(1)}, f32[72,128]{1,0:T(8,128)S(1)}, u32[]{:S(2)}, u32[]{:S(2)}) %collective-permute-start.16) | collective-permute-done | bytes 36896 | tf_op jit(solution)/shard_map/ppermute | solution.py:390
  47.7 0.0 collective-permute-done.12.g2
  47.7 0.0 collective-permute-done.13.g1
  47.7 0.0 collective-permute-done.14.g3
  47.7 0.2 project_own.1
  47.8 0.1 collective-permute-start.20
  47.9 2.0 %collective-permute-start.21 = (f32[192,128]{1,0:T(8,128)S(1)}, f32[192,128]{1,0:T(8,128)S(1)}, u32[]{:S(2)}, u32[]{:S(2)}) collective-permute-start(f32[192,128]{1,0:T(8,128)S(1)} %get-tuple-element.71), channel_id=1, source_target_pairs={{1,0},{2,1},{3,2},{4,3},{5,4},{6,5},{7,6},{8,7},{9,8},{10,9},{11,1... | collective-permute-start | bytes 294920 | tf_op jit(solution)/shard_map/ppermute | solution.py:390
  49.9 0.0 collective-permute-start.17
  50.0 1.1 %static_last.1 = (f32[96,128]{1,0:T(8,128)S(1)}, f32[96,128]{1,0:T(8,128)S(1)}) custom-call(f32[72,128]{1,0:T(8,128)S(1)} %get-tuple-element.75.low, f32[72,128]{1,0:T(8,128)S(1)} %get-tuple-element.76.high, f32[192,128]{1,0:T(8,128)S(1)} %get-tuple-element.63.g0.grad, f32[200,128]{1,0:T(8,128)S(1)} %get-tuple-element.77.coefs, ...), custom_call_target="tpu_custom_call" | custom-call | flops 5000000000 | bytes 1000000 | tf_op jit(solution)/shard_map/static_last/pallas_call | solution.py:471
  51.0 0.0 copy-start.2
  51.1 0.0 collective-permute-done.11.g0
  51.1 0.5 collective-permute-done.17.rest
  51.5 0.1 project_other.1
  51.7 2.3 %collective-permute-start.18 = (f32[192,128]{1,0:T(8,128)S(1)}, f32[192,128]{1,0:T(8,128)S(1)}, u32[]{:S(2)}, u32[]{:S(2)}) collective-permute-start(f32[192,128]{1,0:T(8,128)S(1)} %get-tuple-element.67), channel_id=1, source_target_pairs={{0,1},{1,2},{2,3},{3,4},{4,5},{5,6},{6,7},{7,8},{8,9},{9,10},{10,1... | collective-permute-start | bytes 294920 | tf_op jit(solution)/shard_map/ppermute | solution.py:390
  53.9 0.0 collective-permute-start.19
  53.9 0.0 collective-permute-done.20.low
  53.9 1.1 %collective-permute-done.21.high = f32[192,128]{1,0:T(8,128)S(1)} collective-permute-done((f32[192,128]{1,0:T(8,128)S(1)}, f32[192,128]{1,0:T(8,128)S(1)}, u32[]{:S(2)}, u32[]{:S(2)}) %collective-permute-start.21) | collective-permute-done | bytes 98336 | tf_op jit(solution)/shard_map/ppermute | solution.py:390
  55.0 1.6 %third.1 = (f32[256,128]{1,0:T(8,128)S(1)}, f32[256,128]{1,0:T(8,128)S(1)}) custom-call(f32[192,128]{1,0:T(8,128)S(1)} %collective-permute-done.20.low, f32[192,128]{1,0:T(8,128)S(1)} %collective-permute-done.21.high, f32[256,128]{1,0:T(8,128)S(1)} %get-tuple-element.72.middle, f32[200,128]{1,0:T(8,128)S(1)} %get-tuple-element.51.coefs, ...), custom_call_target="tpu_custom_call" | custom-call | flops 5000000000 | bytes 1000000 | tf_op jit(solution)/shard_map/third/pallas_call | solution.py:474
  56.6 0.5 collective-permute-done.18.low
  57.1 3.6 %collective-permute-done.19.high = f32[192,128]{1,0:T(8,128)S(1)} collective-permute-done((f32[192,128]{1,0:T(8,128)S(1)}, f32[192,128]{1,0:T(8,128)S(1)}, u32[]{:S(2)}, u32[]{:S(2)}) %collective-permute-start.19) | collective-permute-done | bytes 98336 | tf_op jit(solution)/shard_map/ppermute | solution.py:390
  60.7 2.3 %fourth.1 = (f32[2,8,2,16,128]{4,3,2,1,0:T(8,128)}, f32[2,8,2,16,128]{4,3,2,1,0:T(8,128)}, f32[96,128]{1,0:T(8,128)}, f32[96,128]{1,0:T(8,128)}) custom-call(f32[192,128]{1,0:T(8,128)S(1)} %collective-permute-done.18.low, f32[192,128]{1,0:T(8,128)S(1)} %collective-permute-done.19.high, f32[256,128]{1,0:T(8,128)S(1)} %get-tuple-element.69.middle, ...), custom_call_target="tpu_custom_call" | custom-call | flops 1000000 | bytes 1000000 | tf_op jit(solution)/shard_map/fourth/pallas_call | solution.py:477
  (10 shorter events, 0.1 us)
Async XLA Ops:
  0.6 5.2 %copy-start.5 = (f32[2,16,128]{2,1,0:T(8,128)S(1)}, f32[2,16,128]{2,1,0:T(8,128)}, u32[]{:S(2)}) copy-start(f32[2,16,128]{2,1,0:T(8,128)} %param.17) | copy-start | bytes 49156
  2.4 11.0 %collective-permute-start.2 = (f32[216,128]{1,0:T(8,128)}, f32[216,128]{1,0:T(8,128)S(1)}, u32[]{:S(2)}, u32[]{:S(2)}) collective-permute-start(f32[216,128]{1,0:T(8,128)} %get-tuple-element.46), channel_id=1, source_target_pairs={{0,1},{1,2},{2,3},{3,4},{4,5},{5,6},{6,7},{7,8},{8,9},{9,10},{10,1... | collective-permute-start | bytes 331784 | tf_op jit(solution)/shard_map/ppermute | solution.py:390
  5.9 7.6 %collective-permute-start.3 = (f32[216,128]{1,0:T(8,128)}, f32[216,128]{1,0:T(8,128)S(1)}, u32[]{:S(2)}, u32[]{:S(2)}) collective-permute-start(f32[216,128]{1,0:T(8,128)} %get-tuple-element.47), channel_id=1, source_target_pairs={{1,0},{2,1},{3,2},{4,3},{5,4},{6,5},{7,6},{8,7},{9,8},{10,9},{11,1... | collective-permute-start | bytes 331784 | tf_op jit(solution)/shard_map/ppermute | solution.py:390
  5.9 0.7 %copy-start.7 = (s32[1,1024]{1,0:T(1,128)S(1)}, s32[1,1024]{1,0:T(1,128)}, u32[]{:S(2)}) copy-start(s32[1,1024]{1,0:T(1,128)} %param.19) | copy-start | bytes 12292
  5.9 0.7 %copy-start.6 = (s32[1,1024]{1,0:T(1,128)S(1)}, s32[1,1024]{1,0:T(1,128)}, u32[]{:S(2)}) copy-start(s32[1,1024]{1,0:T(1,128)} %param.18) | copy-start | bytes 12292
  7.7 7.5 %collective-permute-start = (f32[192,128]{1,0:T(8,128)S(1)}, f32[192,128]{1,0:T(8,128)S(1)}, u32[]{:S(2)}, u32[]{:S(2)}) collective-permute-start(f32[192,128]{1,0:T(8,128)S(1)} %get-tuple-element.44), channel_id=1, source_target_pairs={{0,1},{1,2},{2,3},{3,4},{4,5},{5,6},{6,7},{7,8},{8,9},{9,10},{10,1... | collective-permute-start | bytes 294920 | tf_op jit(solution)/shard_map/ppermute | solution.py:390
  12.0 6.7 %collective-permute-start.1 = (f32[192,128]{1,0:T(8,128)S(1)}, f32[192,128]{1,0:T(8,128)S(1)}, u32[]{:S(2)}, u32[]{:S(2)}) collective-permute-start(f32[192,128]{1,0:T(8,128)S(1)} %get-tuple-element.45), channel_id=1, source_target_pairs={{1,0},{2,1},{3,2},{4,3},{5,4},{6,5},{7,6},{8,7},{9,8},{10,9},{11,1... | collective-permute-start | bytes 294920 | tf_op jit(solution)/shard_map/ppermute | solution.py:390
  12.0 1.5 %copy-start = (bf16[2,6,16,16,128]{4,3,2,1,0:T(8,128)(2,1)S(1)}, bf16[2,6,16,16,128]{4,3,2,1,0:T(8,128)(2,1)}, u32[]{:S(2)}) copy-start(bf16[2,6,16,16,128]{4,3,2,1,0:T(8,128)(2,1)} %perturb.7) | copy-start | bytes 2359300
  12.0 1.5 %copy-start.1 = (f32[2,16,16,128]{3,2,1,0:T(8,128)S(1)}, f32[2,16,16,128]{3,2,1,0:T(8,128)}, u32[]{:S(2)}) copy-start(f32[2,16,16,128]{3,2,1,0:T(8,128)} %param.12) | copy-start | bytes 786436
  12.0 1.5 %copy-start.3 = (f32[2,16,128]{2,1,0:T(8,128)S(1)}, f32[2,16,128]{2,1,0:T(8,128)}, u32[]{:S(2)}) copy-start(f32[2,16,128]{2,1,0:T(8,128)} %param.16) | copy-start | bytes 49156
  15.1 5.1 %collective-permute-start.4 = (f32[8,6,16,128]{3,2,1,0:T(8,128)S(1)}, f32[8,6,16,128]{3,2,1,0:T(8,128)S(1)}, u32[]{:S(2)}, u32[]{:S(2)}) collective-permute-start(f32[8,6,16,128]{3,2,1,0:T(8,128)S(1)} %get-tuple-element.52), channel_id=1, source_target_pairs={{0,16},{16,0},{32,48},{48,32},{64,80},{80,64},{96,112},{112,96},{1... | collective-permute-start | bytes 1179656 | tf_op jit(solution)/shard_map/ppermute | solution.py:387
  20.3 8.5 %collective-permute-start.5 = (f32[192,128]{1,0:T(8,128)S(1)}, f32[192,128]{1,0:T(8,128)S(1)}, u32[]{:S(2)}, u32[]{:S(2)}) collective-permute-start(f32[192,128]{1,0:T(8,128)S(1)} %get-tuple-element.54), channel_id=1, source_target_pairs={{0,64},{16,80},{32,96},{48,112},{64,0},{80,16},{96,32},{112,48},{1... | collective-permute-start | bytes 294920 | tf_op jit(solution)/shard_map/ppermute | solution.py:387
  23.6 5.2 %collective-permute-start.6 = (f32[192,128]{1,0:T(8,128)S(1)}, f32[192,128]{1,0:T(8,128)S(1)}, u32[]{:S(2)}, u32[]{:S(2)}) collective-permute-start(f32[192,128]{1,0:T(8,128)S(1)} %get-tuple-element.55), channel_id=1, source_target_pairs={{0,32},{16,48},{32,0},{48,16},{64,96},{80,112},{96,64},{112,80},{1... | collective-permute-start | bytes 294920 | tf_op jit(solution)/shard_map/ppermute | solution.py:387
  24.3 5.8 %collective-permute-start.7 = (f32[192,128]{1,0:T(8,128)S(1)}, f32[192,128]{1,0:T(8,128)S(1)}, u32[]{:S(2)}, u32[]{:S(2)}) collective-permute-start(f32[192,128]{1,0:T(8,128)S(1)} %get-tuple-element.56), channel_id=1, source_target_pairs={{0,96},{16,112},{32,64},{48,80},{64,32},{80,48},{96,0},{112,16},{1... | collective-permute-start | bytes 294920 | tf_op jit(solution)/shard_map/ppermute | solution.py:387
  24.7 6.9 %collective-permute-start.10 = (f32[192,128]{1,0:T(8,128)S(1)}, f32[192,128]{1,0:T(8,128)S(1)}, u32[]{:S(2)}, u32[]{:S(2)}) collective-permute-start(f32[192,128]{1,0:T(8,128)S(1)} %get-tuple-element.60), channel_id=1, source_target_pairs={{1,0},{2,1},{3,2},{4,3},{5,4},{6,5},{7,6},{8,7},{9,8},{10,9},{11,1... | collective-permute-start | bytes 294920 | tf_op jit(solution)/shard_map/ppermute | solution.py:390
  24.7 6.9 %collective-permute-start.9 = (f32[192,128]{1,0:T(8,128)S(1)}, f32[192,128]{1,0:T(8,128)S(1)}, u32[]{:S(2)}, u32[]{:S(2)}) collective-permute-start(f32[192,128]{1,0:T(8,128)S(1)} %get-tuple-element.59), channel_id=1, source_target_pairs={{0,1},{1,2},{2,3},{3,4},{4,5},{5,6},{6,7},{7,8},{8,9},{9,10},{10,1... | collective-permute-start | bytes 294920 | tf_op jit(solution)/shard_map/ppermute | solution.py:390
  30.2 6.4 %collective-permute-start.8 = (f32[192,128]{1,0:T(8,128)S(1)}, f32[192,128]{1,0:T(8,128)S(1)}, u32[]{:S(2)}, u32[]{:S(2)}) collective-permute-start(f32[192,128]{1,0:T(8,128)S(1)} %add_add_fusion.mine), channel_id=1, source_target_pairs={{0,128},{16,144},{32,160},{48,176},{64,192},{80,208},{96,224},{112... | collective-permute-start | bytes 294920 | tf_op jit(solution)/shard_map/ppermute | solution.py:387
  36.6 11.1 %collective-permute-start.12 = (f32[192,128]{1,0:T(8,128)S(1)}, f32[192,128]{1,0:T(8,128)S(1)}, u32[]{:S(2)}, u32[]{:S(2)}) collective-permute-start(f32[192,128]{1,0:T(8,128)S(1)} %get-tuple-element.63.g0.grad), channel_id=1, source_target_pairs={{0,64},{16,80},{32,96},{48,112},{64,0},{80,16},{96,32},{112,48},{1... | collective-permute-start | bytes 294920 | tf_op jit(solution)/shard_map/ppermute | solution.py:387
  38.4 9.3 %collective-permute-start.13 = (f32[192,128]{1,0:T(8,128)S(1)}, f32[192,128]{1,0:T(8,128)S(1)}, u32[]{:S(2)}, u32[]{:S(2)}) collective-permute-start(f32[192,128]{1,0:T(8,128)S(1)} %get-tuple-element.63.g0.grad), channel_id=1, source_target_pairs={{0,32},{16,48},{32,0},{48,16},{64,96},{80,112},{96,64},{112,80},{1... | collective-permute-start | bytes 294920 | tf_op jit(solution)/shard_map/ppermute | solution.py:387
  39.1 8.6 %collective-permute-start.14 = (f32[192,128]{1,0:T(8,128)S(1)}, f32[192,128]{1,0:T(8,128)S(1)}, u32[]{:S(2)}, u32[]{:S(2)}) collective-permute-start(f32[192,128]{1,0:T(8,128)S(1)} %get-tuple-element.63.g0.grad), channel_id=1, source_target_pairs={{0,96},{16,112},{32,64},{48,80},{64,32},{80,48},{96,0},{112,16},{1... | collective-permute-start | bytes 294920 | tf_op jit(solution)/shard_map/ppermute | solution.py:387
  40.8 4.0 %collective-permute-start.15 = (f32[72,128]{1,0:T(8,128)S(1)}, f32[72,128]{1,0:T(8,128)S(1)}, u32[]{:S(2)}, u32[]{:S(2)}) collective-permute-start(f32[72,128]{1,0:T(8,128)S(1)} %get-tuple-element.64), channel_id=1, source_target_pairs={{0,1},{1,2},{2,3},{3,4},{4,5},{5,6},{6,7},{7,8},{8,9},{9,10},{10,1... | collective-permute-start | bytes 110600 | tf_op jit(solution)/shard_map/ppermute | solution.py:390
  41.6 8.3 %copy-start.4 = (f32[6,1,16,128]{3,2,1,0:T(8,128)S(1)}, f32[6,1,16,128]{3,2,1,0:T(8,128)}, u32[]{:S(2)}) copy-start(f32[6,1,16,128]{3,2,1,0:T(8,128)} %param.15) | copy-start | bytes 147460
  41.6 6.1 %collective-permute-start.16 = (f32[72,128]{1,0:T(8,128)S(1)}, f32[72,128]{1,0:T(8,128)S(1)}, u32[]{:S(2)}, u32[]{:S(2)}) collective-permute-start(f32[72,128]{1,0:T(8,128)S(1)} %get-tuple-element.65), channel_id=1, source_target_pairs={{1,0},{2,1},{3,2},{4,3},{5,4},{6,5},{7,6},{8,7},{9,8},{10,9},{11,1... | collective-permute-start | bytes 110600 | tf_op jit(solution)/shard_map/ppermute | solution.py:390
  44.7 6.3 %collective-permute-start.11 = (f32[192,128]{1,0:T(8,128)S(1)}, f32[192,128]{1,0:T(8,128)S(1)}, u32[]{:S(2)}, u32[]{:S(2)}) collective-permute-start(f32[192,128]{1,0:T(8,128)S(1)} %get-tuple-element.63.g0.grad), channel_id=1, source_target_pairs={{0,16},{16,0},{32,48},{48,32},{64,80},{80,64},{96,112},{112,96},{1... | collective-permute-start | bytes 294920 | tf_op jit(solution)/shard_map/ppermute | solution.py:387
  47.8 6.1 %collective-permute-start.20 = (f32[192,128]{1,0:T(8,128)S(1)}, f32[192,128]{1,0:T(8,128)S(1)}, u32[]{:S(2)}, u32[]{:S(2)}) collective-permute-start(f32[192,128]{1,0:T(8,128)S(1)} %get-tuple-element.70), channel_id=1, source_target_pairs={{0,1},{1,2},{2,3},{3,4},{4,5},{5,6},{6,7},{7,8},{8,9},{9,10},{10,1... | collective-permute-start | bytes 294920 | tf_op jit(solution)/shard_map/ppermute | solution.py:390
  47.9 7.1 %collective-permute-start.21 = (f32[192,128]{1,0:T(8,128)S(1)}, f32[192,128]{1,0:T(8,128)S(1)}, u32[]{:S(2)}, u32[]{:S(2)}) collective-permute-start(f32[192,128]{1,0:T(8,128)S(1)} %get-tuple-element.71), channel_id=1, source_target_pairs={{1,0},{2,1},{3,2},{4,3},{5,4},{6,5},{7,6},{8,7},{9,8},{10,9},{11,1... | collective-permute-start | bytes 294920 | tf_op jit(solution)/shard_map/ppermute | solution.py:390
  49.9 1.6 %collective-permute-start.17 = (f32[576,128]{1,0:T(8,128)S(1)}, f32[576,128]{1,0:T(8,128)S(1)}, u32[]{:S(2)}, u32[]{:S(2)}) collective-permute-start(f32[576,128]{1,0:T(8,128)S(1)} %get-tuple-element.66), channel_id=1, source_target_pairs={{0,16},{16,0},{32,48},{48,32},{64,80},{80,64},{96,112},{112,96},{1... | collective-permute-start | bytes 884744 | tf_op jit(solution)/shard_map/ppermute | solution.py:387
  51.0 4.0 %copy-start.2 = (f32[2,16,16,128]{3,2,1,0:T(8,128)S(1)}, f32[2,16,16,128]{3,2,1,0:T(8,128)}, u32[]{:S(2)}) copy-start(f32[2,16,16,128]{3,2,1,0:T(8,128)} %param.13) | copy-start | bytes 786436
  51.7 5.4 %collective-permute-start.18 = (f32[192,128]{1,0:T(8,128)S(1)}, f32[192,128]{1,0:T(8,128)S(1)}, u32[]{:S(2)}, u32[]{:S(2)}) collective-permute-start(f32[192,128]{1,0:T(8,128)S(1)} %get-tuple-element.67), channel_id=1, source_target_pairs={{0,1},{1,2},{2,3},{3,4},{4,5},{5,6},{6,7},{7,8},{8,9},{9,10},{10,1... | collective-permute-start | bytes 294920 | tf_op jit(solution)/shard_map/ppermute | solution.py:390
  53.9 6.7 %collective-permute-start.19 = (f32[192,128]{1,0:T(8,128)S(1)}, f32[192,128]{1,0:T(8,128)S(1)}, u32[]{:S(2)}, u32[]{:S(2)}) collective-permute-start(f32[192,128]{1,0:T(8,128)S(1)} %get-tuple-element.68), channel_id=1, source_target_pairs={{1,0},{2,1},{3,2},{4,3},{5,4},{6,5},{7,6},{8,7},{9,8},{10,9},{11,1... | collective-permute-start | bytes 294920 | tf_op jit(solution)/shard_map/ppermute | solution.py:390

commit v5 on v4

--- a/solution.py
+++ b/solution.py
@@ -258,11 +258,9 @@
             sums[pl.ds(block * 2 + r, 24, stride=ROWS), :] = total[:, r * LANES : (r + 1) * LANES]
 
 
-def gradient_body(mine, other, static, sums, grad, forward, backward):
-    x, _, _ = place()
+def gradient_body(mine, other, static, sums, grad):
     total = mine[...] + other[...] + static[...]
     grad[...] = sums[0:192, :] * total - sums[192:384, :]
-    pack_rows(lambda row: grad[pl.ds(x * 96 + row, VARS, stride=ROWS), :], VARS, forward, backward)
 
 
 def project(g, k, parity, perturb, middle):
@@ -278,15 +276,15 @@
             middle[pl.ds(pl.multiple_of((m * HALF + s) * 16, 16), 16), :] = total
 
 
-def project_own_body(g0, g2, g1, g3, perturb, low, high, forward, backward, middle, rest, low_out, high_out):
-    _, _, c = place()
-    low_out[...] = low[...]
-    high_out[...] = high[...]
+def project_own_body(g0, mate, g3, g1, g2, perturb, forward, backward, middle, rest, kept):
+    x, _, c = place()
+    kept[...] = mate[...]
     for k, g in enumerate((g0, g1, g2, g3)):
         project(g, k, c, perturb, middle)
         if k > 0:
             rest[(k - 1) * 192 : k * 192, :] = g[...]
     pack_rows(lambda row: middle[pl.ds(row, 16, stride=ROWS), :], 16, forward, backward)
+    pack_rows(lambda row: g0[pl.ds(x * 96 + row, VARS, stride=ROWS), :], VARS, forward, backward, 192)
 
 
 def project_other_body(g0, rest, perturb, forward, backward, middle):
@@ -308,7 +306,7 @@
             stage0[here, :] = old - step_rate * moved
 
 
-def third_body(low, high, middle, coefs, alpha, mom, stage0, stage1, buf0, buf1, out):
+def third_body(low, high, middle, coefs, alpha, mom, after, stage0, stage1, buf0, buf1, out):
     def emit(row, value):
         out[pl.ds(row, 16, stride=ROWS), :] = value
 
@@ -317,9 +315,9 @@
     update_alpha(lax.axis_index("mem") % 2, out, alpha, mom, stage0, stage1)
 
 
-def static_last_body(low, high, grad, coefs, field, static_mom, new_static, new_static_mom, buf0, buf1, out):
+def static_last_body(low, high, grad, coefs, field, static_mom, after, new_static, new_static_mom, buf0, buf1, out):
     x, _, _ = place()
-    load = halo_loader(low, high, lambda row: grad[pl.ds(x * 96 + row, VARS, stride=ROWS), :], VARS)
+    load = halo_loader(low, high, lambda row: grad[pl.ds(x * 96 + row, VARS, stride=ROWS), :], VARS, 192)
     for row in range(SPAN):
         buf0[row * 8 : row * 8 + VARS, :] = load(row)
 
@@ -450,29 +448,26 @@
         [raw] + bufs16 + [f32(256, LANES)],
         flops=BUSY,
     )(c_low, c_high, field)
-    narrow = shape(72, LANES)
-    grad, g_f, g_b = call(gradient_body, "gradient", [VM] * 4, [quarter, narrow, narrow])(mine, other, static, sums)
+    (grad,) = call(gradient_body, "gradient", [VM] * 4, [quarter])(mine, other, static, sums)
     g2, g1, g3 = swap(grad, 4), swap(grad, 2), swap(grad, 6)
-    g_low, g_high = halo(g_f, g_b)
     p0 = swap(grad, 1)
-    gs = [grad, g2, g1, g3]
-    p_f, p_b, p_m, rest, g_low, g_high = call(
+    p_f, p_b, p_m, rest, p0 = call(
         project_own_body,
         "project_own",
-        [VM] * 7,
-        [quarter, quarter, half, shape(576, LANES), narrow, narrow],
-    )(*gs, perturb, g_low, g_high)
+        [VM] * 6,
+        [shape(264, LANES), shape(264, LANES), half, shape(576, LANES), quarter],
+    )(grad, p0, g3, g1, g2, perturb)
     p_low, p_high = halo(p_f, p_b)
     rest = swap(rest, 1)
     q_f, q_b, q_m = call(project_other_body, "project_other", [VM] * 3, [quarter, quarter, half])(p0, rest, perturb)
     q_low, q_high = halo(q_f, q_b)
     whole = shape(2, HALF, 2, ROWS, LANES)
     work = bufs16 + [f32(256, LANES)]
-    static_ready = call(static_last_body, "static_last", [VM] * 6, [shape(96, LANES)] * 2, work, flops=BUSY)(
-        g_low, g_high, grad, static_k, field, static_mom.reshape(96, LANES)
-    )
-    ready = call(third_body, "third", [VM] * 6, [half, half], work, flops=BUSY)(
-        p_low, p_high, p_m, loc_k, alpha2, mom2
+    static_ready = call(static_last_body, "static_last", [VM] * 7, [shape(96, LANES)] * 2, work, flops=BUSY)(
+        p_low, p_high, grad, static_k, field, static_mom.reshape(96, LANES), q_m
+    )
+    ready = call(third_body, "third", [VM] * 7, [half, half], work, flops=BUSY)(
+        p_low, p_high, p_m, loc_k, alpha2, mom2, q_m
     )
     new_alpha, new_alpha_mom, new_static, new_static_mom = call(
         fourth_body,

time: 63.4 us -> 62.6 us (0.987)
  the two profiles are of different devices: /device:TPU:102 before, /device:TPU:4 now
where the time goes in v5:
time: 62.6 us; the launch traced here: 62.4 us
  starting transfers between devices  33.2 us (53%)
  Pallas kernels  14.5 us (23%)
  waiting for transfers between devices  12.9 us (21%)
  between operations  1.01 us (2%)
  local copies, waits for them, and re-layouts  0.72 us (1%)
    ppermute x5, starting transfers between devices, halo(): lax.ppermute(backward, 'tile', down)  21.9 us
    ppermute x10, starting transfers between devices, swap(): return lax.ppermute(value, 'mem', [(i, i ^ bits) for i in range(members)])  9.79 us
    ppermute x10, waiting for transfers between devices, swap(): return lax.ppermute(value, 'mem', [(i, i ^ bits) for i in range(members)])  9.41 us
    ppermute x5, waiting for transfers between devices, halo(): lax.ppermute(backward, 'tile', down)  3.32 us
    pallas_call x1, Pallas kernels, local(): call(fourth_body, 'fourth', [VM] * 10, [whole, whole, shape(96, LANES), s...  2.34 us
    pallas_call x1, Pallas kernels, local(): call(pack_body, 'pack', [HBM] * 2, [shape(216, LANES)] * 2, [f32(512, LAN...  1.73 us
    pallas_call x1, Pallas kernels, local(): call(first_body, 'first', [VM] * 6, [shape(HALF, VARS, ROWS, LANES), shap...  1.66 us
    pallas_call x1, Pallas kernels, local(): call(third_body, 'third', [VM] * 7, [half, half], work, flops=BUSY)  1.59 us
  transfers between devices with their start and end apart: 20, of which 10 were waited for; matrix products, arithmetic and copies ran while one was open for 0% of the time, Pallas kernels for 16%

profile of v5, /device:TPU:4, one launch (start us, length us, event | category | flops | bytes accessed | tf_op | source)
XLA Modules:
  0.0 62.4 jit_solution(2635487021994208698)
XLA Ops:
  0.6 0.0 copy-start.5
  0.6 1.7 %pack.1 = (f32[216,128]{1,0:T(8,128)}, f32[216,128]{1,0:T(8,128)}) custom-call(f32[512,128]{1,0:T(8,128)} %bitcast.17, f32[32,128]{1,0:T(8,128)} %bitcast.25), custom_call_target="tpu_custom_call" | custom-call | flops 1000000 | bytes 1000000 | tf_op jit(solution)/shard_map/pack/pallas_call | solution.py:398
  2.4 1.3 %collective-permute-start.2 = (f32[216,128]{1,0:T(8,128)}, f32[216,128]{1,0:T(8,128)S(1)}, u32[]{:S(2)}, u32[]{:S(2)}) collective-permute-start(f32[216,128]{1,0:T(8,128)} %get-tuple-element.42), channel_id=1, source_target_pairs={{0,1},{1,2},{2,3},{3,4},{4,5},{5,6},{6,7},{7,8},{8,9},{9,10},{10,1... | collective-permute-start | bytes 331784 | tf_op jit(solution)/shard_map/ppermute | solution.py:388
  3.7 5.4 %collective-permute-start.3 = (f32[216,128]{1,0:T(8,128)}, f32[216,128]{1,0:T(8,128)S(1)}, u32[]{:S(2)}, u32[]{:S(2)}) collective-permute-start(f32[216,128]{1,0:T(8,128)} %get-tuple-element.43), channel_id=1, source_target_pairs={{1,0},{2,1},{3,2},{4,3},{5,4},{6,5},{7,6},{8,7},{9,8},{10,9},{11,1... | collective-permute-start | bytes 331784 | tf_op jit(solution)/shard_map/ppermute | solution.py:388
  9.0 0.0 copy-start.7
  9.0 0.0 copy-start.6
  9.0 0.0 copy-done.5
  9.0 0.7 %copy-done.7 = s32[1,1024]{1,0:T(1,128)S(1)} copy-done((s32[1,1024]{1,0:T(1,128)S(1)}, s32[1,1024]{1,0:T(1,128)}, u32[]{:S(2)}) %copy-start.7) | copy-done | bytes 4120
  9.7 0.0 copy-done.6
  9.7 1.2 %fetch.1 = (f32[192,128]{1,0:T(8,128)S(1)}, f32[192,128]{1,0:T(8,128)S(1)}, f32[192,128]{1,0:T(8,128)S(1)}, f32[192,128]{1,0:T(8,128)S(1)}, f32[256,128]{1,0:T(8...) custom-call(f32[512,128]{1,0:T(8,128)} %bitcast.18, s32[8,128]{1,0:T(8,128)S(1)} %bitcast.29, ...), custom_call_target="tpu_custom_call" | custom-call | flops 5000000000 | bytes 1000000 | tf_op jit(solution)/shard_map/fetch/pallas_call | solution.py:408
  10.9 0.1 collective-permute-start
  11.0 4.1 %collective-permute-start.1 = (f32[192,128]{1,0:T(8,128)S(1)}, f32[192,128]{1,0:T(8,128)S(1)}, u32[]{:S(2)}, u32[]{:S(2)}) collective-permute-start(f32[192,128]{1,0:T(8,128)S(1)} %get-tuple-element.41), channel_id=1, source_target_pairs={{1,0},{2,1},{3,2},{4,3},{5,4},{6,5},{7,6},{8,7},{9,8},{10,9},{11,1... | collective-permute-start | bytes 294920 | tf_op jit(solution)/shard_map/ppermute | solution.py:388
  15.1 0.0 copy-start
  15.1 1.4 %prepare.1.ready.sums = f32[384,128]{1,0:T(8,128)S(1)} custom-call(s32[8,128]{1,0:T(8,128)S(1)} %get-tuple-element.44.cell, s32[8,128]{1,0:T(8,128)S(1)} %get-tuple-element.45.mask, f32[192,128]{1,0:T(8,128)S(1)} %get-tuple-element.46.held), custom_call_target="tpu_custom_call" | custom-call | flops 5000000000 | bytes 1000000 | tf_op jit(solution)/shard_map/prepare/pallas_call | solution.py:426
  16.6 0.0 collective-permute-done.2.low
  16.6 0.0 collective-permute-done.3.high
  16.6 0.0 copy-done
  16.6 0.0 copy-done.1
  16.6 0.0 copy-done.3
  16.6 1.7 %first.1 = (f32[8,6,16,128]{3,2,1,0:T(8,128)S(1)}, f32[200,128]{1,0:T(8,128)S(1)}) custom-call(f32[512,128]{1,0:T(8,128)S(1)} %bitcast.19, f32[216,128]{1,0:T(8,128)S(1)} %collective-permute-done.2.low, f32[216,128]{1,0:T(8,128)S(1)} %collective-permute-done.3.high, f32[32,128]{1,0:T(8,128)S(1)} %bitcast.26, bf16[2,6,16,16,128]{4,3,2,1,0:T(8,128)(2,1)S(1)} %copy-done, ...), custom_call_target="tpu_custom_call" | custom-call | flops 5000000000 | bytes 1000000 | tf_op jit(solution)/shard_map/first/pallas_call | solution.py:428
  18.3 0.1 collective-permute-start.4
  18.4 0.0 collective-permute-done.low
  18.4 0.0 collective-permute-done.1.high
  18.4 1.5 %second.1.local = f32[256,128]{1,0:T(8,128)S(1)} custom-call(f32[512,128]{1,0:T(8,128)S(1)} %bitcast.20, f32[192,128]{1,0:T(8,128)S(1)} %collective-permute-done.low, f32[192,128]{1,0:T(8,128)S(1)} %collective-permute-done.1.high, f32[200,128]{1,0:T(8,128)S(1)} %get-tuple-element.47.coefs), custom_call_target="tpu_custom_call" | custom-call | flops 5000000000 | bytes 1000000 | tf_op jit(solution)/shard_map/second/pallas_call | solution.py:437
  20.0 0.2 collective-permute-done.4.received
  20.1 0.1 sum.1
  20.2 3.3 %collective-permute-start.5 = (f32[192,128]{1,0:T(8,128)S(1)}, f32[192,128]{1,0:T(8,128)S(1)}, u32[]{:S(2)}, u32[]{:S(2)}) collective-permute-start(f32[192,128]{1,0:T(8,128)S(1)} %get-tuple-element.50), channel_id=1, source_target_pairs={{0,64},{16,80},{32,96},{48,112},{64,0},{80,16},{96,32},{112,48},{1... | collective-permute-start | bytes 294920 | tf_op jit(solution)/shard_map/ppermute | solution.py:385
  23.5 0.7 %collective-permute-start.6 = (f32[192,128]{1,0:T(8,128)S(1)}, f32[192,128]{1,0:T(8,128)S(1)}, u32[]{:S(2)}, u32[]{:S(2)}) collective-permute-start(f32[192,128]{1,0:T(8,128)S(1)} %get-tuple-element.51), channel_id=1, source_target_pairs={{0,32},{16,48},{32,0},{48,16},{64,96},{80,112},{96,64},{112,80},{1... | collective-permute-start | bytes 294920 | tf_op jit(solution)/shard_map/ppermute | solution.py:385
  24.2 0.4 collective-permute-start.7
  24.5 0.0 collective-permute-start.9
  24.6 4.1 %collective-permute-start.10 = (f32[192,128]{1,0:T(8,128)S(1)}, f32[192,128]{1,0:T(8,128)S(1)}, u32[]{:S(2)}, u32[]{:S(2)}) collective-permute-start(f32[192,128]{1,0:T(8,128)S(1)} %get-tuple-element.56), channel_id=1, source_target_pairs={{1,0},{2,1},{3,2},{4,3},{5,4},{6,5},{7,6},{8,7},{9,8},{10,9},{11,1... | collective-permute-start | bytes 294920 | tf_op jit(solution)/shard_map/ppermute | solution.py:388
  28.7 0.0 collective-permute-done.5
  28.7 0.6 collective-permute-done.6
  29.3 0.7 %collective-permute-done.7 = f32[192,128]{1,0:T(8,128)S(1)} collective-permute-done((f32[192,128]{1,0:T(8,128)S(1)}, f32[192,128]{1,0:T(8,128)S(1)}, u32[]{:S(2)}, u32[]{:S(2)}) %collective-permute-start.7) | collective-permute-done | bytes 98336 | tf_op jit(solution)/shard_map/ppermute | solution.py:385
  30.0 1.1 %collective-permute-start.8 = (f32[192,128]{1,0:T(8,128)S(1)}, f32[192,128]{1,0:T(8,128)S(1)}, u32[]{:S(2)}, u32[]{:S(2)}) collective-permute-start(f32[192,128]{1,0:T(8,128)S(1)} %add_add_fusion.mine), channel_id=1, source_target_pairs={{0,128},{16,144},{32,160},{48,176},{64,192},{80,208},{96,224},{112... | collective-permute-start | bytes 294920 | tf_op jit(solution)/shard_map/ppermute | solution.py:385
  31.1 0.2 collective-permute-done.9.low
  31.3 0.3 collective-permute-done.10.high
  31.6 1.6 %static_first.1 = (f32[192,128]{1,0:T(8,128)S(1)}, f32[200,128]{1,0:T(8,128)S(1)}) custom-call(f32[192,128]{1,0:T(8,128)S(1)} %collective-permute-done.9.low, f32[192,128]{1,0:T(8,128)S(1)} %collective-permute-done.10.high, f32[256,128]{1,0:T(8,128)S(1)} %get-tuple-element.57.field), custom_call_target="tpu_custom_call" | custom-call | flops 5000000000 | bytes 1000000 | tf_op jit(solution)/shard_map/static_first/pallas_call | solution.py:443
  33.2 3.3 %collective-permute-done.8.other = f32[192,128]{1,0:T(8,128)S(1)} collective-permute-done((f32[192,128]{1,0:T(8,128)S(1)}, f32[192,128]{1,0:T(8,128)S(1)}, u32[]{:S(2)}, u32[]{:S(2)}) %collective-permute-start.8) | collective-permute-done | bytes 98336 | tf_op jit(solution)/shard_map/ppermute | solution.py:385
  36.4 2.3 %collective-permute-start.14 = (f32[192,128]{1,0:T(8,128)S(1)}, f32[192,128]{1,0:T(8,128)S(1)}, u32[]{:S(2)}, u32[]{:S(2)}) collective-permute-start(f32[192,128]{1,0:T(8,128)S(1)} %gradient.1.g0.grad), channel_id=1, source_target_pairs={{0,64},{16,80},{32,96},{48,112},{64,0},{80,16},{96,32},{112,48},{1... | collective-permute-start | bytes 294920 | tf_op jit(solution)/shard_map/ppermute | solution.py:385
  38.8 0.7 %collective-permute-start.13 = (f32[192,128]{1,0:T(8,128)S(1)}, f32[192,128]{1,0:T(8,128)S(1)}, u32[]{:S(2)}, u32[]{:S(2)}) collective-permute-start(f32[192,128]{1,0:T(8,128)S(1)} %gradient.1.g0.grad), channel_id=1, source_target_pairs={{0,32},{16,48},{32,0},{48,16},{64,96},{80,112},{96,64},{112,80},{1... | collective-permute-start | bytes 294920 | tf_op jit(solution)/shard_map/ppermute | solution.py:385
  39.5 1.1 %collective-permute-start.12 = (f32[192,128]{1,0:T(8,128)S(1)}, f32[192,128]{1,0:T(8,128)S(1)}, u32[]{:S(2)}, u32[]{:S(2)}) collective-permute-start(f32[192,128]{1,0:T(8,128)S(1)} %gradient.1.g0.grad), channel_id=1, source_target_pairs={{0,96},{16,112},{32,64},{48,80},{64,32},{80,48},{96,0},{112,16},{1... | collective-permute-start | bytes 294920 | tf_op jit(solution)/shard_map/ppermute | solution.py:385
  40.6 0.0 collective-permute-start.11
  40.6 2.1 %collective-permute-done.14.g2 = f32[192,128]{1,0:T(8,128)S(1)} collective-permute-done((f32[192,128]{1,0:T(8,128)S(1)}, f32[192,128]{1,0:T(8,128)S(1)}, u32[]{:S(2)}, u32[]{:S(2)}) %collective-permute-start.14) | collective-permute-done | bytes 98336 | tf_op jit(solution)/shard_map/ppermute | solution.py:385
  42.7 0.7 %collective-permute-done.13.g1 = f32[192,128]{1,0:T(8,128)S(1)} collective-permute-done((f32[192,128]{1,0:T(8,128)S(1)}, f32[192,128]{1,0:T(8,128)S(1)}, u32[]{:S(2)}, u32[]{:S(2)}) %collective-permute-start.13) | collective-permute-done | bytes 98336 | tf_op jit(solution)/shard_map/ppermute | solution.py:385
  43.4 1.9 %collective-permute-done.12.g3 = f32[192,128]{1,0:T(8,128)S(1)} collective-permute-done((f32[192,128]{1,0:T(8,128)S(1)}, f32[192,128]{1,0:T(8,128)S(1)}, u32[]{:S(2)}, u32[]{:S(2)}) %collective-permute-start.12) | collective-permute-done | bytes 98336 | tf_op jit(solution)/shard_map/ppermute | solution.py:385
  45.3 0.0 collective-permute-done.11.mate
  45.3 0.2 project_own.1
  45.5 0.1 collective-permute-start.15
  45.6 0.1 collective-permute-start.18
  45.7 4.1 %collective-permute-start.19 = (f32[264,128]{1,0:T(8,128)S(1)}, f32[264,128]{1,0:T(8,128)S(1)}, u32[]{:S(2)}, u32[]{:S(2)}) collective-permute-start(f32[264,128]{1,0:T(8,128)S(1)} %get-tuple-element.65), channel_id=1, source_target_pairs={{1,0},{2,1},{3,2},{4,3},{5,4},{6,5},{7,6},{8,7},{9,8},{10,9},{11,1... | collective-permute-start | bytes 405512 | tf_op jit(solution)/shard_map/ppermute | solution.py:388
  49.8 0.0 collective-permute-done.15.rest
  49.8 0.1 project_other.1
  49.9 0.1 collective-permute-start.16
  50.0 4.1 %collective-permute-start.17 = (f32[192,128]{1,0:T(8,128)S(1)}, f32[192,128]{1,0:T(8,128)S(1)}, u32[]{:S(2)}, u32[]{:S(2)}) collective-permute-start(f32[192,128]{1,0:T(8,128)S(1)} %get-tuple-element.62), channel_id=1, source_target_pairs={{1,0},{2,1},{3,2},{4,3},{5,4},{6,5},{7,6},{8,7},{9,8},{10,9},{11,1... | collective-permute-start | bytes 294920 | tf_op jit(solution)/shard_map/ppermute | solution.py:388
  54.1 0.0 collective-permute-done.18.low
  54.1 3.0 %collective-permute-done.19.high = f32[264,128]{1,0:T(8,128)S(1)} collective-permute-done((f32[264,128]{1,0:T(8,128)S(1)}, f32[264,128]{1,0:T(8,128)S(1)}, u32[]{:S(2)}, u32[]{:S(2)}) %collective-permute-start.19) | collective-permute-done | bytes 135200 | tf_op jit(solution)/shard_map/ppermute | solution.py:388
  57.2 0.0 copy-done.4
  57.2 1.1 %static_last.1 = (f32[96,128]{1,0:T(8,128)S(1)}, f32[96,128]{1,0:T(8,128)S(1)}) custom-call(f32[264,128]{1,0:T(8,128)S(1)} %collective-permute-done.18.low, f32[264,128]{1,0:T(8,128)S(1)} %collective-permute-done.19.high, f32[192,128]{1,0:T(8,128)S(1)} %gradient.1.g0.grad, f32[200,128]{1,0:T(8,128)S(1)} %get-tuple-element.69.coefs, ...), custom_call_target="tpu_custom_call" | custom-call | flops 5000000000 | bytes 1000000 | tf_op jit(solution)/shard_map/static_last/pallas_call | solution.py:466
  58.3 0.0 copy-done.2
  58.3 1.6 %third.1 = (f32[256,128]{1,0:T(8,128)S(1)}, f32[256,128]{1,0:T(8,128)S(1)}) custom-call(f32[264,128]{1,0:T(8,128)S(1)} %collective-permute-done.18.low, f32[264,128]{1,0:T(8,128)S(1)} %collective-permute-done.19.high, f32[256,128]{1,0:T(8,128)S(1)} %get-tuple-element.66.middle, f32[200,128]{1,0:T(8,128)S(1)} %get-tuple-element.47.coefs, ...), custom_call_target="tpu_custom_call" | custom-call | flops 5000000000 | bytes 1000000 | tf_op jit(solution)/shard_map/third/pallas_call | solution.py:469
  59.9 0.0 collective-permute-done.16.low
  59.9 0.0 collective-permute-done.17.high
  59.9 2.3 %fourth.1 = (f32[2,8,2,16,128]{4,3,2,1,0:T(8,128)}, f32[2,8,2,16,128]{4,3,2,1,0:T(8,128)}, f32[96,128]{1,0:T(8,128)}, f32[96,128]{1,0:T(8,128)}) custom-call(f32[192,128]{1,0:T(8,128)S(1)} %collective-permute-done.16.low, f32[192,128]{1,0:T(8,128)S(1)} %collective-permute-done.17.high, f32[256,128]{1,0:T(8,128)S(1)} %get-tuple-element.63.after.middle, ...), custom_call_target="tpu_custom_call" | custom-call | flops 1000000 | bytes 1000000 | tf_op jit(solution)/shard_map/fourth/pallas_call | solution.py:472
  (6 shorter events, 0.1 us)
Async XLA Ops:
  0.6 8.4 %copy-start.5 = (f32[2,16,128]{2,1,0:T(8,128)S(1)}, f32[2,16,128]{2,1,0:T(8,128)}, u32[]{:S(2)}) copy-start(f32[2,16,128]{2,1,0:T(8,128)} %param.17) | copy-start | bytes 49156
  2.4 14.2 %collective-permute-start.2 = (f32[216,128]{1,0:T(8,128)}, f32[216,128]{1,0:T(8,128)S(1)}, u32[]{:S(2)}, u32[]{:S(2)}) collective-permute-start(f32[216,128]{1,0:T(8,128)} %get-tuple-element.42), channel_id=1, source_target_pairs={{0,1},{1,2},{2,3},{3,4},{4,5},{5,6},{6,7},{7,8},{8,9},{9,10},{10,1... | collective-permute-start | bytes 331784 | tf_op jit(solution)/shard_map/ppermute | solution.py:388
  3.7 12.9 %collective-permute-start.3 = (f32[216,128]{1,0:T(8,128)}, f32[216,128]{1,0:T(8,128)S(1)}, u32[]{:S(2)}, u32[]{:S(2)}) collective-permute-start(f32[216,128]{1,0:T(8,128)} %get-tuple-element.43), channel_id=1, source_target_pairs={{1,0},{2,1},{3,2},{4,3},{5,4},{6,5},{7,6},{8,7},{9,8},{10,9},{11,1... | collective-permute-start | bytes 331784 | tf_op jit(solution)/shard_map/ppermute | solution.py:388
  9.0 0.7 %copy-start.7 = (s32[1,1024]{1,0:T(1,128)S(1)}, s32[1,1024]{1,0:T(1,128)}, u32[]{:S(2)}) copy-start(s32[1,1024]{1,0:T(1,128)} %param.19) | copy-start | bytes 12292
  9.0 0.7 %copy-start.6 = (s32[1,1024]{1,0:T(1,128)S(1)}, s32[1,1024]{1,0:T(1,128)}, u32[]{:S(2)}) copy-start(s32[1,1024]{1,0:T(1,128)} %param.18) | copy-start | bytes 12292
  10.9 7.5 %collective-permute-start = (f32[192,128]{1,0:T(8,128)S(1)}, f32[192,128]{1,0:T(8,128)S(1)}, u32[]{:S(2)}, u32[]{:S(2)}) collective-permute-start(f32[192,128]{1,0:T(8,128)S(1)} %get-tuple-element.40), channel_id=1, source_target_pairs={{0,1},{1,2},{2,3},{3,4},{4,5},{5,6},{6,7},{7,8},{8,9},{9,10},{10,1... | collective-permute-start | bytes 294920 | tf_op jit(solution)/shard_map/ppermute | solution.py:388
  11.0 7.4 %collective-permute-start.1 = (f32[192,128]{1,0:T(8,128)S(1)}, f32[192,128]{1,0:T(8,128)S(1)}, u32[]{:S(2)}, u32[]{:S(2)}) collective-permute-start(f32[192,128]{1,0:T(8,128)S(1)} %get-tuple-element.41), channel_id=1, source_target_pairs={{1,0},{2,1},{3,2},{4,3},{5,4},{6,5},{7,6},{8,7},{9,8},{10,9},{11,1... | collective-permute-start | bytes 294920 | tf_op jit(solution)/shard_map/ppermute | solution.py:388
  15.1 1.5 %copy-start = (bf16[2,6,16,16,128]{4,3,2,1,0:T(8,128)(2,1)S(1)}, bf16[2,6,16,16,128]{4,3,2,1,0:T(8,128)(2,1)}, u32[]{:S(2)}) copy-start(bf16[2,6,16,16,128]{4,3,2,1,0:T(8,128)(2,1)} %perturb.7) | copy-start | bytes 2359300
  15.1 1.5 %copy-start.1 = (f32[2,16,16,128]{3,2,1,0:T(8,128)S(1)}, f32[2,16,16,128]{3,2,1,0:T(8,128)}, u32[]{:S(2)}) copy-start(f32[2,16,16,128]{3,2,1,0:T(8,128)} %param.12) | copy-start | bytes 786436
  15.1 1.5 %copy-start.3 = (f32[2,16,128]{2,1,0:T(8,128)S(1)}, f32[2,16,128]{2,1,0:T(8,128)}, u32[]{:S(2)}) copy-start(f32[2,16,128]{2,1,0:T(8,128)} %param.16) | copy-start | bytes 49156
  18.3 1.8 %collective-permute-start.4 = (f32[8,6,16,128]{3,2,1,0:T(8,128)S(1)}, f32[8,6,16,128]{3,2,1,0:T(8,128)S(1)}, u32[]{:S(2)}, u32[]{:S(2)}) collective-permute-start(f32[8,6,16,128]{3,2,1,0:T(8,128)S(1)} %get-tuple-element.48), channel_id=1, source_target_pairs={{0,16},{16,0},{32,48},{48,32},{64,80},{80,64},{96,112},{112,96},{1... | collective-permute-start | bytes 1179656 | tf_op jit(solution)/shard_map/ppermute | solution.py:385
  20.2 8.5 %collective-permute-start.5 = (f32[192,128]{1,0:T(8,128)S(1)}, f32[192,128]{1,0:T(8,128)S(1)}, u32[]{:S(2)}, u32[]{:S(2)}) collective-permute-start(f32[192,128]{1,0:T(8,128)S(1)} %get-tuple-element.50), channel_id=1, source_target_pairs={{0,64},{16,80},{32,96},{48,112},{64,0},{80,16},{96,32},{112,48},{1... | collective-permute-start | bytes 294920 | tf_op jit(solution)/shard_map/ppermute | solution.py:385
  23.5 5.8 %collective-permute-start.6 = (f32[192,128]{1,0:T(8,128)S(1)}, f32[192,128]{1,0:T(8,128)S(1)}, u32[]{:S(2)}, u32[]{:S(2)}) collective-permute-start(f32[192,128]{1,0:T(8,128)S(1)} %get-tuple-element.51), channel_id=1, source_target_pairs={{0,32},{16,48},{32,0},{48,16},{64,96},{80,112},{96,64},{112,80},{1... | collective-permute-start | bytes 294920 | tf_op jit(solution)/shard_map/ppermute | solution.py:385
  24.2 5.8 %collective-permute-start.7 = (f32[192,128]{1,0:T(8,128)S(1)}, f32[192,128]{1,0:T(8,128)S(1)}, u32[]{:S(2)}, u32[]{:S(2)}) collective-permute-start(f32[192,128]{1,0:T(8,128)S(1)} %get-tuple-element.52), channel_id=1, source_target_pairs={{0,96},{16,112},{32,64},{48,80},{64,32},{80,48},{96,0},{112,16},{1... | collective-permute-start | bytes 294920 | tf_op jit(solution)/shard_map/ppermute | solution.py:385
  24.5 6.7 %collective-permute-start.9 = (f32[192,128]{1,0:T(8,128)S(1)}, f32[192,128]{1,0:T(8,128)S(1)}, u32[]{:S(2)}, u32[]{:S(2)}) collective-permute-start(f32[192,128]{1,0:T(8,128)S(1)} %get-tuple-element.55), channel_id=1, source_target_pairs={{0,1},{1,2},{2,3},{3,4},{4,5},{5,6},{6,7},{7,8},{8,9},{9,10},{10,1... | collective-permute-start | bytes 294920 | tf_op jit(solution)/shard_map/ppermute | solution.py:388
  24.6 7.0 %collective-permute-start.10 = (f32[192,128]{1,0:T(8,128)S(1)}, f32[192,128]{1,0:T(8,128)S(1)}, u32[]{:S(2)}, u32[]{:S(2)}) collective-permute-start(f32[192,128]{1,0:T(8,128)S(1)} %get-tuple-element.56), channel_id=1, source_target_pairs={{1,0},{2,1},{3,2},{4,3},{5,4},{6,5},{7,6},{8,7},{9,8},{10,9},{11,1... | collective-permute-start | bytes 294920 | tf_op jit(solution)/shard_map/ppermute | solution.py:388
  30.0 6.4 %collective-permute-start.8 = (f32[192,128]{1,0:T(8,128)S(1)}, f32[192,128]{1,0:T(8,128)S(1)}, u32[]{:S(2)}, u32[]{:S(2)}) collective-permute-start(f32[192,128]{1,0:T(8,128)S(1)} %add_add_fusion.mine), channel_id=1, source_target_pairs={{0,128},{16,144},{32,160},{48,176},{64,192},{80,208},{96,224},{112... | collective-permute-start | bytes 294920 | tf_op jit(solution)/shard_map/ppermute | solution.py:385
  36.4 6.3 %collective-permute-start.14 = (f32[192,128]{1,0:T(8,128)S(1)}, f32[192,128]{1,0:T(8,128)S(1)}, u32[]{:S(2)}, u32[]{:S(2)}) collective-permute-start(f32[192,128]{1,0:T(8,128)S(1)} %gradient.1.g0.grad), channel_id=1, source_target_pairs={{0,64},{16,80},{32,96},{48,112},{64,0},{80,16},{96,32},{112,48},{1... | collective-permute-start | bytes 294920 | tf_op jit(solution)/shard_map/ppermute | solution.py:385
  38.8 4.7 %collective-permute-start.13 = (f32[192,128]{1,0:T(8,128)S(1)}, f32[192,128]{1,0:T(8,128)S(1)}, u32[]{:S(2)}, u32[]{:S(2)}) collective-permute-start(f32[192,128]{1,0:T(8,128)S(1)} %gradient.1.g0.grad), channel_id=1, source_target_pairs={{0,32},{16,48},{32,0},{48,16},{64,96},{80,112},{96,64},{112,80},{1... | collective-permute-start | bytes 294920 | tf_op jit(solution)/shard_map/ppermute | solution.py:385
  39.5 5.8 %collective-permute-start.12 = (f32[192,128]{1,0:T(8,128)S(1)}, f32[192,128]{1,0:T(8,128)S(1)}, u32[]{:S(2)}, u32[]{:S(2)}) collective-permute-start(f32[192,128]{1,0:T(8,128)S(1)} %gradient.1.g0.grad), channel_id=1, source_target_pairs={{0,96},{16,112},{32,64},{48,80},{64,32},{80,48},{96,0},{112,16},{1... | collective-permute-start | bytes 294920 | tf_op jit(solution)/shard_map/ppermute | solution.py:385
  40.6 4.7 %collective-permute-start.11 = (f32[192,128]{1,0:T(8,128)S(1)}, f32[192,128]{1,0:T(8,128)S(1)}, u32[]{:S(2)}, u32[]{:S(2)}) collective-permute-start(f32[192,128]{1,0:T(8,128)S(1)} %gradient.1.g0.grad), channel_id=1, source_target_pairs={{0,16},{16,0},{32,48},{48,32},{64,80},{80,64},{96,112},{112,96},{1... | collective-permute-start | bytes 294920 | tf_op jit(solution)/shard_map/ppermute | solution.py:385
  45.5 4.3 %collective-permute-start.15 = (f32[576,128]{1,0:T(8,128)S(1)}, f32[576,128]{1,0:T(8,128)S(1)}, u32[]{:S(2)}, u32[]{:S(2)}) collective-permute-start(f32[576,128]{1,0:T(8,128)S(1)} %get-tuple-element.60), channel_id=1, source_target_pairs={{0,16},{16,0},{32,48},{48,32},{64,80},{80,64},{96,112},{112,96},{1... | collective-permute-start | bytes 884744 | tf_op jit(solution)/shard_map/ppermute | solution.py:385
  45.6 8.6 %collective-permute-start.18 = (f32[264,128]{1,0:T(8,128)S(1)}, f32[264,128]{1,0:T(8,128)S(1)}, u32[]{:S(2)}, u32[]{:S(2)}) collective-permute-start(f32[264,128]{1,0:T(8,128)S(1)} %get-tuple-element.64), channel_id=1, source_target_pairs={{0,1},{1,2},{2,3},{3,4},{4,5},{5,6},{6,7},{7,8},{8,9},{9,10},{10,1... | collective-permute-start | bytes 405512 | tf_op jit(solution)/shard_map/ppermute | solution.py:388
  45.7 11.5 %collective-permute-start.19 = (f32[264,128]{1,0:T(8,128)S(1)}, f32[264,128]{1,0:T(8,128)S(1)}, u32[]{:S(2)}, u32[]{:S(2)}) collective-permute-start(f32[264,128]{1,0:T(8,128)S(1)} %get-tuple-element.65), channel_id=1, source_target_pairs={{1,0},{2,1},{3,2},{4,3},{5,4},{6,5},{7,6},{8,7},{9,8},{10,9},{11,1... | collective-permute-start | bytes 405512 | tf_op jit(solution)/shard_map/ppermute | solution.py:388
  49.8 7.4 %copy-start.4 = (f32[6,1,16,128]{3,2,1,0:T(8,128)S(1)}, f32[6,1,16,128]{3,2,1,0:T(8,128)}, u32[]{:S(2)}) copy-start(f32[6,1,16,128]{3,2,1,0:T(8,128)} %param.15) | copy-start | bytes 147460
  49.9 10.0 %collective-permute-start.16 = (f32[192,128]{1,0:T(8,128)S(1)}, f32[192,128]{1,0:T(8,128)S(1)}, u32[]{:S(2)}, u32[]{:S(2)}) collective-permute-start(f32[192,128]{1,0:T(8,128)S(1)} %get-tuple-element.61), channel_id=1, source_target_pairs={{0,1},{1,2},{2,3},{3,4},{4,5},{5,6},{6,7},{7,8},{8,9},{9,10},{10,1... | collective-permute-start | bytes 294920 | tf_op jit(solution)/shard_map/ppermute | solution.py:388
  50.0 9.9 %collective-permute-start.17 = (f32[192,128]{1,0:T(8,128)S(1)}, f32[192,128]{1,0:T(8,128)S(1)}, u32[]{:S(2)}, u32[]{:S(2)}) collective-permute-start(f32[192,128]{1,0:T(8,128)S(1)} %get-tuple-element.62), channel_id=1, source_target_pairs={{1,0},{2,1},{3,2},{4,3},{5,4},{6,5},{7,6},{8,7},{9,8},{10,9},{11,1... | collective-permute-start | bytes 294920 | tf_op jit(solution)/shard_map/ppermute | solution.py:388
  57.2 1.1 %copy-start.2 = (f32[2,16,16,128]{3,2,1,0:T(8,128)S(1)}, f32[2,16,16,128]{3,2,1,0:T(8,128)}, u32[]{:S(2)}) copy-start(f32[2,16,16,128]{3,2,1,0:T(8,128)} %param.13) | copy-start | bytes 786436

commit v6 on v4

--- a/solution.py
+++ b/solution.py
@@ -258,66 +258,82 @@
             sums[pl.ds(block * 2 + r, 24, stride=ROWS), :] = total[:, r * LANES : (r + 1) * LANES]
 
 
-def gradient_body(mine, other, static, sums, grad, forward, backward):
-    x, _, _ = place()
-    total = mine[...] + other[...] + static[...]
-    grad[...] = sums[0:192, :] * total - sums[192:384, :]
-    pack_rows(lambda row: grad[pl.ds(x * 96 + row, VARS, stride=ROWS), :], VARS, forward, backward)
-
-
 def project(g, k, parity, perturb, middle):
     _, y, _ = place()
     for j in range(2):
-        s = (y ^ k) + 4 * j
-        level = 2 * s + parity
+        level = 2 * ((y ^ k) + 4 * j) + parity
         fields = [g[j * 96 + v * 16 : j * 96 + v * 16 + 16, :] for v in range(VARS)]
         for m in range(2):
             total = perturb[m, 0, level].astype(jnp.float32) * fields[0]
             for v in range(1, VARS):
                 total = total + perturb[m, v, level].astype(jnp.float32) * fields[v]
-            middle[pl.ds(pl.multiple_of((m * HALF + s) * 16, 16), 16), :] = total
-
-
-def project_own_body(g0, g2, g1, g3, perturb, low, high, forward, backward, middle, rest, low_out, high_out):
-    _, _, c = place()
+            at = (k * 4 + m * 2 + j) * 16
+            middle[at : at + 16, :] = total
+
+
+def gradient_body(mine, other, static, sums, perturb, grad, forward, backward, middle):
+    x, _, c = place()
+    total = mine[...] + other[...] + static[...]
+    grad[...] = sums[0:192, :] * total - sums[192:384, :]
+    project(grad, 0, c, perturb, middle)
+    pack_rows(lambda row: grad[pl.ds(x * 96 + row, VARS, stride=ROWS), :], VARS, forward, backward)
+    pack_rows(lambda row: middle[pl.ds(row, 4, stride=ROWS), :], 4, forward, backward, 72)
+
+
+def project_own_body(g0, g3, g1, g2, perturb, start, low, high, forward, backward, middle, rest, low_out, high_out):
+    c = lax.axis_index("mem") % 2
     low_out[...] = low[...]
     high_out[...] = high[...]
-    for k, g in enumerate((g0, g1, g2, g3)):
+    middle[0:64, :] = start[...]
+    rest[0:192, :] = g0[...]
+    for k, g in ((1, g1), (2, g2), (3, g3)):
         project(g, k, c, perturb, middle)
-        if k > 0:
-            rest[(k - 1) * 192 : k * 192, :] = g[...]
+        rest[k * 192 : k * 192 + 192, :] = g[...]
+    pack_rows(lambda row: middle[pl.ds(64 + row, 12, stride=ROWS), :], 12, forward, backward)
+
+
+def project_other_body(rest, perturb, forward, backward, middle):
+    c = lax.axis_index("mem") % 2
+    for k in range(4):
+        project(rest.at[k * 192 : k * 192 + 192], k, 1 - c, perturb, middle)
     pack_rows(lambda row: middle[pl.ds(row, 16, stride=ROWS), :], 16, forward, backward)
 
 
-def project_other_body(g0, rest, perturb, forward, backward, middle):
-    _, _, c = place()
-    project(g0, 0, 1 - c, perturb, middle)
-    for k in range(1, 4):
-        project(rest.at[(k - 1) * 192 : k * 192], k, 1 - c, perturb, middle)
-    pack_rows(lambda row: middle[pl.ds(row, 16, stride=ROWS), :], 16, forward, backward)
-
-
 def update_alpha(parity, out, alpha, mom, stage0, stage1):
-    for m in range(2):
-        for s in range(HALF):
-            at = pl.ds(pl.multiple_of(m * 256 + (2 * s + parity) * 16, 16), 16)
-            here = slice((m * HALF + s) * 16, (m * HALF + s) * 16 + 16)
-            old = alpha[at, :]
-            moved = momentum_rate * mom[at, :] + (old + out[here, :])
-            stage1[here, :] = moved
-            stage0[here, :] = old - step_rate * moved
-
-
-def third_body(low, high, middle, coefs, alpha, mom, stage0, stage1, buf0, buf1, out):
+    _, y, _ = place()
+    for k in range(4):
+        for m in range(2):
+            for j in range(2):
+                t = (k * 4 + m * 2 + j) * 16
+                s = (y ^ k) + 4 * j
+                at = pl.ds(pl.multiple_of(m * 256 + (2 * s + parity) * 16, 16), 16)
+                here = pl.ds(pl.multiple_of((m * HALF + s) * 16, 16), 16)
+                old = alpha[at, :]
+                moved = momentum_rate * mom[at, :] + (old + out[t : t + 16, :])
+                stage1[here, :] = moved
+                stage0[here, :] = old - step_rate * moved
+
+
+def third_body(
+    early_low, early_high, low, high, middle, coefs, alpha, mom, after, stage0, stage1, buf0, buf1, out,
+):
+    for row in range(SPAN):
+        at = row * 16
+        if STEPS <= row < STEPS + ROWS:
+            buf0[at : at + 16, :] = middle[pl.ds(row - STEPS, 16, stride=ROWS), :]
+        else:
+            near, far, k = (early_low, low, row) if row < STEPS else (early_high, high, row - STEPS - ROWS)
+            buf0[at : at + 4, :] = near[72 + k * 4 : 76 + k * 4, :]
+            buf0[at + 4 : at + 16, :] = far[k * 12 : k * 12 + 12, :]
+
     def emit(row, value):
         out[pl.ds(row, 16, stride=ROWS), :] = value
 
-    load = halo_loader(low, high, lambda row: middle[pl.ds(row, 16, stride=ROWS), :], 16)
-    diffuse(load, 16, 16, coefs, (buf0, buf1), emit)
+    diffuse(lambda row: buf0[row * 16 : row * 16 + 16, :], 16, 16, coefs, (buf0, buf1), emit)
     update_alpha(lax.axis_index("mem") % 2, out, alpha, mom, stage0, stage1)
 
 
-def static_last_body(low, high, grad, coefs, field, static_mom, new_static, new_static_mom, buf0, buf1, out):
+def static_last_body(low, high, grad, coefs, field, static_mom, after, new_static, new_static_mom, buf0, buf1, out):
     x, _, _ = place()
     load = halo_loader(low, high, lambda row: grad[pl.ds(x * 96 + row, VARS, stride=ROWS), :], VARS)
     for row in range(SPAN):
@@ -450,29 +466,30 @@
         [raw] + bufs16 + [f32(256, LANES)],
         flops=BUSY,
     )(c_low, c_high, field)
-    narrow = shape(72, LANES)
-    grad, g_f, g_b = call(gradient_body, "gradient", [VM] * 4, [quarter, narrow, narrow])(mine, other, static, sums)
+    early = shape(120, LANES)
+    grad, g_f, g_b, start = call(
+        gradient_body, "gradient", [VM] * 5, [quarter, early, early, shape(64, LANES)]
+    )(mine, other, static, sums, perturb)
     g2, g1, g3 = swap(grad, 4), swap(grad, 2), swap(grad, 6)
     g_low, g_high = halo(g_f, g_b)
-    p0 = swap(grad, 1)
-    gs = [grad, g2, g1, g3]
+    far = shape(144, LANES)
     p_f, p_b, p_m, rest, g_low, g_high = call(
         project_own_body,
         "project_own",
-        [VM] * 7,
-        [quarter, quarter, half, shape(576, LANES), narrow, narrow],
-    )(*gs, perturb, g_low, g_high)
+        [VM] * 8,
+        [far, far, half, shape(768, LANES), early, early],
+    )(grad, g3, g1, g2, perturb, start, g_low, g_high)
     p_low, p_high = halo(p_f, p_b)
     rest = swap(rest, 1)
-    q_f, q_b, q_m = call(project_other_body, "project_other", [VM] * 3, [quarter, quarter, half])(p0, rest, perturb)
+    q_f, q_b, q_m = call(project_other_body, "project_other", [VM] * 2, [quarter, quarter, half])(rest, perturb)
     q_low, q_high = halo(q_f, q_b)
     whole = shape(2, HALF, 2, ROWS, LANES)
     work = bufs16 + [f32(256, LANES)]
-    static_ready = call(static_last_body, "static_last", [VM] * 6, [shape(96, LANES)] * 2, work, flops=BUSY)(
-        g_low, g_high, grad, static_k, field, static_mom.reshape(96, LANES)
-    )
-    ready = call(third_body, "third", [VM] * 6, [half, half], work, flops=BUSY)(
-        p_low, p_high, p_m, loc_k, alpha2, mom2
+    static_ready = call(static_last_body, "static_last", [VM] * 7, [shape(96, LANES)] * 2, work, flops=BUSY)(
+        g_low, g_high, grad, static_k, field, static_mom.reshape(96, LANES), q_m
+    )
+    ready = call(third_body, "third", [VM] * 9, [half, half], work, flops=BUSY)(
+        g_low, g_high, p_low, p_high, p_m, loc_k, alpha2, mom2, q_m
     )
     new_alpha, new_alpha_mom, new_static, new_static_mom = call(
         fourth_body,

time: 63.4 us -> 62 us (0.978)
  starting transfers between devices: 28.2 us -> 26.2 us
  waiting for transfers between devices: 18.7 us -> 19.6 us
    ppermute x6, starting transfers between devices: 15 us -> 11.7 us  [halo(): lax.ppermute(forward, 'tile', up)]
    ppermute x6, starting transfers between devices: 3.22 us -> 4.46 us  [halo(): lax.ppermute(backward, 'tile', down)]
    ppermute x10 -> x9, waiting for transfers between devices: 5.29 us -> 6.19 us  [swap(): return lax.ppermute(value, 'mem', [(i, i ^ bits) for i in range(members)])]
    ppermute x10 -> x9, starting transfers between devices: 9.99 us -> 10.1 us  [swap(): return lax.ppermute(value, 'mem', [(i, i ^ bits) for i in range(members)])]
  transfers between devices with their start and end apart: 22 -> 21, of which waited for: 9 -> 9; matrix products, arithmetic and copies ran while one was open for 0% -> 0% of each run, Pallas kernels for 16% -> 16%
where the time goes in v6:
time: 62 us; the launch traced here: 61.8 us
  starting transfers between devices  26.2 us (42%)
  waiting for transfers between devices  19.6 us (32%)
  Pallas kernels  14.3 us (23%)
  between operations  1.02 us (2%)
  local copies, waits for them, and re-layouts  0.72 us (1%)
    ppermute x6, starting transfers between devices, halo(): lax.ppermute(forward, 'tile', up)  11.7 us
    ppermute x6, waiting for transfers between devices, halo(): lax.ppermute(backward, 'tile', down)  11.1 us
    ppermute x9, starting transfers between devices, swap(): return lax.ppermute(value, 'mem', [(i, i ^ bits) for i in range(members)])  10.1 us
    ppermute x9, waiting for transfers between devices, swap(): return lax.ppermute(value, 'mem', [(i, i ^ bits) for i in range(members)])  6.19 us
    ppermute x6, starting transfers between devices, halo(): lax.ppermute(backward, 'tile', down)  4.46 us
    pallas_call x1, Pallas kernels, local(): call(fourth_body, 'fourth', [VM] * 10, [whole, whole, shape(96, LANES), s...  2.27 us
    ppermute x6, waiting for transfers between devices, halo(): lax.ppermute(forward, 'tile', up)  2.23 us
    pallas_call x1, Pallas kernels, local(): call(pack_body, 'pack', [HBM] * 2, [shape(216, LANES)] * 2, [f32(512, LAN...  1.73 us
  transfers between devices with their start and end apart: 21, of which 9 were waited for; matrix products, arithmetic and copies ran while one was open for 0% of the time, Pallas kernels for 16%

profile of v6, /device:TPU:102, one launch (start us, length us, event | category | flops | bytes accessed | tf_op | source)
XLA Modules:
  0.0 61.8 jit_solution(982983950885674437)
XLA Ops:
  0.6 0.0 copy-start.5
  0.6 1.7 %pack.1 = (f32[216,128]{1,0:T(8,128)}, f32[216,128]{1,0:T(8,128)}) custom-call(f32[512,128]{1,0:T(8,128)} %bitcast.17, f32[32,128]{1,0:T(8,128)} %bitcast.25), custom_call_target="tpu_custom_call" | custom-call | flops 1000000 | bytes 1000000 | tf_op jit(solution)/shard_map/pack/pallas_call | solution.py:416
  2.4 3.5 %collective-permute-start.2 = (f32[216,128]{1,0:T(8,128)}, f32[216,128]{1,0:T(8,128)S(1)}, u32[]{:S(2)}, u32[]{:S(2)}) collective-permute-start(f32[216,128]{1,0:T(8,128)} %get-tuple-element.47), channel_id=1, source_target_pairs={{0,1},{1,2},{2,3},{3,4},{4,5},{5,6},{6,7},{7,8},{8,9},{9,10},{10,1... | collective-permute-start | bytes 331784 | tf_op jit(solution)/shard_map/ppermute | solution.py:406
  5.9 0.0 collective-permute-start.3
  5.9 0.0 copy-done.5
  5.9 0.7 %copy-done.7 = s32[1,1024]{1,0:T(1,128)S(1)} copy-done((s32[1,1024]{1,0:T(1,128)S(1)}, s32[1,1024]{1,0:T(1,128)}, u32[]{:S(2)}) %copy-start.7) | copy-done | bytes 4120
  6.5 0.0 copy-done.6
  6.6 1.2 %fetch.1 = (f32[192,128]{1,0:T(8,128)S(1)}, f32[192,128]{1,0:T(8,128)S(1)}, f32[192,128]{1,0:T(8,128)S(1)}, f32[192,128]{1,0:T(8,128)S(1)}, f32[256,128]{1,0:T(8...) custom-call(f32[512,128]{1,0:T(8,128)} %bitcast.18, s32[8,128]{1,0:T(8,128)S(1)} %bitcast.29, ...), custom_call_target="tpu_custom_call" | custom-call | flops 5000000000 | bytes 1000000 | tf_op jit(solution)/shard_map/fetch/pallas_call | solution.py:426
  7.7 4.2 %collective-permute-start = (f32[192,128]{1,0:T(8,128)S(1)}, f32[192,128]{1,0:T(8,128)S(1)}, u32[]{:S(2)}, u32[]{:S(2)}) collective-permute-start(f32[192,128]{1,0:T(8,128)S(1)} %get-tuple-element.45), channel_id=1, source_target_pairs={{0,1},{1,2},{2,3},{3,4},{4,5},{5,6},{6,7},{7,8},{8,9},{9,10},{10,1... | collective-permute-start | bytes 294920 | tf_op jit(solution)/shard_map/ppermute | solution.py:406
  12.0 0.0 collective-permute-start.1
  12.0 1.4 %prepare.1.ready.sums = f32[384,128]{1,0:T(8,128)S(1)} custom-call(s32[8,128]{1,0:T(8,128)S(1)} %get-tuple-element.49.cell, s32[8,128]{1,0:T(8,128)S(1)} %get-tuple-element.50.mask, f32[192,128]{1,0:T(8,128)S(1)} %get-tuple-element.51.held), custom_call_target="tpu_custom_call" | custom-call | flops 5000000000 | bytes 1000000 | tf_op jit(solution)/shard_map/prepare/pallas_call | solution.py:444
  13.4 0.0 collective-permute-done.2.low
  13.4 0.0 collective-permute-done.3.high
  13.4 0.0 copy-done
  13.4 0.0 copy-done.1
  13.4 0.0 copy-done.3
  13.4 1.6 %first.1 = (f32[8,6,16,128]{3,2,1,0:T(8,128)S(1)}, f32[200,128]{1,0:T(8,128)S(1)}) custom-call(f32[512,128]{1,0:T(8,128)S(1)} %bitcast.19, f32[216,128]{1,0:T(8,128)S(1)} %collective-permute-done.2.low, f32[216,128]{1,0:T(8,128)S(1)} %collective-permute-done.3.high, f32[32,128]{1,0:T(8,128)S(1)} %bitcast.26, bf16[2,6,16,16,128]{4,3,2,1,0:T(8,128)(2,1)S(1)} %copy-done, ...), custom_call_target="tpu_custom_call" | custom-call | flops 5000000000 | bytes 1000000 | tf_op jit(solution)/shard_map/first/pallas_call | solution.py:446
  15.0 0.1 collective-permute-start.4
  15.1 0.0 collective-permute-done.low
  15.2 3.5 %collective-permute-done.1.high = f32[192,128]{1,0:T(8,128)S(1)} collective-permute-done((f32[192,128]{1,0:T(8,128)S(1)}, f32[192,128]{1,0:T(8,128)S(1)}, u32[]{:S(2)}, u32[]{:S(2)}) %collective-permute-start.1) | collective-permute-done | bytes 98336 | tf_op jit(solution)/shard_map/ppermute | solution.py:406
  18.7 1.5 %second.1.local = f32[256,128]{1,0:T(8,128)S(1)} custom-call(f32[512,128]{1,0:T(8,128)S(1)} %bitcast.20, f32[192,128]{1,0:T(8,128)S(1)} %collective-permute-done.low, f32[192,128]{1,0:T(8,128)S(1)} %collective-permute-done.1.high, f32[200,128]{1,0:T(8,128)S(1)} %get-tuple-element.52.coefs), custom_call_target="tpu_custom_call" | custom-call | flops 5000000000 | bytes 1000000 | tf_op jit(solution)/shard_map/second/pallas_call | solution.py:455
  20.1 0.0 collective-permute-done.4.received
  20.2 0.1 sum.1
  20.3 3.3 %collective-permute-start.5 = (f32[192,128]{1,0:T(8,128)S(1)}, f32[192,128]{1,0:T(8,128)S(1)}, u32[]{:S(2)}, u32[]{:S(2)}) collective-permute-start(f32[192,128]{1,0:T(8,128)S(1)} %get-tuple-element.55), channel_id=1, source_target_pairs={{0,64},{16,80},{32,96},{48,112},{64,0},{80,16},{96,32},{112,48},{1... | collective-permute-start | bytes 294920 | tf_op jit(solution)/shard_map/ppermute | solution.py:403
  23.6 0.7 %collective-permute-start.6 = (f32[192,128]{1,0:T(8,128)S(1)}, f32[192,128]{1,0:T(8,128)S(1)}, u32[]{:S(2)}, u32[]{:S(2)}) collective-permute-start(f32[192,128]{1,0:T(8,128)S(1)} %get-tuple-element.56), channel_id=1, source_target_pairs={{0,32},{16,48},{32,0},{48,16},{64,96},{80,112},{96,64},{112,80},{1... | collective-permute-start | bytes 294920 | tf_op jit(solution)/shard_map/ppermute | solution.py:403
  24.2 0.4 collective-permute-start.7
  24.6 0.8 %collective-permute-start.9 = (f32[192,128]{1,0:T(8,128)S(1)}, f32[192,128]{1,0:T(8,128)S(1)}, u32[]{:S(2)}, u32[]{:S(2)}) collective-permute-start(f32[192,128]{1,0:T(8,128)S(1)} %get-tuple-element.60), channel_id=1, source_target_pairs={{0,1},{1,2},{2,3},{3,4},{4,5},{5,6},{6,7},{7,8},{8,9},{9,10},{10,1... | collective-permute-start | bytes 294920 | tf_op jit(solution)/shard_map/ppermute | solution.py:406
  25.4 1.2 %collective-permute-start.10 = (f32[192,128]{1,0:T(8,128)S(1)}, f32[192,128]{1,0:T(8,128)S(1)}, u32[]{:S(2)}, u32[]{:S(2)}) collective-permute-start(f32[192,128]{1,0:T(8,128)S(1)} %get-tuple-element.61), channel_id=1, source_target_pairs={{1,0},{2,1},{3,2},{4,3},{5,4},{6,5},{7,6},{8,7},{9,8},{10,9},{11,1... | collective-permute-start | bytes 294920 | tf_op jit(solution)/shard_map/ppermute | solution.py:406
  26.6 0.0 collective-permute-done.5
  26.6 1.5 %collective-permute-done.6 = f32[192,128]{1,0:T(8,128)S(1)} collective-permute-done((f32[192,128]{1,0:T(8,128)S(1)}, f32[192,128]{1,0:T(8,128)S(1)}, u32[]{:S(2)}, u32[]{:S(2)}) %collective-permute-start.6) | collective-permute-done | bytes 98336 | tf_op jit(solution)/shard_map/ppermute | solution.py:403
  28.2 1.9 %collective-permute-done.7 = f32[192,128]{1,0:T(8,128)S(1)} collective-permute-done((f32[192,128]{1,0:T(8,128)S(1)}, f32[192,128]{1,0:T(8,128)S(1)}, u32[]{:S(2)}, u32[]{:S(2)}) %collective-permute-start.7) | collective-permute-done | bytes 98336 | tf_op jit(solution)/shard_map/ppermute | solution.py:403
  30.1 1.4 %collective-permute-start.8 = (f32[192,128]{1,0:T(8,128)S(1)}, f32[192,128]{1,0:T(8,128)S(1)}, u32[]{:S(2)}, u32[]{:S(2)}) collective-permute-start(f32[192,128]{1,0:T(8,128)S(1)} %add_add_fusion.mine), channel_id=1, source_target_pairs={{0,128},{16,144},{32,160},{48,176},{64,192},{80,208},{96,224},{112... | collective-permute-start | bytes 294920 | tf_op jit(solution)/shard_map/ppermute | solution.py:403
  31.5 0.0 collective-permute-done.9.low
  31.5 0.7 %collective-permute-done.10.high = f32[192,128]{1,0:T(8,128)S(1)} collective-permute-done((f32[192,128]{1,0:T(8,128)S(1)}, f32[192,128]{1,0:T(8,128)S(1)}, u32[]{:S(2)}, u32[]{:S(2)}) %collective-permute-start.10) | collective-permute-done | bytes 98336 | tf_op jit(solution)/shard_map/ppermute | solution.py:406
  32.1 1.6 %static_first.1 = (f32[192,128]{1,0:T(8,128)S(1)}, f32[200,128]{1,0:T(8,128)S(1)}) custom-call(f32[192,128]{1,0:T(8,128)S(1)} %collective-permute-done.9.low, f32[192,128]{1,0:T(8,128)S(1)} %collective-permute-done.10.high, f32[256,128]{1,0:T(8,128)S(1)} %get-tuple-element.62.field), custom_call_target="tpu_custom_call" | custom-call | flops 5000000000 | bytes 1000000 | tf_op jit(solution)/shard_map/static_first/pallas_call | solution.py:461
  33.7 2.8 %collective-permute-done.8.other = f32[192,128]{1,0:T(8,128)S(1)} collective-permute-done((f32[192,128]{1,0:T(8,128)S(1)}, f32[192,128]{1,0:T(8,128)S(1)}, u32[]{:S(2)}, u32[]{:S(2)}) %collective-permute-start.8) | collective-permute-done | bytes 98336 | tf_op jit(solution)/shard_map/ppermute | solution.py:403
  36.5 0.1 gradient.1
  36.6 0.8 %collective-permute-start.13 = (f32[192,128]{1,0:T(8,128)S(1)}, f32[192,128]{1,0:T(8,128)S(1)}, u32[]{:S(2)}, u32[]{:S(2)}) collective-permute-start(f32[192,128]{1,0:T(8,128)S(1)} %get-tuple-element.64.g0.grad), channel_id=1, source_target_pairs={{0,64},{16,80},{32,96},{48,112},{64,0},{80,16},{96,32},{112,48},{1... | collective-permute-start | bytes 294920 | tf_op jit(solution)/shard_map/ppermute | solution.py:403
  37.3 0.7 %collective-permute-start.12 = (f32[192,128]{1,0:T(8,128)S(1)}, f32[192,128]{1,0:T(8,128)S(1)}, u32[]{:S(2)}, u32[]{:S(2)}) collective-permute-start(f32[192,128]{1,0:T(8,128)S(1)} %get-tuple-element.64.g0.grad), channel_id=1, source_target_pairs={{0,32},{16,48},{32,0},{48,16},{64,96},{80,112},{96,64},{112,80},{1... | collective-permute-start | bytes 294920 | tf_op jit(solution)/shard_map/ppermute | solution.py:403
  38.0 2.7 %collective-permute-start.11 = (f32[192,128]{1,0:T(8,128)S(1)}, f32[192,128]{1,0:T(8,128)S(1)}, u32[]{:S(2)}, u32[]{:S(2)}) collective-permute-start(f32[192,128]{1,0:T(8,128)S(1)} %get-tuple-element.64.g0.grad), channel_id=1, source_target_pairs={{0,96},{16,112},{32,64},{48,80},{64,32},{80,48},{96,0},{112,16},{1... | collective-permute-start | bytes 294920 | tf_op jit(solution)/shard_map/ppermute | solution.py:403
  40.7 0.8 %collective-permute-start.14 = (f32[120,128]{1,0:T(8,128)S(1)}, f32[120,128]{1,0:T(8,128)S(1)}, u32[]{:S(2)}, u32[]{:S(2)}) collective-permute-start(f32[120,128]{1,0:T(8,128)S(1)} %get-tuple-element.66), channel_id=1, source_target_pairs={{0,1},{1,2},{2,3},{3,4},{4,5},{5,6},{6,7},{7,8},{8,9},{9,10},{10,1... | collective-permute-start | bytes 184328 | tf_op jit(solution)/shard_map/ppermute | solution.py:406
  41.5 1.2 %collective-permute-start.15 = (f32[120,128]{1,0:T(8,128)S(1)}, f32[120,128]{1,0:T(8,128)S(1)}, u32[]{:S(2)}, u32[]{:S(2)}) collective-permute-start(f32[120,128]{1,0:T(8,128)S(1)} %get-tuple-element.67), channel_id=1, source_target_pairs={{1,0},{2,1},{3,2},{4,3},{5,4},{6,5},{7,6},{8,7},{9,8},{10,9},{11,1... | collective-permute-start | bytes 184328 | tf_op jit(solution)/shard_map/ppermute | solution.py:406
  42.8 2.2 %collective-permute-done.14.low = f32[120,128]{1,0:T(8,128)S(1)} collective-permute-done((f32[120,128]{1,0:T(8,128)S(1)}, f32[120,128]{1,0:T(8,128)S(1)}, u32[]{:S(2)}, u32[]{:S(2)}) %collective-permute-start.14) | collective-permute-done | bytes 61472 | tf_op jit(solution)/shard_map/ppermute | solution.py:406
  45.0 2.9 %collective-permute-done.15.high = f32[120,128]{1,0:T(8,128)S(1)} collective-permute-done((f32[120,128]{1,0:T(8,128)S(1)}, f32[120,128]{1,0:T(8,128)S(1)}, u32[]{:S(2)}, u32[]{:S(2)}) %collective-permute-start.15) | collective-permute-done | bytes 61472 | tf_op jit(solution)/shard_map/ppermute | solution.py:406
  47.9 0.0 collective-permute-done.13.g2
  47.9 0.0 collective-permute-done.12.g1
  47.9 0.0 collective-permute-done.11.g3
  47.9 0.1 project_own.1
  48.0 0.1 collective-permute-start.16
  48.1 0.1 collective-permute-start.19
  48.2 0.0 copy-start.4
  48.2 2.0 %collective-permute-start.20 = (f32[144,128]{1,0:T(8,128)S(1)}, f32[144,128]{1,0:T(8,128)S(1)}, u32[]{:S(2)}, u32[]{:S(2)}) collective-permute-start(f32[144,128]{1,0:T(8,128)S(1)} %get-tuple-element.75), channel_id=1, source_target_pairs={{1,0},{2,1},{3,2},{4,3},{5,4},{6,5},{7,6},{8,7},{9,8},{10,9},{11,1... | collective-permute-start | bytes 221192 | tf_op jit(solution)/shard_map/ppermute | solution.py:406
  50.2 0.0 collective-permute-done.16.rest
  50.2 0.1 project_other.1
  50.4 2.3 %collective-permute-start.17 = (f32[192,128]{1,0:T(8,128)S(1)}, f32[192,128]{1,0:T(8,128)S(1)}, u32[]{:S(2)}, u32[]{:S(2)}) collective-permute-start(f32[192,128]{1,0:T(8,128)S(1)} %get-tuple-element.69), channel_id=1, source_target_pairs={{0,1},{1,2},{2,3},{3,4},{4,5},{5,6},{6,7},{7,8},{8,9},{9,10},{10,1... | collective-permute-start | bytes 294920 | tf_op jit(solution)/shard_map/ppermute | solution.py:406
  52.6 0.0 collective-permute-start.18
  52.6 0.0 copy-done.4
  52.6 1.1 %static_last.1 = (f32[96,128]{1,0:T(8,128)S(1)}, f32[96,128]{1,0:T(8,128)S(1)}) custom-call(f32[120,128]{1,0:T(8,128)S(1)} %get-tuple-element.72.early_low.low, f32[120,128]{1,0:T(8,128)S(1)} %get-tuple-element.73.early_high.high, f32[192,128]{1,0:T(8,128)S(1)} %get-tuple-element.64.g0.grad, f32[200,128]{1,0:T(8,128)S(1)} %get-tuple-element.79.coefs, ...), custom_call_target="tpu_custom_call" | custom-call | flops 5000000000 | bytes 1000000 | tf_op jit(solution)/shard_map/static_last/pallas_call | solution.py:488
  53.8 0.0 collective-permute-done.19.low
  53.8 1.2 %collective-permute-done.20.high = f32[144,128]{1,0:T(8,128)S(1)} collective-permute-done((f32[144,128]{1,0:T(8,128)S(1)}, f32[144,128]{1,0:T(8,128)S(1)}, u32[]{:S(2)}, u32[]{:S(2)}) %collective-permute-start.20) | collective-permute-done | bytes 73760 | tf_op jit(solution)/shard_map/ppermute | solution.py:406
  55.0 1.5 %third.1 = (f32[256,128]{1,0:T(8,128)S(1)}, f32[256,128]{1,0:T(8,128)S(1)}) custom-call(f32[120,128]{1,0:T(8,128)S(1)} %get-tuple-element.72.early_low.low, f32[120,128]{1,0:T(8,128)S(1)} %get-tuple-element.73.early_high.high, f32[144,128]{1,0:T(8,128)S(1)} %collective-permute-done.19.low, f32[144,128]{1,0:T(8,128)S(1)} %collective-permute-done.20.high, ...), custom_call_target="tpu_custom_call" | custom-call | flops 5000000000 | bytes 1000000 | tf_op jit(solution)/shard_map/third/pallas_call | solution.py:491
  56.6 0.0 collective-permute-done.17.low
  56.6 2.8 %collective-permute-done.18.high = f32[192,128]{1,0:T(8,128)S(1)} collective-permute-done((f32[192,128]{1,0:T(8,128)S(1)}, f32[192,128]{1,0:T(8,128)S(1)}, u32[]{:S(2)}, u32[]{:S(2)}) %collective-permute-start.18) | collective-permute-done | bytes 98336 | tf_op jit(solution)/shard_map/ppermute | solution.py:406
  59.4 2.3 %fourth.1 = (f32[2,8,2,16,128]{4,3,2,1,0:T(8,128)}, f32[2,8,2,16,128]{4,3,2,1,0:T(8,128)}, f32[96,128]{1,0:T(8,128)}, f32[96,128]{1,0:T(8,128)}) custom-call(f32[192,128]{1,0:T(8,128)S(1)} %collective-permute-done.17.low, f32[192,128]{1,0:T(8,128)S(1)} %collective-permute-done.18.high, f32[256,128]{1,0:T(8,128)S(1)} %get-tuple-element.71.after.middle, ...), custom_call_target="tpu_custom_call" | custom-call | flops 1000000 | bytes 1000000 | tf_op jit(solution)/shard_map/fourth/pallas_call | solution.py:494
  (8 shorter events, 0.0 us)
Async XLA Ops:
  0.6 5.2 %copy-start.5 = (f32[2,16,128]{2,1,0:T(8,128)S(1)}, f32[2,16,128]{2,1,0:T(8,128)}, u32[]{:S(2)}) copy-start(f32[2,16,128]{2,1,0:T(8,128)} %param.17) | copy-start | bytes 49156
  2.4 11.0 %collective-permute-start.2 = (f32[216,128]{1,0:T(8,128)}, f32[216,128]{1,0:T(8,128)S(1)}, u32[]{:S(2)}, u32[]{:S(2)}) collective-permute-start(f32[216,128]{1,0:T(8,128)} %get-tuple-element.47), channel_id=1, source_target_pairs={{0,1},{1,2},{2,3},{3,4},{4,5},{5,6},{6,7},{7,8},{8,9},{9,10},{10,1... | collective-permute-start | bytes 331784 | tf_op jit(solution)/shard_map/ppermute | solution.py:406
  5.9 7.6 %collective-permute-start.3 = (f32[216,128]{1,0:T(8,128)}, f32[216,128]{1,0:T(8,128)S(1)}, u32[]{:S(2)}, u32[]{:S(2)}) collective-permute-start(f32[216,128]{1,0:T(8,128)} %get-tuple-element.48), channel_id=1, source_target_pairs={{1,0},{2,1},{3,2},{4,3},{5,4},{6,5},{7,6},{8,7},{9,8},{10,9},{11,1... | collective-permute-start | bytes 331784 | tf_op jit(solution)/shard_map/ppermute | solution.py:406
  5.9 0.7 %copy-start.7 = (s32[1,1024]{1,0:T(1,128)S(1)}, s32[1,1024]{1,0:T(1,128)}, u32[]{:S(2)}) copy-start(s32[1,1024]{1,0:T(1,128)} %param.19) | copy-start | bytes 12292
  5.9 0.7 %copy-start.6 = (s32[1,1024]{1,0:T(1,128)S(1)}, s32[1,1024]{1,0:T(1,128)}, u32[]{:S(2)}) copy-start(s32[1,1024]{1,0:T(1,128)} %param.18) | copy-start | bytes 12292
  7.7 7.4 %collective-permute-start = (f32[192,128]{1,0:T(8,128)S(1)}, f32[192,128]{1,0:T(8,128)S(1)}, u32[]{:S(2)}, u32[]{:S(2)}) collective-permute-start(f32[192,128]{1,0:T(8,128)S(1)} %get-tuple-element.45), channel_id=1, source_target_pairs={{0,1},{1,2},{2,3},{3,4},{4,5},{5,6},{6,7},{7,8},{8,9},{9,10},{10,1... | collective-permute-start | bytes 294920 | tf_op jit(solution)/shard_map/ppermute | solution.py:406
  12.0 6.7 %collective-permute-start.1 = (f32[192,128]{1,0:T(8,128)S(1)}, f32[192,128]{1,0:T(8,128)S(1)}, u32[]{:S(2)}, u32[]{:S(2)}) collective-permute-start(f32[192,128]{1,0:T(8,128)S(1)} %get-tuple-element.46), channel_id=1, source_target_pairs={{1,0},{2,1},{3,2},{4,3},{5,4},{6,5},{7,6},{8,7},{9,8},{10,9},{11,1... | collective-permute-start | bytes 294920 | tf_op jit(solution)/shard_map/ppermute | solution.py:406
  12.0 1.5 %copy-start = (bf16[2,6,16,16,128]{4,3,2,1,0:T(8,128)(2,1)S(1)}, bf16[2,6,16,16,128]{4,3,2,1,0:T(8,128)(2,1)}, u32[]{:S(2)}) copy-start(bf16[2,6,16,16,128]{4,3,2,1,0:T(8,128)(2,1)} %perturb.9) | copy-start | bytes 2359300
  12.0 1.5 %copy-start.1 = (f32[2,16,16,128]{3,2,1,0:T(8,128)S(1)}, f32[2,16,16,128]{3,2,1,0:T(8,128)}, u32[]{:S(2)}) copy-start(f32[2,16,16,128]{3,2,1,0:T(8,128)} %param.12) | copy-start | bytes 786436
  12.0 1.5 %copy-start.3 = (f32[2,16,128]{2,1,0:T(8,128)S(1)}, f32[2,16,128]{2,1,0:T(8,128)}, u32[]{:S(2)}) copy-start(f32[2,16,128]{2,1,0:T(8,128)} %param.16) | copy-start | bytes 49156
  15.0 5.1 %collective-permute-start.4 = (f32[8,6,16,128]{3,2,1,0:T(8,128)S(1)}, f32[8,6,16,128]{3,2,1,0:T(8,128)S(1)}, u32[]{:S(2)}, u32[]{:S(2)}) collective-permute-start(f32[8,6,16,128]{3,2,1,0:T(8,128)S(1)} %get-tuple-element.53), channel_id=1, source_target_pairs={{0,16},{16,0},{32,48},{48,32},{64,80},{80,64},{96,112},{112,96},{1... | collective-permute-start | bytes 1179656 | tf_op jit(solution)/shard_map/ppermute | solution.py:403
  20.3 6.4 %collective-permute-start.5 = (f32[192,128]{1,0:T(8,128)S(1)}, f32[192,128]{1,0:T(8,128)S(1)}, u32[]{:S(2)}, u32[]{:S(2)}) collective-permute-start(f32[192,128]{1,0:T(8,128)S(1)} %get-tuple-element.55), channel_id=1, source_target_pairs={{0,64},{16,80},{32,96},{48,112},{64,0},{80,16},{96,32},{112,48},{1... | collective-permute-start | bytes 294920 | tf_op jit(solution)/shard_map/ppermute | solution.py:403
  23.6 4.6 %collective-permute-start.6 = (f32[192,128]{1,0:T(8,128)S(1)}, f32[192,128]{1,0:T(8,128)S(1)}, u32[]{:S(2)}, u32[]{:S(2)}) collective-permute-start(f32[192,128]{1,0:T(8,128)S(1)} %get-tuple-element.56), channel_id=1, source_target_pairs={{0,32},{16,48},{32,0},{48,16},{64,96},{80,112},{96,64},{112,80},{1... | collective-permute-start | bytes 294920 | tf_op jit(solution)/shard_map/ppermute | solution.py:403
  24.2 5.8 %collective-permute-start.7 = (f32[192,128]{1,0:T(8,128)S(1)}, f32[192,128]{1,0:T(8,128)S(1)}, u32[]{:S(2)}, u32[]{:S(2)}) collective-permute-start(f32[192,128]{1,0:T(8,128)S(1)} %get-tuple-element.57), channel_id=1, source_target_pairs={{0,96},{16,112},{32,64},{48,80},{64,32},{80,48},{96,0},{112,16},{1... | collective-permute-start | bytes 294920 | tf_op jit(solution)/shard_map/ppermute | solution.py:403
  24.6 6.9 %collective-permute-start.9 = (f32[192,128]{1,0:T(8,128)S(1)}, f32[192,128]{1,0:T(8,128)S(1)}, u32[]{:S(2)}, u32[]{:S(2)}) collective-permute-start(f32[192,128]{1,0:T(8,128)S(1)} %get-tuple-element.60), channel_id=1, source_target_pairs={{0,1},{1,2},{2,3},{3,4},{4,5},{5,6},{6,7},{7,8},{8,9},{9,10},{10,1... | collective-permute-start | bytes 294920 | tf_op jit(solution)/shard_map/ppermute | solution.py:406
  25.4 6.7 %collective-permute-start.10 = (f32[192,128]{1,0:T(8,128)S(1)}, f32[192,128]{1,0:T(8,128)S(1)}, u32[]{:S(2)}, u32[]{:S(2)}) collective-permute-start(f32[192,128]{1,0:T(8,128)S(1)} %get-tuple-element.61), channel_id=1, source_target_pairs={{1,0},{2,1},{3,2},{4,3},{5,4},{6,5},{7,6},{8,7},{9,8},{10,9},{11,1... | collective-permute-start | bytes 294920 | tf_op jit(solution)/shard_map/ppermute | solution.py:406
  30.1 6.4 %collective-permute-start.8 = (f32[192,128]{1,0:T(8,128)S(1)}, f32[192,128]{1,0:T(8,128)S(1)}, u32[]{:S(2)}, u32[]{:S(2)}) collective-permute-start(f32[192,128]{1,0:T(8,128)S(1)} %add_add_fusion.mine), channel_id=1, source_target_pairs={{0,128},{16,144},{32,160},{48,176},{64,192},{80,208},{96,224},{112... | collective-permute-start | bytes 294920 | tf_op jit(solution)/shard_map/ppermute | solution.py:403
  36.6 11.3 %collective-permute-start.13 = (f32[192,128]{1,0:T(8,128)S(1)}, f32[192,128]{1,0:T(8,128)S(1)}, u32[]{:S(2)}, u32[]{:S(2)}) collective-permute-start(f32[192,128]{1,0:T(8,128)S(1)} %get-tuple-element.64.g0.grad), channel_id=1, source_target_pairs={{0,64},{16,80},{32,96},{48,112},{64,0},{80,16},{96,32},{112,48},{1... | collective-permute-start | bytes 294920 | tf_op jit(solution)/shard_map/ppermute | solution.py:403
  37.3 10.6 %collective-permute-start.12 = (f32[192,128]{1,0:T(8,128)S(1)}, f32[192,128]{1,0:T(8,128)S(1)}, u32[]{:S(2)}, u32[]{:S(2)}) collective-permute-start(f32[192,128]{1,0:T(8,128)S(1)} %get-tuple-element.64.g0.grad), channel_id=1, source_target_pairs={{0,32},{16,48},{32,0},{48,16},{64,96},{80,112},{96,64},{112,80},{1... | collective-permute-start | bytes 294920 | tf_op jit(solution)/shard_map/ppermute | solution.py:403
  38.0 9.9 %collective-permute-start.11 = (f32[192,128]{1,0:T(8,128)S(1)}, f32[192,128]{1,0:T(8,128)S(1)}, u32[]{:S(2)}, u32[]{:S(2)}) collective-permute-start(f32[192,128]{1,0:T(8,128)S(1)} %get-tuple-element.64.g0.grad), channel_id=1, source_target_pairs={{0,96},{16,112},{32,64},{48,80},{64,32},{80,48},{96,0},{112,16},{1... | collective-permute-start | bytes 294920 | tf_op jit(solution)/shard_map/ppermute | solution.py:403
  40.7 4.2 %collective-permute-start.14 = (f32[120,128]{1,0:T(8,128)S(1)}, f32[120,128]{1,0:T(8,128)S(1)}, u32[]{:S(2)}, u32[]{:S(2)}) collective-permute-start(f32[120,128]{1,0:T(8,128)S(1)} %get-tuple-element.66), channel_id=1, source_target_pairs={{0,1},{1,2},{2,3},{3,4},{4,5},{5,6},{6,7},{7,8},{8,9},{9,10},{10,1... | collective-permute-start | bytes 184328 | tf_op jit(solution)/shard_map/ppermute | solution.py:406
  41.5 6.3 %collective-permute-start.15 = (f32[120,128]{1,0:T(8,128)S(1)}, f32[120,128]{1,0:T(8,128)S(1)}, u32[]{:S(2)}, u32[]{:S(2)}) collective-permute-start(f32[120,128]{1,0:T(8,128)S(1)} %get-tuple-element.67), channel_id=1, source_target_pairs={{1,0},{2,1},{3,2},{4,3},{5,4},{6,5},{7,6},{8,7},{9,8},{10,9},{11,1... | collective-permute-start | bytes 184328 | tf_op jit(solution)/shard_map/ppermute | solution.py:406
  48.0 2.2 %collective-permute-start.16 = (f32[768,128]{1,0:T(8,128)S(1)}, f32[768,128]{1,0:T(8,128)S(1)}, u32[]{:S(2)}, u32[]{:S(2)}) collective-permute-start(f32[768,128]{1,0:T(8,128)S(1)} %get-tuple-element.68), channel_id=1, source_target_pairs={{0,16},{16,0},{32,48},{48,32},{64,80},{80,64},{96,112},{112,96},{1... | collective-permute-start | bytes 1179656 | tf_op jit(solution)/shard_map/ppermute | solution.py:403
  48.1 5.7 %collective-permute-start.19 = (f32[144,128]{1,0:T(8,128)S(1)}, f32[144,128]{1,0:T(8,128)S(1)}, u32[]{:S(2)}, u32[]{:S(2)}) collective-permute-start(f32[144,128]{1,0:T(8,128)S(1)} %get-tuple-element.74), channel_id=1, source_target_pairs={{0,1},{1,2},{2,3},{3,4},{4,5},{5,6},{6,7},{7,8},{8,9},{9,10},{10,1... | collective-permute-start | bytes 221192 | tf_op jit(solution)/shard_map/ppermute | solution.py:406
  48.2 4.4 %copy-start.4 = (f32[6,1,16,128]{3,2,1,0:T(8,128)S(1)}, f32[6,1,16,128]{3,2,1,0:T(8,128)}, u32[]{:S(2)}) copy-start(f32[6,1,16,128]{3,2,1,0:T(8,128)} %param.15) | copy-start | bytes 147460
  48.2 6.8 %collective-permute-start.20 = (f32[144,128]{1,0:T(8,128)S(1)}, f32[144,128]{1,0:T(8,128)S(1)}, u32[]{:S(2)}, u32[]{:S(2)}) collective-permute-start(f32[144,128]{1,0:T(8,128)S(1)} %get-tuple-element.75), channel_id=1, source_target_pairs={{1,0},{2,1},{3,2},{4,3},{5,4},{6,5},{7,6},{8,7},{9,8},{10,9},{11,1... | collective-permute-start | bytes 221192 | tf_op jit(solution)/shard_map/ppermute | solution.py:406
  50.4 6.2 %collective-permute-start.17 = (f32[192,128]{1,0:T(8,128)S(1)}, f32[192,128]{1,0:T(8,128)S(1)}, u32[]{:S(2)}, u32[]{:S(2)}) collective-permute-start(f32[192,128]{1,0:T(8,128)S(1)} %get-tuple-element.69), channel_id=1, source_target_pairs={{0,1},{1,2},{2,3},{3,4},{4,5},{5,6},{6,7},{7,8},{8,9},{9,10},{10,1... | collective-permute-start | bytes 294920 | tf_op jit(solution)/shard_map/ppermute | solution.py:406
  52.6 6.7 %collective-permute-start.18 = (f32[192,128]{1,0:T(8,128)S(1)}, f32[192,128]{1,0:T(8,128)S(1)}, u32[]{:S(2)}, u32[]{:S(2)}) collective-permute-start(f32[192,128]{1,0:T(8,128)S(1)} %get-tuple-element.70), channel_id=1, source_target_pairs={{1,0},{2,1},{3,2},{4,3},{5,4},{6,5},{7,6},{8,7},{9,8},{10,9},{11,1... | collective-permute-start | bytes 294920 | tf_op jit(solution)/shard_map/ppermute | solution.py:406
  52.6 2.4 %copy-start.2 = (f32[2,16,16,128]{3,2,1,0:T(8,128)S(1)}, f32[2,16,16,128]{3,2,1,0:T(8,128)}, u32[]{:S(2)}) copy-start(f32[2,16,16,128]{3,2,1,0:T(8,128)} %param.13) | copy-start | bytes 786436

commit v7 on v6

--- a/solution.py
+++ b/solution.py
@@ -208,24 +208,21 @@
 
 
 def fetch_body(
-    alpha_in, cell_in, mask_in, value, weight, static_ctl, static_coef,
-    b_f, b_b, c_f, c_b, field, held, cell, mask, alpha, sem,
+    alpha_in, value, weight, static_ctl, static_coef, b_f, b_b, c_f, c_b, field, held, alpha, sem,
 ):
     _, y, c = place()
     first = pltpu.make_async_copy(alpha_in, alpha, sem.at[0])
     first.start()
     copies = [
-        pltpu.make_async_copy(cell_in, cell, sem.at[1]),
-        pltpu.make_async_copy(mask_in, mask, sem.at[2]),
-        pltpu.make_async_copy(static_coef, field.at[96:128], sem.at[3]),
+        pltpu.make_async_copy(static_coef, field.at[96:128], sem.at[1]),
     ]
     for j in range(2):
         level = 2 * y + c + 8 * j
         for k, source in enumerate((weight, value)):
             spot = held.reshape(2, 2, VARS, 8, LANES).at[k, j]
-            copies.append(pltpu.make_async_copy(source.at[:, level], spot, sem.at[4 + 3 * j + k]))
+            copies.append(pltpu.make_async_copy(source.at[:, level], spot, sem.at[2 + 3 * j + k]))
         spot = field.reshape(16, ROWS, LANES).at[8 * j : 8 * j + VARS]
-        copies.append(pltpu.make_async_copy(static_ctl.at[:, level], spot, sem.at[6 + 3 * j]))
+        copies.append(pltpu.make_async_copy(static_ctl.at[:, level], spot, sem.at[4 + 3 * j]))
     for copy in copies:
         copy.start()
     field[224:256, :] = jnp.zeros((32, LANES), jnp.float32)
@@ -280,15 +277,18 @@
     pack_rows(lambda row: middle[pl.ds(row, 4, stride=ROWS), :], 4, forward, backward, 72)
 
 
-def project_own_body(g0, g3, g1, g2, perturb, start, low, high, forward, backward, middle, rest, low_out, high_out):
+def join_body(g3, g1, g2, g0, out):
+    for k, g in enumerate((g0, g1, g2, g3)):
+        out[k * 192 : k * 192 + 192, :] = g[...]
+
+
+def project_own_body(g3, g1, g2, perturb, start, low, high, forward, backward, middle, low_out, high_out):
     c = lax.axis_index("mem") % 2
     low_out[...] = low[...]
     high_out[...] = high[...]
     middle[0:64, :] = start[...]
-    rest[0:192, :] = g0[...]
     for k, g in ((1, g1), (2, g2), (3, g3)):
         project(g, k, c, perturb, middle)
-        rest[k * 192 : k * 192 + 192, :] = g[...]
     pack_rows(lambda row: middle[pl.ds(64 + row, 12, stride=ROWS), :], 12, forward, backward)
 
 
@@ -422,26 +422,25 @@
         grant=GRANT,
     )(alpha2, loc2)
     a_low, a_high = halo(a_f, a_b)
-    ints = jax.ShapeDtypeStruct((8, LANES), jnp.int32)
-    b_f, b_b, c_f, c_b, field, held, cell, mask = call(
+    b_f, b_b, c_f, c_b, field, held = call(
         fetch_body,
         "fetch",
-        [HBM] * 7,
-        [quarter] * 4 + [half, quarter, ints, ints],
-        [f32(512, LANES), pltpu.SemaphoreType.DMA((10,))],
+        [HBM] * 5,
+        [quarter] * 4 + [half, quarter],
+        [f32(512, LANES), pltpu.SemaphoreType.DMA((8,))],
         flops=BUSY,
         grant=GRANT2,
     )(
         alpha2,
-        obs_cell.reshape(8, LANES),
-        obs_mask.reshape(8, LANES),
         obs_value.reshape(VARS, 16, 8, LANES),
         obs_weight.reshape(VARS, 16, 8, LANES),
         static_ctl,
         static_coef.reshape(32, LANES),
     )
     b_low, b_high = halo(b_f, b_b)
-    (sums,) = call(prepare_body, "prepare", [VM] * 3, [shape(384, LANES)], flops=BUSY)(cell, mask, held)
+    (sums,) = call(prepare_body, "prepare", [VM] * 3, [shape(384, LANES)], flops=BUSY)(
+        obs_cell.reshape(8, LANES), obs_mask.reshape(8, LANES), held
+    )
 
     part_a, loc_k = call(
         first_body,
@@ -473,14 +472,16 @@
     g2, g1, g3 = swap(grad, 4), swap(grad, 2), swap(grad, 6)
     g_low, g_high = halo(g_f, g_b)
     far = shape(144, LANES)
-    p_f, p_b, p_m, rest, g_low, g_high = call(
+    (rest,) = call(join_body, "join", [VM] * 4, [shape(768, LANES)], flops=0)(g3, g1, g2, grad)
+    rest = swap(rest, 1)
+    p_f, p_b, p_m, g_low, g_high = call(
         project_own_body,
         "project_own",
-        [VM] * 8,
-        [far, far, half, shape(768, LANES), early, early],
-    )(grad, g3, g1, g2, perturb, start, g_low, g_high)
+        [VM] * 7,
+        [far, far, half, early, early],
+        flops=BUSY,
+    )(g3, g1, g2, perturb, start, g_low, g_high)
     p_low, p_high = halo(p_f, p_b)
-    rest = swap(rest, 1)
     q_f, q_b, q_m = call(project_other_body, "project_other", [VM] * 2, [quarter, quarter, half])(rest, perturb)
     q_low, q_high = halo(q_f, q_b)
     whole = shape(2, HALF, 2, ROWS, LANES)

time: 62 us -> 61.4 us (level)
  local copies, waits for them, and re-layouts: 0.72 us -> 0.05 us
    ppermute x6, waiting for transfers between devices: 11.1 us -> 10.1 us  [halo(): lax.ppermute(backward, 'tile', down)]
    ppermute x9, waiting for transfers between devices: 6.19 us -> 7.17 us  [swap(): return lax.ppermute(value, 'mem', [(i, i ^ bits) for i in range(members)])]
    unnamed x16, local copies, waits for them, and re-layouts: 0.72 us -> 0.05 us
    pallas_call x2 -> x3, Pallas kernels: 1.31 us -> 1.29 us  [the longest x1 1.16 us: local(): call(fetch_body, 'fetch', [HBM] * 5, [quarter] * 4 + [half, quarter], [f3...]
  transfers between devices with their start and end apart: 21 -> 21, of which waited for: 9 -> 12; matrix products, arithmetic and copies ran while one was open for 0% -> 0% of each run, Pallas kernels for 16% -> 17%
where the time goes in v7:
time: 61.4 us; the launch traced here: 61.3 us
  starting transfers between devices  26.2 us (43%)
  waiting for transfers between devices  19.4 us (32%)
  Pallas kernels  14.6 us (24%)
  between operations  1.03 us (2%)
    ppermute x6, starting transfers between devices, halo(): lax.ppermute(forward, 'tile', up)  11.7 us
    ppermute x9, starting transfers between devices, swap(): return lax.ppermute(value, 'mem', [(i, i ^ bits) for i in range(members)])  10.1 us
    ppermute x6, waiting for transfers between devices, halo(): lax.ppermute(backward, 'tile', down)  10.1 us
    ppermute x9, waiting for transfers between devices, swap(): return lax.ppermute(value, 'mem', [(i, i ^ bits) for i in range(members)])  7.17 us
    ppermute x6, starting transfers between devices, halo(): lax.ppermute(backward, 'tile', down)  4.38 us
    pallas_call x1, Pallas kernels, local(): call(fourth_body, 'fourth', [VM] * 10, [whole, whole, shape(96, LANES), s...  2.34 us
    ppermute x6, waiting for transfers between devices, halo(): lax.ppermute(forward, 'tile', up)  2.17 us
    pallas_call x1, Pallas kernels, local(): call(pack_body, 'pack', [HBM] * 2, [shape(216, LANES)] * 2, [f32(512, LAN...  1.73 us
  transfers between devices with their start and end apart: 21, of which 12 were waited for; matrix products, arithmetic and copies ran while one was open for 0% of the time, Pallas kernels for 17%

profile of v7, /device:TPU:102, one launch (start us, length us, event | category | flops | bytes accessed | tf_op | source)
XLA Modules:
  0.0 61.3 jit_solution(5892824098290243345)
XLA Ops:
  0.6 0.0 copy-start.5
  0.6 1.7 %pack.1 = (f32[216,128]{1,0:T(8,128)}, f32[216,128]{1,0:T(8,128)}) custom-call(f32[512,128]{1,0:T(8,128)} %bitcast.17, f32[32,128]{1,0:T(8,128)} %bitcast.25), custom_call_target="tpu_custom_call" | custom-call | flops 1000000 | bytes 1000000 | tf_op jit(solution)/shard_map/pack/pallas_call | solution.py:416
  2.4 3.5 %collective-permute-start.2 = (f32[216,128]{1,0:T(8,128)}, f32[216,128]{1,0:T(8,128)S(1)}, u32[]{:S(2)}, u32[]{:S(2)}) collective-permute-start(f32[216,128]{1,0:T(8,128)} %get-tuple-element.44), channel_id=1, source_target_pairs={{0,1},{1,2},{2,3},{3,4},{4,5},{5,6},{6,7},{7,8},{8,9},{9,10},{10,1... | collective-permute-start | bytes 331784 | tf_op jit(solution)/shard_map/ppermute | solution.py:406
  5.9 0.0 collective-permute-start.3
  5.9 0.0 copy-done.5
  5.9 1.2 %fetch.1 = (f32[192,128]{1,0:T(8,128)S(1)}, f32[192,128]{1,0:T(8,128)S(1)}, f32[192,128]{1,0:T(8,128)S(1)}, f32[192,128]{1,0:T(8,128)S(1)}, f32[256,128]{1,0:T(8,128)S(1)}, /*index=5*/f32[192,128]{1,0:T(8,128)S(1)}) custom-call(f32[512,128]{1,0:T(8,128)} %bitcast.18, f32[6,16,8,128]{3,2,1,0:T(8,128)} %bitcast.31, f32[6,16,8,128]{3,2,1,0:T(8,128)} %bitcast.32, ...), custom_call_target="tpu_custom_call" | custom-call | flops 5000000000 | bytes 1000000 | tf_op jit(solution)/shard_map/fetch/pallas_call | solution.py:425
  7.0 0.0 copy-start.7
  7.0 0.0 copy-start.6
  7.0 4.2 %collective-permute-start = (f32[192,128]{1,0:T(8,128)S(1)}, f32[192,128]{1,0:T(8,128)S(1)}, u32[]{:S(2)}, u32[]{:S(2)}) collective-permute-start(f32[192,128]{1,0:T(8,128)S(1)} %get-tuple-element.42), channel_id=1, source_target_pairs={{0,1},{1,2},{2,3},{3,4},{4,5},{5,6},{6,7},{7,8},{8,9},{9,10},{10,1... | collective-permute-start | bytes 294920 | tf_op jit(solution)/shard_map/ppermute | solution.py:406
  11.3 0.0 collective-permute-start.1
  11.3 0.0 copy-done.7
  11.3 0.0 copy-start
  11.3 0.0 copy-start.1
  11.3 0.0 copy-start.3
  11.3 1.4 %prepare.1.ready.sums = f32[384,128]{1,0:T(8,128)S(1)} custom-call(s32[8,128]{1,0:T(8,128)S(1)} %bitcast.29, s32[8,128]{1,0:T(8,128)S(1)} %bitcast.30, f32[192,128]{1,0:T(8,128)S(1)} %get-tuple-element.46.held), custom_call_target="tpu_custom_call" | custom-call | flops 5000000000 | bytes 1000000 | tf_op jit(solution)/shard_map/prepare/pallas_call | solution.py:441
  12.7 0.0 collective-permute-done.2.low
  12.7 0.2 collective-permute-done.3.high
  13.0 1.7 %first.1 = (f32[8,6,16,128]{3,2,1,0:T(8,128)S(1)}, f32[200,128]{1,0:T(8,128)S(1)}) custom-call(f32[512,128]{1,0:T(8,128)S(1)} %bitcast.19, f32[216,128]{1,0:T(8,128)S(1)} %collective-permute-done.2.low, f32[216,128]{1,0:T(8,128)S(1)} %collective-permute-done.3.high, f32[32,128]{1,0:T(8,128)S(1)} %bitcast.26, bf16[2,6,16,16,128]{4,3,2,1,0:T(8,128)(2,1)S(1)} %copy-done, ...), custom_call_target="tpu_custom_call" | custom-call | flops 5000000000 | bytes 1000000 | tf_op jit(solution)/shard_map/first/pallas_call | solution.py:445
  14.7 0.1 collective-permute-start.4
  14.8 0.0 collective-permute-done.low
  14.8 3.2 %collective-permute-done.1.high = f32[192,128]{1,0:T(8,128)S(1)} collective-permute-done((f32[192,128]{1,0:T(8,128)S(1)}, f32[192,128]{1,0:T(8,128)S(1)}, u32[]{:S(2)}, u32[]{:S(2)}) %collective-permute-start.1) | collective-permute-done | bytes 98336 | tf_op jit(solution)/shard_map/ppermute | solution.py:406
  18.0 1.5 %second.1.local = f32[256,128]{1,0:T(8,128)S(1)} custom-call(f32[512,128]{1,0:T(8,128)S(1)} %bitcast.20, f32[192,128]{1,0:T(8,128)S(1)} %collective-permute-done.low, f32[192,128]{1,0:T(8,128)S(1)} %collective-permute-done.1.high, f32[200,128]{1,0:T(8,128)S(1)} %get-tuple-element.47.coefs), custom_call_target="tpu_custom_call" | custom-call | flops 5000000000 | bytes 1000000 | tf_op jit(solution)/shard_map/second/pallas_call | solution.py:454
  19.5 0.0 collective-permute-done.4.received
  19.5 0.1 sum.1
  19.6 3.3 %collective-permute-start.5 = (f32[192,128]{1,0:T(8,128)S(1)}, f32[192,128]{1,0:T(8,128)S(1)}, u32[]{:S(2)}, u32[]{:S(2)}) collective-permute-start(f32[192,128]{1,0:T(8,128)S(1)} %get-tuple-element.50), channel_id=1, source_target_pairs={{0,64},{16,80},{32,96},{48,112},{64,0},{80,16},{96,32},{112,48},{1... | collective-permute-start | bytes 294920 | tf_op jit(solution)/shard_map/ppermute | solution.py:403
  22.9 0.7 %collective-permute-start.6 = (f32[192,128]{1,0:T(8,128)S(1)}, f32[192,128]{1,0:T(8,128)S(1)}, u32[]{:S(2)}, u32[]{:S(2)}) collective-permute-start(f32[192,128]{1,0:T(8,128)S(1)} %get-tuple-element.51), channel_id=1, source_target_pairs={{0,32},{16,48},{32,0},{48,16},{64,96},{80,112},{96,64},{112,80},{1... | collective-permute-start | bytes 294920 | tf_op jit(solution)/shard_map/ppermute | solution.py:403
  23.6 0.4 collective-permute-start.7
  24.0 0.8 %collective-permute-start.9 = (f32[192,128]{1,0:T(8,128)S(1)}, f32[192,128]{1,0:T(8,128)S(1)}, u32[]{:S(2)}, u32[]{:S(2)}) collective-permute-start(f32[192,128]{1,0:T(8,128)S(1)} %get-tuple-element.55), channel_id=1, source_target_pairs={{0,1},{1,2},{2,3},{3,4},{4,5},{5,6},{6,7},{7,8},{8,9},{9,10},{10,1... | collective-permute-start | bytes 294920 | tf_op jit(solution)/shard_map/ppermute | solution.py:406
  24.8 1.2 %collective-permute-start.10 = (f32[192,128]{1,0:T(8,128)S(1)}, f32[192,128]{1,0:T(8,128)S(1)}, u32[]{:S(2)}, u32[]{:S(2)}) collective-permute-start(f32[192,128]{1,0:T(8,128)S(1)} %get-tuple-element.56), channel_id=1, source_target_pairs={{1,0},{2,1},{3,2},{4,3},{5,4},{6,5},{7,6},{8,7},{9,8},{10,9},{11,1... | collective-permute-start | bytes 294920 | tf_op jit(solution)/shard_map/ppermute | solution.py:406
  26.0 0.0 collective-permute-done.5
  26.0 1.5 %collective-permute-done.6 = f32[192,128]{1,0:T(8,128)S(1)} collective-permute-done((f32[192,128]{1,0:T(8,128)S(1)}, f32[192,128]{1,0:T(8,128)S(1)}, u32[]{:S(2)}, u32[]{:S(2)}) %collective-permute-start.6) | collective-permute-done | bytes 98336 | tf_op jit(solution)/shard_map/ppermute | solution.py:403
  27.5 1.9 %collective-permute-done.7 = f32[192,128]{1,0:T(8,128)S(1)} collective-permute-done((f32[192,128]{1,0:T(8,128)S(1)}, f32[192,128]{1,0:T(8,128)S(1)}, u32[]{:S(2)}, u32[]{:S(2)}) %collective-permute-start.7) | collective-permute-done | bytes 98336 | tf_op jit(solution)/shard_map/ppermute | solution.py:403
  29.5 1.4 %collective-permute-start.8 = (f32[192,128]{1,0:T(8,128)S(1)}, f32[192,128]{1,0:T(8,128)S(1)}, u32[]{:S(2)}, u32[]{:S(2)}) collective-permute-start(f32[192,128]{1,0:T(8,128)S(1)} %add_add_fusion.mine), channel_id=1, source_target_pairs={{0,128},{16,144},{32,160},{48,176},{64,192},{80,208},{96,224},{112... | collective-permute-start | bytes 294920 | tf_op jit(solution)/shard_map/ppermute | solution.py:403
  30.8 0.7 %collective-permute-done.9.low = f32[192,128]{1,0:T(8,128)S(1)} collective-permute-done((f32[192,128]{1,0:T(8,128)S(1)}, f32[192,128]{1,0:T(8,128)S(1)}, u32[]{:S(2)}, u32[]{:S(2)}) %collective-permute-start.9) | collective-permute-done | bytes 98336 | tf_op jit(solution)/shard_map/ppermute | solution.py:406
  31.6 0.0 collective-permute-done.10.high
  31.6 1.6 %static_first.1 = (f32[192,128]{1,0:T(8,128)S(1)}, f32[200,128]{1,0:T(8,128)S(1)}) custom-call(f32[192,128]{1,0:T(8,128)S(1)} %collective-permute-done.9.low, f32[192,128]{1,0:T(8,128)S(1)} %collective-permute-done.10.high, f32[256,128]{1,0:T(8,128)S(1)} %get-tuple-element.57.field), custom_call_target="tpu_custom_call" | custom-call | flops 5000000000 | bytes 1000000 | tf_op jit(solution)/shard_map/static_first/pallas_call | solution.py:460
  33.2 2.7 %collective-permute-done.8.other = f32[192,128]{1,0:T(8,128)S(1)} collective-permute-done((f32[192,128]{1,0:T(8,128)S(1)}, f32[192,128]{1,0:T(8,128)S(1)}, u32[]{:S(2)}, u32[]{:S(2)}) %collective-permute-start.8) | collective-permute-done | bytes 98336 | tf_op jit(solution)/shard_map/ppermute | solution.py:403
  35.9 0.1 gradient.1
  35.9 0.8 %collective-permute-start.13 = (f32[192,128]{1,0:T(8,128)S(1)}, f32[192,128]{1,0:T(8,128)S(1)}, u32[]{:S(2)}, u32[]{:S(2)}) collective-permute-start(f32[192,128]{1,0:T(8,128)S(1)} %get-tuple-element.59.g0.grad), channel_id=1, source_target_pairs={{0,64},{16,80},{32,96},{48,112},{64,0},{80,16},{96,32},{112,48},{1... | collective-permute-start | bytes 294920 | tf_op jit(solution)/shard_map/ppermute | solution.py:403
  36.7 0.7 %collective-permute-start.12 = (f32[192,128]{1,0:T(8,128)S(1)}, f32[192,128]{1,0:T(8,128)S(1)}, u32[]{:S(2)}, u32[]{:S(2)}) collective-permute-start(f32[192,128]{1,0:T(8,128)S(1)} %get-tuple-element.59.g0.grad), channel_id=1, source_target_pairs={{0,32},{16,48},{32,0},{48,16},{64,96},{80,112},{96,64},{112,80},{1... | collective-permute-start | bytes 294920 | tf_op jit(solution)/shard_map/ppermute | solution.py:403
  37.4 2.7 %collective-permute-start.11 = (f32[192,128]{1,0:T(8,128)S(1)}, f32[192,128]{1,0:T(8,128)S(1)}, u32[]{:S(2)}, u32[]{:S(2)}) collective-permute-start(f32[192,128]{1,0:T(8,128)S(1)} %get-tuple-element.59.g0.grad), channel_id=1, source_target_pairs={{0,96},{16,112},{32,64},{48,80},{64,32},{80,48},{96,0},{112,16},{1... | collective-permute-start | bytes 294920 | tf_op jit(solution)/shard_map/ppermute | solution.py:403
  40.1 0.8 %collective-permute-start.17 = (f32[120,128]{1,0:T(8,128)S(1)}, f32[120,128]{1,0:T(8,128)S(1)}, u32[]{:S(2)}, u32[]{:S(2)}) collective-permute-start(f32[120,128]{1,0:T(8,128)S(1)} %get-tuple-element.64), channel_id=1, source_target_pairs={{0,1},{1,2},{2,3},{3,4},{4,5},{5,6},{6,7},{7,8},{8,9},{9,10},{10,1... | collective-permute-start | bytes 184328 | tf_op jit(solution)/shard_map/ppermute | solution.py:406
  41.0 1.2 %collective-permute-start.18 = (f32[120,128]{1,0:T(8,128)S(1)}, f32[120,128]{1,0:T(8,128)S(1)}, u32[]{:S(2)}, u32[]{:S(2)}) collective-permute-start(f32[120,128]{1,0:T(8,128)S(1)} %get-tuple-element.65), channel_id=1, source_target_pairs={{1,0},{2,1},{3,2},{4,3},{5,4},{6,5},{7,6},{8,7},{9,8},{10,9},{11,1... | collective-permute-start | bytes 184328 | tf_op jit(solution)/shard_map/ppermute | solution.py:406
  42.1 0.0 collective-permute-done.13.g2
  42.1 0.0 collective-permute-done.12.g1
  42.1 1.0 %collective-permute-done.11.g3 = f32[192,128]{1,0:T(8,128)S(1)} collective-permute-done((f32[192,128]{1,0:T(8,128)S(1)}, f32[192,128]{1,0:T(8,128)S(1)}, u32[]{:S(2)}, u32[]{:S(2)}) %collective-permute-start.11) | collective-permute-done | bytes 98336 | tf_op jit(solution)/shard_map/ppermute | solution.py:403
  43.2 0.1 collective-permute-start.14
  43.3 1.0 %collective-permute-done.17.low = f32[120,128]{1,0:T(8,128)S(1)} collective-permute-done((f32[120,128]{1,0:T(8,128)S(1)}, f32[120,128]{1,0:T(8,128)S(1)}, u32[]{:S(2)}, u32[]{:S(2)}) %collective-permute-start.17) | collective-permute-done | bytes 61472 | tf_op jit(solution)/shard_map/ppermute | solution.py:406
  44.3 3.1 %collective-permute-done.18.high = f32[120,128]{1,0:T(8,128)S(1)} collective-permute-done((f32[120,128]{1,0:T(8,128)S(1)}, f32[120,128]{1,0:T(8,128)S(1)}, u32[]{:S(2)}, u32[]{:S(2)}) %collective-permute-start.18) | collective-permute-done | bytes 61472 | tf_op jit(solution)/shard_map/ppermute | solution.py:406
  47.4 0.1 project_own.1
  47.5 0.1 collective-permute-start.19
  47.6 0.0 copy-start.4
  47.6 2.0 %collective-permute-start.20 = (f32[144,128]{1,0:T(8,128)S(1)}, f32[144,128]{1,0:T(8,128)S(1)}, u32[]{:S(2)}, u32[]{:S(2)}) collective-permute-start(f32[144,128]{1,0:T(8,128)S(1)} %get-tuple-element.69), channel_id=1, source_target_pairs={{1,0},{2,1},{3,2},{4,3},{5,4},{6,5},{7,6},{8,7},{9,8},{10,9},{11,1... | collective-permute-start | bytes 221192 | tf_op jit(solution)/shard_map/ppermute | solution.py:406
  49.6 0.0 collective-permute-done.14.rest
  49.6 0.1 project_other.1
  49.7 2.3 %collective-permute-start.15 = (f32[192,128]{1,0:T(8,128)S(1)}, f32[192,128]{1,0:T(8,128)S(1)}, u32[]{:S(2)}, u32[]{:S(2)}) collective-permute-start(f32[192,128]{1,0:T(8,128)S(1)} %get-tuple-element.60), channel_id=1, source_target_pairs={{0,1},{1,2},{2,3},{3,4},{4,5},{5,6},{6,7},{7,8},{8,9},{9,10},{10,1... | collective-permute-start | bytes 294920 | tf_op jit(solution)/shard_map/ppermute | solution.py:406
  52.0 0.0 collective-permute-start.16
  52.0 1.1 %static_last.1 = (f32[96,128]{1,0:T(8,128)S(1)}, f32[96,128]{1,0:T(8,128)S(1)}) custom-call(f32[120,128]{1,0:T(8,128)S(1)} %get-tuple-element.66.early_low.low, f32[120,128]{1,0:T(8,128)S(1)} %get-tuple-element.67.early_high.high, f32[192,128]{1,0:T(8,128)S(1)} %get-tuple-element.59.g0.grad, f32[200,128]{1,0:T(8,128)S(1)} %get-tuple-element.73.coefs, ...), custom_call_target="tpu_custom_call" | custom-call | flops 5000000000 | bytes 1000000 | tf_op jit(solution)/shard_map/static_last/pallas_call | solution.py:489
  53.1 0.0 collective-permute-done.19.low
  53.2 1.1 %collective-permute-done.20.high = f32[144,128]{1,0:T(8,128)S(1)} collective-permute-done((f32[144,128]{1,0:T(8,128)S(1)}, f32[144,128]{1,0:T(8,128)S(1)}, u32[]{:S(2)}, u32[]{:S(2)}) %collective-permute-start.20) | collective-permute-done | bytes 73760 | tf_op jit(solution)/shard_map/ppermute | solution.py:406
  54.2 1.6 %third.1 = (f32[256,128]{1,0:T(8,128)S(1)}, f32[256,128]{1,0:T(8,128)S(1)}) custom-call(f32[120,128]{1,0:T(8,128)S(1)} %get-tuple-element.66.early_low.low, f32[120,128]{1,0:T(8,128)S(1)} %get-tuple-element.67.early_high.high, f32[144,128]{1,0:T(8,128)S(1)} %collective-permute-done.19.low, f32[144,128]{1,0:T(8,128)S(1)} %collective-permute-done.20.high, ...), custom_call_target="tpu_custom_call" | custom-call | flops 5000000000 | bytes 1000000 | tf_op jit(solution)/shard_map/third/pallas_call | solution.py:492
  55.8 0.4 collective-permute-done.15.low
  56.3 2.5 %collective-permute-done.16.high = f32[192,128]{1,0:T(8,128)S(1)} collective-permute-done((f32[192,128]{1,0:T(8,128)S(1)}, f32[192,128]{1,0:T(8,128)S(1)}, u32[]{:S(2)}, u32[]{:S(2)}) %collective-permute-start.16) | collective-permute-done | bytes 98336 | tf_op jit(solution)/shard_map/ppermute | solution.py:406
  58.7 2.3 %fourth.1 = (f32[2,8,2,16,128]{4,3,2,1,0:T(8,128)}, f32[2,8,2,16,128]{4,3,2,1,0:T(8,128)}, f32[96,128]{1,0:T(8,128)}, f32[96,128]{1,0:T(8,128)}) custom-call(f32[192,128]{1,0:T(8,128)S(1)} %collective-permute-done.15.low, f32[192,128]{1,0:T(8,128)S(1)} %collective-permute-done.16.high, f32[256,128]{1,0:T(8,128)S(1)} %get-tuple-element.62.after.middle, ...), custom_call_target="tpu_custom_call" | custom-call | flops 1000000 | bytes 1000000 | tf_op jit(solution)/shard_map/fourth/pallas_call | solution.py:495
  (9 shorter events, 0.1 us)
Async XLA Ops:
  0.6 5.2 %copy-start.5 = (f32[2,16,128]{2,1,0:T(8,128)S(1)}, f32[2,16,128]{2,1,0:T(8,128)}, u32[]{:S(2)}) copy-start(f32[2,16,128]{2,1,0:T(8,128)} %param.17) | copy-start | bytes 49156
  2.4 10.4 %collective-permute-start.2 = (f32[216,128]{1,0:T(8,128)}, f32[216,128]{1,0:T(8,128)S(1)}, u32[]{:S(2)}, u32[]{:S(2)}) collective-permute-start(f32[216,128]{1,0:T(8,128)} %get-tuple-element.44), channel_id=1, source_target_pairs={{0,1},{1,2},{2,3},{3,4},{4,5},{5,6},{6,7},{7,8},{8,9},{9,10},{10,1... | collective-permute-start | bytes 331784 | tf_op jit(solution)/shard_map/ppermute | solution.py:406
  5.9 7.1 %collective-permute-start.3 = (f32[216,128]{1,0:T(8,128)}, f32[216,128]{1,0:T(8,128)S(1)}, u32[]{:S(2)}, u32[]{:S(2)}) collective-permute-start(f32[216,128]{1,0:T(8,128)} %get-tuple-element.45), channel_id=1, source_target_pairs={{1,0},{2,1},{3,2},{4,3},{5,4},{6,5},{7,6},{8,7},{9,8},{10,9},{11,1... | collective-permute-start | bytes 331784 | tf_op jit(solution)/shard_map/ppermute | solution.py:406
  7.0 4.2 %copy-start.7 = (s32[1,1024]{1,0:T(1,128)S(1)}, s32[1,1024]{1,0:T(1,128)}, u32[]{:S(2)}) copy-start(s32[1,1024]{1,0:T(1,128)} %param.19) | copy-start | bytes 12292
  7.0 4.2 %copy-start.6 = (s32[1,1024]{1,0:T(1,128)S(1)}, s32[1,1024]{1,0:T(1,128)}, u32[]{:S(2)}) copy-start(s32[1,1024]{1,0:T(1,128)} %param.18) | copy-start | bytes 12292
  7.0 7.7 %collective-permute-start = (f32[192,128]{1,0:T(8,128)S(1)}, f32[192,128]{1,0:T(8,128)S(1)}, u32[]{:S(2)}, u32[]{:S(2)}) collective-permute-start(f32[192,128]{1,0:T(8,128)S(1)} %get-tuple-element.42), channel_id=1, source_target_pairs={{0,1},{1,2},{2,3},{3,4},{4,5},{5,6},{6,7},{7,8},{8,9},{9,10},{10,1... | collective-permute-start | bytes 294920 | tf_op jit(solution)/shard_map/ppermute | solution.py:406
  11.3 6.7 %collective-permute-start.1 = (f32[192,128]{1,0:T(8,128)S(1)}, f32[192,128]{1,0:T(8,128)S(1)}, u32[]{:S(2)}, u32[]{:S(2)}) collective-permute-start(f32[192,128]{1,0:T(8,128)S(1)} %get-tuple-element.43), channel_id=1, source_target_pairs={{1,0},{2,1},{3,2},{4,3},{5,4},{6,5},{7,6},{8,7},{9,8},{10,9},{11,1... | collective-permute-start | bytes 294920 | tf_op jit(solution)/shard_map/ppermute | solution.py:406
  11.3 1.7 %copy-start = (bf16[2,6,16,16,128]{4,3,2,1,0:T(8,128)(2,1)S(1)}, bf16[2,6,16,16,128]{4,3,2,1,0:T(8,128)(2,1)}, u32[]{:S(2)}) copy-start(bf16[2,6,16,16,128]{4,3,2,1,0:T(8,128)(2,1)} %perturb.9) | copy-start | bytes 2359300
  11.3 1.7 %copy-start.1 = (f32[2,16,16,128]{3,2,1,0:T(8,128)S(1)}, f32[2,16,16,128]{3,2,1,0:T(8,128)}, u32[]{:S(2)}) copy-start(f32[2,16,16,128]{3,2,1,0:T(8,128)} %param.12) | copy-start | bytes 786436
  11.3 1.7 %copy-start.3 = (f32[2,16,128]{2,1,0:T(8,128)S(1)}, f32[2,16,128]{2,1,0:T(8,128)}, u32[]{:S(2)}) copy-start(f32[2,16,128]{2,1,0:T(8,128)} %param.16) | copy-start | bytes 49156
  14.7 4.9 %collective-permute-start.4 = (f32[8,6,16,128]{3,2,1,0:T(8,128)S(1)}, f32[8,6,16,128]{3,2,1,0:T(8,128)S(1)}, u32[]{:S(2)}, u32[]{:S(2)}) collective-permute-start(f32[8,6,16,128]{3,2,1,0:T(8,128)S(1)} %get-tuple-element.48), channel_id=1, source_target_pairs={{0,16},{16,0},{32,48},{48,32},{64,80},{80,64},{96,112},{112,96},{1... | collective-permute-start | bytes 1179656 | tf_op jit(solution)/shard_map/ppermute | solution.py:403
  19.6 6.4 %collective-permute-start.5 = (f32[192,128]{1,0:T(8,128)S(1)}, f32[192,128]{1,0:T(8,128)S(1)}, u32[]{:S(2)}, u32[]{:S(2)}) collective-permute-start(f32[192,128]{1,0:T(8,128)S(1)} %get-tuple-element.50), channel_id=1, source_target_pairs={{0,64},{16,80},{32,96},{48,112},{64,0},{80,16},{96,32},{112,48},{1... | collective-permute-start | bytes 294920 | tf_op jit(solution)/shard_map/ppermute | solution.py:403
  22.9 4.6 %collective-permute-start.6 = (f32[192,128]{1,0:T(8,128)S(1)}, f32[192,128]{1,0:T(8,128)S(1)}, u32[]{:S(2)}, u32[]{:S(2)}) collective-permute-start(f32[192,128]{1,0:T(8,128)S(1)} %get-tuple-element.51), channel_id=1, source_target_pairs={{0,32},{16,48},{32,0},{48,16},{64,96},{80,112},{96,64},{112,80},{1... | collective-permute-start | bytes 294920 | tf_op jit(solution)/shard_map/ppermute | solution.py:403
  23.6 5.8 %collective-permute-start.7 = (f32[192,128]{1,0:T(8,128)S(1)}, f32[192,128]{1,0:T(8,128)S(1)}, u32[]{:S(2)}, u32[]{:S(2)}) collective-permute-start(f32[192,128]{1,0:T(8,128)S(1)} %get-tuple-element.52), channel_id=1, source_target_pairs={{0,96},{16,112},{32,64},{48,80},{64,32},{80,48},{96,0},{112,16},{1... | collective-permute-start | bytes 294920 | tf_op jit(solution)/shard_map/ppermute | solution.py:403
  24.0 7.6 %collective-permute-start.9 = (f32[192,128]{1,0:T(8,128)S(1)}, f32[192,128]{1,0:T(8,128)S(1)}, u32[]{:S(2)}, u32[]{:S(2)}) collective-permute-start(f32[192,128]{1,0:T(8,128)S(1)} %get-tuple-element.55), channel_id=1, source_target_pairs={{0,1},{1,2},{2,3},{3,4},{4,5},{5,6},{6,7},{7,8},{8,9},{9,10},{10,1... | collective-permute-start | bytes 294920 | tf_op jit(solution)/shard_map/ppermute | solution.py:406
  24.8 6.8 %collective-permute-start.10 = (f32[192,128]{1,0:T(8,128)S(1)}, f32[192,128]{1,0:T(8,128)S(1)}, u32[]{:S(2)}, u32[]{:S(2)}) collective-permute-start(f32[192,128]{1,0:T(8,128)S(1)} %get-tuple-element.56), channel_id=1, source_target_pairs={{1,0},{2,1},{3,2},{4,3},{5,4},{6,5},{7,6},{8,7},{9,8},{10,9},{11,1... | collective-permute-start | bytes 294920 | tf_op jit(solution)/shard_map/ppermute | solution.py:406
  29.5 6.4 %collective-permute-start.8 = (f32[192,128]{1,0:T(8,128)S(1)}, f32[192,128]{1,0:T(8,128)S(1)}, u32[]{:S(2)}, u32[]{:S(2)}) collective-permute-start(f32[192,128]{1,0:T(8,128)S(1)} %add_add_fusion.mine), channel_id=1, source_target_pairs={{0,128},{16,144},{32,160},{48,176},{64,192},{80,208},{96,224},{112... | collective-permute-start | bytes 294920 | tf_op jit(solution)/shard_map/ppermute | solution.py:403
  35.9 6.2 %collective-permute-start.13 = (f32[192,128]{1,0:T(8,128)S(1)}, f32[192,128]{1,0:T(8,128)S(1)}, u32[]{:S(2)}, u32[]{:S(2)}) collective-permute-start(f32[192,128]{1,0:T(8,128)S(1)} %get-tuple-element.59.g0.grad), channel_id=1, source_target_pairs={{0,64},{16,80},{32,96},{48,112},{64,0},{80,16},{96,32},{112,48},{1... | collective-permute-start | bytes 294920 | tf_op jit(solution)/shard_map/ppermute | solution.py:403
  36.7 5.5 %collective-permute-start.12 = (f32[192,128]{1,0:T(8,128)S(1)}, f32[192,128]{1,0:T(8,128)S(1)}, u32[]{:S(2)}, u32[]{:S(2)}) collective-permute-start(f32[192,128]{1,0:T(8,128)S(1)} %get-tuple-element.59.g0.grad), channel_id=1, source_target_pairs={{0,32},{16,48},{32,0},{48,16},{64,96},{80,112},{96,64},{112,80},{1... | collective-permute-start | bytes 294920 | tf_op jit(solution)/shard_map/ppermute | solution.py:403
  37.4 5.8 %collective-permute-start.11 = (f32[192,128]{1,0:T(8,128)S(1)}, f32[192,128]{1,0:T(8,128)S(1)}, u32[]{:S(2)}, u32[]{:S(2)}) collective-permute-start(f32[192,128]{1,0:T(8,128)S(1)} %get-tuple-element.59.g0.grad), channel_id=1, source_target_pairs={{0,96},{16,112},{32,64},{48,80},{64,32},{80,48},{96,0},{112,16},{1... | collective-permute-start | bytes 294920 | tf_op jit(solution)/shard_map/ppermute | solution.py:403
  40.1 4.2 %collective-permute-start.17 = (f32[120,128]{1,0:T(8,128)S(1)}, f32[120,128]{1,0:T(8,128)S(1)}, u32[]{:S(2)}, u32[]{:S(2)}) collective-permute-start(f32[120,128]{1,0:T(8,128)S(1)} %get-tuple-element.64), channel_id=1, source_target_pairs={{0,1},{1,2},{2,3},{3,4},{4,5},{5,6},{6,7},{7,8},{8,9},{9,10},{10,1... | collective-permute-start | bytes 184328 | tf_op jit(solution)/shard_map/ppermute | solution.py:406
  41.0 6.4 %collective-permute-start.18 = (f32[120,128]{1,0:T(8,128)S(1)}, f32[120,128]{1,0:T(8,128)S(1)}, u32[]{:S(2)}, u32[]{:S(2)}) collective-permute-start(f32[120,128]{1,0:T(8,128)S(1)} %get-tuple-element.65), channel_id=1, source_target_pairs={{1,0},{2,1},{3,2},{4,3},{5,4},{6,5},{7,6},{8,7},{9,8},{10,9},{11,1... | collective-permute-start | bytes 184328 | tf_op jit(solution)/shard_map/ppermute | solution.py:406
  43.2 6.4 %collective-permute-start.14 = (f32[768,128]{1,0:T(8,128)S(1)}, f32[768,128]{1,0:T(8,128)S(1)}, u32[]{:S(2)}, u32[]{:S(2)}) collective-permute-start(f32[768,128]{1,0:T(8,128)S(1)} %join.1), channel_id=1, source_target_pairs={{0,16},{16,0},{32,48},{48,32},{64,80},{80,64},{96,112},{112,96},{1... | collective-permute-start | bytes 1179656 | tf_op jit(solution)/shard_map/ppermute | solution.py:403
  47.5 5.6 %collective-permute-start.19 = (f32[144,128]{1,0:T(8,128)S(1)}, f32[144,128]{1,0:T(8,128)S(1)}, u32[]{:S(2)}, u32[]{:S(2)}) collective-permute-start(f32[144,128]{1,0:T(8,128)S(1)} %get-tuple-element.68), channel_id=1, source_target_pairs={{0,1},{1,2},{2,3},{3,4},{4,5},{5,6},{6,7},{7,8},{8,9},{9,10},{10,1... | collective-permute-start | bytes 221192 | tf_op jit(solution)/shard_map/ppermute | solution.py:406
  47.6 4.4 %copy-start.4 = (f32[6,1,16,128]{3,2,1,0:T(8,128)S(1)}, f32[6,1,16,128]{3,2,1,0:T(8,128)}, u32[]{:S(2)}) copy-start(f32[6,1,16,128]{3,2,1,0:T(8,128)} %param.15) | copy-start | bytes 147460
  47.6 6.6 %collective-permute-start.20 = (f32[144,128]{1,0:T(8,128)S(1)}, f32[144,128]{1,0:T(8,128)S(1)}, u32[]{:S(2)}, u32[]{:S(2)}) collective-permute-start(f32[144,128]{1,0:T(8,128)S(1)} %get-tuple-element.69), channel_id=1, source_target_pairs={{1,0},{2,1},{3,2},{4,3},{5,4},{6,5},{7,6},{8,7},{9,8},{10,9},{11,1... | collective-permute-start | bytes 221192 | tf_op jit(solution)/shard_map/ppermute | solution.py:406
  49.7 6.5 %collective-permute-start.15 = (f32[192,128]{1,0:T(8,128)S(1)}, f32[192,128]{1,0:T(8,128)S(1)}, u32[]{:S(2)}, u32[]{:S(2)}) collective-permute-start(f32[192,128]{1,0:T(8,128)S(1)} %get-tuple-element.60), channel_id=1, source_target_pairs={{0,1},{1,2},{2,3},{3,4},{4,5},{5,6},{6,7},{7,8},{8,9},{9,10},{10,1... | collective-permute-start | bytes 294920 | tf_op jit(solution)/shard_map/ppermute | solution.py:406
  52.0 6.7 %collective-permute-start.16 = (f32[192,128]{1,0:T(8,128)S(1)}, f32[192,128]{1,0:T(8,128)S(1)}, u32[]{:S(2)}, u32[]{:S(2)}) collective-permute-start(f32[192,128]{1,0:T(8,128)S(1)} %get-tuple-element.61), channel_id=1, source_target_pairs={{1,0},{2,1},{3,2},{4,3},{5,4},{6,5},{7,6},{8,7},{9,8},{10,9},{11,1... | collective-permute-start | bytes 294920 | tf_op jit(solution)/shard_map/ppermute | solution.py:406
  52.0 2.2 %copy-start.2 = (f32[2,16,16,128]{3,2,1,0:T(8,128)S(1)}, f32[2,16,16,128]{3,2,1,0:T(8,128)}, u32[]{:S(2)}) copy-start(f32[2,16,16,128]{3,2,1,0:T(8,128)} %param.13) | copy-start | bytes 786436

commit v8 on v7

--- a/solution.py
+++ b/solution.py
@@ -299,10 +299,10 @@
     pack_rows(lambda row: middle[pl.ds(row, 16, stride=ROWS), :], 16, forward, backward)
 
 
-def update_alpha(parity, out, alpha, mom, stage0, stage1):
+def update_alpha(parity, out, alpha, mom, stage0, stage1, finish=None):
     _, y, _ = place()
-    for k in range(4):
-        for m in range(2):
+    for m in range(2):
+        for k in range(4):
             for j in range(2):
                 t = (k * 4 + m * 2 + j) * 16
                 s = (y ^ k) + 4 * j
@@ -312,6 +312,8 @@
                 moved = momentum_rate * mom[at, :] + (old + out[t : t + 16, :])
                 stage1[here, :] = moved
                 stage0[here, :] = old - step_rate * moved
+        if finish is not None:
+            finish(m)
 
 
 def third_body(
@@ -373,11 +375,15 @@
 
     load = halo_loader(low, high, lambda row: middle[pl.ds(row, 16, stride=ROWS), :], 16)
     diffuse(load, 16, 16, coefs, (buf0, buf1), emit)
-    update_alpha(1 - c, out, alpha, mom, stage0, stage1)
-    last = [leave(stage0, new_alpha, 1 - c, 4), leave(stage1, new_mom, 1 - c, 5)]
-    for copy in last:
-        copy.start()
-    for copy in copies + last:
+    def finish(m):
+        for k, (stage, target) in enumerate(((stage0, new_alpha), (stage1, new_mom))):
+            part = stage.at[m * 128 : m * 128 + 128].reshape(HALF, ROWS, LANES)
+            copy = pltpu.make_async_copy(part, target.at[m, :, 1 - c], sem.at[4 + 2 * m + k])
+            copy.start()
+            copies.append(copy)
+
+    update_alpha(1 - c, out, alpha, mom, stage0, stage1, finish)
+    for copy in copies:
         copy.wait()
 
 
@@ -497,7 +503,7 @@
         "fourth",
         [VM] * 10,
         [whole, whole, shape(96, LANES), shape(96, LANES)],
-        bufs16 + [f32(256, LANES)] * 3 + [pltpu.SemaphoreType.DMA((6,))],
+        bufs16 + [f32(256, LANES)] * 3 + [pltpu.SemaphoreType.DMA((8,))],
         out_specs=[HBM] * 4,
     )(q_low, q_high, q_m, loc_k, alpha2, mom2, *ready, *static_ready)
     return (

time: 61.4 us -> 61.4 us (level)
  no operation moved by 1% of the time
where the time goes in v8:
time: 61.4 us; the launch traced here: 61.3 us
  starting transfers between devices  26.2 us (43%)
  waiting for transfers between devices  19.4 us (32%)
  Pallas kernels  14.6 us (24%)
  between operations  1.03 us (2%)
    ppermute x6, starting transfers between devices, halo(): lax.ppermute(forward, 'tile', up)  11.7 us
    ppermute x9, starting transfers between devices, swap(): return lax.ppermute(value, 'mem', [(i, i ^ bits) for i in range(members)])  10.1 us
    ppermute x6, waiting for transfers between devices, halo(): lax.ppermute(backward, 'tile', down)  10.1 us
    ppermute x9, waiting for transfers between devices, swap(): return lax.ppermute(value, 'mem', [(i, i ^ bits) for i in range(members)])  7.17 us
    ppermute x6, starting transfers between devices, halo(): lax.ppermute(backward, 'tile', down)  4.38 us
    pallas_call x1, Pallas kernels, local(): call(fourth_body, 'fourth', [VM] * 10, [whole, whole, shape(96, LANES), s...  2.36 us
    ppermute x6, waiting for transfers between devices, halo(): lax.ppermute(forward, 'tile', up)  2.15 us
    pallas_call x1, Pallas kernels, local(): call(pack_body, 'pack', [HBM] * 2, [shape(216, LANES)] * 2, [f32(512, LAN...  1.73 us
  transfers between devices with their start and end apart: 21, of which 12 were waited for; matrix products, arithmetic and copies ran while one was open for 0% of the time, Pallas kernels for 17%

profile of v8, /device:TPU:102, one launch (start us, length us, event | category | flops | bytes accessed | tf_op | source)
XLA Modules:
  0.0 61.3 jit_solution(7370417386613339314)
XLA Ops:
  0.6 0.0 copy-start.5
  0.6 1.7 %pack.1 = (f32[216,128]{1,0:T(8,128)}, f32[216,128]{1,0:T(8,128)}) custom-call(f32[512,128]{1,0:T(8,128)} %bitcast.17, f32[32,128]{1,0:T(8,128)} %bitcast.25), custom_call_target="tpu_custom_call" | custom-call | flops 1000000 | bytes 1000000 | tf_op jit(solution)/shard_map/pack/pallas_call | solution.py:422
  2.4 3.5 %collective-permute-start.2 = (f32[216,128]{1,0:T(8,128)}, f32[216,128]{1,0:T(8,128)S(1)}, u32[]{:S(2)}, u32[]{:S(2)}) collective-permute-start(f32[216,128]{1,0:T(8,128)} %get-tuple-element.44), channel_id=1, source_target_pairs={{0,1},{1,2},{2,3},{3,4},{4,5},{5,6},{6,7},{7,8},{8,9},{9,10},{10,1... | collective-permute-start | bytes 331784 | tf_op jit(solution)/shard_map/ppermute | solution.py:412
  5.9 0.0 collective-permute-start.3
  5.9 0.0 copy-done.5
  5.9 1.2 %fetch.1 = (f32[192,128]{1,0:T(8,128)S(1)}, f32[192,128]{1,0:T(8,128)S(1)}, f32[192,128]{1,0:T(8,128)S(1)}, f32[192,128]{1,0:T(8,128)S(1)}, f32[256,128]{1,0:T(8,128)S(1)}, /*index=5*/f32[192,128]{1,0:T(8,128)S(1)}) custom-call(f32[512,128]{1,0:T(8,128)} %bitcast.18, f32[6,16,8,128]{3,2,1,0:T(8,128)} %bitcast.31, f32[6,16,8,128]{3,2,1,0:T(8,128)} %bitcast.32, ...), custom_call_target="tpu_custom_call" | custom-call | flops 5000000000 | bytes 1000000 | tf_op jit(solution)/shard_map/fetch/pallas_call | solution.py:431
  7.0 0.0 copy-start.7
  7.0 0.0 copy-start.6
  7.0 4.2 %collective-permute-start = (f32[192,128]{1,0:T(8,128)S(1)}, f32[192,128]{1,0:T(8,128)S(1)}, u32[]{:S(2)}, u32[]{:S(2)}) collective-permute-start(f32[192,128]{1,0:T(8,128)S(1)} %get-tuple-element.42), channel_id=1, source_target_pairs={{0,1},{1,2},{2,3},{3,4},{4,5},{5,6},{6,7},{7,8},{8,9},{9,10},{10,1... | collective-permute-start | bytes 294920 | tf_op jit(solution)/shard_map/ppermute | solution.py:412
  11.3 0.0 collective-permute-start.1
  11.3 0.0 copy-done.7
  11.3 0.0 copy-start
  11.3 0.0 copy-start.1
  11.3 0.0 copy-start.3
  11.3 1.4 %prepare.1.ready.sums = f32[384,128]{1,0:T(8,128)S(1)} custom-call(s32[8,128]{1,0:T(8,128)S(1)} %bitcast.29, s32[8,128]{1,0:T(8,128)S(1)} %bitcast.30, f32[192,128]{1,0:T(8,128)S(1)} %get-tuple-element.46.held), custom_call_target="tpu_custom_call" | custom-call | flops 5000000000 | bytes 1000000 | tf_op jit(solution)/shard_map/prepare/pallas_call | solution.py:447
  12.7 0.0 collective-permute-done.2.low
  12.7 0.2 collective-permute-done.3.high
  13.0 1.7 %first.1 = (f32[8,6,16,128]{3,2,1,0:T(8,128)S(1)}, f32[200,128]{1,0:T(8,128)S(1)}) custom-call(f32[512,128]{1,0:T(8,128)S(1)} %bitcast.19, f32[216,128]{1,0:T(8,128)S(1)} %collective-permute-done.2.low, f32[216,128]{1,0:T(8,128)S(1)} %collective-permute-done.3.high, f32[32,128]{1,0:T(8,128)S(1)} %bitcast.26, bf16[2,6,16,16,128]{4,3,2,1,0:T(8,128)(2,1)S(1)} %copy-done, ...), custom_call_target="tpu_custom_call" | custom-call | flops 5000000000 | bytes 1000000 | tf_op jit(solution)/shard_map/first/pallas_call | solution.py:451
  14.7 0.1 collective-permute-start.4
  14.8 0.0 collective-permute-done.low
  14.8 3.2 %collective-permute-done.1.high = f32[192,128]{1,0:T(8,128)S(1)} collective-permute-done((f32[192,128]{1,0:T(8,128)S(1)}, f32[192,128]{1,0:T(8,128)S(1)}, u32[]{:S(2)}, u32[]{:S(2)}) %collective-permute-start.1) | collective-permute-done | bytes 98336 | tf_op jit(solution)/shard_map/ppermute | solution.py:412
  18.0 1.5 %second.1.local = f32[256,128]{1,0:T(8,128)S(1)} custom-call(f32[512,128]{1,0:T(8,128)S(1)} %bitcast.20, f32[192,128]{1,0:T(8,128)S(1)} %collective-permute-done.low, f32[192,128]{1,0:T(8,128)S(1)} %collective-permute-done.1.high, f32[200,128]{1,0:T(8,128)S(1)} %get-tuple-element.47.coefs), custom_call_target="tpu_custom_call" | custom-call | flops 5000000000 | bytes 1000000 | tf_op jit(solution)/shard_map/second/pallas_call | solution.py:460
  19.5 0.0 collective-permute-done.4.received
  19.5 0.1 sum.1
  19.6 3.3 %collective-permute-start.5 = (f32[192,128]{1,0:T(8,128)S(1)}, f32[192,128]{1,0:T(8,128)S(1)}, u32[]{:S(2)}, u32[]{:S(2)}) collective-permute-start(f32[192,128]{1,0:T(8,128)S(1)} %get-tuple-element.50), channel_id=1, source_target_pairs={{0,64},{16,80},{32,96},{48,112},{64,0},{80,16},{96,32},{112,48},{1... | collective-permute-start | bytes 294920 | tf_op jit(solution)/shard_map/ppermute | solution.py:409
  22.9 0.7 %collective-permute-start.6 = (f32[192,128]{1,0:T(8,128)S(1)}, f32[192,128]{1,0:T(8,128)S(1)}, u32[]{:S(2)}, u32[]{:S(2)}) collective-permute-start(f32[192,128]{1,0:T(8,128)S(1)} %get-tuple-element.51), channel_id=1, source_target_pairs={{0,32},{16,48},{32,0},{48,16},{64,96},{80,112},{96,64},{112,80},{1... | collective-permute-start | bytes 294920 | tf_op jit(solution)/shard_map/ppermute | solution.py:409
  23.6 0.4 collective-permute-start.7
  24.0 0.8 %collective-permute-start.9 = (f32[192,128]{1,0:T(8,128)S(1)}, f32[192,128]{1,0:T(8,128)S(1)}, u32[]{:S(2)}, u32[]{:S(2)}) collective-permute-start(f32[192,128]{1,0:T(8,128)S(1)} %get-tuple-element.55), channel_id=1, source_target_pairs={{0,1},{1,2},{2,3},{3,4},{4,5},{5,6},{6,7},{7,8},{8,9},{9,10},{10,1... | collective-permute-start | bytes 294920 | tf_op jit(solution)/shard_map/ppermute | solution.py:412
  24.8 1.2 %collective-permute-start.10 = (f32[192,128]{1,0:T(8,128)S(1)}, f32[192,128]{1,0:T(8,128)S(1)}, u32[]{:S(2)}, u32[]{:S(2)}) collective-permute-start(f32[192,128]{1,0:T(8,128)S(1)} %get-tuple-element.56), channel_id=1, source_target_pairs={{1,0},{2,1},{3,2},{4,3},{5,4},{6,5},{7,6},{8,7},{9,8},{10,9},{11,1... | collective-permute-start | bytes 294920 | tf_op jit(solution)/shard_map/ppermute | solution.py:412
  26.0 0.0 collective-permute-done.5
  26.0 1.5 %collective-permute-done.6 = f32[192,128]{1,0:T(8,128)S(1)} collective-permute-done((f32[192,128]{1,0:T(8,128)S(1)}, f32[192,128]{1,0:T(8,128)S(1)}, u32[]{:S(2)}, u32[]{:S(2)}) %collective-permute-start.6) | collective-permute-done | bytes 98336 | tf_op jit(solution)/shard_map/ppermute | solution.py:409
  27.5 1.9 %collective-permute-done.7 = f32[192,128]{1,0:T(8,128)S(1)} collective-permute-done((f32[192,128]{1,0:T(8,128)S(1)}, f32[192,128]{1,0:T(8,128)S(1)}, u32[]{:S(2)}, u32[]{:S(2)}) %collective-permute-start.7) | collective-permute-done | bytes 98336 | tf_op jit(solution)/shard_map/ppermute | solution.py:409
  29.5 1.4 %collective-permute-start.8 = (f32[192,128]{1,0:T(8,128)S(1)}, f32[192,128]{1,0:T(8,128)S(1)}, u32[]{:S(2)}, u32[]{:S(2)}) collective-permute-start(f32[192,128]{1,0:T(8,128)S(1)} %add_add_fusion.mine), channel_id=1, source_target_pairs={{0,128},{16,144},{32,160},{48,176},{64,192},{80,208},{96,224},{112... | collective-permute-start | bytes 294920 | tf_op jit(solution)/shard_map/ppermute | solution.py:409
  30.8 0.7 %collective-permute-done.9.low = f32[192,128]{1,0:T(8,128)S(1)} collective-permute-done((f32[192,128]{1,0:T(8,128)S(1)}, f32[192,128]{1,0:T(8,128)S(1)}, u32[]{:S(2)}, u32[]{:S(2)}) %collective-permute-start.9) | collective-permute-done | bytes 98336 | tf_op jit(solution)/shard_map/ppermute | solution.py:412
  31.6 0.0 collective-permute-done.10.high
  31.6 1.6 %static_first.1 = (f32[192,128]{1,0:T(8,128)S(1)}, f32[200,128]{1,0:T(8,128)S(1)}) custom-call(f32[192,128]{1,0:T(8,128)S(1)} %collective-permute-done.9.low, f32[192,128]{1,0:T(8,128)S(1)} %collective-permute-done.10.high, f32[256,128]{1,0:T(8,128)S(1)} %get-tuple-element.57.field), custom_call_target="tpu_custom_call" | custom-call | flops 5000000000 | bytes 1000000 | tf_op jit(solution)/shard_map/static_first/pallas_call | solution.py:466
  33.2 2.7 %collective-permute-done.8.other = f32[192,128]{1,0:T(8,128)S(1)} collective-permute-done((f32[192,128]{1,0:T(8,128)S(1)}, f32[192,128]{1,0:T(8,128)S(1)}, u32[]{:S(2)}, u32[]{:S(2)}) %collective-permute-start.8) | collective-permute-done | bytes 98336 | tf_op jit(solution)/shard_map/ppermute | solution.py:409
  35.9 0.1 gradient.1
  35.9 0.8 %collective-permute-start.13 = (f32[192,128]{1,0:T(8,128)S(1)}, f32[192,128]{1,0:T(8,128)S(1)}, u32[]{:S(2)}, u32[]{:S(2)}) collective-permute-start(f32[192,128]{1,0:T(8,128)S(1)} %get-tuple-element.59.g0.grad), channel_id=1, source_target_pairs={{0,64},{16,80},{32,96},{48,112},{64,0},{80,16},{96,32},{112,48},{1... | collective-permute-start | bytes 294920 | tf_op jit(solution)/shard_map/ppermute | solution.py:409
  36.7 0.7 %collective-permute-start.12 = (f32[192,128]{1,0:T(8,128)S(1)}, f32[192,128]{1,0:T(8,128)S(1)}, u32[]{:S(2)}, u32[]{:S(2)}) collective-permute-start(f32[192,128]{1,0:T(8,128)S(1)} %get-tuple-element.59.g0.grad), channel_id=1, source_target_pairs={{0,32},{16,48},{32,0},{48,16},{64,96},{80,112},{96,64},{112,80},{1... | collective-permute-start | bytes 294920 | tf_op jit(solution)/shard_map/ppermute | solution.py:409
  37.4 2.7 %collective-permute-start.11 = (f32[192,128]{1,0:T(8,128)S(1)}, f32[192,128]{1,0:T(8,128)S(1)}, u32[]{:S(2)}, u32[]{:S(2)}) collective-permute-start(f32[192,128]{1,0:T(8,128)S(1)} %get-tuple-element.59.g0.grad), channel_id=1, source_target_pairs={{0,96},{16,112},{32,64},{48,80},{64,32},{80,48},{96,0},{112,16},{1... | collective-permute-start | bytes 294920 | tf_op jit(solution)/shard_map/ppermute | solution.py:409
  40.1 0.8 %collective-permute-start.17 = (f32[120,128]{1,0:T(8,128)S(1)}, f32[120,128]{1,0:T(8,128)S(1)}, u32[]{:S(2)}, u32[]{:S(2)}) collective-permute-start(f32[120,128]{1,0:T(8,128)S(1)} %get-tuple-element.64), channel_id=1, source_target_pairs={{0,1},{1,2},{2,3},{3,4},{4,5},{5,6},{6,7},{7,8},{8,9},{9,10},{10,1... | collective-permute-start | bytes 184328 | tf_op jit(solution)/shard_map/ppermute | solution.py:412
  41.0 1.2 %collective-permute-start.18 = (f32[120,128]{1,0:T(8,128)S(1)}, f32[120,128]{1,0:T(8,128)S(1)}, u32[]{:S(2)}, u32[]{:S(2)}) collective-permute-start(f32[120,128]{1,0:T(8,128)S(1)} %get-tuple-element.65), channel_id=1, source_target_pairs={{1,0},{2,1},{3,2},{4,3},{5,4},{6,5},{7,6},{8,7},{9,8},{10,9},{11,1... | collective-permute-start | bytes 184328 | tf_op jit(solution)/shard_map/ppermute | solution.py:412
  42.1 0.0 collective-permute-done.13.g2
  42.1 0.0 collective-permute-done.12.g1
  42.1 1.0 %collective-permute-done.11.g3 = f32[192,128]{1,0:T(8,128)S(1)} collective-permute-done((f32[192,128]{1,0:T(8,128)S(1)}, f32[192,128]{1,0:T(8,128)S(1)}, u32[]{:S(2)}, u32[]{:S(2)}) %collective-permute-start.11) | collective-permute-done | bytes 98336 | tf_op jit(solution)/shard_map/ppermute | solution.py:409
  43.2 0.1 collective-permute-start.14
  43.3 1.0 %collective-permute-done.17.low = f32[120,128]{1,0:T(8,128)S(1)} collective-permute-done((f32[120,128]{1,0:T(8,128)S(1)}, f32[120,128]{1,0:T(8,128)S(1)}, u32[]{:S(2)}, u32[]{:S(2)}) %collective-permute-start.17) | collective-permute-done | bytes 61472 | tf_op jit(solution)/shard_map/ppermute | solution.py:412
  44.3 3.1 %collective-permute-done.18.high = f32[120,128]{1,0:T(8,128)S(1)} collective-permute-done((f32[120,128]{1,0:T(8,128)S(1)}, f32[120,128]{1,0:T(8,128)S(1)}, u32[]{:S(2)}, u32[]{:S(2)}) %collective-permute-start.18) | collective-permute-done | bytes 61472 | tf_op jit(solution)/shard_map/ppermute | solution.py:412
  47.4 0.1 project_own.1
  47.5 0.1 collective-permute-start.19
  47.6 0.0 copy-start.4
  47.6 2.0 %collective-permute-start.20 = (f32[144,128]{1,0:T(8,128)S(1)}, f32[144,128]{1,0:T(8,128)S(1)}, u32[]{:S(2)}, u32[]{:S(2)}) collective-permute-start(f32[144,128]{1,0:T(8,128)S(1)} %get-tuple-element.69), channel_id=1, source_target_pairs={{1,0},{2,1},{3,2},{4,3},{5,4},{6,5},{7,6},{8,7},{9,8},{10,9},{11,1... | collective-permute-start | bytes 221192 | tf_op jit(solution)/shard_map/ppermute | solution.py:412
  49.6 0.0 collective-permute-done.14.rest
  49.6 0.1 project_other.1
  49.7 2.3 %collective-permute-start.15 = (f32[192,128]{1,0:T(8,128)S(1)}, f32[192,128]{1,0:T(8,128)S(1)}, u32[]{:S(2)}, u32[]{:S(2)}) collective-permute-start(f32[192,128]{1,0:T(8,128)S(1)} %get-tuple-element.60), channel_id=1, source_target_pairs={{0,1},{1,2},{2,3},{3,4},{4,5},{5,6},{6,7},{7,8},{8,9},{9,10},{10,1... | collective-permute-start | bytes 294920 | tf_op jit(solution)/shard_map/ppermute | solution.py:412
  52.0 0.0 collective-permute-start.16
  52.0 1.1 %static_last.1 = (f32[96,128]{1,0:T(8,128)S(1)}, f32[96,128]{1,0:T(8,128)S(1)}) custom-call(f32[120,128]{1,0:T(8,128)S(1)} %get-tuple-element.66.early_low.low, f32[120,128]{1,0:T(8,128)S(1)} %get-tuple-element.67.early_high.high, f32[192,128]{1,0:T(8,128)S(1)} %get-tuple-element.59.g0.grad, f32[200,128]{1,0:T(8,128)S(1)} %get-tuple-element.73.coefs, ...), custom_call_target="tpu_custom_call" | custom-call | flops 5000000000 | bytes 1000000 | tf_op jit(solution)/shard_map/static_last/pallas_call | solution.py:495
  53.1 0.0 collective-permute-done.19.low
  53.2 1.1 %collective-permute-done.20.high = f32[144,128]{1,0:T(8,128)S(1)} collective-permute-done((f32[144,128]{1,0:T(8,128)S(1)}, f32[144,128]{1,0:T(8,128)S(1)}, u32[]{:S(2)}, u32[]{:S(2)}) %collective-permute-start.20) | collective-permute-done | bytes 73760 | tf_op jit(solution)/shard_map/ppermute | solution.py:412
  54.2 1.6 %third.1 = (f32[256,128]{1,0:T(8,128)S(1)}, f32[256,128]{1,0:T(8,128)S(1)}) custom-call(f32[120,128]{1,0:T(8,128)S(1)} %get-tuple-element.66.early_low.low, f32[120,128]{1,0:T(8,128)S(1)} %get-tuple-element.67.early_high.high, f32[144,128]{1,0:T(8,128)S(1)} %collective-permute-done.19.low, f32[144,128]{1,0:T(8,128)S(1)} %collective-permute-done.20.high, ...), custom_call_target="tpu_custom_call" | custom-call | flops 5000000000 | bytes 1000000 | tf_op jit(solution)/shard_map/third/pallas_call | solution.py:498
  55.9 0.4 collective-permute-done.15.low
  56.3 2.5 %collective-permute-done.16.high = f32[192,128]{1,0:T(8,128)S(1)} collective-permute-done((f32[192,128]{1,0:T(8,128)S(1)}, f32[192,128]{1,0:T(8,128)S(1)}, u32[]{:S(2)}, u32[]{:S(2)}) %collective-permute-start.16) | collective-permute-done | bytes 98336 | tf_op jit(solution)/shard_map/ppermute | solution.py:412
  58.7 2.4 %fourth.1 = (f32[2,8,2,16,128]{4,3,2,1,0:T(8,128)}, f32[2,8,2,16,128]{4,3,2,1,0:T(8,128)}, f32[96,128]{1,0:T(8,128)}, f32[96,128]{1,0:T(8,128)}) custom-call(f32[192,128]{1,0:T(8,128)S(1)} %collective-permute-done.15.low, f32[192,128]{1,0:T(8,128)S(1)} %collective-permute-done.16.high, f32[256,128]{1,0:T(8,128)S(1)} %get-tuple-element.62.after.middle, ...), custom_call_target="tpu_custom_call" | custom-call | flops 1000000 | bytes 1000000 | tf_op jit(solution)/shard_map/fourth/pallas_call | solution.py:501
  (9 shorter events, 0.1 us)
Async XLA Ops:
  0.6 5.2 %copy-start.5 = (f32[2,16,128]{2,1,0:T(8,128)S(1)}, f32[2,16,128]{2,1,0:T(8,128)}, u32[]{:S(2)}) copy-start(f32[2,16,128]{2,1,0:T(8,128)} %param.17) | copy-start | bytes 49156
  2.4 10.4 %collective-permute-start.2 = (f32[216,128]{1,0:T(8,128)}, f32[216,128]{1,0:T(8,128)S(1)}, u32[]{:S(2)}, u32[]{:S(2)}) collective-permute-start(f32[216,128]{1,0:T(8,128)} %get-tuple-element.44), channel_id=1, source_target_pairs={{0,1},{1,2},{2,3},{3,4},{4,5},{5,6},{6,7},{7,8},{8,9},{9,10},{10,1... | collective-permute-start | bytes 331784 | tf_op jit(solution)/shard_map/ppermute | solution.py:412
  5.9 7.1 %collective-permute-start.3 = (f32[216,128]{1,0:T(8,128)}, f32[216,128]{1,0:T(8,128)S(1)}, u32[]{:S(2)}, u32[]{:S(2)}) collective-permute-start(f32[216,128]{1,0:T(8,128)} %get-tuple-element.45), channel_id=1, source_target_pairs={{1,0},{2,1},{3,2},{4,3},{5,4},{6,5},{7,6},{8,7},{9,8},{10,9},{11,1... | collective-permute-start | bytes 331784 | tf_op jit(solution)/shard_map/ppermute | solution.py:412
  7.0 4.2 %copy-start.7 = (s32[1,1024]{1,0:T(1,128)S(1)}, s32[1,1024]{1,0:T(1,128)}, u32[]{:S(2)}) copy-start(s32[1,1024]{1,0:T(1,128)} %param.19) | copy-start | bytes 12292
  7.0 4.2 %copy-start.6 = (s32[1,1024]{1,0:T(1,128)S(1)}, s32[1,1024]{1,0:T(1,128)}, u32[]{:S(2)}) copy-start(s32[1,1024]{1,0:T(1,128)} %param.18) | copy-start | bytes 12292
  7.0 7.7 %collective-permute-start = (f32[192,128]{1,0:T(8,128)S(1)}, f32[192,128]{1,0:T(8,128)S(1)}, u32[]{:S(2)}, u32[]{:S(2)}) collective-permute-start(f32[192,128]{1,0:T(8,128)S(1)} %get-tuple-element.42), channel_id=1, source_target_pairs={{0,1},{1,2},{2,3},{3,4},{4,5},{5,6},{6,7},{7,8},{8,9},{9,10},{10,1... | collective-permute-start | bytes 294920 | tf_op jit(solution)/shard_map/ppermute | solution.py:412
  11.3 6.7 %collective-permute-start.1 = (f32[192,128]{1,0:T(8,128)S(1)}, f32[192,128]{1,0:T(8,128)S(1)}, u32[]{:S(2)}, u32[]{:S(2)}) collective-permute-start(f32[192,128]{1,0:T(8,128)S(1)} %get-tuple-element.43), channel_id=1, source_target_pairs={{1,0},{2,1},{3,2},{4,3},{5,4},{6,5},{7,6},{8,7},{9,8},{10,9},{11,1... | collective-permute-start | bytes 294920 | tf_op jit(solution)/shard_map/ppermute | solution.py:412
  11.3 1.7 %copy-start = (bf16[2,6,16,16,128]{4,3,2,1,0:T(8,128)(2,1)S(1)}, bf16[2,6,16,16,128]{4,3,2,1,0:T(8,128)(2,1)}, u32[]{:S(2)}) copy-start(bf16[2,6,16,16,128]{4,3,2,1,0:T(8,128)(2,1)} %perturb.9) | copy-start | bytes 2359300
  11.3 1.7 %copy-start.1 = (f32[2,16,16,128]{3,2,1,0:T(8,128)S(1)}, f32[2,16,16,128]{3,2,1,0:T(8,128)}, u32[]{:S(2)}) copy-start(f32[2,16,16,128]{3,2,1,0:T(8,128)} %param.12) | copy-start | bytes 786436
  11.3 1.7 %copy-start.3 = (f32[2,16,128]{2,1,0:T(8,128)S(1)}, f32[2,16,128]{2,1,0:T(8,128)}, u32[]{:S(2)}) copy-start(f32[2,16,128]{2,1,0:T(8,128)} %param.16) | copy-start | bytes 49156
  14.7 4.9 %collective-permute-start.4 = (f32[8,6,16,128]{3,2,1,0:T(8,128)S(1)}, f32[8,6,16,128]{3,2,1,0:T(8,128)S(1)}, u32[]{:S(2)}, u32[]{:S(2)}) collective-permute-start(f32[8,6,16,128]{3,2,1,0:T(8,128)S(1)} %get-tuple-element.48), channel_id=1, source_target_pairs={{0,16},{16,0},{32,48},{48,32},{64,80},{80,64},{96,112},{112,96},{1... | collective-permute-start | bytes 1179656 | tf_op jit(solution)/shard_map/ppermute | solution.py:409
  19.6 6.4 %collective-permute-start.5 = (f32[192,128]{1,0:T(8,128)S(1)}, f32[192,128]{1,0:T(8,128)S(1)}, u32[]{:S(2)}, u32[]{:S(2)}) collective-permute-start(f32[192,128]{1,0:T(8,128)S(1)} %get-tuple-element.50), channel_id=1, source_target_pairs={{0,64},{16,80},{32,96},{48,112},{64,0},{80,16},{96,32},{112,48},{1... | collective-permute-start | bytes 294920 | tf_op jit(solution)/shard_map/ppermute | solution.py:409
  22.9 4.6 %collective-permute-start.6 = (f32[192,128]{1,0:T(8,128)S(1)}, f32[192,128]{1,0:T(8,128)S(1)}, u32[]{:S(2)}, u32[]{:S(2)}) collective-permute-start(f32[192,128]{1,0:T(8,128)S(1)} %get-tuple-element.51), channel_id=1, source_target_pairs={{0,32},{16,48},{32,0},{48,16},{64,96},{80,112},{96,64},{112,80},{1... | collective-permute-start | bytes 294920 | tf_op jit(solution)/shard_map/ppermute | solution.py:409
  23.6 5.8 %collective-permute-start.7 = (f32[192,128]{1,0:T(8,128)S(1)}, f32[192,128]{1,0:T(8,128)S(1)}, u32[]{:S(2)}, u32[]{:S(2)}) collective-permute-start(f32[192,128]{1,0:T(8,128)S(1)} %get-tuple-element.52), channel_id=1, source_target_pairs={{0,96},{16,112},{32,64},{48,80},{64,32},{80,48},{96,0},{112,16},{1... | collective-permute-start | bytes 294920 | tf_op jit(solution)/shard_map/ppermute | solution.py:409
  24.0 7.6 %collective-permute-start.9 = (f32[192,128]{1,0:T(8,128)S(1)}, f32[192,128]{1,0:T(8,128)S(1)}, u32[]{:S(2)}, u32[]{:S(2)}) collective-permute-start(f32[192,128]{1,0:T(8,128)S(1)} %get-tuple-element.55), channel_id=1, source_target_pairs={{0,1},{1,2},{2,3},{3,4},{4,5},{5,6},{6,7},{7,8},{8,9},{9,10},{10,1... | collective-permute-start | bytes 294920 | tf_op jit(solution)/shard_map/ppermute | solution.py:412
  24.8 6.8 %collective-permute-start.10 = (f32[192,128]{1,0:T(8,128)S(1)}, f32[192,128]{1,0:T(8,128)S(1)}, u32[]{:S(2)}, u32[]{:S(2)}) collective-permute-start(f32[192,128]{1,0:T(8,128)S(1)} %get-tuple-element.56), channel_id=1, source_target_pairs={{1,0},{2,1},{3,2},{4,3},{5,4},{6,5},{7,6},{8,7},{9,8},{10,9},{11,1... | collective-permute-start | bytes 294920 | tf_op jit(solution)/shard_map/ppermute | solution.py:412
  29.5 6.4 %collective-permute-start.8 = (f32[192,128]{1,0:T(8,128)S(1)}, f32[192,128]{1,0:T(8,128)S(1)}, u32[]{:S(2)}, u32[]{:S(2)}) collective-permute-start(f32[192,128]{1,0:T(8,128)S(1)} %add_add_fusion.mine), channel_id=1, source_target_pairs={{0,128},{16,144},{32,160},{48,176},{64,192},{80,208},{96,224},{112... | collective-permute-start | bytes 294920 | tf_op jit(solution)/shard_map/ppermute | solution.py:409
  35.9 6.2 %collective-permute-start.13 = (f32[192,128]{1,0:T(8,128)S(1)}, f32[192,128]{1,0:T(8,128)S(1)}, u32[]{:S(2)}, u32[]{:S(2)}) collective-permute-start(f32[192,128]{1,0:T(8,128)S(1)} %get-tuple-element.59.g0.grad), channel_id=1, source_target_pairs={{0,64},{16,80},{32,96},{48,112},{64,0},{80,16},{96,32},{112,48},{1... | collective-permute-start | bytes 294920 | tf_op jit(solution)/shard_map/ppermute | solution.py:409
  36.7 5.5 %collective-permute-start.12 = (f32[192,128]{1,0:T(8,128)S(1)}, f32[192,128]{1,0:T(8,128)S(1)}, u32[]{:S(2)}, u32[]{:S(2)}) collective-permute-start(f32[192,128]{1,0:T(8,128)S(1)} %get-tuple-element.59.g0.grad), channel_id=1, source_target_pairs={{0,32},{16,48},{32,0},{48,16},{64,96},{80,112},{96,64},{112,80},{1... | collective-permute-start | bytes 294920 | tf_op jit(solution)/shard_map/ppermute | solution.py:409
  37.4 5.8 %collective-permute-start.11 = (f32[192,128]{1,0:T(8,128)S(1)}, f32[192,128]{1,0:T(8,128)S(1)}, u32[]{:S(2)}, u32[]{:S(2)}) collective-permute-start(f32[192,128]{1,0:T(8,128)S(1)} %get-tuple-element.59.g0.grad), channel_id=1, source_target_pairs={{0,96},{16,112},{32,64},{48,80},{64,32},{80,48},{96,0},{112,16},{1... | collective-permute-start | bytes 294920 | tf_op jit(solution)/shard_map/ppermute | solution.py:409
  40.1 4.2 %collective-permute-start.17 = (f32[120,128]{1,0:T(8,128)S(1)}, f32[120,128]{1,0:T(8,128)S(1)}, u32[]{:S(2)}, u32[]{:S(2)}) collective-permute-start(f32[120,128]{1,0:T(8,128)S(1)} %get-tuple-element.64), channel_id=1, source_target_pairs={{0,1},{1,2},{2,3},{3,4},{4,5},{5,6},{6,7},{7,8},{8,9},{9,10},{10,1... | collective-permute-start | bytes 184328 | tf_op jit(solution)/shard_map/ppermute | solution.py:412
  41.0 6.4 %collective-permute-start.18 = (f32[120,128]{1,0:T(8,128)S(1)}, f32[120,128]{1,0:T(8,128)S(1)}, u32[]{:S(2)}, u32[]{:S(2)}) collective-permute-start(f32[120,128]{1,0:T(8,128)S(1)} %get-tuple-element.65), channel_id=1, source_target_pairs={{1,0},{2,1},{3,2},{4,3},{5,4},{6,5},{7,6},{8,7},{9,8},{10,9},{11,1... | collective-permute-start | bytes 184328 | tf_op jit(solution)/shard_map/ppermute | solution.py:412
  43.2 6.4 %collective-permute-start.14 = (f32[768,128]{1,0:T(8,128)S(1)}, f32[768,128]{1,0:T(8,128)S(1)}, u32[]{:S(2)}, u32[]{:S(2)}) collective-permute-start(f32[768,128]{1,0:T(8,128)S(1)} %join.1), channel_id=1, source_target_pairs={{0,16},{16,0},{32,48},{48,32},{64,80},{80,64},{96,112},{112,96},{1... | collective-permute-start | bytes 1179656 | tf_op jit(solution)/shard_map/ppermute | solution.py:409
  47.5 5.6 %collective-permute-start.19 = (f32[144,128]{1,0:T(8,128)S(1)}, f32[144,128]{1,0:T(8,128)S(1)}, u32[]{:S(2)}, u32[]{:S(2)}) collective-permute-start(f32[144,128]{1,0:T(8,128)S(1)} %get-tuple-element.68), channel_id=1, source_target_pairs={{0,1},{1,2},{2,3},{3,4},{4,5},{5,6},{6,7},{7,8},{8,9},{9,10},{10,1... | collective-permute-start | bytes 221192 | tf_op jit(solution)/shard_map/ppermute | solution.py:412
  47.6 4.4 %copy-start.4 = (f32[6,1,16,128]{3,2,1,0:T(8,128)S(1)}, f32[6,1,16,128]{3,2,1,0:T(8,128)}, u32[]{:S(2)}) copy-start(f32[6,1,16,128]{3,2,1,0:T(8,128)} %param.15) | copy-start | bytes 147460
  47.6 6.6 %collective-permute-start.20 = (f32[144,128]{1,0:T(8,128)S(1)}, f32[144,128]{1,0:T(8,128)S(1)}, u32[]{:S(2)}, u32[]{:S(2)}) collective-permute-start(f32[144,128]{1,0:T(8,128)S(1)} %get-tuple-element.69), channel_id=1, source_target_pairs={{1,0},{2,1},{3,2},{4,3},{5,4},{6,5},{7,6},{8,7},{9,8},{10,9},{11,1... | collective-permute-start | bytes 221192 | tf_op jit(solution)/shard_map/ppermute | solution.py:412
  49.7 6.5 %collective-permute-start.15 = (f32[192,128]{1,0:T(8,128)S(1)}, f32[192,128]{1,0:T(8,128)S(1)}, u32[]{:S(2)}, u32[]{:S(2)}) collective-permute-start(f32[192,128]{1,0:T(8,128)S(1)} %get-tuple-element.60), channel_id=1, source_target_pairs={{0,1},{1,2},{2,3},{3,4},{4,5},{5,6},{6,7},{7,8},{8,9},{9,10},{10,1... | collective-permute-start | bytes 294920 | tf_op jit(solution)/shard_map/ppermute | solution.py:412
  52.0 6.7 %collective-permute-start.16 = (f32[192,128]{1,0:T(8,128)S(1)}, f32[192,128]{1,0:T(8,128)S(1)}, u32[]{:S(2)}, u32[]{:S(2)}) collective-permute-start(f32[192,128]{1,0:T(8,128)S(1)} %get-tuple-element.61), channel_id=1, source_target_pairs={{1,0},{2,1},{3,2},{4,3},{5,4},{6,5},{7,6},{8,7},{9,8},{10,9},{11,1... | collective-permute-start | bytes 294920 | tf_op jit(solution)/shard_map/ppermute | solution.py:412
  52.0 2.2 %copy-start.2 = (f32[2,16,16,128]{3,2,1,0:T(8,128)S(1)}, f32[2,16,16,128]{3,2,1,0:T(8,128)}, u32[]{:S(2)}) copy-start(f32[2,16,16,128]{3,2,1,0:T(8,128)} %param.13) | copy-start | bytes 786436

commit v9 on v8

--- a/solution.py
+++ b/solution.py
@@ -269,27 +269,27 @@
 
 
 def gradient_body(mine, other, static, sums, perturb, grad, forward, backward, middle):
-    x, _, c = place()
+    c = lax.axis_index("mem") % 2
     total = mine[...] + other[...] + static[...]
     grad[...] = sums[0:192, :] * total - sums[192:384, :]
     project(grad, 0, c, perturb, middle)
-    pack_rows(lambda row: grad[pl.ds(x * 96 + row, VARS, stride=ROWS), :], VARS, forward, backward)
-    pack_rows(lambda row: middle[pl.ds(row, 4, stride=ROWS), :], 4, forward, backward, 72)
-
-
-def join_body(g3, g1, g2, g0, out):
+    pack_rows(lambda row: middle[pl.ds(row, 4, stride=ROWS), :], 4, forward, backward)
+
+
+def join_body(g2, g1, g3, g0, out):
     for k, g in enumerate((g0, g1, g2, g3)):
         out[k * 192 : k * 192 + 192, :] = g[...]
 
 
-def project_own_body(g3, g1, g2, perturb, start, low, high, forward, backward, middle, low_out, high_out):
-    c = lax.axis_index("mem") % 2
+def project_own_body(g2, g1, g3, g0, perturb, start, low, high, forward, backward, middle, low_out, high_out):
+    x, _, c = place()
     low_out[...] = low[...]
     high_out[...] = high[...]
     middle[0:64, :] = start[...]
     for k, g in ((1, g1), (2, g2), (3, g3)):
         project(g, k, c, perturb, middle)
     pack_rows(lambda row: middle[pl.ds(64 + row, 12, stride=ROWS), :], 12, forward, backward)
+    pack_rows(lambda row: g0[pl.ds(x * 96 + row, VARS, stride=ROWS), :], VARS, forward, backward, 144)
 
 
 def project_other_body(rest, perturb, forward, backward, middle):
@@ -325,7 +325,7 @@
             buf0[at : at + 16, :] = middle[pl.ds(row - STEPS, 16, stride=ROWS), :]
         else:
             near, far, k = (early_low, low, row) if row < STEPS else (early_high, high, row - STEPS - ROWS)
-            buf0[at : at + 4, :] = near[72 + k * 4 : 76 + k * 4, :]
+            buf0[at : at + 4, :] = near[k * 4 : k * 4 + 4, :]
             buf0[at + 4 : at + 16, :] = far[k * 12 : k * 12 + 12, :]
 
     def emit(row, value):
@@ -337,7 +337,7 @@
 
 def static_last_body(low, high, grad, coefs, field, static_mom, after, new_static, new_static_mom, buf0, buf1, out):
     x, _, _ = place()
-    load = halo_loader(low, high, lambda row: grad[pl.ds(x * 96 + row, VARS, stride=ROWS), :], VARS)
+    load = halo_loader(low, high, lambda row: grad[pl.ds(x * 96 + row, VARS, stride=ROWS), :], VARS, 144)
     for row in range(SPAN):
         buf0[row * 8 : row * 8 + VARS, :] = load(row)
 
@@ -471,29 +471,29 @@
         [raw] + bufs16 + [f32(256, LANES)],
         flops=BUSY,
     )(c_low, c_high, field)
-    early = shape(120, LANES)
+    early = shape(48, LANES)
     grad, g_f, g_b, start = call(
         gradient_body, "gradient", [VM] * 5, [quarter, early, early, shape(64, LANES)]
     )(mine, other, static, sums, perturb)
     g2, g1, g3 = swap(grad, 4), swap(grad, 2), swap(grad, 6)
     g_low, g_high = halo(g_f, g_b)
-    far = shape(144, LANES)
-    (rest,) = call(join_body, "join", [VM] * 4, [shape(768, LANES)], flops=0)(g3, g1, g2, grad)
+    far = shape(216, LANES)
+    (rest,) = call(join_body, "join", [VM] * 4, [shape(768, LANES)], flops=0)(g2, g1, g3, grad)
     rest = swap(rest, 1)
     p_f, p_b, p_m, g_low, g_high = call(
         project_own_body,
         "project_own",
-        [VM] * 7,
+        [VM] * 8,
         [far, far, half, early, early],
         flops=BUSY,
-    )(g3, g1, g2, perturb, start, g_low, g_high)
+    )(g2, g1, g3, grad, perturb, start, g_low, g_high)
     p_low, p_high = halo(p_f, p_b)
     q_f, q_b, q_m = call(project_other_body, "project_other", [VM] * 2, [quarter, quarter, half])(rest, perturb)
     q_low, q_high = halo(q_f, q_b)
     whole = shape(2, HALF, 2, ROWS, LANES)
     work = bufs16 + [f32(256, LANES)]
     static_ready = call(static_last_body, "static_last", [VM] * 7, [shape(96, LANES)] * 2, work, flops=BUSY)(
-        g_low, g_high, grad, static_k, field, static_mom.reshape(96, LANES), q_m
+        p_low, p_high, grad, static_k, field, static_mom.reshape(96, LANES), q_m
     )
     ready = call(third_body, "third", [VM] * 9, [half, half], work, flops=BUSY)(
         g_low, g_high, p_low, p_high, p_m, loc_k, alpha2, mom2, q_m

time: 61.4 us -> 65.2 us (1.062)
  the two profiles are of different devices: /device:TPU:102 before, /device:TPU:66 now
where the time goes in v9:
time: 65.2 us; the launch traced here: 65 us
  starting transfers between devices  29.3 us (45%)
  waiting for transfers between devices  19.3 us (30%)
  Pallas kernels  14.6 us (22%)
  between operations  1.03 us (2%)
  local copies, waits for them, and re-layouts  0.75 us (1%)
    ppermute x6, starting transfers between devices, halo(): lax.ppermute(forward, 'tile', up)  15.8 us
    ppermute x9, starting transfers between devices, swap(): return lax.ppermute(value, 'mem', [(i, i ^ bits) for i in range(members)])  11.9 us
    ppermute x6, waiting for transfers between devices, halo(): lax.ppermute(forward, 'tile', up)  9.8 us
    ppermute x6, waiting for transfers between devices, halo(): lax.ppermute(backward, 'tile', down)  7 us
    ppermute x9, waiting for transfers between devices, swap(): return lax.ppermute(value, 'mem', [(i, i ^ bits) for i in range(members)])  2.5 us
    pallas_call x1, Pallas kernels, local(): call(fourth_body, 'fourth', [VM] * 10, [whole, whole, shape(96, LANES), s...  2.37 us
    pallas_call x1, Pallas kernels, local(): call(pack_body, 'pack', [HBM] * 2, [shape(216, LANES)] * 2, [f32(512, LAN...  1.73 us
    ppermute x6, starting transfers between devices, halo(): lax.ppermute(backward, 'tile', down)  1.69 us
  transfers between devices with their start and end apart: 21, of which 10 were waited for; matrix products, arithmetic and copies ran while one was open for 0% of the time, Pallas kernels for 17%

profile of v9, /device:TPU:66, one launch (start us, length us, event | category | flops | bytes accessed | tf_op | source)
XLA Modules:
  0.0 65.0 jit_solution(17809455731230966245)
XLA Ops:
  0.6 0.0 copy-start.5
  0.6 0.7 %copy-done.5 = f32[2,16,128]{2,1,0:T(8,128)S(1)} copy-done((f32[2,16,128]{2,1,0:T(8,128)S(1)}, f32[2,16,128]{2,1,0:T(8,128)}, u32[]{:S(2)}) %copy-start.5) | copy-done | bytes 16408
  1.4 1.2 %fetch.1 = (f32[192,128]{1,0:T(8,128)S(1)}, f32[192,128]{1,0:T(8,128)S(1)}, f32[192,128]{1,0:T(8,128)S(1)}, f32[192,128]{1,0:T(8,128)S(1)}, f32[256,128]{1,0:T(8,128)S(1)}, /*index=5*/f32[192,128]{1,0:T(8,128)S(1)}) custom-call(f32[512,128]{1,0:T(8,128)} %bitcast.17, f32[6,16,8,128]{3,2,1,0:T(8,128)} %bitcast.31, f32[6,16,8,128]{3,2,1,0:T(8,128)} %bitcast.32, ...), custom_call_target="tpu_custom_call" | custom-call | flops 5000000000 | bytes 1000000 | tf_op jit(solution)/shard_map/fetch/pallas_call | solution.py:431
  2.5 2.0 %collective-permute-start = (f32[192,128]{1,0:T(8,128)S(1)}, f32[192,128]{1,0:T(8,128)S(1)}, u32[]{:S(2)}, u32[]{:S(2)}) collective-permute-start(f32[192,128]{1,0:T(8,128)S(1)} %get-tuple-element.42), channel_id=1, source_target_pairs={{0,1},{1,2},{2,3},{3,4},{4,5},{5,6},{6,7},{7,8},{8,9},{9,10},{10,1... | collective-permute-start | bytes 294920 | tf_op jit(solution)/shard_map/ppermute | solution.py:412
  4.5 0.1 collective-permute-start.1
  4.6 1.7 %pack.1 = (f32[216,128]{1,0:T(8,128)}, f32[216,128]{1,0:T(8,128)}) custom-call(f32[512,128]{1,0:T(8,128)} %bitcast.18, f32[32,128]{1,0:T(8,128)} %bitcast.25), custom_call_target="tpu_custom_call" | custom-call | flops 1000000 | bytes 1000000 | tf_op jit(solution)/shard_map/pack/pallas_call | solution.py:422
  6.4 0.0 copy-start.7
  6.4 0.0 copy-start.6
  6.4 2.9 %collective-permute-start.2 = (f32[216,128]{1,0:T(8,128)}, f32[216,128]{1,0:T(8,128)S(1)}, u32[]{:S(2)}, u32[]{:S(2)}) collective-permute-start(f32[216,128]{1,0:T(8,128)} %get-tuple-element.44), channel_id=1, source_target_pairs={{0,1},{1,2},{2,3},{3,4},{4,5},{5,6},{6,7},{7,8},{8,9},{9,10},{10,1... | collective-permute-start | bytes 331784 | tf_op jit(solution)/shard_map/ppermute | solution.py:412
  9.2 0.0 collective-permute-start.3
  9.3 0.0 copy-start
  9.3 0.0 copy-start.1
  9.3 0.0 copy-start.3
  9.3 1.4 %prepare.1.ready.sums = f32[384,128]{1,0:T(8,128)S(1)} custom-call(s32[8,128]{1,0:T(8,128)S(1)} %bitcast.29, s32[8,128]{1,0:T(8,128)S(1)} %bitcast.30, f32[192,128]{1,0:T(8,128)S(1)} %get-tuple-element.46.held), custom_call_target="tpu_custom_call" | custom-call | flops 5000000000 | bytes 1000000 | tf_op jit(solution)/shard_map/prepare/pallas_call | solution.py:447
  10.7 2.6 %collective-permute-done.2.low = f32[216,128]{1,0:T(8,128)S(1)} collective-permute-done((f32[216,128]{1,0:T(8,128)}, f32[216,128]{1,0:T(8,128)S(1)}, u32[]{:S(2)}, u32[]{:S(2)}) %collective-permute-start.2) | collective-permute-done | bytes 110624 | tf_op jit(solution)/shard_map/ppermute | solution.py:412
  13.3 1.8 %collective-permute-done.3.high = f32[216,128]{1,0:T(8,128)S(1)} collective-permute-done((f32[216,128]{1,0:T(8,128)}, f32[216,128]{1,0:T(8,128)S(1)}, u32[]{:S(2)}, u32[]{:S(2)}) %collective-permute-start.3) | collective-permute-done | bytes 110624 | tf_op jit(solution)/shard_map/ppermute | solution.py:412
  15.1 0.0 copy-done
  15.1 0.0 copy-done.3
  15.1 1.7 %first.1 = (f32[8,6,16,128]{3,2,1,0:T(8,128)S(1)}, f32[200,128]{1,0:T(8,128)S(1)}) custom-call(f32[512,128]{1,0:T(8,128)S(1)} %bitcast.19, f32[216,128]{1,0:T(8,128)S(1)} %collective-permute-done.2.low, f32[216,128]{1,0:T(8,128)S(1)} %collective-permute-done.3.high, f32[32,128]{1,0:T(8,128)S(1)} %bitcast.26, bf16[2,6,16,16,128]{4,3,2,1,0:T(8,128)(2,1)S(1)} %copy-done, ...), custom_call_target="tpu_custom_call" | custom-call | flops 5000000000 | bytes 1000000 | tf_op jit(solution)/shard_map/first/pallas_call | solution.py:451
  16.8 0.1 collective-permute-start.4
  16.9 0.0 collective-permute-done.low
  16.9 0.0 collective-permute-done.1.high
  16.9 1.5 %second.1.local = f32[256,128]{1,0:T(8,128)S(1)} custom-call(f32[512,128]{1,0:T(8,128)S(1)} %bitcast.20, f32[192,128]{1,0:T(8,128)S(1)} %collective-permute-done.low, f32[192,128]{1,0:T(8,128)S(1)} %collective-permute-done.1.high, f32[200,128]{1,0:T(8,128)S(1)} %get-tuple-element.47.coefs), custom_call_target="tpu_custom_call" | custom-call | flops 5000000000 | bytes 1000000 | tf_op jit(solution)/shard_map/second/pallas_call | solution.py:460
  18.4 0.2 collective-permute-done.4.received
  18.6 0.1 sum.1
  18.7 3.1 %collective-permute-start.7 = (f32[192,128]{1,0:T(8,128)S(1)}, f32[192,128]{1,0:T(8,128)S(1)}, u32[]{:S(2)}, u32[]{:S(2)}) collective-permute-start(f32[192,128]{1,0:T(8,128)S(1)} %get-tuple-element.52), channel_id=1, source_target_pairs={{0,96},{16,112},{32,64},{48,80},{64,32},{80,48},{96,0},{112,16},{1... | collective-permute-start | bytes 294920 | tf_op jit(solution)/shard_map/ppermute | solution.py:409
  21.8 0.1 collective-permute-start.6
  21.9 1.5 %collective-permute-start.5 = (f32[192,128]{1,0:T(8,128)S(1)}, f32[192,128]{1,0:T(8,128)S(1)}, u32[]{:S(2)}, u32[]{:S(2)}) collective-permute-start(f32[192,128]{1,0:T(8,128)S(1)} %get-tuple-element.50), channel_id=1, source_target_pairs={{0,64},{16,80},{32,96},{48,112},{64,0},{80,16},{96,32},{112,48},{1... | collective-permute-start | bytes 294920 | tf_op jit(solution)/shard_map/ppermute | solution.py:409
  23.5 2.9 %collective-permute-start.9 = (f32[192,128]{1,0:T(8,128)S(1)}, f32[192,128]{1,0:T(8,128)S(1)}, u32[]{:S(2)}, u32[]{:S(2)}) collective-permute-start(f32[192,128]{1,0:T(8,128)S(1)} %get-tuple-element.55), channel_id=1, source_target_pairs={{0,1},{1,2},{2,3},{3,4},{4,5},{5,6},{6,7},{7,8},{8,9},{9,10},{10,1... | collective-permute-start | bytes 294920 | tf_op jit(solution)/shard_map/ppermute | solution.py:412
  26.4 0.0 collective-permute-start.10
  26.4 0.0 collective-permute-done.7
  26.4 1.1 %collective-permute-done.6 = f32[192,128]{1,0:T(8,128)S(1)} collective-permute-done((f32[192,128]{1,0:T(8,128)S(1)}, f32[192,128]{1,0:T(8,128)S(1)}, u32[]{:S(2)}, u32[]{:S(2)}) %collective-permute-start.6) | collective-permute-done | bytes 98336 | tf_op jit(solution)/shard_map/ppermute | solution.py:409
  27.4 1.0 %collective-permute-done.5 = f32[192,128]{1,0:T(8,128)S(1)} collective-permute-done((f32[192,128]{1,0:T(8,128)S(1)}, f32[192,128]{1,0:T(8,128)S(1)}, u32[]{:S(2)}, u32[]{:S(2)}) %collective-permute-start.5) | collective-permute-done | bytes 98336 | tf_op jit(solution)/shard_map/ppermute | solution.py:409
  28.5 2.7 %collective-permute-start.8 = (f32[192,128]{1,0:T(8,128)S(1)}, f32[192,128]{1,0:T(8,128)S(1)}, u32[]{:S(2)}, u32[]{:S(2)}) collective-permute-start(f32[192,128]{1,0:T(8,128)S(1)} %add_add_fusion.mine), channel_id=1, source_target_pairs={{0,128},{16,144},{32,160},{48,176},{64,192},{80,208},{96,224},{112... | collective-permute-start | bytes 294920 | tf_op jit(solution)/shard_map/ppermute | solution.py:409
  31.2 0.0 collective-permute-done.9.low
  31.2 2.0 %collective-permute-done.10.high = f32[192,128]{1,0:T(8,128)S(1)} collective-permute-done((f32[192,128]{1,0:T(8,128)S(1)}, f32[192,128]{1,0:T(8,128)S(1)}, u32[]{:S(2)}, u32[]{:S(2)}) %collective-permute-start.10) | collective-permute-done | bytes 98336 | tf_op jit(solution)/shard_map/ppermute | solution.py:412
  33.2 1.6 %static_first.1 = (f32[192,128]{1,0:T(8,128)S(1)}, f32[200,128]{1,0:T(8,128)S(1)}) custom-call(f32[192,128]{1,0:T(8,128)S(1)} %collective-permute-done.9.low, f32[192,128]{1,0:T(8,128)S(1)} %collective-permute-done.10.high, f32[256,128]{1,0:T(8,128)S(1)} %get-tuple-element.57.field), custom_call_target="tpu_custom_call" | custom-call | flops 5000000000 | bytes 1000000 | tf_op jit(solution)/shard_map/static_first/pallas_call | solution.py:466
  34.7 0.2 collective-permute-done.8.other
  34.9 0.1 gradient.1
  35.0 2.1 %collective-permute-start.11 = (f32[192,128]{1,0:T(8,128)S(1)}, f32[192,128]{1,0:T(8,128)S(1)}, u32[]{:S(2)}, u32[]{:S(2)}) collective-permute-start(f32[192,128]{1,0:T(8,128)S(1)} %get-tuple-element.59.g0.grad), channel_id=1, source_target_pairs={{0,64},{16,80},{32,96},{48,112},{64,0},{80,16},{96,32},{112,48},{1... | collective-permute-start | bytes 294920 | tf_op jit(solution)/shard_map/ppermute | solution.py:409
  37.0 1.8 %collective-permute-start.12 = (f32[192,128]{1,0:T(8,128)S(1)}, f32[192,128]{1,0:T(8,128)S(1)}, u32[]{:S(2)}, u32[]{:S(2)}) collective-permute-start(f32[192,128]{1,0:T(8,128)S(1)} %get-tuple-element.59.g0.grad), channel_id=1, source_target_pairs={{0,32},{16,48},{32,0},{48,16},{64,96},{80,112},{96,64},{112,80},{1... | collective-permute-start | bytes 294920 | tf_op jit(solution)/shard_map/ppermute | solution.py:409
  38.8 0.4 collective-permute-start.13
  39.2 5.4 %collective-permute-start.17 = (f32[48,128]{1,0:T(8,128)S(1)}, f32[48,128]{1,0:T(8,128)S(1)}, u32[]{:S(2)}, u32[]{:S(2)}) collective-permute-start(f32[48,128]{1,0:T(8,128)S(1)} %get-tuple-element.64), channel_id=1, source_target_pairs={{0,1},{1,2},{2,3},{3,4},{4,5},{5,6},{6,7},{7,8},{8,9},{9,10},{10,1... | collective-permute-start | bytes 73736 | tf_op jit(solution)/shard_map/ppermute | solution.py:412
  44.6 0.0 collective-permute-start.18
  44.6 0.0 collective-permute-done.11.g2
  44.6 0.0 collective-permute-done.12.g1
  44.6 0.0 collective-permute-done.13.g3
  44.7 0.1 collective-permute-start.14
  44.8 1.3 %collective-permute-done.17.low = f32[48,128]{1,0:T(8,128)S(1)} collective-permute-done((f32[48,128]{1,0:T(8,128)S(1)}, f32[48,128]{1,0:T(8,128)S(1)}, u32[]{:S(2)}, u32[]{:S(2)}) %collective-permute-start.17) | collective-permute-done | bytes 24608 | tf_op jit(solution)/shard_map/ppermute | solution.py:412
  46.1 3.2 %collective-permute-done.18.high = f32[48,128]{1,0:T(8,128)S(1)} collective-permute-done((f32[48,128]{1,0:T(8,128)S(1)}, f32[48,128]{1,0:T(8,128)S(1)}, u32[]{:S(2)}, u32[]{:S(2)}) %collective-permute-start.18) | collective-permute-done | bytes 24608 | tf_op jit(solution)/shard_map/ppermute | solution.py:412
  49.3 0.1 project_own.1
  49.4 0.9 %collective-permute-start.19 = (f32[216,128]{1,0:T(8,128)S(1)}, f32[216,128]{1,0:T(8,128)S(1)}, u32[]{:S(2)}, u32[]{:S(2)}) collective-permute-start(f32[216,128]{1,0:T(8,128)S(1)} %get-tuple-element.68), channel_id=1, source_target_pairs={{0,1},{1,2},{2,3},{3,4},{4,5},{5,6},{6,7},{7,8},{8,9},{9,10},{10,1... | collective-permute-start | bytes 331784 | tf_op jit(solution)/shard_map/ppermute | solution.py:412
  50.3 1.2 %collective-permute-start.20 = (f32[216,128]{1,0:T(8,128)S(1)}, f32[216,128]{1,0:T(8,128)S(1)}, u32[]{:S(2)}, u32[]{:S(2)}) collective-permute-start(f32[216,128]{1,0:T(8,128)S(1)} %get-tuple-element.69), channel_id=1, source_target_pairs={{1,0},{2,1},{3,2},{4,3},{5,4},{6,5},{7,6},{8,7},{9,8},{10,9},{11,1... | collective-permute-start | bytes 331784 | tf_op jit(solution)/shard_map/ppermute | solution.py:412
  51.6 0.0 collective-permute-done.14.rest
  51.6 0.1 project_other.1
  51.7 1.8 %collective-permute-start.15 = (f32[192,128]{1,0:T(8,128)S(1)}, f32[192,128]{1,0:T(8,128)S(1)}, u32[]{:S(2)}, u32[]{:S(2)}) collective-permute-start(f32[192,128]{1,0:T(8,128)S(1)} %get-tuple-element.60), channel_id=1, source_target_pairs={{0,1},{1,2},{2,3},{3,4},{4,5},{5,6},{6,7},{7,8},{8,9},{9,10},{10,1... | collective-permute-start | bytes 294920 | tf_op jit(solution)/shard_map/ppermute | solution.py:412
  53.5 0.3 collective-permute-start.16
  53.8 5.9 %collective-permute-done.19.low = f32[216,128]{1,0:T(8,128)S(1)} collective-permute-done((f32[216,128]{1,0:T(8,128)S(1)}, f32[216,128]{1,0:T(8,128)S(1)}, u32[]{:S(2)}, u32[]{:S(2)}) %collective-permute-start.19) | collective-permute-done | bytes 110624 | tf_op jit(solution)/shard_map/ppermute | solution.py:412
  59.7 0.0 collective-permute-done.20.high
  59.7 1.1 %static_last.1 = (f32[96,128]{1,0:T(8,128)S(1)}, f32[96,128]{1,0:T(8,128)S(1)}) custom-call(f32[216,128]{1,0:T(8,128)S(1)} %collective-permute-done.19.low, f32[216,128]{1,0:T(8,128)S(1)} %collective-permute-done.20.high, f32[192,128]{1,0:T(8,128)S(1)} %get-tuple-element.59.g0.grad, f32[200,128]{1,0:T(8,128)S(1)} %get-tuple-element.73.coefs, ...), custom_call_target="tpu_custom_call" | custom-call | flops 5000000000 | bytes 1000000 | tf_op jit(solution)/shard_map/static_last/pallas_call | solution.py:495
  60.8 1.6 %third.1 = (f32[256,128]{1,0:T(8,128)S(1)}, f32[256,128]{1,0:T(8,128)S(1)}) custom-call(f32[48,128]{1,0:T(8,128)S(1)} %get-tuple-element.66.early_low, f32[48,128]{1,0:T(8,128)S(1)} %get-tuple-element.67.early_high, f32[216,128]{1,0:T(8,128)S(1)} %collective-permute-done.19.low, f32[216,128]{1,0:T(8,128)S(1)} %collective-permute-done.20.high, ...), custom_call_target="tpu_custom_call" | custom-call | flops 5000000000 | bytes 1000000 | tf_op jit(solution)/shard_map/third/pallas_call | solution.py:498
  62.4 0.0 collective-permute-done.15.low
  62.4 0.0 collective-permute-done.16.high
  62.5 2.4 %fourth.1 = (f32[2,8,2,16,128]{4,3,2,1,0:T(8,128)}, f32[2,8,2,16,128]{4,3,2,1,0:T(8,128)}, f32[96,128]{1,0:T(8,128)}, f32[96,128]{1,0:T(8,128)}) custom-call(f32[192,128]{1,0:T(8,128)S(1)} %collective-permute-done.15.low, f32[192,128]{1,0:T(8,128)S(1)} %collective-permute-done.16.high, f32[256,128]{1,0:T(8,128)S(1)} %get-tuple-element.62.after.middle, ...), custom_call_target="tpu_custom_call" | custom-call | flops 1000000 | bytes 1000000 | tf_op jit(solution)/shard_map/fourth/pallas_call | solution.py:501
  (9 shorter events, 0.1 us)
Async XLA Ops:
  0.6 0.7 %copy-start.5 = (f32[2,16,128]{2,1,0:T(8,128)S(1)}, f32[2,16,128]{2,1,0:T(8,128)}, u32[]{:S(2)}) copy-start(f32[2,16,128]{2,1,0:T(8,128)} %param.17) | copy-start | bytes 49156
  2.5 14.4 %collective-permute-start = (f32[192,128]{1,0:T(8,128)S(1)}, f32[192,128]{1,0:T(8,128)S(1)}, u32[]{:S(2)}, u32[]{:S(2)}) collective-permute-start(f32[192,128]{1,0:T(8,128)S(1)} %get-tuple-element.42), channel_id=1, source_target_pairs={{0,1},{1,2},{2,3},{3,4},{4,5},{5,6},{6,7},{7,8},{8,9},{9,10},{10,1... | collective-permute-start | bytes 294920 | tf_op jit(solution)/shard_map/ppermute | solution.py:412
  4.5 12.4 %collective-permute-start.1 = (f32[192,128]{1,0:T(8,128)S(1)}, f32[192,128]{1,0:T(8,128)S(1)}, u32[]{:S(2)}, u32[]{:S(2)}) collective-permute-start(f32[192,128]{1,0:T(8,128)S(1)} %get-tuple-element.43), channel_id=1, source_target_pairs={{1,0},{2,1},{3,2},{4,3},{5,4},{6,5},{7,6},{8,7},{9,8},{10,9},{11,1... | collective-permute-start | bytes 294920 | tf_op jit(solution)/shard_map/ppermute | solution.py:412
  6.4 2.9 %copy-start.7 = (s32[1,1024]{1,0:T(1,128)S(1)}, s32[1,1024]{1,0:T(1,128)}, u32[]{:S(2)}) copy-start(s32[1,1024]{1,0:T(1,128)} %param.19) | copy-start | bytes 12292
  6.4 2.9 %copy-start.6 = (s32[1,1024]{1,0:T(1,128)S(1)}, s32[1,1024]{1,0:T(1,128)}, u32[]{:S(2)}) copy-start(s32[1,1024]{1,0:T(1,128)} %param.18) | copy-start | bytes 12292
  6.4 6.9 %collective-permute-start.2 = (f32[216,128]{1,0:T(8,128)}, f32[216,128]{1,0:T(8,128)S(1)}, u32[]{:S(2)}, u32[]{:S(2)}) collective-permute-start(f32[216,128]{1,0:T(8,128)} %get-tuple-element.44), channel_id=1, source_target_pairs={{0,1},{1,2},{2,3},{3,4},{4,5},{5,6},{6,7},{7,8},{8,9},{9,10},{10,1... | collective-permute-start | bytes 331784 | tf_op jit(solution)/shard_map/ppermute | solution.py:412
  9.2 5.9 %collective-permute-start.3 = (f32[216,128]{1,0:T(8,128)}, f32[216,128]{1,0:T(8,128)S(1)}, u32[]{:S(2)}, u32[]{:S(2)}) collective-permute-start(f32[216,128]{1,0:T(8,128)} %get-tuple-element.45), channel_id=1, source_target_pairs={{1,0},{2,1},{3,2},{4,3},{5,4},{6,5},{7,6},{8,7},{9,8},{10,9},{11,1... | collective-permute-start | bytes 331784 | tf_op jit(solution)/shard_map/ppermute | solution.py:412
  9.3 5.8 %copy-start = (bf16[2,6,16,16,128]{4,3,2,1,0:T(8,128)(2,1)S(1)}, bf16[2,6,16,16,128]{4,3,2,1,0:T(8,128)(2,1)}, u32[]{:S(2)}) copy-start(bf16[2,6,16,16,128]{4,3,2,1,0:T(8,128)(2,1)} %perturb.9) | copy-start | bytes 2359300
  9.3 5.8 %copy-start.1 = (f32[2,16,16,128]{3,2,1,0:T(8,128)S(1)}, f32[2,16,16,128]{3,2,1,0:T(8,128)}, u32[]{:S(2)}) copy-start(f32[2,16,16,128]{3,2,1,0:T(8,128)} %param.12) | copy-start | bytes 786436
  9.3 5.8 %copy-start.3 = (f32[2,16,128]{2,1,0:T(8,128)S(1)}, f32[2,16,128]{2,1,0:T(8,128)}, u32[]{:S(2)}) copy-start(f32[2,16,128]{2,1,0:T(8,128)} %param.16) | copy-start | bytes 49156
  16.8 1.8 %collective-permute-start.4 = (f32[8,6,16,128]{3,2,1,0:T(8,128)S(1)}, f32[8,6,16,128]{3,2,1,0:T(8,128)S(1)}, u32[]{:S(2)}, u32[]{:S(2)}) collective-permute-start(f32[8,6,16,128]{3,2,1,0:T(8,128)S(1)} %get-tuple-element.48), channel_id=1, source_target_pairs={{0,16},{16,0},{32,48},{48,32},{64,80},{80,64},{96,112},{112,96},{1... | collective-permute-start | bytes 1179656 | tf_op jit(solution)/shard_map/ppermute | solution.py:409
  18.7 7.7 %collective-permute-start.7 = (f32[192,128]{1,0:T(8,128)S(1)}, f32[192,128]{1,0:T(8,128)S(1)}, u32[]{:S(2)}, u32[]{:S(2)}) collective-permute-start(f32[192,128]{1,0:T(8,128)S(1)} %get-tuple-element.52), channel_id=1, source_target_pairs={{0,96},{16,112},{32,64},{48,80},{64,32},{80,48},{96,0},{112,16},{1... | collective-permute-start | bytes 294920 | tf_op jit(solution)/shard_map/ppermute | solution.py:409
  21.8 5.6 %collective-permute-start.6 = (f32[192,128]{1,0:T(8,128)S(1)}, f32[192,128]{1,0:T(8,128)S(1)}, u32[]{:S(2)}, u32[]{:S(2)}) collective-permute-start(f32[192,128]{1,0:T(8,128)S(1)} %get-tuple-element.51), channel_id=1, source_target_pairs={{0,32},{16,48},{32,0},{48,16},{64,96},{80,112},{96,64},{112,80},{1... | collective-permute-start | bytes 294920 | tf_op jit(solution)/shard_map/ppermute | solution.py:409
  21.9 6.6 %collective-permute-start.5 = (f32[192,128]{1,0:T(8,128)S(1)}, f32[192,128]{1,0:T(8,128)S(1)}, u32[]{:S(2)}, u32[]{:S(2)}) collective-permute-start(f32[192,128]{1,0:T(8,128)S(1)} %get-tuple-element.50), channel_id=1, source_target_pairs={{0,64},{16,80},{32,96},{48,112},{64,0},{80,16},{96,32},{112,48},{1... | collective-permute-start | bytes 294920 | tf_op jit(solution)/shard_map/ppermute | solution.py:409
  23.5 7.7 %collective-permute-start.9 = (f32[192,128]{1,0:T(8,128)S(1)}, f32[192,128]{1,0:T(8,128)S(1)}, u32[]{:S(2)}, u32[]{:S(2)}) collective-permute-start(f32[192,128]{1,0:T(8,128)S(1)} %get-tuple-element.55), channel_id=1, source_target_pairs={{0,1},{1,2},{2,3},{3,4},{4,5},{5,6},{6,7},{7,8},{8,9},{9,10},{10,1... | collective-permute-start | bytes 294920 | tf_op jit(solution)/shard_map/ppermute | solution.py:412
  26.4 6.8 %collective-permute-start.10 = (f32[192,128]{1,0:T(8,128)S(1)}, f32[192,128]{1,0:T(8,128)S(1)}, u32[]{:S(2)}, u32[]{:S(2)}) collective-permute-start(f32[192,128]{1,0:T(8,128)S(1)} %get-tuple-element.56), channel_id=1, source_target_pairs={{1,0},{2,1},{3,2},{4,3},{5,4},{6,5},{7,6},{8,7},{9,8},{10,9},{11,1... | collective-permute-start | bytes 294920 | tf_op jit(solution)/shard_map/ppermute | solution.py:412
  28.5 6.4 %collective-permute-start.8 = (f32[192,128]{1,0:T(8,128)S(1)}, f32[192,128]{1,0:T(8,128)S(1)}, u32[]{:S(2)}, u32[]{:S(2)}) collective-permute-start(f32[192,128]{1,0:T(8,128)S(1)} %add_add_fusion.mine), channel_id=1, source_target_pairs={{0,128},{16,144},{32,160},{48,176},{64,192},{80,208},{96,224},{112... | collective-permute-start | bytes 294920 | tf_op jit(solution)/shard_map/ppermute | solution.py:409
  35.0 9.6 %collective-permute-start.11 = (f32[192,128]{1,0:T(8,128)S(1)}, f32[192,128]{1,0:T(8,128)S(1)}, u32[]{:S(2)}, u32[]{:S(2)}) collective-permute-start(f32[192,128]{1,0:T(8,128)S(1)} %get-tuple-element.59.g0.grad), channel_id=1, source_target_pairs={{0,64},{16,80},{32,96},{48,112},{64,0},{80,16},{96,32},{112,48},{1... | collective-permute-start | bytes 294920 | tf_op jit(solution)/shard_map/ppermute | solution.py:409
  37.0 7.5 %collective-permute-start.12 = (f32[192,128]{1,0:T(8,128)S(1)}, f32[192,128]{1,0:T(8,128)S(1)}, u32[]{:S(2)}, u32[]{:S(2)}) collective-permute-start(f32[192,128]{1,0:T(8,128)S(1)} %get-tuple-element.59.g0.grad), channel_id=1, source_target_pairs={{0,32},{16,48},{32,0},{48,16},{64,96},{80,112},{96,64},{112,80},{1... | collective-permute-start | bytes 294920 | tf_op jit(solution)/shard_map/ppermute | solution.py:409
  38.8 5.8 %collective-permute-start.13 = (f32[192,128]{1,0:T(8,128)S(1)}, f32[192,128]{1,0:T(8,128)S(1)}, u32[]{:S(2)}, u32[]{:S(2)}) collective-permute-start(f32[192,128]{1,0:T(8,128)S(1)} %get-tuple-element.59.g0.grad), channel_id=1, source_target_pairs={{0,96},{16,112},{32,64},{48,80},{64,32},{80,48},{96,0},{112,16},{1... | collective-permute-start | bytes 294920 | tf_op jit(solution)/shard_map/ppermute | solution.py:409
  39.2 6.9 %collective-permute-start.17 = (f32[48,128]{1,0:T(8,128)S(1)}, f32[48,128]{1,0:T(8,128)S(1)}, u32[]{:S(2)}, u32[]{:S(2)}) collective-permute-start(f32[48,128]{1,0:T(8,128)S(1)} %get-tuple-element.64), channel_id=1, source_target_pairs={{0,1},{1,2},{2,3},{3,4},{4,5},{5,6},{6,7},{7,8},{8,9},{9,10},{10,1... | collective-permute-start | bytes 73736 | tf_op jit(solution)/shard_map/ppermute | solution.py:412
  44.6 4.7 %collective-permute-start.18 = (f32[48,128]{1,0:T(8,128)S(1)}, f32[48,128]{1,0:T(8,128)S(1)}, u32[]{:S(2)}, u32[]{:S(2)}) collective-permute-start(f32[48,128]{1,0:T(8,128)S(1)} %get-tuple-element.65), channel_id=1, source_target_pairs={{1,0},{2,1},{3,2},{4,3},{5,4},{6,5},{7,6},{8,7},{9,8},{10,9},{11,1... | collective-permute-start | bytes 73736 | tf_op jit(solution)/shard_map/ppermute | solution.py:412
  44.7 6.9 %collective-permute-start.14 = (f32[768,128]{1,0:T(8,128)S(1)}, f32[768,128]{1,0:T(8,128)S(1)}, u32[]{:S(2)}, u32[]{:S(2)}) collective-permute-start(f32[768,128]{1,0:T(8,128)S(1)} %join.1), channel_id=1, source_target_pairs={{0,16},{16,0},{32,48},{48,32},{64,80},{80,64},{96,112},{112,96},{1... | collective-permute-start | bytes 1179656 | tf_op jit(solution)/shard_map/ppermute | solution.py:409
  49.4 10.2 %collective-permute-start.19 = (f32[216,128]{1,0:T(8,128)S(1)}, f32[216,128]{1,0:T(8,128)S(1)}, u32[]{:S(2)}, u32[]{:S(2)}) collective-permute-start(f32[216,128]{1,0:T(8,128)S(1)} %get-tuple-element.68), channel_id=1, source_target_pairs={{0,1},{1,2},{2,3},{3,4},{4,5},{5,6},{6,7},{7,8},{8,9},{9,10},{10,1... | collective-permute-start | bytes 331784 | tf_op jit(solution)/shard_map/ppermute | solution.py:412
  50.3 9.3 %copy-start.4 = (f32[6,1,16,128]{3,2,1,0:T(8,128)S(1)}, f32[6,1,16,128]{3,2,1,0:T(8,128)}, u32[]{:S(2)}) copy-start(f32[6,1,16,128]{3,2,1,0:T(8,128)} %param.15) | copy-start | bytes 147460
  50.3 9.3 %collective-permute-start.20 = (f32[216,128]{1,0:T(8,128)S(1)}, f32[216,128]{1,0:T(8,128)S(1)}, u32[]{:S(2)}, u32[]{:S(2)}) collective-permute-start(f32[216,128]{1,0:T(8,128)S(1)} %get-tuple-element.69), channel_id=1, source_target_pairs={{1,0},{2,1},{3,2},{4,3},{5,4},{6,5},{7,6},{8,7},{9,8},{10,9},{11,1... | collective-permute-start | bytes 331784 | tf_op jit(solution)/shard_map/ppermute | solution.py:412
  51.7 10.8 %collective-permute-start.15 = (f32[192,128]{1,0:T(8,128)S(1)}, f32[192,128]{1,0:T(8,128)S(1)}, u32[]{:S(2)}, u32[]{:S(2)}) collective-permute-start(f32[192,128]{1,0:T(8,128)S(1)} %get-tuple-element.60), channel_id=1, source_target_pairs={{0,1},{1,2},{2,3},{3,4},{4,5},{5,6},{6,7},{7,8},{8,9},{9,10},{10,1... | collective-permute-start | bytes 294920 | tf_op jit(solution)/shard_map/ppermute | solution.py:412
  53.5 9.0 %collective-permute-start.16 = (f32[192,128]{1,0:T(8,128)S(1)}, f32[192,128]{1,0:T(8,128)S(1)}, u32[]{:S(2)}, u32[]{:S(2)}) collective-permute-start(f32[192,128]{1,0:T(8,128)S(1)} %get-tuple-element.61), channel_id=1, source_target_pairs={{1,0},{2,1},{3,2},{4,3},{5,4},{6,5},{7,6},{8,7},{9,8},{10,9},{11,1... | collective-permute-start | bytes 294920 | tf_op jit(solution)/shard_map/ppermute | solution.py:412
  59.7 1.1 %copy-start.2 = (f32[2,16,16,128]{3,2,1,0:T(8,128)S(1)}, f32[2,16,16,128]{3,2,1,0:T(8,128)}, u32[]{:S(2)}) copy-start(f32[2,16,16,128]{3,2,1,0:T(8,128)} %param.13) | copy-start | bytes 786436
